TPU v7x, 32 devices: a whole 2x2x4 slice. The times are simulated.
32 devices in a mesh: wide: 8 (over y, x, core), narrow: 4 (over z).
Axes of the slice: x: 2, y: 2, z: 4, core: 2. Of those that a mesh axis runs over, the one named last changes fastest.
Arguments:
- samples: bfloat16 [256, 128, 768], P(('wide', 'narrow')), may hold values from -6 to 6
- cotangent: bfloat16 [256, 128, 768], P(('wide', 'narrow')), may hold values from -6 to 6
- visible: int32 [256], P(('wide', 'narrow')), may hold values from 8 to 128, as said below
- master_attn: float32 [2359296], P(('wide', 'narrow')), may hold values from -0.57735027 to 0.57735027
- first_attn: float32 [2359296], P(('wide', 'narrow')), may hold values from -192 to 192
- second_attn: float32 [2359296], P(('wide', 'narrow')), may hold values from 983.04 to 3932.16
- master_mlp: float32 [4718592], P(('wide', 'narrow')), may hold values from -0.14433757 to 0.14433757
- first_mlp: float32 [4718592], P(('wide', 'narrow')), may hold values from -192 to 192
- second_mlp: float32 [4718592], P(('wide', 'narrow')), may hold values from 983.04 to 3932.16
- master_small: float32 [9216], P(('wide', 'narrow')), may hold values from -1 to 2
- first_small: float32 [9216], P(('wide', 'narrow')), may hold values from -384 to 384
- second_small: float32 [9216], P(('wide', 'narrow')), may hold values from 4259.84 to 16384
Outputs:
- output: bfloat16 [256, 128, 768], P(('wide', 'narrow'))
- grad_samples: bfloat16 [256, 128, 768], P(('wide', 'narrow'))
- new_attn: float32 [2359296], P(('wide', 'narrow'))
- new_first_attn: float32 [2359296], P(('wide', 'narrow'))
- new_second_attn: float32 [2359296], P(('wide', 'narrow'))
- new_mlp: float32 [4718592], P(('wide', 'narrow'))
- new_first_mlp: float32 [4718592], P(('wide', 'narrow'))
- new_second_mlp: float32 [4718592], P(('wide', 'narrow'))
- new_small: float32 [9216], P(('wide', 'narrow'))
- new_first_small: float32 [9216], P(('wide', 'narrow'))
- new_second_small: float32 [9216], P(('wide', 'narrow'))
Inputs may be any that keep to these rules, and one draw needn't show every extreme that they name: Slots j < visible[s] of each sample are visible; the counts are heavy-tailed, and every draw has a sample with all 128 visible and one with 8.
All inputs are finite; a program needn't handle non-finite values.
Results may differ from a plain program's by a relative error of at most 0.013.
Values may be sent and summed in bfloat16 or wider, within the bound.
No kernel may reach another device: no remote copies, remote signals or barrier semaphores. Data moves between devices by JAX's collectives and lax.ppermute only.
A program may use at most 192 MiB of HBM per device.

v0:
```python
import math

import jax
import jax.numpy as jnp
from jax import lax
from jax.sharding import PartitionSpec as P

D = 768
FF = 3072
H = 12
HD = 64
STEP = 10


eps_norm = 1e-06
rate_matrix = 0.03
rate_small = 0.2
eps_adam = 1e-08
inv_root_two = 0.7071067811865476
inv_root_tau = 0.3989422804014327


def split_small(small):
    edges = [0, D, 2 * D, 3 * D, 4 * D, 5 * D, 6 * D, 7 * D, 7 * D + FF, 8 * D + FF]
    return [small[edges[i] : edges[i + 1]] for i in range(9)]


def standard(values):
    centre = values - jnp.mean(values, -1, keepdims=True)
    factor = lax.rsqrt(jnp.mean(centre * centre, -1, keepdims=True) + eps_norm)
    return (centre * factor, factor)


def norm_backward(grad, normed, factor, gain):
    grad_gain = jnp.sum(grad * normed, 0)
    grad_bias = jnp.sum(grad, 0)
    scaled = grad * gain
    inner_mean = jnp.mean(scaled * normed, -1, keepdims=True)
    grad_input = factor * (scaled - jnp.mean(scaled, -1, keepdims=True) - normed * inner_mean)
    return (grad_gain, grad_bias, grad_input)


def masked_scores(query, keys, key_mask):
    raw = jnp.einsum("sqhd,skhd->shqk", query, keys, preferred_element_type=jnp.float32) * (
        1.0 / math.sqrt(HD)
    )
    return jnp.where(key_mask, raw, -1e30)


def adamw(master, first, second, grad, decay, step_rate):
    first_new = 0.5 * first + 0.5 * grad
    second_new = 0.5 * second + 0.5 * grad * grad
    first_hat = first_new / (1.0 - 0.5**STEP)
    second_hat = second_new / (1.0 - 0.5**STEP)
    master_new = master - step_rate * (
        first_hat / (jnp.sqrt(second_hat) + eps_adam) + decay * master
    )
    return (master_new, first_new, second_new)


def on_device(
    samples,
    cotangent,
    visible,
    master_attn,
    first_attn,
    second_attn,
    master_mlp,
    first_mlp,
    second_mlp,
    master_small,
    first_small,
    second_small,
):
    count, length, width = samples.shape
    total_rows = count * length
    scale = 1.0 / math.sqrt(HD)
    attn_full, mlp_full, small_full = (
        lax.all_gather(master_attn.astype(jnp.bfloat16), ("wide", "narrow"), axis=0, tiled=True),
        lax.all_gather(master_mlp.astype(jnp.bfloat16), ("wide", "narrow"), axis=0, tiled=True),
        lax.all_gather(master_small.astype(jnp.bfloat16), ("wide", "narrow"), axis=0, tiled=True),
    )
    w_qkv = attn_full[: 3 * D * D].reshape(D, 3 * D)
    w_out = attn_full[3 * D * D :].reshape(D, D)
    (
        gain_one,
        bias_one,
        bias_query,
        bias_value,
        bias_out,
        gain_two,
        bias_two,
        bias_inner,
        bias_outer,
    ) = split_small(small_full.astype(jnp.float32))
    valid = jnp.arange(length)[None, :] < visible[:, None]
    key_mask = valid[:, None, None, :]
    row_mask = valid.reshape(total_rows, 1)
    rows = samples.astype(jnp.float32).reshape(total_rows, D)
    normed_one, factor_one = standard(rows)
    first_in = (normed_one * gain_one + bias_one).astype(jnp.bfloat16)
    shift = jnp.concatenate([bias_query, jnp.zeros_like(bias_query), bias_value])
    qkv = jnp.dot(first_in, w_qkv, preferred_element_type=jnp.float32) + shift
    qkv_low = qkv.astype(jnp.bfloat16).reshape(count, length, 3, H, HD)
    query = qkv_low[:, :, 0]
    keys = qkv_low[:, :, 1]
    values = qkv_low[:, :, 2]
    scores = masked_scores(query, keys, key_mask)
    top = jnp.max(scores, -1, keepdims=True)
    expo = jnp.exp(scores - top)
    totals = jnp.sum(expo, -1, keepdims=True)
    log_total = top + jnp.log(totals)
    probs_low = (expo / totals).astype(jnp.bfloat16)
    context = jnp.einsum("shqk,skhd->sqhd", probs_low, values, preferred_element_type=jnp.float32)
    context_low = context.astype(jnp.bfloat16).reshape(total_rows, D)
    middle = rows + jnp.dot(context_low, w_out, preferred_element_type=jnp.float32) + bias_out
    w_one = mlp_full[: D * FF].reshape(D, FF)
    w_two = mlp_full[D * FF :].reshape(FF, D)
    normed_two, factor_two = standard(middle)
    second_in = (normed_two * gain_two + bias_two).astype(jnp.bfloat16)
    inner = jnp.dot(second_in, w_one, preferred_element_type=jnp.float32) + bias_inner
    active = jax.nn.gelu(inner, approximate=False).astype(jnp.bfloat16)
    result = middle + jnp.dot(active, w_two, preferred_element_type=jnp.float32) + bias_outer
    output = jnp.where(row_mask, result, 0.0).reshape(count, length, D).astype(jnp.bfloat16)
    grad_result = jnp.where(row_mask, cotangent.astype(jnp.float32).reshape(total_rows, D), 0.0)
    grad_branch = grad_result.astype(jnp.bfloat16)
    grad_w_two = jnp.einsum("rf,rd->fd", active, grad_branch, preferred_element_type=jnp.float32)
    grad_bias_outer = jnp.sum(grad_branch, 0, dtype=jnp.float32)
    grad_active = jnp.einsum("rd,fd->rf", grad_branch, w_two, preferred_element_type=jnp.float32)
    slope = (
        0.5 * (1.0 + jax.scipy.special.erf(inner * inv_root_two))
        + inner * jnp.exp(-0.5 * inner * inner) * inv_root_tau
    )
    grad_inner = (grad_active * slope).astype(jnp.bfloat16)
    grad_w_one = jnp.einsum("rd,rf->df", second_in, grad_inner, preferred_element_type=jnp.float32)
    grad_bias_inner = jnp.sum(grad_inner, 0, dtype=jnp.float32)
    grad_second_in = jnp.einsum("rf,df->rd", grad_inner, w_one, preferred_element_type=jnp.float32)
    grad_gain_two, grad_bias_two, grad_middle_norm = norm_backward(
        grad_second_in, normed_two, factor_two, gain_two
    )
    grad_middle = grad_result + grad_middle_norm
    grad_mlp = jnp.concatenate([grad_w_one.reshape(-1), grad_w_two.reshape(-1)])
    grad_proj = grad_middle.astype(jnp.bfloat16)
    grad_w_out = jnp.einsum("rc,rd->cd", context_low, grad_proj, preferred_element_type=jnp.float32)
    grad_bias_out = jnp.sum(grad_proj, 0, dtype=jnp.float32)
    grad_context = jnp.einsum("rd,cd->rc", grad_proj, w_out, preferred_element_type=jnp.float32)
    grad_context = grad_context.astype(jnp.bfloat16).reshape(count, length, H, HD)
    probs = jnp.exp(masked_scores(query, keys, key_mask) - log_total)
    probs_again = probs.astype(jnp.bfloat16)
    grad_values = jnp.einsum(
        "shqk,sqhd->skhd", probs_again, grad_context, preferred_element_type=jnp.float32
    )
    grad_probs = jnp.einsum(
        "sqhd,skhd->shqk", grad_context, values, preferred_element_type=jnp.float32
    )
    inner_sum = jnp.sum(grad_probs * probs, -1, keepdims=True)
    grad_scores = (probs * (grad_probs - inner_sum)).astype(jnp.bfloat16)
    grad_query = (
        jnp.einsum("shqk,skhd->sqhd", grad_scores, keys, preferred_element_type=jnp.float32) * scale
    )
    grad_keys = (
        jnp.einsum("shqk,sqhd->skhd", grad_scores, query, preferred_element_type=jnp.float32)
        * scale
    )
    grad_qkv = (
        jnp.stack([grad_query, grad_keys, grad_values], 2)
        .reshape(total_rows, 3 * D)
        .astype(jnp.bfloat16)
    )
    grad_w_qkv = jnp.einsum("rd,re->de", first_in, grad_qkv, preferred_element_type=jnp.float32)
    grad_bias_qkv = jnp.sum(grad_qkv, 0, dtype=jnp.float32)
    grad_first_in = jnp.einsum("re,de->rd", grad_qkv, w_qkv, preferred_element_type=jnp.float32)
    grad_gain_one, grad_bias_one, grad_rows_norm = norm_backward(
        grad_first_in, normed_one, factor_one, gain_one
    )
    grad_rows = grad_middle + grad_rows_norm
    grad_samples = grad_rows.reshape(count, length, D).astype(jnp.bfloat16)
    grad_attn = jnp.concatenate([grad_w_qkv.reshape(-1), grad_w_out.reshape(-1)])
    grad_small = jnp.concatenate(
        [
            grad_gain_one,
            grad_bias_one,
            grad_bias_qkv[:D],
            grad_bias_qkv[2 * D :],
            grad_bias_out,
            grad_gain_two,
            grad_bias_two,
            grad_bias_inner,
            grad_bias_outer,
        ]
    )
    summed_attn, summed_mlp, summed_small = (
        lax.psum_scatter(grad_attn, ("wide", "narrow"), scatter_dimension=0, tiled=True),
        lax.psum_scatter(grad_mlp, ("wide", "narrow"), scatter_dimension=0, tiled=True),
        lax.psum_scatter(grad_small, ("wide", "narrow"), scatter_dimension=0, tiled=True),
    )
    new_attn, new_first_attn, new_second_attn = adamw(
        master_attn, first_attn, second_attn, summed_attn, 0.1, rate_matrix
    )
    new_mlp, new_first_mlp, new_second_mlp = adamw(
        master_mlp, first_mlp, second_mlp, summed_mlp, 0.1, rate_matrix
    )
    new_small, new_first_small, new_second_small = adamw(
        master_small, first_small, second_small, summed_small, 0.0, rate_small
    )
    return (
        output,
        grad_samples,
        new_attn,
        new_first_attn,
        new_second_attn,
        new_mlp,
        new_first_mlp,
        new_second_mlp,
        new_small,
        new_first_small,
        new_second_small,
    )


def solution(mesh):
    in_specs = (
        P(("wide", "narrow"), None, None),
        P(("wide", "narrow"), None, None),
        P(("wide", "narrow")),
        P(("wide", "narrow")),
        P(("wide", "narrow")),
        P(("wide", "narrow")),
        P(("wide", "narrow")),
        P(("wide", "narrow")),
        P(("wide", "narrow")),
        P(("wide", "narrow")),
        P(("wide", "narrow")),
        P(("wide", "narrow")),
    )
    out_specs = (
        P(("wide", "narrow"), None, None),
        P(("wide", "narrow"), None, None),
        P(("wide", "narrow")),
        P(("wide", "narrow")),
        P(("wide", "narrow")),
        P(("wide", "narrow")),
        P(("wide", "narrow")),
        P(("wide", "narrow")),
        P(("wide", "narrow")),
        P(("wide", "narrow")),
        P(("wide", "narrow")),
    )
    return jax.shard_map(
        on_device, mesh=mesh, in_specs=in_specs, out_specs=out_specs, check_vma=False
    )
```

profile of v0, /device:TPU:0, one launch (start us, length us, event | category | flops | bytes accessed | tf_op | source)
XLA Modules:
  0.0 807.1 jit_solution(10441761739860756984)
XLA Ops:
  7.3 1.8 convert_element_type.109
  9.1 1.8 convert_element_type.115
  11.0 0.7 convert_element_type.106
  11.9 42.4 %all-reduce = bf16[9216]{0:T(1024)(128)(2,1)S(1)} all-reduce(bf16[9216]{0:T(1024)(128)(2,1)S(1)} %dynamic-update-slice), channel_id=1, replica_groups=mesh['wide'=8,'narrow'=4] {'wide','narrow'}, use_global_device_ids=true, to_apply=%add | all-reduce | flops 9216 | bytes 36864
  54.3 0.6 fusion.77
  54.9 1.7 convert_reduce_fusion.2
  57.3 1.5 fusion.48
  58.8 1.8 fusion.31
  60.6 1.8 fusion.38
  62.3 15.5 %all-gather.3.cloned.1.call-done = bf16[2359296]{0:T(1024)(128)(2,1)} async-done(((bf16[73728]{0:T(1024)(128)(2,1)}), bf16[2359296]{0:T(1024)(128)(2,1)}) %all-gather.3.cloned.1.call-update) | async-done | bytes 4718608 | tf_op jit(solution)/shard_map/all_gather | solution.py:79
  77.8 1.3 slice-done.7
  79.1 1.9 slice.110
  81.0 3.3 slice.126
  84.3 7.8 slice.103
  92.1 7.5 add_convert_fusion
  99.6 6.6 copy.45
  106.2 3.8 copy.65
  110.5 2.4 fusion.78
  112.9 1.7 fusion.16
  114.6 0.9 copy-done
  115.5 1.3 fusion.56
  116.8 1.2 copy.50
  118.0 1.7 fusion.79
  119.7 1.6 copy-done.3
  121.9 40.2 %all-gather.5.cloned.1.call-done = bf16[4718592]{0:T(1024)(128)(2,1)} async-done(((bf16[147456]{0:T(1024)(128)(2,1)}), bf16[4718592]{0:T(1024)(128)(2,1)}) %all-gather.5.cloned.1.call-update) | async-done | bytes 9437200 | tf_op jit(solution)/shard_map/all_gather | solution.py:80
  162.1 8.2 %fusion.74 = (bf16[2359296]{0:T(1024)(128)(2,1)}, bf16[2359296]{0:T(1024)(128)(2,1)}) fusion(bf16[4718592]{0:T(1024)(128)(2,1)} %all-gather.5.cloned.1.call-done), kind=kLoop, calls=%fused_computation.143 | loop fusion | bytes 18874368 | tf_op jit(solution)/shard_map/slice | solution.py:118
  170.3 8.2 %slice.115 = bf16[768,3072]{1,0:T(8,128)(2,1)} reshape(bf16[2359296]{0:T(1024)(128)(2,1)} %get-tuple-element.35) | data formatting | bytes 9437184 | tf_op jit(solution)/shard_map/slice | solution.py:117
  178.5 9.4 %slice.118 = bf16[3072,768]{1,0:T(8,128)(2,1)} reshape(bf16[2359296]{0:T(1024)(128)(2,1)} %get-tuple-element.34) | data formatting | bytes 9437184 | tf_op jit(solution)/shard_map/slice | solution.py:118
  187.9 37.4 %fusion.2 = (bf16[1024,3072]{1,0:T(8,128)(2,1)}, f32[1024,3072]{1,0:T(8,128)}) fusion(f32[3072]{0:T(1024)S(1)} %slice.137, bf16[768,3072]{1,0:T(8,128)(2,1)} %slice.115, f32[1024,768]{1,0:T(8,128)S(1)} %copy-done.4, f32[768]{0:T(1024)S(1)} %get-tuple-element.43, f32[768]{0:T(1024)S(1)} %get-tuple-element.42, f32[1024]{0:T(1024)S(1)} %add_rsqrt_fusion, ...), kind=kOutput, calls=%fused_computation.5 | convolution fusion | flops 5043388416 | bytes 26765312 | tf_op jit(solution)/shard_map/dot_general | solution.py:121
  225.3 12.3 %convert_reduce_fusion = (f32[3072]{0:T(1024)S(1)}, bf16[1024,3072]{1,0:T(8,128)(2,1)S(1)}) fusion(f32[1024,3072]{1,0:T(8,128)} %get-tuple-element.60, f32[3072]{0:T(1024)S(1)} %slice.137, bf16[1024,768]{1,0:T(8,128)(2,1)S(1)} %copy-done.22, bf16[3072,768]{1,0:T(8,128)(2,1)S(1)} %copy-done.19), kind=kOutput, calls=%fused_computation.12 | convolution fusion | flops 4872729600 | bytes 25190400 | tf_op jit(solution)/shard_map/rd,fd->rf/dot_general | solution.py:129
  237.7 5.7 multiply_reduce_fusion.1
  243.4 1.5 convert_reduce_fusion.4
  244.9 1.7 copy-done.10
  246.6 2.6 convolution_convert_fusion
  249.2 2.9 copy.51
  252.1 1.8 copy.67
  254.0 6.3 fusion.49
  260.4 1.9 multiply_reduce_fusion
  262.2 2.0 multiply_convert_fusion
  264.3 3.8 multiply_bitcast_fusion
  268.1 1.0 multiply_bitcast_fusion.1
  269.1 0.9 copy-done.11
  270.0 2.8 fusion.53
  272.8 1.0 slice-done.6
  273.8 8.4 %convolution_bitcast_fusion = f32[96,24,8,128]{3,2,1,0:T(8,128)} fusion(bf16[1024,3072]{1,0:T(8,128)(2,1)S(1)} %bitcast.142, f32[1024,768]{1,0:T(8,128)S(1)} %copy-done.5, f32[768]{0:T(1024)S(1)} %get-tuple-element.43, f32[768]{0:T(1024)S(1)} %get-tuple-element.42, f32[1024]{0:T(1024)S(1)} %add_rsqrt_fusion, f32[1024]{0:T(1024)S(1)} %broadcast_multiply_fusion.4), kind=kOutput, calls=%fused_computation.46 | convolution fusion | flops 4835770368 | bytes 18888704 | tf_op jit(solution)/shard_map/rd,rf->df/dot_general | solution.py:135
  282.2 1.9 convert_reduce_fusion.1
  284.0 11.5 %copy.57 = bf16[8,128,3,12,64]{1,0,4,3,2:T(8,128)(2,1)} copy(bf16[8,128,3,12,64]{1,4,3,0,2:T(8,128)(2,1)S(1)} %get-tuple-element.27) | data formatting | bytes 9437184 | tf_op jit(solution)/shard_map/convert_element_type | solution.py:168
  295.5 2.8 reshape.241
  298.3 9.5 %fusion.18 = f32[768,2304]{1,0:T(8,128)} fusion(bf16[1024,768]{1,0:T(8,128)(2,1)} %bitcast.146, bf16[288,8,8,128]{3,2,1,0:T(8,128)(2,1)} %bitcast.144), kind=kOutput, calls=%fused_computation.40 | convolution fusion | flops 3623878656 | bytes 13369344 | tf_op jit(solution)/shard_map/rd,re->de/dot_general | solution.py:170
  307.8 7.9 reshape.240
  315.7 9.9 %fusion.80 = f32[3072,768]{1,0:T(8,128)} fusion(bf16[1024,3072]{1,0:T(8,128)(2,1)} %get-tuple-element.59, bf16[1024,768]{1,0:T(8,128)(2,1)} %fusion.48), kind=kOutput, calls=%fused_computation.149 | convolution fusion | flops 4831838208 | bytes 17301504 | tf_op jit(solution)/shard_map/rf,rd->fd/dot_general | solution.py:127
  325.6 10.7 %reshape.243 = f32[2359296]{0:T(1024)} reshape(f32[3072,768]{1,0:T(8,128)} %fusion.80) | data formatting | bytes 18874368 | tf_op jit(solution)/shard_map/reshape | solution.py:142
  336.3 6.0 copy.69
  342.4 7.9 pad_maximum_fusion.1
  350.3 15.6 %pad_maximum_fusion = f32[4718592]{0:T(1024)} fusion(f32[2359296]{0:T(1024)S(1)} %bitcast.135, f32[2359296]{0:T(1024)S(1)} %bitcast.136), kind=kLoop, calls=%fused_computation.2 | loop fusion | flops 4718592 | bytes 37748736 | tf_op jit(solution)/shard_map/concatenate | solution.py:142
  365.9 1.3 copy-done.9
  367.8 10.8 %fusion.44 = (f32[768]{0:T(1024)S(1)}, f32[1024]{0:T(1024)S(1)}, f32[1024]{0:T(1024)S(1)}, f32[768]{0:T(1024)S(1)}, f32[1024,768]{1,0:T(8,128)}) fusion(bf16[8,128,768]{2,1,0:T(8,128)(2,1)S(1)} %copy-done.2, f32[1024]{0:T(1024)S(1)} %copy-done.38, f32[1024]{0:T(1024)S(1)} %copy-done.36, f32[768]{0:T(1024)S(1)} %copy-done.34, bf16[768,2304]{1,0:T(8,128)(2,1)} %slice.103, ...), kind=kOutput, calls=%fused_computation.71 | convolution fusion | flops 3631739392 | bytes 13001728 | tf_op jit(solution)/shard_map/re,de->rd/dot_general | solution.py:172
  378.7 41.2 %all-reduce.3 = f32[9216]{0:T(1024)S(1)} all-reduce(f32[9216]{0:T(1024)S(1)} %constant_dynamic-update-slice_fusion), channel_id=4, replica_groups=mesh['wide'=8,'narrow'=4] {'wide','narrow'}, use_global_device_ids=true, to_apply=%region_21.22.clone | all-reduce | flops 9216 | bytes 73728
  420.0 0.7 multiply_subtract_fusion.2
  420.7 4.6 fusion.43
  425.4 9.7 %select_convert_fusion.1 = bf16[1024,768]{1,0:T(8,128)(2,1)} fusion(f32[1024,768]{1,0:T(8,128)S(1)} %copy-done.6, bf16[1024,3072]{1,0:T(8,128)(2,1)} %get-tuple-element.59, bf16[3072,768]{1,0:T(8,128)(2,1)} %slice.118, f32[768]{0:T(1024)S(1)} %copy-done.42, pred[1024]{0:T(1024)(128)(4,1)S(1)} %copy-done.40), kind=kOutput, calls=%fused_computation.82 | convolution fusion | flops 4834983936 | bytes 15732736 | tf_op jit(solution)/shard_map/dot_general | solution.py:123
  435.0 360.8 %all-reduce.7.cloned.1.call-done = (f32[2359296]{0:T(1024)}, f32[4718592]{0:T(1024)}) async-done(((f32[2359296]{0:T(1024)}, f32[4718592]{0:T(1024)}), (f32[2359296]{0:T(1024)}, f32[4718592]{0:T(1024)})) %all-reduce.7.cloned.1.call-update) | async-done | bytes 28311568
  795.8 2.0 multiply_subtract_fusion.1
  797.8 2.6 multiply_subtract_fusion
  (145 shorter events, 2.9 us)
Async XLA Ops:
  7.2 49.5 %copy-start.1 = (bf16[8,128,768]{2,1,0:T(8,128)(2,1)S(1)}, bf16[8,128,768]{2,1,0:T(8,128)(2,1)}, u32[]{:S(2)}) copy-start(bf16[8,128,768]{2,1,0:T(8,128)(2,1)} %param.12) | copy-start | bytes 4718596
  7.2 49.4 %copy-start.47 = (s32[8]{0:T(128)S(1)}, s32[8]{0:T(128)}, u32[]{:S(2)}) copy-start(s32[8]{0:T(128)} %param.14) | copy-start | bytes 100
  7.2 50.1 %copy-start.7 = (bf16[8,128,768]{2,1,0:T(8,128)(2,1)S(1)}, bf16[8,128,768]{2,1,0:T(8,128)(2,1)}, u32[]{:S(2)}) copy-start(bf16[8,128,768]{2,1,0:T(8,128)(2,1)} %param.13) | copy-start | bytes 4718596
  7.2 70.6 %all-gather.3.cloned.1.call-start = ((), (), s32[]{:S(2)}) async-start(), calls=%async_computation | async-start | bytes 4866048 | tf_op jit(solution)/shard_map/all_gather | solution.py:79
  9.1 153.0 %all-gather.5.cloned.1.call-start = ((), (), s32[]{:S(2)}) async-start(), calls=%async_computation.1 | async-start | bytes 9732096 | tf_op jit(solution)/shard_map/all_gather | solution.py:80
  11.0 784.8 %all-reduce.7.cloned.1.call-start = ((), (), s32[]{:S(2)}) async-start(), calls=%async_computation.2 | async-start | bytes 56623104
  54.8 5.7 copy-start.33
  56.6 3.9 copy-start.39
  56.6 53.8 %copy-start.43 = (pred[8,128]{1,0:T(8,128)(4,1)}, pred[8,128]{1,0:T(8,128)(4,1)S(1)}, u32[]{:S(2)}) copy-start(pred[8,128]{1,0:T(8,128)(4,1)S(1)} %get-tuple-element.54) | copy-start | bytes 3076
  56.6 3.9 copy-start.35
  57.3 3.3 copy-start.37
  77.8 1.3 slice-start.7
  84.3 7.8 copy-start.25
  110.4 2.5 copy-start.13
  110.4 2.5 copy-start.15
  110.4 4.1 copy-start.17
  112.9 2.6 copy-start
  116.8 1.3 copy-start.27
  118.0 1.7 copy-start.23
  119.7 1.6 copy-start.3
  178.5 9.4 %copy-start.4 = (f32[1024,768]{1,0:T(8,128)S(1)}, f32[1024,768]{1,0:T(8,128)}, u32[]{:S(2)}) copy-start(f32[1024,768]{1,0:T(8,128)} %copy-done.3) | copy-start | bytes 9437188
  187.9 37.4 %copy-start.19 = (bf16[3072,768]{1,0:T(8,128)(2,1)S(1)}, bf16[3072,768]{1,0:T(8,128)(2,1)}, u32[]{:S(2)}) copy-start(bf16[3072,768]{1,0:T(8,128)(2,1)} %slice.118) | copy-start | bytes 14155780
  187.9 37.4 %copy-start.22 = (bf16[1024,768]{1,0:T(8,128)(2,1)S(1)}, bf16[1024,768]{1,0:T(8,128)(2,1)}, u32[]{:S(2)}) copy-start(bf16[1024,768]{1,0:T(8,128)(2,1)} %fusion.48) | copy-start | bytes 4718596
  225.3 12.3 %copy-start.20 = (bf16[768,3072]{1,0:T(8,128)(2,1)S(1)}, bf16[768,3072]{1,0:T(8,128)(2,1)}, u32[]{:S(2)}) copy-start(bf16[768,3072]{1,0:T(8,128)(2,1)} %slice.115) | copy-start | bytes 14155780
  237.6 5.7 copy-start.12
  237.7 5.7 copy-start.8
  237.7 5.7 copy-start.40
  243.4 3.2 copy-start.28
  244.9 1.8 copy-start.10
  249.2 11.1 %slice-start = ((s8[6291456]{0:T(1024)(128)(4,1)}), s8[2097152]{0:T(1024)(128)(4,1)S(1)}, s32[]{:S(2)}) async-start(s8[6291456]{0:T(1024)(128)(4,1)} %bitcast.132), calls=%async_computation.3 | async-start | bytes 4194304
  254.0 6.4 slice-start.1
  254.0 6.4 copy-start.18
  264.2 3.8 copy-start.14
  264.3 4.8 copy-start.24
  268.1 1.9 copy-start.11
  268.1 4.7 slice-start.5
  270.0 2.8 copy-start.5
  270.0 3.8 slice-start.6
  273.8 8.4 %copy-start.16 = (bf16[8,128,1,12,64]{1,4,3,0,2:T(8,128)(2,1)S(1)}, bf16[8,128,1,12,64]{1,4,3,0,2:T(8,128)(2,1)}, u32[]{:S(2)}) copy-start(bf16[8,128,1,12,64]{1,4,3,0,2:T(8,128)(2,1)} %fusion.49) | copy-start | bytes 4718596
  336.3 13.9 %slice-start.2 = ((s8[9437184]{0:T(1024)(128)(4,1)}), s8[4194304]{0:T(1024)(128)(4,1)S(1)}, s32[]{:S(2)}) async-start(s8[9437184]{0:T(1024)(128)(4,1)} %bitcast.134), calls=%async_computation.5 | async-start | bytes 8388608
  336.3 13.9 %slice-start.3 = ((s8[9437184]{0:T(1024)(128)(4,1)}), s8[1048576]{0:T(1024)(128)(4,1)S(1)}, s32[]{:S(2)}) async-start(s8[9437184]{0:T(1024)(128)(4,1)} %bitcast.134), calls=%async_computation.6 | async-start | bytes 2097152
  342.4 7.9 slice-start.4
  365.8 1.4 copy-start.9
  365.8 1.4 copy-start.44
  365.8 2.0 copy-start.2
  365.8 2.0 copy-start.34
  365.8 2.0 copy-start.36
  365.8 2.0 copy-start.38
  367.8 52.1 %copy-start.41 = (f32[288]{0:T(512)S(1)}, f32[288]{0:T(512)}, u32[]{:S(2)}) copy-start(f32[288]{0:T(512)} %param.21) | copy-start | bytes 3460
  367.8 52.1 %copy-start.45 = (f32[288]{0:T(512)S(1)}, f32[288]{0:T(512)}, u32[]{:S(2)}) copy-start(f32[288]{0:T(512)} %param.22) | copy-start | bytes 3460
  367.8 52.1 %copy-start.46 = (f32[288]{0:T(512)S(1)}, f32[288]{0:T(512)}, u32[]{:S(2)}) copy-start(f32[288]{0:T(512)} %param.23) | copy-start | bytes 3460
  420.7 4.6 copy-start.6
  420.7 4.6 copy-start.42
  425.3 370.5 %copy-start.26 = (f32[73728]{0:T(1024)S(1)}, f32[73728]{0:T(1024)}, u32[]{:S(2)}) copy-start(f32[73728]{0:T(1024)} %param.15) | copy-start | bytes 884740
  425.3 370.5 %copy-start.31 = (f32[73728]{0:T(1024)S(1)}, f32[73728]{0:T(1024)}, u32[]{:S(2)}) copy-start(f32[73728]{0:T(1024)} %param.16) | copy-start | bytes 884740
  425.3 370.5 %copy-start.32 = (f32[73728]{0:T(1024)S(1)}, f32[73728]{0:T(1024)}, u32[]{:S(2)}) copy-start(f32[73728]{0:T(1024)} %param.17) | copy-start | bytes 884740
  425.3 372.5 %copy-start.21 = (f32[147456]{0:T(1024)S(1)}, f32[147456]{0:T(1024)}, u32[]{:S(2)}) copy-start(f32[147456]{0:T(1024)} %param.18) | copy-start | bytes 1769476
  425.3 372.5 %copy-start.29 = (f32[147456]{0:T(1024)S(1)}, f32[147456]{0:T(1024)}, u32[]{:S(2)}) copy-start(f32[147456]{0:T(1024)} %param.19) | copy-start | bytes 1769476
  425.3 372.5 %copy-start.30 = (f32[147456]{0:T(1024)S(1)}, f32[147456]{0:T(1024)}, u32[]{:S(2)}) copy-start(f32[147456]{0:T(1024)} %param.20) | copy-start | bytes 1769476
Sparse Core Ops, SparseCore 0:
  11.4 66.3 all-gather.2
  81.2 80.8 all-gather.4
  366.0 429.7 all-reduce.6
where the time goes:
time: 816 us; the launch traced here: 807 us
  waiting for transfers between devices  417 us (51%)
  matrix products  135 us (17%)
  local copies, waits for them, and re-layouts  104 us (13%)
  blocking collectives  83.5 us (10%)
  other arithmetic  52.9 us (6%)
  between operations  14.8 us (2%)
    unnamed x4, waiting for transfers between devices  361 us
    unnamed x2, blocking collectives  83.5 us
    all_gather x1, waiting for transfers between devices, on_device(): lax.all_gather(master_mlp.astype(jnp.bfloat16), ('wide', 'narrow'), axis=...  40.2 us
    dot_general x1, matrix products, on_device(): jnp.dot(second_in, w_one, preferred_element_type=jnp.float32) + bias_inner  37.4 us
    unnamed x123, local copies, waits for them, and re-layouts  19.6 us
    slice x2, local copies, waits for them, and re-layouts, on_device(): w_two = mlp_full[D * FF:].reshape(FF, D)  17.6 us
  transfers between devices with their start and end apart: 3, of which 3 were waited for; matrix products, arithmetic and copies ran while one was open for 10% of the time, Pallas kernels for 0%

commit v1 on v0

--- a/solution.py
+++ b/solution.py
@@ -56,6 +56,12 @@
         first_hat / (jnp.sqrt(second_hat) + eps_adam) + decay * master
     )
     return (master_new, first_new, second_new)
+
+
+def scatter_sum(grad):
+    lanes = grad.astype(jnp.bfloat16).reshape(-1, 128)
+    own = lax.psum_scatter(lanes, ("wide", "narrow"), scatter_dimension=0, tiled=True)
+    return own.reshape(-1).astype(jnp.float32)
 
 
 def on_device(
@@ -190,8 +196,8 @@
         ]
     )
     summed_attn, summed_mlp, summed_small = (
-        lax.psum_scatter(grad_attn, ("wide", "narrow"), scatter_dimension=0, tiled=True),
-        lax.psum_scatter(grad_mlp, ("wide", "narrow"), scatter_dimension=0, tiled=True),
+        scatter_sum(grad_attn),
+        scatter_sum(grad_mlp),
         lax.psum_scatter(grad_small, ("wide", "narrow"), scatter_dimension=0, tiled=True),
     )
     new_attn, new_first_attn, new_second_attn = adamw(

time: 816 us -> 572 us (0.70)
  waiting for transfers between devices: 417 us -> 183 us
    unnamed x4, waiting for transfers between devices: 361 us -> 0.07 us
    reduce_scatter x0 -> x2, waiting for transfers between devices: none -> 128 us  [scatter_sum(): lax.psum_scatter(lanes, ('wide', 'narrow'), scatter_dimension=0, tiled=True)]
    concatenate x0 -> x2, local copies, waits for them, and re-layouts: none -> 17.8 us  [on_device(): grad_mlp = jnp.concatenate([grad_w_one.reshape(-1), grad_w_two.reshape(-1)])]
    reshape x1 -> x0, local copies, waits for them, and re-layouts: 10.7 us -> none  [on_device(): grad_mlp = jnp.concatenate([grad_w_one.reshape(-1), grad_w_two.reshape(-1)])]
    convert_element_type x0 -> x1, other arithmetic: none -> 8.61 us  [scatter_sum(): lanes = grad.astype(jnp.bfloat16).reshape(-1, 128)]
    unnamed x123 -> x124, local copies, waits for them, and re-layouts: 19.6 us -> 15.6 us
  transfers between devices with their start and end apart: 3 -> 4, of which waited for: 3 -> 3; matrix products, arithmetic and copies ran while one was open for 10% -> 23% of each run, Pallas kernels for 0% -> 0%
where the time goes in v1:
time: 572 us; the launch traced here: 564 us
  waiting for transfers between devices  183 us (32%)
  matrix products  131 us (23%)
  local copies, waits for them, and re-layouts  104 us (18%)
  blocking collectives  82.4 us (14%)
  other arithmetic  48.2 us (8%)
  between operations  14.8 us (3%)
    reduce_scatter x2, waiting for transfers between devices, scatter_sum(): lax.psum_scatter(lanes, ('wide', 'narrow'), scatter_dimension=0, tiled=True)  128 us
    unnamed x2, blocking collectives  82.4 us
    all_gather x1, waiting for transfers between devices, on_device(): lax.all_gather(master_mlp.astype(jnp.bfloat16), ('wide', 'narrow'), axis=...  38.8 us
    dot_general x1, matrix products, on_device(): jnp.dot(second_in, w_one, preferred_element_type=jnp.float32) + bias_inner  37.3 us
    concatenate x2, local copies, waits for them, and re-layouts, on_device(): grad_mlp = jnp.concatenate([grad_w_one.reshape(-1), grad_w_two.reshape(-1)])  17.8 us
    slice x2, local copies, waits for them, and re-layouts, on_device(): w_two = mlp_full[D * FF:].reshape(FF, D)  17.7 us
    all_gather x1, waiting for transfers between devices, on_device(): lax.all_gather(master_attn.astype(jnp.bfloat16), ('wide', 'narrow'), axis...  16.6 us
    unnamed x124, local copies, waits for them, and re-layouts  15.6 us
  transfers between devices with their start and end apart: 4, of which 3 were waited for; matrix products, arithmetic and copies ran while one was open for 23% of the time, Pallas kernels for 0%

profile of v1, /device:TPU:0, one launch (start us, length us, event | category | flops | bytes accessed | tf_op | source)
XLA Modules:
  0.0 563.5 jit_solution(996623981859105864)
XLA Ops:
  7.3 1.8 convert_element_type.128
  9.1 1.8 convert_element_type.134
  11.0 0.7 convert_element_type.125
  11.9 42.3 %all-reduce = bf16[9216]{0:T(1024)(128)(2,1)S(1)} all-reduce(bf16[9216]{0:T(1024)(128)(2,1)S(1)} %dynamic-update-slice), channel_id=1, replica_groups=mesh['wide'=8,'narrow'=4] {'wide','narrow'}, use_global_device_ids=true, to_apply=%add | all-reduce | flops 9216 | bytes 36864
  54.2 0.6 fusion.79
  54.8 1.7 convert_reduce_fusion.2
  56.6 0.6 fusion.27
  57.3 1.5 fusion.47
  58.7 1.8 fusion.30
  60.5 0.6 fusion.37
  61.2 16.6 %all-gather.3.cloned.1.call-done = bf16[2359296]{0:T(1024)(128)(2,1)} async-done(((bf16[73728]{0:T(1024)(128)(2,1)}), bf16[2359296]{0:T(1024)(128)(2,1)}) %all-gather.3.cloned.1.call-update) | async-done | bytes 4718608 | tf_op jit(solution)/shard_map/all_gather | solution.py:85
  77.8 3.4 slice.126
  81.1 7.6 %slice.103 = bf16[768,2304]{1,0:T(8,128)(2,1)} reshape(bf16[1769472]{0:T(1024)(128)(2,1)} %slice.126) | data formatting | bytes 7077888 | tf_op jit(solution)/shard_map/slice | solution.py:89
  88.7 7.5 %add_convert_fusion = bf16[1024,2304]{1,0:T(8,128)(2,1)} fusion(bf16[1024,768]{1,0:T(8,128)(2,1)S(1)} %fusion.37, bf16[768,2304]{1,0:T(8,128)(2,1)} %slice.103, f32[2304]{0:T(1024)S(1)} %pad_maximum_fusion.1), kind=kOutput, calls=%fused_computation.30 | convolution fusion | flops 3628597248 | bytes 9839616 | tf_op jit(solution)/shard_map/dot_general | solution.py:109
  96.2 6.6 %copy.45 = bf16[1024,2304]{0,1:T(8,128)(2,1)} copy(bf16[1024,2304]{1,0:T(8,128)(2,1)} %add_convert_fusion) | data formatting | bytes 9437184 | tf_op jit(solution)/shard_map/convert_element_type | solution.py:110
  102.8 3.6 copy.65
  106.9 2.4 fusion.80
  109.3 1.7 fusion.16
  111.0 0.9 copy-done
  111.9 1.3 fusion.58
  113.2 2.4 copy.50
  115.6 1.9 slice.110
  117.5 3.5 fusion.81
  121.0 1.7 copy-done.6
  123.2 38.8 %all-gather.5.cloned.1.call-done = bf16[4718592]{0:T(1024)(128)(2,1)} async-done(((bf16[147456]{0:T(1024)(128)(2,1)}), bf16[4718592]{0:T(1024)(128)(2,1)}) %all-gather.5.cloned.1.call-update) | async-done | bytes 9437200 | tf_op jit(solution)/shard_map/all_gather | solution.py:86
  162.0 8.3 %fusion.76 = (bf16[2359296]{0:T(1024)(128)(2,1)}, bf16[2359296]{0:T(1024)(128)(2,1)}) fusion(bf16[4718592]{0:T(1024)(128)(2,1)} %all-gather.5.cloned.1.call-done), kind=kLoop, calls=%fused_computation.145 | loop fusion | bytes 18874368 | tf_op jit(solution)/shard_map/slice | solution.py:124
  170.3 8.2 %slice.115 = bf16[768,3072]{1,0:T(8,128)(2,1)} reshape(bf16[2359296]{0:T(1024)(128)(2,1)} %get-tuple-element.33) | data formatting | bytes 9437184 | tf_op jit(solution)/shard_map/slice | solution.py:123
  178.5 9.5 %slice.118 = bf16[3072,768]{1,0:T(8,128)(2,1)} reshape(bf16[2359296]{0:T(1024)(128)(2,1)} %get-tuple-element.32) | data formatting | bytes 9437184 | tf_op jit(solution)/shard_map/slice | solution.py:124
  188.0 37.3 %fusion.2 = (bf16[1024,3072]{1,0:T(8,128)(2,1)}, f32[1024,3072]{1,0:T(8,128)}) fusion(f32[3072]{0:T(1024)S(1)} %slice.137, bf16[768,3072]{1,0:T(8,128)(2,1)} %slice.115, f32[1024,768]{1,0:T(8,128)S(1)} %copy-done.7, f32[768]{0:T(1024)S(1)} %get-tuple-element.41, f32[768]{0:T(1024)S(1)} %get-tuple-element.40, f32[1024]{0:T(1024)S(1)} %add_rsqrt_fusion, ...), kind=kOutput, calls=%fused_computation.4 | convolution fusion | flops 5043388416 | bytes 26765312 | tf_op jit(solution)/shard_map/dot_general | solution.py:127
  225.3 12.9 %convert_reduce_fusion = (f32[3072]{0:T(1024)}, bf16[1024,3072]{1,0:T(8,128)(2,1)S(1)}) fusion(f32[1024,3072]{1,0:T(8,128)} %get-tuple-element.58, f32[3072]{0:T(1024)S(1)} %slice.137, bf16[1024,768]{1,0:T(8,128)(2,1)S(1)} %copy-done.21, bf16[3072,768]{1,0:T(8,128)(2,1)S(1)} %copy-done.17), kind=kOutput, calls=%fused_computation.11 | convolution fusion | flops 4872729600 | bytes 25190400 | tf_op jit(solution)/shard_map/rd,fd->rf/dot_general | solution.py:135
  238.2 6.1 %multiply_reduce_fusion.1 = (f32[768]{0:T(1024)}, f32[1024]{0:T(1024)S(1)}, f32[1024]{0:T(1024)S(1)}, f32[768]{0:T(1024)}, f32[1024,768]{1,0:T(8,128)S(1)}) fusion(f32[1024,768]{1,0:T(8,128)S(1)} %copy-done.7, f32[1024]{0:T(1024)S(1)} %add_rsqrt_fusion, f32[1024]{0:T(1024)S(1)} %broadcast_multiply_fusion.4, f32[768]{0:T(1024)S(1)} %get-tuple-element.40, ...), kind=kOutput, calls=%fused_computation.76 | convolution fusion | flops 4838912000 | bytes 17327104 | tf_op jit(solution)/shard_map/rf,df->rd/dot_general | solution.py:143
  244.4 1.5 convert_reduce_fusion.4
  245.9 1.7 copy-done.10
  247.6 1.4 convolution_convert_fusion.3
  249.0 1.8 copy.51
  250.9 2.0 copy.67
  252.9 4.8 multiply_reduce_fusion
  257.7 2.0 multiply_convert_fusion
  259.7 2.5 multiply_bitcast_fusion.1
  262.2 2.3 multiply_bitcast_fusion
  264.5 2.3 fusion.48
  266.9 2.4 fusion.55
  269.3 2.3 convert_reduce_fusion.1
  271.5 9.2 %copy.57 = bf16[8,128,3,12,64]{1,0,4,3,2:T(8,128)(2,1)S(1)} copy(bf16[8,128,3,12,64]{1,4,3,0,2:T(8,128)(2,1)S(1)} %get-tuple-element.25) | data formatting | bytes 9437184 | tf_op jit(solution)/shard_map/convert_element_type | solution.py:174
  280.8 2.1 copy-done.18
  282.9 5.4 convolution_convert_fusion.2
  288.3 6.8 %reshape.254 = bf16[1769472]{0:T(1024)(128)(2,1)S(1)} reshape(bf16[768,2304]{1,0:T(8,128)(2,1)} %convolution_convert_fusion.2) | data formatting | bytes 7077888 | tf_op jit(solution)/shard_map/reshape | solution.py:184
  295.1 3.4 reshape.255
  298.5 8.6 %maximum_bitcast_fusion = bf16[18432,128]{1,0:T(8,128)(2,1)} fusion(bf16[589824]{0:T(1024)(128)(2,1)} %reshape.255, bf16[1769472]{0:T(1024)(128)(2,1)S(1)} %reshape.254), kind=kLoop, calls=%fused_computation.45 | loop fusion | flops 9437184 | bytes 9437184 | tf_op jit(solution)/shard_map/convert_element_type | solution.py:62
  307.2 1.8 copy-done.8
  309.0 10.0 %convolution_convert_fusion.1 = bf16[768,3072]{1,0:T(8,128)(2,1)} fusion(bf16[1024,3072]{1,0:T(8,128)(2,1)} %copy-done.53, f32[1024,768]{1,0:T(8,128)S(1)} %copy-done.8, f32[768]{0:T(1024)S(1)} %copy-done.45, f32[768]{0:T(1024)S(1)} %get-tuple-element.40, f32[1024]{0:T(1024)S(1)} %add_rsqrt_fusion, f32[1024]{0:T(1024)S(1)} %broadcast_multiply_fusion.4), kind=kOutput, calls=%fused_computation.39 | convolution fusion | flops 4838129664 | bytes 14170112 | tf_op jit(solution)/shard_map/rd,rf->df/dot_general | solution.py:141
  318.9 8.5 %concatenate.21 = bf16[18432,128]{1,0:T(8,128)(2,1)} reshape(bf16[768,3072]{1,0:T(8,128)(2,1)} %convolution_convert_fusion.1) | data formatting | bytes 9437184 | tf_op jit(solution)/shard_map/concatenate | solution.py:148
  327.4 9.9 %convolution_convert_fusion = bf16[3072,768]{1,0:T(8,128)(2,1)} fusion(bf16[1024,3072]{1,0:T(8,128)(2,1)} %get-tuple-element.57, bf16[1024,768]{1,0:T(8,128)(2,1)S(1)} %copy-done.22), kind=kOutput, calls=%fused_computation.38 | convolution fusion | flops 4834197504 | bytes 12582912 | tf_op jit(solution)/shard_map/rf,rd->fd/dot_general | solution.py:133
  337.3 9.3 %concatenate.22 = bf16[18432,128]{1,0:T(8,128)(2,1)} reshape(bf16[3072,768]{1,0:T(8,128)(2,1)} %convolution_convert_fusion) | data formatting | bytes 9437184 | tf_op jit(solution)/shard_map/concatenate | solution.py:148
  346.6 11.1 %pad_maximum_fusion = bf16[36864,128]{1,0:T(8,128)(2,1)} fusion(bf16[18432,128]{1,0:T(8,128)(2,1)} %concatenate.22, bf16[18432,128]{1,0:T(8,128)(2,1)} %concatenate.21), kind=kLoop, calls=%fused_computation.28 | loop fusion | flops 18874368 | bytes 18874368 | tf_op jit(solution)/shard_map/concatenate | solution.py:148
  357.8 1.3 copy-done.5
  359.8 9.6 %fusion.43 = (f32[768]{0:T(1024)S(1)}, f32[1024]{0:T(1024)S(1)}, f32[1024]{0:T(1024)S(1)}, f32[768]{0:T(1024)S(1)}, f32[1024,768]{1,0:T(8,128)}) fusion(bf16[8,128,768]{2,1,0:T(8,128)(2,1)S(1)} %copy-done.2, f32[1024]{0:T(1024)S(1)} %copy-done.37, f32[1024]{0:T(1024)S(1)} %copy-done.35, f32[768]{0:T(1024)S(1)} %copy-done.33, bf16[768,2304]{1,0:T(8,128)(2,1)} %slice.103, ...), kind=kOutput, calls=%fused_computation.72 | convolution fusion | flops 3631739392 | bytes 13001728 | tf_op jit(solution)/shard_map/re,de->rd/dot_general | solution.py:178
  369.5 40.1 %all-reduce.1 = f32[9216]{0:T(1024)S(1)} all-reduce(f32[9216]{0:T(1024)S(1)} %constant_dynamic-update-slice_fusion), channel_id=4, replica_groups=mesh['wide'=8,'narrow'=4] {'wide','narrow'}, use_global_device_ids=true, to_apply=%region_21.22.clone | all-reduce | flops 9216 | bytes 73728
  409.7 0.7 multiply_subtract_fusion.2
  410.4 4.5 fusion.42
  415.0 9.6 %select_convert_fusion.1 = bf16[1024,768]{1,0:T(8,128)(2,1)} fusion(f32[1024,768]{1,0:T(8,128)S(1)} %copy-done.9, bf16[1024,3072]{1,0:T(8,128)(2,1)} %get-tuple-element.57, bf16[3072,768]{1,0:T(8,128)(2,1)} %slice.118, f32[768]{0:T(1024)S(1)} %copy-done.43, pred[1024]{0:T(1024)(128)(4,1)S(1)} %copy-done.41), kind=kOutput, calls=%fused_computation.83 | convolution fusion | flops 4834983936 | bytes 15732736 | tf_op jit(solution)/shard_map/dot_general | solution.py:129
  424.5 1.9 multiply_subtract_fusion.1
  426.5 127.9 %reduce-scatter.5.cloned.1.call-done = bf16[1152,128]{1,0:T(8,128)(2,1)} async-done(((bf16[36864,128]{1,0:T(8,128)(2,1)}), bf16[1152,128]{1,0:T(8,128)(2,1)}) %reduce-scatter.5.cloned.1.call-update) | async-done | bytes 294928 | tf_op jit(solution)/shard_map/reduce_scatter | solution.py:63
  554.4 2.4 multiply_subtract_fusion
  (148 shorter events, 2.4 us)
Async XLA Ops:
  7.2 49.5 %copy-start.1 = (bf16[8,128,768]{2,1,0:T(8,128)(2,1)S(1)}, bf16[8,128,768]{2,1,0:T(8,128)(2,1)}, u32[]{:S(2)}) copy-start(bf16[8,128,768]{2,1,0:T(8,128)(2,1)} %param.12) | copy-start | bytes 4718596
  7.2 49.3 %copy-start.52 = (s32[8]{0:T(128)S(1)}, s32[8]{0:T(128)}, u32[]{:S(2)}) copy-start(s32[8]{0:T(128)} %param.14) | copy-start | bytes 100
  7.2 50.1 %copy-start.3 = (bf16[8,128,768]{2,1,0:T(8,128)(2,1)S(1)}, bf16[8,128,768]{2,1,0:T(8,128)(2,1)}, u32[]{:S(2)}) copy-start(bf16[8,128,768]{2,1,0:T(8,128)(2,1)} %param.13) | copy-start | bytes 4718596
  7.2 70.6 %all-gather.3.cloned.1.call-start = ((), (), s32[]{:S(2)}) async-start(), calls=%async_computation.2 | async-start | bytes 4866048 | tf_op jit(solution)/shard_map/all_gather | solution.py:85
  9.1 152.9 %all-gather.5.cloned.1.call-start = ((), (), s32[]{:S(2)}) async-start(), calls=%async_computation.3 | async-start | bytes 9732096 | tf_op jit(solution)/shard_map/all_gather | solution.py:86
  11.0 413.6 %reduce-scatter.3.cloned.1.call-start = ((), (), s32[]{:S(2)}) async-start(), calls=%async_computation.4 | async-start | bytes 4866048 | tf_op jit(solution)/shard_map/reduce_scatter | solution.py:63
  54.8 5.7 %copy-start.32 = (f32[768]{0:T(1024)}, f32[768]{0:T(1024)S(1)}, u32[]{:S(2)}) copy-start(f32[768]{0:T(1024)S(1)} %get-tuple-element.44) | copy-start | bytes 9220
  54.8 133.1 %copy-start.44 = (f32[768]{0:T(1024)}, f32[768]{0:T(1024)S(1)}, u32[]{:S(2)}) copy-start(f32[768]{0:T(1024)S(1)} %get-tuple-element.41) | copy-start | bytes 9220
  56.6 3.9 copy-start.39
  56.6 50.2 %copy-start.48 = (pred[8,128]{1,0:T(8,128)(4,1)}, pred[8,128]{1,0:T(8,128)(4,1)S(1)}, u32[]{:S(2)}) copy-start(pred[8,128]{1,0:T(8,128)(4,1)S(1)} %get-tuple-element.52) | copy-start | bytes 3076
  56.6 3.9 copy-start.34
  57.2 3.3 copy-start.36
  106.8 2.4 copy-start.12
  106.8 2.4 copy-start.14
  106.8 4.1 copy-start.15
  109.3 2.6 copy-start
  113.2 2.4 slice-start.2
  120.9 1.7 copy-start.6
  178.5 9.5 %copy-start.7 = (f32[1024,768]{1,0:T(8,128)S(1)}, f32[1024,768]{1,0:T(8,128)}, u32[]{:S(2)}) copy-start(f32[1024,768]{1,0:T(8,128)} %copy-done.6) | copy-start | bytes 9437188
  188.0 37.4 %copy-start.17 = (bf16[3072,768]{1,0:T(8,128)(2,1)S(1)}, bf16[3072,768]{1,0:T(8,128)(2,1)}, u32[]{:S(2)}) copy-start(bf16[3072,768]{1,0:T(8,128)(2,1)} %slice.118) | copy-start | bytes 14155780
  188.0 37.3 %copy-start.21 = (bf16[1024,768]{1,0:T(8,128)(2,1)S(1)}, bf16[1024,768]{1,0:T(8,128)(2,1)}, u32[]{:S(2)}) copy-start(bf16[1024,768]{1,0:T(8,128)(2,1)} %fusion.47) | copy-start | bytes 4718596
  225.3 12.9 %copy-start.19 = (bf16[768,3072]{1,0:T(8,128)(2,1)S(1)}, bf16[768,3072]{1,0:T(8,128)(2,1)}, u32[]{:S(2)}) copy-start(bf16[768,3072]{1,0:T(8,128)(2,1)} %slice.115) | copy-start | bytes 14155780
  238.2 6.1 %copy-start.53 = (bf16[1024,3072]{1,0:T(8,128)(2,1)}, bf16[1024,3072]{1,0:T(8,128)(2,1)S(1)}, u32[]{:S(2)}) copy-start(bf16[1024,3072]{1,0:T(8,128)(2,1)S(1)} %get-tuple-element.64) | copy-start | bytes 18874372
  238.2 6.1 %copy-start.4 = (bf16[8,128,768]{2,1,0:T(8,128)(2,1)S(1)}, bf16[8,128,768]{2,1,0:T(8,128)(2,1)}, u32[]{:S(2)}) copy-start(bf16[8,128,768]{2,1,0:T(8,128)(2,1)} %param.13) | copy-start | bytes 4718596
  238.2 6.1 %copy-start.40 = (pred[1024]{0:T(1024)(128)(4,1)S(1)}, pred[1024]{0:T(1024)(128)(4,1)}, u32[]{:S(2)}) copy-start(pred[1024]{0:T(1024)(128)(4,1)} %copy-done.39) | copy-start | bytes 3076
  244.4 3.2 copy-start.25
  245.9 1.7 copy-start.10
  250.9 2.0 copy-start.16
  252.8 4.9 slice-start
  252.9 4.9 slice-start.1
  259.7 2.5 copy-start.13
  264.5 2.3 copy-start.11
  264.5 2.3 copy-start.24
  271.5 11.3 %copy-start.23 = (bf16[8,128,768]{2,1,0:T(8,128)(2,1)S(1)}, bf16[8,128,768]{2,1,0:T(8,128)(2,1)}, u32[]{:S(2)}) copy-start(bf16[8,128,768]{2,1,0:T(8,128)(2,1)} %fusion.30) | copy-start | bytes 4718596
  280.8 2.1 copy-start.18
  307.1 1.9 copy-start.8
  307.1 1.9 copy-start.45
  307.1 247.3 %reduce-scatter.5.cloned.1.call-start = ((), (), s32[]{:S(2)}) async-start(), calls=%async_computation.5 | async-start | bytes 9732096 | tf_op jit(solution)/shard_map/reduce_scatter | solution.py:63
  318.9 8.5 %copy-start.22 = (bf16[1024,768]{1,0:T(8,128)(2,1)S(1)}, bf16[1024,768]{1,0:T(8,128)(2,1)}, u32[]{:S(2)}) copy-start(bf16[1024,768]{1,0:T(8,128)(2,1)} %fusion.47) | copy-start | bytes 4718596
  357.7 1.4 copy-start.5
  357.7 1.4 copy-start.49
  357.7 1.8 copy-start.31
  357.7 1.9 copy-start.2
  357.8 1.9 copy-start.33
  357.8 1.9 copy-start.35
  357.8 1.9 copy-start.37
  359.7 9.8 %copy-start.47 = (f32[768]{0:T(1024)S(1)}, f32[768]{0:T(1024)}, u32[]{:S(2)}) copy-start(f32[768]{0:T(1024)} %get-tuple-element.11) | copy-start | bytes 9220
  359.7 9.8 %copy-start.46 = (f32[768]{0:T(1024)S(1)}, f32[768]{0:T(1024)}, u32[]{:S(2)}) copy-start(f32[768]{0:T(1024)} %get-tuple-element.17) | copy-start | bytes 9220
  359.7 9.8 %copy-start.38 = (f32[3072]{0:T(1024)S(1)}, f32[3072]{0:T(1024)}, u32[]{:S(2)}) copy-start(f32[3072]{0:T(1024)} %get-tuple-element.63) | copy-start | bytes 36868
  359.7 50.0 %copy-start.42 = (f32[288]{0:T(512)S(1)}, f32[288]{0:T(512)}, u32[]{:S(2)}) copy-start(f32[288]{0:T(512)} %param.21) | copy-start | bytes 3460
  359.7 50.0 %copy-start.50 = (f32[288]{0:T(512)S(1)}, f32[288]{0:T(512)}, u32[]{:S(2)}) copy-start(f32[288]{0:T(512)} %param.22) | copy-start | bytes 3460
  359.8 50.0 %copy-start.51 = (f32[288]{0:T(512)S(1)}, f32[288]{0:T(512)}, u32[]{:S(2)}) copy-start(f32[288]{0:T(512)} %param.23) | copy-start | bytes 3460
  410.4 4.5 copy-start.9
  410.4 4.5 copy-start.41
  410.4 4.5 copy-start.43
  414.9 9.6 %copy-start.26 = (f32[73728]{0:T(1024)S(1)}, f32[73728]{0:T(1024)}, u32[]{:S(2)}) copy-start(f32[73728]{0:T(1024)} %param.15) | copy-start | bytes 884740
  414.9 9.6 %copy-start.29 = (f32[73728]{0:T(1024)S(1)}, f32[73728]{0:T(1024)}, u32[]{:S(2)}) copy-start(f32[73728]{0:T(1024)} %param.16) | copy-start | bytes 884740
  414.9 9.6 %copy-start.30 = (f32[73728]{0:T(1024)S(1)}, f32[73728]{0:T(1024)}, u32[]{:S(2)}) copy-start(f32[73728]{0:T(1024)} %param.17) | copy-start | bytes 884740
  414.9 139.4 %copy-start.20 = (f32[147456]{0:T(1024)S(1)}, f32[147456]{0:T(1024)}, u32[]{:S(2)}) copy-start(f32[147456]{0:T(1024)} %param.18) | copy-start | bytes 1769476
  414.9 139.4 %copy-start.27 = (f32[147456]{0:T(1024)S(1)}, f32[147456]{0:T(1024)}, u32[]{:S(2)}) copy-start(f32[147456]{0:T(1024)} %param.19) | copy-start | bytes 1769476
  415.0 139.4 %copy-start.28 = (f32[147456]{0:T(1024)S(1)}, f32[147456]{0:T(1024)}, u32[]{:S(2)}) copy-start(f32[147456]{0:T(1024)} %param.20) | copy-start | bytes 1769476
Sparse Core Ops, SparseCore 0:
  11.4 66.2 all-gather.2
  81.1 80.8 all-gather.4
  307.2 105.5 reduce-scatter.2
  419.6 134.7 reduce-scatter.4

commit v2 on v1

--- a/solution.py
+++ b/solution.py
@@ -3,6 +3,8 @@
 import jax
 import jax.numpy as jnp
 from jax import lax
+from jax.experimental import pallas as pl
+from jax.experimental.pallas import tpu as pltpu
 from jax.sharding import PartitionSpec as P
 
 D = 768
@@ -224,6 +226,734 @@
     )
 
 
+bf16 = jnp.bfloat16
+f32 = jnp.float32
+BLOCK = 256
+BIN = 128
+AXES = ("wide", "narrow")
+ROW = 128
+SMALL_ROWS = 72
+
+
+def place_of(i):
+    wide, z = divmod(i, 4)
+    return wide // 4, (wide // 2) % 2, wide % 2, z
+
+
+def index_of(y, x, c, z):
+    return ((y * 2 + x) * 2 + c) * 4 + z
+
+
+def pairs_of(move):
+    return [(i, index_of(*move(*place_of(i)))) for i in range(32)]
+
+
+TO_X = pairs_of(lambda y, x, c, z: (y, 1 - x, c, z))
+TO_Y = pairs_of(lambda y, x, c, z: (1 - y, x, c, z))
+TO_CORE = pairs_of(lambda y, x, c, z: (y, x, 1 - c, z))
+TO_Z = [pairs_of(lambda y, x, c, z, k=k: (y, x, c, z ^ k)) for k in range(4)]
+SWAP_ATTN = pairs_of(lambda y, x, c, z: (y, x, c if y and x else 1 - c, z))
+SWAP_MLP = pairs_of(lambda y, x, c, z: (y, x, c if y else 1 - c, z))
+
+
+def send(value, pairs):
+    return lax.ppermute(value, AXES, pairs)
+
+
+def dot(a, b, dims=((1,), (0,))):
+    return lax.dot_general(a, b, (dims, ((), ())), preferred_element_type=f32)
+
+
+def at_rows(ref, start, size):
+    return ref[pl.ds(start, size), :]
+
+
+def attn_block(core, j):
+    return (j // 3) * 6 + 3 * core + j % 3
+
+
+def mlp_block(core, j):
+    return (j // 6) * 12 + 6 * core + j % 6
+
+
+def cut_masters(idx, attn, mlp, keep_a, send_a, keep_m, send_m, half_a, half_m):
+    wide, core = idx[0], idx[3]
+
+    @pl.when(wide < 6)
+    def _():
+        for c in range(2):
+            for j in range(9):
+                rows = attn[pl.ds(attn_block(c, j), 32, stride=18), :]
+                half_a[c, j * 32 : (j + 1) * 32, :] = rows.astype(bf16)
+
+    @pl.when(wide >= 6)
+    def _():
+        for j in range(6):
+            rows = attn[pl.ds(j, 96, stride=6), :]
+            half_a[j // 3, (j % 3) * 96 : (j % 3 + 1) * 96, :] = rows.astype(bf16)
+
+    @pl.when(wide < 4)
+    def _():
+        for c in range(2):
+            for j in range(12):
+                rows = mlp[pl.ds(mlp_block(c, j), 48, stride=24), :]
+                half_m[c, j * 48 : (j + 1) * 48, :] = rows.astype(bf16)
+
+    @pl.when(wide >= 4)
+    def _():
+        for j in range(6):
+            rows = mlp[pl.ds(j, 192, stride=6), :]
+            half_m[j // 3, (j % 3) * 192 : (j % 3 + 1) * 192, :] = rows.astype(bf16)
+
+    first_a = jnp.where(wide < 6, core, 0)
+    first_m = jnp.where(wide < 4, core, 0)
+    keep_a[...] = half_a[first_a]
+    send_a[...] = half_a[1 - first_a]
+    keep_m[...] = half_m[first_m]
+    send_m[...] = half_m[1 - first_m]
+
+
+def pack_rows(idx, vis_own, vis_other, x_own, x_other, cot_own, cot_other, x_out, cot_out, meta, fill):
+    core = idx[3]
+    for b in range(16):
+        fill[b] = 0
+    bins = jnp.int32(0)
+    for s in range(16):
+        mine = core == s // 8
+        seen = jnp.where(mine, vis_own[s % 8], vis_other[s % 8])
+        need = ((seen + 15) >> 4) << 4
+        chosen = jnp.int32(15)
+        for b in reversed(range(s + 1)):
+            chosen = jnp.where(fill[b] + need <= BIN, b, chosen)
+        start = chosen * BIN + fill[chosen]
+        fill[chosen] = fill[chosen] + need
+        bins = jnp.maximum(bins, chosen + 1)
+        meta[8 + s] = start
+        meta[24 + s] = seen
+    blocks = (bins + 1) >> 1
+    meta[0] = blocks
+
+    def clear(b, carry):
+        at = pl.ds(pl.multiple_of(b * BLOCK, BLOCK), BLOCK)
+        x_out[at, :] = jnp.zeros((BLOCK, D), bf16)
+        cot_out[at, :] = jnp.zeros((BLOCK, D), bf16)
+        return carry
+
+    lax.fori_loop(0, blocks, clear, 0)
+    row = lax.broadcasted_iota(jnp.int32, (16, D), 0)
+    for s in range(16):
+        start, seen = meta[8 + s], meta[24 + s]
+
+        def fetch(x_in, cot_in):
+            def chunk(k, carry):
+                src = pl.ds(pl.multiple_of(k * 16, 16), 16)
+                dst = pl.ds(pl.multiple_of(start + k * 16, 16), 16)
+                x_out[dst, :] = x_in[s % 8, src, :]
+                grad = cot_in[s % 8, src, :].astype(f32)
+                cot_out[dst, :] = jnp.where(row + k * 16 < seen, grad, 0.0).astype(bf16)
+                return carry
+
+            lax.fori_loop(0, (seen + 15) >> 4, chunk, 0)
+
+        @pl.when(core == s // 8)
+        def _():
+            fetch(x_own, cot_own)
+
+        @pl.when(core != s // 8)
+        def _():
+            fetch(x_other, cot_other)
+
+
+def owner_of(idx, column, k):
+    y, x, z = idx[1], idx[2], idx[4]
+    yy = 1 - y if column >= 2 else y
+    xx = 1 - x if column % 2 else x
+    return yy * 2 + xx, jnp.bitwise_xor(z, k)
+
+
+def core_of(idx, part):
+    return 1 - idx[3] if part else idx[3]
+
+
+def lanes_of(small, first, count):
+    rows = [small[q // 9, q % 9 : q % 9 + 1, :] for q in range(first, first + count)]
+    return jnp.concatenate(rows, axis=1)
+
+
+def same_sample(meta, which):
+    lane = lax.broadcasted_iota(jnp.int32, (8, BIN), 1)
+    line = lax.broadcasted_iota(jnp.int32, (BIN, BIN), 0)
+    of_key = jnp.full((8, BIN), -2, jnp.int32)
+    of_query = jnp.full((BIN, BIN), -1, jnp.int32)
+    for s in range(16):
+        start = meta[8 + s] - which * BIN
+        stop = start + meta[24 + s]
+        of_key = jnp.where((lane >= start) & (lane < stop), s, of_key)
+        of_query = jnp.where((line >= start) & (line < stop), s, of_query)
+    return of_query == of_key[0:1, :]
+
+
+def halves(pair):
+    lane = lax.broadcasted_iota(jnp.int32, pair.shape, 1)
+    wide = pair.astype(f32)
+    return jnp.concatenate(
+        [jnp.where(lane < HD, wide, 0.0), jnp.where(lane >= HD, wide, 0.0)], axis=0
+    ).astype(bf16)
+
+
+def probabilities(query, keys, mask):
+    scores = dot(halves(query), keys, ((1,), (1,))) * (1.0 / math.sqrt(HD))
+    scores = jnp.where(mask, scores, -1e30)
+    expo = jnp.exp(scores - jnp.max(scores, -1, keepdims=True))
+    return expo * (1.0 / jnp.sum(expo, -1, keepdims=True))
+
+
+def side_by_side(stacked):
+    return jnp.concatenate([stacked[:BIN], stacked[BIN:]], axis=1)
+
+
+def attn_forward(meta, idx, x_ref, *refs):
+    pieces = refs[:16]
+    qkv_ref, context_ref, part_ref, w_qkv, w_out, vecs, shift, inner_bias, small = refs[16:]
+
+    @pl.when(pl.program_id(0) == 0)
+    def _():
+        small[...] = jnp.zeros(small.shape, f32)
+        for n, piece in enumerate(pieces):
+            chip, z = owner_of(idx, n // 4, n % 4)
+
+            @pl.when(chip < 3)
+            def _():
+                for part in range(2):
+                    owner = (chip * 2 + core_of(idx, part)) * 4 + z
+                    to = pl.ds(pl.multiple_of(owner * 32, 32), 32)
+                    for j in range(9):
+                        at = part * 288 + j * 32
+                        w_qkv[to, j * ROW : (j + 1) * ROW] = piece[at : at + 32, :]
+
+            @pl.when(chip == 3)
+            def _():
+                to = pl.ds(pl.multiple_of(z * 96, 32), 96)
+                for j in range(6):
+                    w_out[to, j * ROW : (j + 1) * ROW] = piece[j * 96 : (j + 1) * 96, :]
+
+            for part in range(2):
+                group = chip * 2 + core_of(idx, part)
+                at = 576 + part * 16
+                small[group] = small[group] + piece[at : at + 16, :].astype(f32)
+        for n, first in enumerate((0, 6, 24, 30, 36, 66)):
+            vecs[n : n + 1, :] = lanes_of(small, first, 6)
+        vecs[6:8, :] = jnp.zeros((2, D), f32)
+        own = idx[3] == 0
+        query_bias = jnp.where(own, lanes_of(small, 12, 3), lanes_of(small, 15, 3))
+        value_bias = jnp.where(own, lanes_of(small, 18, 3), lanes_of(small, 21, 3))
+        shift[...] = jnp.concatenate([query_bias, jnp.zeros((1, D // 2), f32), value_bias], axis=1)
+        low = jnp.where(own, lanes_of(small, 42, 6), lanes_of(small, 48, 6))
+        high = jnp.where(own, lanes_of(small, 54, 6), lanes_of(small, 60, 6))
+        inner_bias[...] = jnp.concatenate([low, high], axis=1)
+
+    @pl.when(pl.program_id(0) < meta[0])
+    def _():
+        normed, _ = standard(x_ref[...].astype(f32))
+        first_in = (normed * vecs[0:1, :] + vecs[1:2, :]).astype(bf16)
+        qkv_ref[...] = (dot(first_in, w_qkv[...]) + shift[...]).astype(bf16)
+        for b in range(BLOCK // BIN):
+            mask = same_sample(meta, pl.program_id(0) * (BLOCK // BIN) + b)
+            mask = jnp.concatenate([mask, mask], axis=0)
+            rows = slice(b * BIN, (b + 1) * BIN)
+            for h in range(3):
+                query, keys, values = (
+                    qkv_ref[rows, (3 * t + h) * ROW : (3 * t + h + 1) * ROW] for t in range(3)
+                )
+                probs = probabilities(query, keys, mask).astype(bf16)
+                context = dot(side_by_side(probs), halves(values))
+                context_ref[rows, h * ROW : (h + 1) * ROW] = context.astype(bf16)
+        part_ref[...] = dot(context_ref[...], w_out[...]).astype(bf16)
+
+
+ERF_TOP = (0.00022905065861350646, 0.0034082910107109506, 0.050955695062380861, 0.18520832239976145, 1.128379143519084)
+ERF_BOTTOM = (-1.1791602954361697e-7, 0.000023547966471313185, 0.0010179625278914885, 0.014070470171167667,
+              0.11098505178285362, 0.49746925110067538, 1.0)
+
+
+def error_function(v):
+    v = jnp.clip(v, -3.832506856900711, 3.832506856900711)
+    square = v * v
+    top, bottom = jnp.full_like(v, ERF_TOP[0]), jnp.full_like(v, ERF_BOTTOM[0])
+    for a in ERF_TOP[1:]:
+        top = top * square + a
+    for b in ERF_BOTTOM[1:]:
+        bottom = bottom * square + b
+    return v * top / bottom
+
+
+def middle_of(x_ref, part_own, part_other, vecs):
+    parts = part_own[...].astype(f32) + part_other[...].astype(f32)
+    return x_ref[...].astype(f32) + parts + vecs[2:3, :]
+
+
+def mlp_both(meta, idx, x_ref, part_own, part_other, cot_ref, vecs, inner_bias, *refs):
+    pieces = refs[:16]
+    (active_ref, back_ref, w_two, sums, inner_sum) = refs[16:21]
+    outs = refs[21:29]
+    w_one, acc_one, acc_two = refs[29:]
+    step = pl.program_id(0)
+
+    @pl.when(step == 0)
+    def _():
+        acc_one[...] = jnp.zeros(acc_one.shape, f32)
+        acc_two[...] = jnp.zeros(acc_two.shape, f32)
+        sums[...] = jnp.zeros(sums.shape, f32)
+        inner_sum[...] = jnp.zeros(inner_sum.shape, f32)
+        for n, piece in enumerate(pieces):
+            chip, z = owner_of(idx, n // 4, n % 4)
+
+            @pl.when(chip < 2)
+            def _():
+                for part in range(2):
+                    owner = (chip * 2 + core_of(idx, part)) * 4 + z
+                    to = pl.ds(pl.multiple_of(owner * 48, 16), 48)
+                    for j in range(12):
+                        at = part * 576 + j * 48
+                        w_one[to, j * ROW : (j + 1) * ROW] = piece[at : at + 48, :]
+
+            @pl.when(chip >= 2)
+            def _():
+                to = pl.ds(pl.multiple_of((chip - 2) * D + z * 192, 64), 192)
+                for j in range(6):
+                    w_two[to, j * ROW : (j + 1) * ROW] = piece[j * 192 : (j + 1) * 192, :]
+
+    @pl.when(pl.program_id(0) < meta[0])
+    def _():
+        normed, _ = standard(middle_of(x_ref, part_own, part_other, vecs))
+        second_in = (normed * vecs[3:4, :] + vecs[4:5, :]).astype(bf16)
+        grad = cot_ref[...]
+        back = jnp.zeros((BLOCK, D), f32)
+        for n in range(2):
+            cols = slice(n * D, (n + 1) * D)
+            inner = dot(second_in, w_one[:, cols]) + inner_bias[:, cols]
+            bell = 0.5 * (1.0 + error_function(inner * inv_root_two))
+            active = (inner * bell).astype(bf16)
+            active_ref[:, cols] = active
+            slope = bell + inner * jnp.exp(-0.5 * inner * inner) * inv_root_tau
+            grad_inner = (dot(grad, w_two[cols, :], ((1,), (1,))) * slope).astype(bf16)
+            acc_two[cols, :] += dot(active, grad, ((0,), (0,)))
+            acc_one[:, cols] += dot(second_in, grad_inner, ((0,), (0,)))
+            inner_sum[:, cols] += jnp.sum(grad_inner.astype(f32), 0, keepdims=True)
+            back = back + dot(grad_inner, w_one[:, cols], ((1,), (1,)))
+        back_ref[...] = back.astype(bf16)
+        sums[0:1, :] += jnp.sum(back * normed, 0, keepdims=True)
+        sums[1:2, :] += jnp.sum(back, 0, keepdims=True)
+        sums[2:3, :] += jnp.sum(grad.astype(f32), 0, keepdims=True)
+
+    @pl.when(step == pl.num_programs(0) - 1)
+    def _():
+        for n in range(16):
+            chip, z = owner_of(idx, n // 4, n % 4)
+            out, k = outs[n // 2], n % 2
+
+            @pl.when(chip < 2)
+            def _():
+                for part in range(2):
+                    owner = (chip * 2 + core_of(idx, part)) * 4 + z
+                    rows = pl.ds(pl.multiple_of(owner * 48, 16), 48)
+                    for j in range(12):
+                        at = part * 576 + j * 48
+                        out[k, at : at + 48, :] = acc_one[rows, j * ROW : (j + 1) * ROW].astype(bf16)
+
+            @pl.when(chip >= 2)
+            def _():
+                rows = pl.ds(pl.multiple_of((chip - 2) * D + z * 192, 64), 192)
+                for j in range(6):
+                    out[k, j * 192 : (j + 1) * 192, :] = acc_two[rows, j * ROW : (j + 1) * ROW].astype(bf16)
+
+
+def mlp_out(meta, active_ref, w_two, part_ref):
+    @pl.when(pl.program_id(0) < meta[0])
+    def _():
+        part_ref[...] = dot(active_ref[...], w_two[...]).astype(bf16)
+
+
+def attn_backward(meta, idx, x_ref, part_own, part_other, cot_ref, back_own, back_other, qkv_ref, context_ref,
+                  w_qkv, w_out, vecs, sums_in, inner_sum, *refs):
+    grad_ref, back_ref = refs[:2]
+    outs = refs[2:10]
+    acc_qkv, acc_out, sums, small, grads = refs[10:]
+    step = pl.program_id(0)
+
+    @pl.when(step == 0)
+    def _():
+        acc_qkv[...] = jnp.zeros(acc_qkv.shape, f32)
+        acc_out[...] = jnp.zeros(acc_out.shape, f32)
+        sums[...] = jnp.zeros(sums.shape, f32)
+
+    @pl.when(pl.program_id(0) < meta[0])
+    def _():
+        normed, factor = standard(middle_of(x_ref, part_own, part_other, vecs))
+        scaled = (back_own[...].astype(f32) + back_other[...].astype(f32)) * vecs[3:4, :]
+        through = scaled - jnp.mean(scaled, -1, keepdims=True)
+        through = through - normed * jnp.mean(scaled * normed, -1, keepdims=True)
+        grad_middle = cot_ref[...].astype(f32) + factor * through
+        grad_ref[...] = grad_middle
+        grad_proj = grad_middle.astype(bf16)
+        context = context_ref[...]
+        acc_out[...] += dot(context, grad_proj, ((0,), (0,)))
+        sums[2:3, :] += jnp.sum(grad_proj.astype(f32), 0, keepdims=True)
+        grad_context = dot(grad_proj, w_out[...], ((1,), (1,))).astype(bf16)
+        scale = 1.0 / math.sqrt(HD)
+        for b in range(BLOCK // BIN):
+            mask = same_sample(meta, step * (BLOCK // BIN) + b)
+            mask = jnp.concatenate([mask, mask], axis=0)
+            rows = slice(b * BIN, (b + 1) * BIN)
+            for h in range(3):
+                cols = [slice((3 * t + h) * ROW, (3 * t + h + 1) * ROW) for t in range(3)]
+                query, keys, values = (qkv_ref[rows, cols[t]] for t in range(3))
+                probs = probabilities(query, keys, mask)
+                grad_out = halves(grad_context[rows, h * ROW : (h + 1) * ROW])
+                grad_values = dot(probs.astype(bf16), grad_out, ((0,), (0,)))
+                grad_probs = dot(grad_out, values, ((1,), (1,)))
+                total = jnp.sum(grad_probs * probs, -1, keepdims=True)
+                grad_scores = (probs * (grad_probs - total)).astype(bf16)
+                grad_query = dot(side_by_side(grad_scores), halves(keys)) * scale
+                grad_keys = dot(grad_scores, halves(query), ((0,), (0,))) * scale
+                grads[rows, cols[0]] = grad_query.astype(bf16)
+                grads[rows, cols[1]] = grad_keys.astype(bf16)
+                grads[rows, cols[2]] = grad_values.astype(bf16)
+        normed, _ = standard(x_ref[...].astype(f32))
+        first_in = (normed * vecs[0:1, :] + vecs[1:2, :]).astype(bf16)
+        grad_qkv = grads[...]
+        acc_qkv[...] += dot(first_in, grad_qkv, ((0,), (0,)))
+        back = dot(grad_qkv, w_qkv[...], ((1,), (1,)))
+        back_ref[...] = back.astype(bf16)
+        sums[0:1, :] += jnp.sum(back * normed, 0, keepdims=True)
+        sums[1:2, :] += jnp.sum(back, 0, keepdims=True)
+        sums[3:4, 0 : D // 2] += jnp.sum(grad_qkv[:, 0 : D // 2].astype(f32), 0, keepdims=True)
+        sums[3:4, D // 2 : D] += jnp.sum(grad_qkv[:, D : D + D // 2].astype(f32), 0, keepdims=True)
+
+    @pl.when(step == pl.num_programs(0) - 1)
+    def _():
+        small[...] = jnp.zeros(small.shape, f32)
+        first = idx[3] == 0
+        once = jnp.where(first, 1.0, 0.0)
+
+        def put(at, rows):
+            for j in range(rows.shape[1] // ROW):
+                q = at + j
+                small[q // 9, q % 9 : q % 9 + 1, :] = rows[:, j * ROW : (j + 1) * ROW]
+
+        put(0, sums[0:1, :])
+        put(6, sums[1:2, :])
+        put(24, sums[2:3, :] * once)
+        put(30, sums_in[0:1, :])
+        put(36, sums_in[1:2, :])
+        put(66, sums_in[2:3, :] * once)
+        for c in range(2):
+
+            @pl.when(idx[3] == c)
+            def _():
+                put(12 + 3 * c, sums[3:4, 0 : D // 2])
+                put(18 + 3 * c, sums[3:4, D // 2 : D])
+                put(42 + 6 * c, inner_sum[:, 0:D])
+                put(54 + 6 * c, inner_sum[:, D : 2 * D])
+
+        for n in range(16):
+            chip, z = owner_of(idx, n // 4, n % 4)
+            out, k = outs[n // 2], n % 2
+
+            @pl.when(chip < 3)
+            def _():
+                for part in range(2):
+                    owner = (chip * 2 + core_of(idx, part)) * 4 + z
+                    rows = pl.ds(pl.multiple_of(owner * 32, 32), 32)
+                    for j in range(9):
+                        at = part * 288 + j * 32
+                        out[k, at : at + 32, :] = acc_qkv[rows, j * ROW : (j + 1) * ROW].astype(bf16)
+
+            @pl.when(chip == 3)
+            def _():
+                rows = pl.ds(pl.multiple_of(z * 96, 32), 96)
+                for j in range(6):
+                    out[k, j * 96 : (j + 1) * 96, :] = acc_out[rows, j * ROW : (j + 1) * ROW].astype(bf16)
+
+            for part in range(2):
+                group = chip * 2 + core_of(idx, part)
+                out[k, 576 + part * 16 : 592 + part * 16, :] = small[group].astype(bf16)
+
+
+def finish_rows(meta, idx, x_ref, part_own, part_other, out_own, out_other, grad_ref, back_own, back_other, vecs,
+                output, grad_samples, packed_out, packed_grad):
+    step = pl.program_id(0)
+    @pl.when(pl.program_id(0) < meta[0])
+    def _():
+        at = pl.ds(pl.multiple_of(step * BLOCK, BLOCK), BLOCK)
+        parts = out_own[...].astype(f32) + out_other[...].astype(f32)
+        result = middle_of(x_ref, part_own, part_other, vecs) + parts + vecs[5:6, :]
+        packed_out[at, :] = result.astype(bf16)
+        normed, factor = standard(x_ref[...].astype(f32))
+        scaled = (back_own[...].astype(f32) + back_other[...].astype(f32)) * vecs[0:1, :]
+        through = scaled - jnp.mean(scaled, -1, keepdims=True)
+        through = through - normed * jnp.mean(scaled * normed, -1, keepdims=True)
+        packed_grad[at, :] = (grad_ref[...] + factor * through).astype(bf16)
+
+    @pl.when(step == pl.num_programs(0) - 1)
+    def _():
+        output[...] = jnp.zeros(output.shape, bf16)
+        grad_samples[...] = jnp.zeros(grad_samples.shape, bf16)
+        row = lax.broadcasted_iota(jnp.int32, (16, D), 0)
+        for s in range(8):
+            start, seen = meta[8 + idx[3] * 8 + s], meta[24 + idx[3] * 8 + s]
+
+            def chunk(k, carry):
+                src = pl.ds(pl.multiple_of(start + k * 16, 16), 16)
+                dst = pl.ds(pl.multiple_of(k * 16, 16), 16)
+                keep = row + k * 16 < seen
+                for packed, out in ((packed_out, output), (packed_grad, grad_samples)):
+                    out[s, dst, :] = jnp.where(keep, packed[src, :].astype(f32), 0.0).astype(bf16)
+                return carry
+
+            lax.fori_loop(0, (seen + 15) >> 4, chunk, 0)
+
+
+def update_refs(master, first, second, grad, outs, decay, step_rate):
+    for out, new in zip(outs, adamw(master[...], first[...], second[...], grad, decay, step_rate)):
+        out[...] = new
+
+
+def step_mlp(idx, master, first, second, keep, other, new, new_first, new_second, half, grad):
+    wide, core = idx[0], idx[3]
+    mine = jnp.where(wide < 4, core, 0)
+    half[mine] = keep[...]
+    half[1 - mine] = other[...]
+
+    @pl.when(wide < 4)
+    def _():
+        for c in range(2):
+            for j in range(12):
+                grad[pl.ds(mlp_block(c, j), 48, stride=24), :] = half[c, j * 48 : (j + 1) * 48, :]
+
+    @pl.when(wide >= 4)
+    def _():
+        for j in range(6):
+            grad[pl.ds(j, 192, stride=6), :] = half[j // 3, (j % 3) * 192 : (j % 3 + 1) * 192, :]
+
+    update_refs(master, first, second, grad[...], (new, new_first, new_second), 0.1, rate_matrix)
+
+
+def step_attn(idx, master, first, second, keep, other, master_s, first_s, second_s, keep_s, other_s,
+              new, new_first, new_second, new_s, new_first_s, new_second_s, half, grad):
+    wide, core = idx[0], idx[3]
+    mine = jnp.where(wide < 6, core, 0)
+    half[mine] = keep[...]
+    half[1 - mine] = other[...]
+
+    @pl.when(wide < 6)
+    def _():
+        for c in range(2):
+            for j in range(9):
+                grad[pl.ds(attn_block(c, j), 32, stride=18), :] = half[c, j * 32 : (j + 1) * 32, :]
+
+    @pl.when(wide >= 6)
+    def _():
+        for j in range(6):
+            grad[pl.ds(j, 96, stride=6), :] = half[j // 3, (j % 3) * 96 : (j % 3 + 1) * 96, :]
+
+    update_refs(master, first, second, grad[...], (new, new_first, new_second), 0.1, rate_matrix)
+    update_refs(master_s, first_s, second_s, keep_s[...] + other_s[...], (new_s, new_first_s, new_second_s), 0.0, rate_small)
+
+
+def gather_chips(piece):
+    by = {(0, 0): piece}
+    by[1, 0] = send(piece, TO_X)
+    by[2, 0] = send(piece, TO_Y)
+    by[0, 1] = send(piece, TO_Z[1])
+    by[3, 0] = send(by[2, 0], TO_X)
+    by[0, 2] = send(piece, TO_Z[2])
+    by[0, 3] = send(piece, TO_Z[3])
+    for k in (1, 2, 3):
+        by[1, k] = send(by[0, k], TO_X)
+        by[2, k] = send(by[0, k], TO_Y)
+        by[3, k] = send(by[1, k], TO_Y) if k % 2 else send(by[2, k], TO_X)
+    return [by[column, k] for column in range(4) for k in range(4)]
+
+
+def plus(*terms):
+    return sum(t.astype(f32) for t in terms)
+
+
+def scatter_chips(own_low, own_high, x_low, x_high, y_low, y_high, both_low, both_high):
+    from_x = send(both_low, TO_X)
+    from_y = send(both_high, TO_Y)
+    x_low_in = send(x_low, TO_X)
+    y_high_in = send(y_high, TO_Y)
+    y_low_in = send(plus(y_low, from_x).astype(bf16), TO_Y)
+    x_high_in = send(plus(x_high, from_y).astype(bf16), TO_X)
+    low = plus(own_low, x_low_in, y_low_in)
+    high = plus(own_high, x_high_in, y_high_in)
+    others = [send(t.astype(bf16), TO_Z[k]) for k, t in ((1, low[1]), (2, high[0]), (3, high[1]))]
+    return plus(low[0], *others)
+
+
+SMEM = pl.BlockSpec(memory_space=pltpu.SMEM)
+
+
+def whole(shape):
+    return pl.BlockSpec(shape, lambda i, *_: (0,) * len(shape))
+
+
+def once_in(shape):
+    return pl.BlockSpec(shape, lambda i, *_: (0,) * len(shape), pipeline_mode=pl.Buffered(1))
+
+
+def rows_spec(width):
+    return pl.BlockSpec((BLOCK, width), lambda i, meta, *_: (jnp.minimum(i, meta[0] - 1), 0))
+
+
+def array(shape, dtype=bf16):
+    return jax.ShapeDtypeStruct(shape, dtype)
+
+
+def params(mib):
+    return pltpu.CompilerParams(vmem_limit_bytes=mib << 20)
+
+
+def cost(flops, nbytes):
+    return pl.CostEstimate(flops=flops, bytes_accessed=nbytes, transcendentals=0)
+
+
+def over_blocks(body, steps, scalars, in_specs, out_specs, out_shape, scratch, mib, flops, nbytes, name):
+    return pl.pallas_call(
+        body,
+        grid_spec=pltpu.PrefetchScalarGridSpec(
+            num_scalar_prefetch=scalars, grid=(steps,), in_specs=in_specs, out_specs=out_specs, scratch_shapes=scratch
+        ),
+        out_shape=out_shape,
+        compiler_params=params(mib),
+        cost_estimate=cost(flops, nbytes),
+        name=name,
+    )
+
+
+def at_once(body, in_specs, out_specs, out_shape, scratch, mib, flops, nbytes, name):
+    return pl.pallas_call(
+        body,
+        in_specs=in_specs,
+        out_specs=out_specs,
+        out_shape=out_shape,
+        scratch_shapes=scratch,
+        compiler_params=params(mib),
+        cost_estimate=cost(flops, nbytes),
+        name=name,
+    )
+
+
+VMEM = pl.BlockSpec(memory_space=pltpu.VMEM)
+
+
+def on_core(
+    samples,
+    cotangent,
+    visible,
+    master_attn,
+    first_attn,
+    second_attn,
+    master_mlp,
+    first_mlp,
+    second_mlp,
+    master_small,
+    first_small,
+    second_small,
+):
+    count, length, _ = samples.shape
+    rows = 2 * count * length
+    wide, z = lax.axis_index("wide"), lax.axis_index("narrow")
+    idx = jnp.stack([wide, wide // 4, (wide // 2) % 2, wide % 2, z]).astype(jnp.int32)
+
+    def lanes(flat):
+        return flat.reshape(-1, ROW)
+
+    def spread(vector):
+        return lanes(lax.dynamic_update_slice(jnp.zeros((16 * ROW,), f32), vector, (z * 288,)))
+
+    small_low = spread(master_small).astype(bf16)
+    half_a, half_m = (288, ROW), (576, ROW)
+    keep_a, send_a, keep_m, send_m = at_once(
+        cut_masters, [SMEM, VMEM, VMEM], [VMEM] * 4,
+        [array(half_a), array(half_a), array(half_m), array(half_m)],
+        [pltpu.VMEM((2, *half_a), bf16), pltpu.VMEM((2, *half_m), bf16)], 16, 10**9, 2 * 10**6, "cut_masters",
+    )(idx, lanes(master_attn), lanes(master_mlp))
+    piece_a = jnp.concatenate([keep_a, send(send_a, SWAP_ATTN), small_low, send(small_low, TO_CORE)])
+    pieces_a = gather_chips(piece_a)
+    piece_m = jnp.concatenate([keep_m, send(send_m, SWAP_MLP)])
+    pieces_m = gather_chips(piece_m)
+
+    x, cot, meta = at_once(
+        pack_rows, [SMEM, SMEM, SMEM] + [VMEM] * 4, [VMEM, VMEM, SMEM],
+        [array((rows, D)), array((rows, D)), array((64,), jnp.int32)],
+        [pltpu.SMEM((16,), jnp.int32)], 32, 10**9, 12 * 10**6, "pack_rows",
+    )(idx, visible, send(visible, TO_CORE), samples, send(samples, TO_CORE), cotangent, send(cotangent, TO_CORE))
+    steps = rows // BLOCK
+
+    row_d, row_half, row_qkv, row_inner = rows_spec(D), rows_spec(D // 2), rows_spec(3 * D // 2), rows_spec(FF // 2)
+    qkv, context, part, w_qkv, w_out, vecs, shift, inner_bias = over_blocks(
+        attn_forward, steps, 2, [row_d] + [once_in((608, ROW))] * 16,
+        [row_qkv, row_half, row_d, whole((D, 3 * D // 2)), whole((D // 2, D)), whole((8, D)), whole((1, 3 * D // 2)), whole((1, FF // 2))],
+        [array((rows, 3 * D // 2)), array((rows, D // 2)), array((rows, D)), array((D, 3 * D // 2)), array((D // 2, D)),
+         array((8, D), f32), array((1, 3 * D // 2), f32), array((1, FF // 2), f32)],
+        [pltpu.VMEM((8, 16, ROW), f32)], 32, 5 * 10**9, 10**7, "attn_forward",
+    )(meta, idx, x, *pieces_a)
+    part_other = send(part, TO_CORE)
+
+    pair_m = (2, 1152, ROW)
+    mlp = over_blocks(
+        mlp_both, steps, 2, [row_d] * 4 + [once_in((8, D)), once_in((1, FF // 2))] + [once_in((1152, ROW))] * 16,
+        [row_inner, row_d, whole((FF // 2, D)), whole((8, D)), whole((1, FF // 2))] + [whole(pair_m)] * 8,
+        [array((rows, FF // 2)), array((rows, D)), array((FF // 2, D)), array((8, D), f32), array((1, FF // 2), f32)] + [array(pair_m)] * 8,
+        [pltpu.VMEM((D, FF // 2), bf16), pltpu.VMEM((D, FF // 2), f32), pltpu.VMEM((FF // 2, D), f32)],
+        56, 10**10, 2 * 10**7, "mlp_both",
+    )(meta, idx, x, part, part_other, cot, vecs, inner_bias, *pieces_m)
+    active, back, w_two, sums, inner_sum = mlp[:5]
+    back_other = send(back, TO_CORE)
+    summed_m = scatter_chips(*mlp[5:])
+
+    out_part = over_blocks(
+        mlp_out, steps, 1, [row_inner, once_in((FF // 2, D))], row_d, array((rows, D)), [], 16, 10**9, 10**7, "mlp_out",
+    )(meta, active, w_two)
+    out_other = send(out_part, TO_CORE)
+
+    pair_a = (2, 608, ROW)
+    attn = over_blocks(
+        attn_backward, steps, 2,
+        [row_d] * 6 + [row_qkv, row_half, once_in((D, 3 * D // 2)), once_in((D // 2, D)), once_in((8, D)), once_in((8, D)), once_in((1, FF // 2))],
+        [row_d, row_d] + [whole(pair_a)] * 8,
+        [array((rows, D), f32), array((rows, D))] + [array(pair_a)] * 8,
+        [pltpu.VMEM((D, 3 * D // 2), f32), pltpu.VMEM((D // 2, D), f32), pltpu.VMEM((8, D), f32), pltpu.VMEM((8, 16, ROW), f32),
+         pltpu.VMEM((BLOCK, 3 * D // 2), bf16)],
+        40, 8 * 10**9, 10**7, "attn_backward",
+    )(meta, idx, x, part, part_other, cot, back, back_other, qkv, context, w_qkv, w_out, vecs, sums, inner_sum)
+    grad_middle, first_back = attn[:2]
+    first_other = send(first_back, TO_CORE)
+    summed_a = scatter_chips(*attn[2:])
+
+    output, grad_samples = over_blocks(
+        finish_rows, steps, 2, [row_d] * 8 + [once_in((8, D))],
+        [whole((count, length, D))] * 2, [array((count, length, D))] * 2,
+        [pltpu.VMEM((rows, D), bf16)] * 2, 32, 10**9, 10**7, "finish_rows",
+    )(meta, idx, x, part, part_other, out_part, out_other, grad_middle, first_back, first_other, vecs)
+
+    shape_m, shape_a, shape_s = (1152, ROW), (576, ROW), (16, ROW)
+    new_mlp = at_once(
+        step_mlp, [SMEM] + [VMEM] * 5, [VMEM] * 3, [array(shape_m, f32)] * 3,
+        [pltpu.VMEM((2, *half_m), f32), pltpu.VMEM(shape_m, f32)], 16, 10**9, 4 * 10**6, "step_mlp",
+    )(idx, lanes(master_mlp), lanes(first_mlp), lanes(second_mlp), summed_m[:576], send(summed_m[576:], SWAP_MLP))
+    new_attn = at_once(
+        step_attn, [SMEM] + [VMEM] * 10, [VMEM] * 6, [array(shape_a, f32)] * 3 + [array(shape_s, f32)] * 3,
+        [pltpu.VMEM((2, *half_a), f32), pltpu.VMEM(shape_a, f32)], 16, 10**9, 2 * 10**6, "step_attn",
+    )(idx, lanes(master_attn), lanes(first_attn), lanes(second_attn), summed_a[:288], send(summed_a[288:576], SWAP_ATTN),
+      spread(master_small), spread(first_small), spread(second_small), summed_a[576:592], send(summed_a[592:], TO_CORE))
+    new_small = [lax.dynamic_slice(v.reshape(-1), (z * 288,), (288,)) for v in new_attn[3:]]
+    return (output, grad_samples, *(v.reshape(-1) for v in new_attn[:3]), *(v.reshape(-1) for v in new_mlp), *new_small)
+
+
 def solution(mesh):
     in_specs = (
         P(("wide", "narrow"), None, None),
@@ -252,6 +982,7 @@
         P(("wide", "narrow")),
         P(("wide", "narrow")),
     )
+    small_slice = mesh.shape["wide"] == 8 and mesh.shape["narrow"] == 4
     return jax.shard_map(
-        on_device, mesh=mesh, in_specs=in_specs, out_specs=out_specs, check_vma=False
-    )
+        on_core if small_slice else on_device, mesh=mesh, in_specs=in_specs, out_specs=out_specs, check_vma=False
+    )

time: 572 us -> 284 us (0.50)
  matrix products: 131 us -> 0 us
  local copies, waits for them, and re-layouts: 104 us -> 15.5 us
  starting transfers between devices: 0.16 us -> 84 us
  blocking collectives: 82.4 us -> 0 us
  waiting for transfers between devices: 183 us -> 113 us
  Pallas kernels: 0 us -> 61.1 us
  other arithmetic: 48.2 us -> 4.89 us
  between operations: 14.8 us -> 1.5 us
    dot_general x18 -> x0, matrix products: 131 us -> none  [the longest x1 37.3 us: on_device(): jnp.dot(second_in, w_one, preferred_element_type=jnp.float32) + bias_inner]
    reduce_scatter x2 -> x0, waiting for transfers between devices: 128 us -> none  [scatter_sum(): lax.psum_scatter(lanes, ('wide', 'narrow'), scatter_dimension=0, tiled=True)]
    ppermute x0 -> x61, waiting for transfers between devices: none -> 113 us  [send(): return lax.ppermute(value, AXES, pairs)]
    ppermute x0 -> x61, starting transfers between devices: none -> 84 us  [send(): return lax.ppermute(value, AXES, pairs)]
    unnamed x2 -> x0, blocking collectives: 82.4 us -> none
    pallas_call x0 -> x9, Pallas kernels: none -> 61.1 us  [the longest x1 20.9 us: on_core(): over_blocks(mlp_both, steps, 2, [row_d] * 4 + [once_in((8, D)), once_in((...]
    all_gather x2 -> x0, waiting for transfers between devices: 55.4 us -> none  [the longest x1 38.8 us: on_device(): lax.all_gather(master_mlp.astype(jnp.bfloat16), ('wide', 'narrow'), axis=...]
    slice x14 -> x3, local copies, waits for them, and re-layouts: 39.9 us -> 0.06 us  [the longest x1 0.04 us: on_core(): summed_m[576:]]
  transfers between devices with their start and end apart: 4 -> 61, of which waited for: 3 -> 24; matrix products, arithmetic and copies ran while one was open for 23% -> 3% of each run, Pallas kernels for 0% -> 10%
where the time goes in v2:
time: 284 us; the launch traced here: 280 us
  waiting for transfers between devices  113 us (40%)
  starting transfers between devices  84 us (30%)
  Pallas kernels  61.1 us (22%)
  local copies, waits for them, and re-layouts  15.5 us (5%)
  other arithmetic  4.89 us (2%)
    ppermute x61, waiting for transfers between devices, send(): return lax.ppermute(value, AXES, pairs)  113 us
    ppermute x61, starting transfers between devices, send(): return lax.ppermute(value, AXES, pairs)  84 us
    pallas_call x1, Pallas kernels, on_core(): over_blocks(mlp_both, steps, 2, [row_d] * 4 + [once_in((8, D)), once_in((...  20.9 us
    pallas_call x1, Pallas kernels, on_core(): over_blocks(attn_backward, steps, 2, [row_d] * 6 + [row_qkv, row_half, on...  16.9 us
    unnamed x129, local copies, waits for them, and re-layouts  12.6 us
    pallas_call x1, Pallas kernels, on_core(): over_blocks(attn_forward, steps, 2, [row_d] + [once_in((608, ROW))] * 16,...  6.46 us
    pallas_call x1, Pallas kernels, on_core(): over_blocks(finish_rows, steps, 2, [row_d] * 8 + [once_in((8, D))], [whol...  6.29 us
  transfers between devices with their start and end apart: 61, of which 24 were waited for; matrix products, arithmetic and copies ran while one was open for 3% of the time, Pallas kernels for 10%

profile of v2, /device:TPU:0, one launch (start us, length us, event | category | flops | bytes accessed | tf_op | source)
XLA Modules:
  0.0 279.5 jit_solution(4894259237452414384)
XLA Ops:
  3.4 1.3 cut_masters.1
  4.7 2.3 collective-permute-start.3
  9.5 2.7 collective-permute-start.12
  12.2 1.4 collective-permute-start.8
  13.7 3.6 %collective-permute-start.7 = (bf16[608,128]{1,0:T(8,128)(2,1)S(1)}, bf16[608,128]{1,0:T(8,128)(2,1)S(1)}, u32[]{:S(2)}, u32[]{:S(2)}) collective-permute-start(bf16[608,128]{1,0:T(8,128)(2,1)S(1)} %pad_maximum_fusion.refs_0_), channel_id=1, source_target_pairs={{0,3},{1,2},{2,1},{3,0},{4,7},{5,6},{6,5},{7,4},{8,11},{9,10},{10,... | collective-permute-start | bytes 466952 | tf_op jit(solution)/shard_map/ppermute | solution.py:260
  17.3 2.3 collective-permute-start.6
  19.6 1.6 collective-permute-start.5
  21.1 1.3 collective-permute-done.7.refs_3_
  23.1 7.7 %collective-permute-done.6.refs_2_ = bf16[608,128]{1,0:T(8,128)(2,1)S(1)} collective-permute-done((bf16[608,128]{1,0:T(8,128)(2,1)S(1)}, bf16[608,128]{1,0:T(8,128)(2,1)S(1)}, u32[]{:S(2)}, u32[]{:S(2)}) %collective-permute-start.6) | collective-permute-done | bytes 155680 | tf_op jit(solution)/shard_map/ppermute | solution.py:260
  32.5 1.5 collective-permute-start.14
  34.0 3.8 %collective-permute-done.15.refs_11_ = bf16[608,128]{1,0:T(8,128)(2,1)S(1)} collective-permute-done((bf16[608,128]{1,0:T(8,128)(2,1)S(1)}, bf16[608,128]{1,0:T(8,128)(2,1)S(1)}, u32[]{:S(2)}, u32[]{:S(2)}) %collective-permute-start.15) | collective-permute-done | bytes 155680 | tf_op jit(solution)/shard_map/ppermute | solution.py:260
  40.0 3.8 %collective-permute-done.9.refs_5_ = bf16[608,128]{1,0:T(8,128)(2,1)S(1)} collective-permute-done((bf16[608,128]{1,0:T(8,128)(2,1)S(1)}, bf16[608,128]{1,0:T(8,128)(2,1)S(1)}, u32[]{:S(2)}, u32[]{:S(2)}) %collective-permute-start.9) | collective-permute-done | bytes 155680 | tf_op jit(solution)/shard_map/ppermute | solution.py:260
  45.0 2.0 collective-permute-start.17
  47.0 3.2 %pack_rows.1 = (bf16[2048,768]{1,0:T(8,128)(2,1)S(1)}, bf16[2048,768]{1,0:T(8,128)(2,1)S(1)}, s32[64]{0:T(128)S(1)}) custom-call(s32[5]{0:T(128)S(1)} %stack.23.idx, s32[8]{0:T(128)S(1)} %copy-done.18, s32[8]{0:T(128)S(1)} %collective-permute-done.vis_other, bf16[8,128,768]{2,1,0:T(8,128)(2,1)S(1)} %copy-done.10, ...), custom_call_target="tpu_custom_call" | custom-call | flops 1000000000 | bytes 12000000 | tf_op jit(solution)/shard_map/pack_rows/pallas_call | solution.py:889
  50.3 1.6 copy-done.19
  51.9 6.5 %attn_forward.1 = (bf16[2048,1152]{1,0:T(8,128)(2,1)S(1)}, bf16[2048,384]{1,0:T(8,128)(2,1)S(1)}, bf16[2048,768]{1,0:T(8,128)(2,1)S(1)}, bf16[768,1152]{1,0:T(8,...) custom-call(s32[64]{0:T(128)S(1)} %get-tuple-element.59.meta, ...), custom_call_target="tpu_custom_call" | custom-call | flops 5000000000 | bytes 10000000 | tf_op jit(solution)/shard_map/attn_forward/pallas_call | solution.py:897
  58.4 2.1 copy-done.28
  60.6 1.3 copy-done.29
  63.8 2.4 collective-permute-start.21
  66.2 3.4 %collective-permute-done.21 = bf16[576,128]{1,0:T(8,128)(2,1)S(1)} collective-permute-done((bf16[576,128]{1,0:T(8,128)(2,1)S(1)}, bf16[576,128]{1,0:T(8,128)(2,1)S(1)}, u32[]{:S(2)}, u32[]{:S(2)}) %collective-permute-start.21) | collective-permute-done | bytes 147488 | tf_op jit(solution)/shard_map/ppermute | solution.py:260
  70.8 2.6 collective-permute-start.24
  73.3 5.5 %collective-permute-done.29.refs_8_ = bf16[1152,128]{1,0:T(8,128)(2,1)S(1)} collective-permute-done((bf16[1152,128]{1,0:T(8,128)(2,1)S(1)}, bf16[1152,128]{1,0:T(8,128)(2,1)S(1)}, u32[]{:S(2)}, u32[]{:S(2)}) %collective-permute-start.29) | collective-permute-done | bytes 294944 | tf_op jit(solution)/shard_map/ppermute | solution.py:260
  79.8 2.7 collective-permute-done.24.refs_3_
  82.5 2.0 collective-permute-start.32
  84.5 12.9 %collective-permute-done.23.refs_2_ = bf16[1152,128]{1,0:T(8,128)(2,1)S(1)} collective-permute-done((bf16[1152,128]{1,0:T(8,128)(2,1)S(1)}, bf16[1152,128]{1,0:T(8,128)(2,1)S(1)}, u32[]{:S(2)}, u32[]{:S(2)}) %collective-permute-start.23) | collective-permute-done | bytes 294944 | tf_op jit(solution)/shard_map/ppermute | solution.py:260
  97.4 1.2 collective-permute-start.28
  98.6 1.7 collective-permute-start.31
  101.1 1.2 collective-permute-start.26
  102.3 5.0 %collective-permute-done.28.refs_7_ = bf16[1152,128]{1,0:T(8,128)(2,1)S(1)} collective-permute-done((bf16[1152,128]{1,0:T(8,128)(2,1)S(1)}, bf16[1152,128]{1,0:T(8,128)(2,1)S(1)}, u32[]{:S(2)}, u32[]{:S(2)}) %collective-permute-start.28) | collective-permute-done | bytes 294944 | tf_op jit(solution)/shard_map/ppermute | solution.py:260
  107.3 1.7 collective-permute-start.30
  109.4 4.3 %collective-permute-done.27.refs_6_ = bf16[1152,128]{1,0:T(8,128)(2,1)S(1)} collective-permute-done((bf16[1152,128]{1,0:T(8,128)(2,1)S(1)}, bf16[1152,128]{1,0:T(8,128)(2,1)S(1)}, u32[]{:S(2)}, u32[]{:S(2)}) %collective-permute-start.27) | collective-permute-done | bytes 294944 | tf_op jit(solution)/shard_map/ppermute | solution.py:260
  114.8 5.1 %collective-permute-done.26.refs_5_ = bf16[1152,128]{1,0:T(8,128)(2,1)S(1)} collective-permute-done((bf16[1152,128]{1,0:T(8,128)(2,1)S(1)}, bf16[1152,128]{1,0:T(8,128)(2,1)S(1)}, u32[]{:S(2)}, u32[]{:S(2)}) %collective-permute-start.26) | collective-permute-done | bytes 294944 | tf_op jit(solution)/shard_map/ppermute | solution.py:260
  120.0 1.7 collective-permute-start.34
  121.7 2.6 collective-permute-done.35.refs_14_
  124.3 2.4 collective-permute-done.34.refs_13_
  128.5 20.9 %mlp_both.1 = (bf16[2048,1536]{1,0:T(8,128)(2,1)}, bf16[2048,768]{1,0:T(8,128)(2,1)}, bf16[1536,768]{1,0:T(8,128)(2,1)}, f32[8,768]{1,0:T(8,128)}, f32[1,1536]{1...) custom-call(s32[64]{0:T(128)} %copy-done.16, ...), custom_call_target="tpu_custom_call" | custom-call | flops 10000000000 | bytes 20000000 | tf_op jit(solution)/shard_map/mlp_both/pallas_call | solution.py:907
  149.4 1.2 collective-permute-start.52
  150.7 5.7 %collective-permute-start.55 = (bf16[2,1152,128]{2,1,0:T(8,128)(2,1)}, bf16[2,1152,128]{2,1,0:T(8,128)(2,1)S(1)}, u32[]{:S(2)}, u32[]{:S(2)}) collective-permute-start(bf16[2,1152,128]{2,1,0:T(8,128)(2,1)} %get-tuple-element.99), channel_id=1, source_target_pairs={{0,16},{1,17},{2,18},{3,19},{4,20},{5,21},{6,22},{7,23},{8,24},{9,... | collective-permute-start | bytes 1769480 | tf_op jit(solution)/shard_map/ppermute | solution.py:260
  156.4 1.9 collective-permute-start.51
  158.2 3.4 %collective-permute-done.52 = bf16[2,1152,128]{2,1,0:T(8,128)(2,1)S(1)} collective-permute-done((bf16[2,1152,128]{2,1,0:T(8,128)(2,1)}, bf16[2,1152,128]{2,1,0:T(8,128)(2,1)S(1)}, u32[]{:S(2)}, u32[]{:S(2)}) %collective-permute-start.52) | collective-permute-done | bytes 589856 | tf_op jit(solution)/shard_map/ppermute | solution.py:260
  161.7 1.4 add_convert_fusion.2
  163.0 11.1 %collective-permute-start.53 = (bf16[2,1152,128]{2,1,0:T(8,128)(2,1)S(1)}, bf16[2,1152,128]{2,1,0:T(8,128)(2,1)}, u32[]{:S(2)}, u32[]{:S(2)}) collective-permute-start(bf16[2,1152,128]{2,1,0:T(8,128)(2,1)S(1)} %add_convert_fusion.2), channel_id=1, source_target_pairs={{0,16},{1,17},{2,18},{3,19},{4,20},{5,21},{6,22},{7,23},{8,24},{9,... | collective-permute-start | bytes 1769480 | tf_op jit(solution)/shard_map/ppermute | solution.py:260
  175.0 13.5 %collective-permute-done.53 = bf16[2,1152,128]{2,1,0:T(8,128)(2,1)} collective-permute-done((bf16[2,1152,128]{2,1,0:T(8,128)(2,1)S(1)}, bf16[2,1152,128]{2,1,0:T(8,128)(2,1)}, u32[]{:S(2)}, u32[]{:S(2)}) %collective-permute-start.53) | collective-permute-done | bytes 589856 | tf_op jit(solution)/shard_map/ppermute | solution.py:260
  188.5 1.7 convert_add_fusion
  190.3 5.4 %collective-permute-done.57 = bf16[2,1152,128]{2,1,0:T(8,128)(2,1)S(1)} collective-permute-done((bf16[2,1152,128]{2,1,0:T(8,128)(2,1)}, bf16[2,1152,128]{2,1,0:T(8,128)(2,1)S(1)}, u32[]{:S(2)}, u32[]{:S(2)}) %collective-permute-start.57) | collective-permute-done | bytes 589856 | tf_op jit(solution)/shard_map/ppermute | solution.py:260
  196.1 16.9 %attn_backward.1 = (f32[2048,768]{1,0:T(8,128)}, bf16[2048,768]{1,0:T(8,128)(2,1)S(1)}, bf16[2,608,128]{2,1,0:T(8,128)(2,1)S(1)}, bf16[2,608,128]{2,1,0:T(8,128)...) custom-call(s32[64]{0:T(128)S(1)} %copy-done.17, ...), custom_call_target="tpu_custom_call" | custom-call | flops 8000000000 | bytes 10000000 | tf_op jit(solution)/shard_map/attn_backward/pallas_call | solution.py:924
  213.0 2.0 collective-permute-start.41
  215.2 1.7 copy-done.9
  216.9 2.2 mlp_out.1.out_own
  220.2 2.0 collective-permute-start.40
  222.3 7.3 %collective-permute-done.58 = bf16[1152,128]{1,0:T(8,128)(2,1)S(1)} collective-permute-done((bf16[1152,128]{1,0:T(8,128)(2,1)S(1)}, bf16[1152,128]{1,0:T(8,128)(2,1)S(1)}, u32[]{:S(2)}, u32[]{:S(2)}) %collective-permute-start.58) | collective-permute-done | bytes 294944 | tf_op jit(solution)/shard_map/ppermute | solution.py:260
  229.5 5.0 %collective-permute-start.44 = (bf16[2,608,128]{2,1,0:T(8,128)(2,1)S(1)}, bf16[2,608,128]{2,1,0:T(8,128)(2,1)S(1)}, u32[]{:S(2)}, u32[]{:S(2)}) collective-permute-start(bf16[2,608,128]{2,1,0:T(8,128)(2,1)S(1)} %get-tuple-element.88), channel_id=1, source_target_pairs={{0,16},{1,17},{2,18},{3,19},{4,20},{5,21},{6,22},{7,23},{8,24},{9,... | collective-permute-start | bytes 933896 | tf_op jit(solution)/shard_map/ppermute | solution.py:260
  234.7 8.1 %collective-permute-done.44 = bf16[2,608,128]{2,1,0:T(8,128)(2,1)S(1)} collective-permute-done((bf16[2,608,128]{2,1,0:T(8,128)(2,1)S(1)}, bf16[2,608,128]{2,1,0:T(8,128)(2,1)S(1)}, u32[]{:S(2)}, u32[]{:S(2)}) %collective-permute-start.44) | collective-permute-done | bytes 311328 | tf_op jit(solution)/shard_map/ppermute | solution.py:260
  242.8 2.0 collective-permute-start.46
  245.0 2.1 collective-permute-start.45
  247.0 1.7 collective-permute-done.42
  248.9 3.1 %collective-permute-done.46 = bf16[2,608,128]{2,1,0:T(8,128)(2,1)S(1)} collective-permute-done((bf16[2,608,128]{2,1,0:T(8,128)(2,1)S(1)}, bf16[2,608,128]{2,1,0:T(8,128)(2,1)S(1)}, u32[]{:S(2)}, u32[]{:S(2)}) %collective-permute-start.46) | collective-permute-done | bytes 311328 | tf_op jit(solution)/shard_map/ppermute | solution.py:260
  252.8 2.6 collective-permute-start.48
  255.5 2.2 collective-permute-start.60
  257.7 7.2 %collective-permute-done.47 = bf16[608,128]{1,0:T(8,128)(2,1)S(1)} collective-permute-done((bf16[608,128]{1,0:T(8,128)(2,1)S(1)}, bf16[608,128]{1,0:T(8,128)(2,1)S(1)}, u32[]{:S(2)}, u32[]{:S(2)}) %collective-permute-start.47) | collective-permute-done | bytes 155680 | tf_op jit(solution)/shard_map/ppermute | solution.py:260
  264.9 1.9 collective-permute-start.49
  267.5 2.1 step_mlp.1
  269.6 1.6 step_attn.1
  273.2 6.3 %finish_rows.1 = (bf16[8,128,768]{2,1,0:T(8,128)(2,1)}, bf16[8,128,768]{2,1,0:T(8,128)(2,1)}) custom-call(s32[64]{0:T(128)S(1)} %copy-done.17, s32[5]{0:T(128)S(1)} %copy-done.15, bf16[2048,768]{1,0:T(8,128)(2,1)S(1)} %copy-done.2, bf16[2048,768]{1,0:T(8,128)(2,1)S(1)} %copy-done.4, bf16[2048,768]{1,0:T(8,128)(2,1)S(1)} %copy-done.6, ...), custom_call_target="tpu_custom_call" | custom-call | flops 1000000000 | bytes 10000000 | tf_op jit(solution)/shard_map/finish_rows/pallas_call | solution.py:937
  (227 shorter events, 25.5 us)
Async XLA Ops:
  0.6 43.2 %collective-permute-start.1 = (bf16[8,128,768]{2,1,0:T(8,128)(2,1)}, bf16[8,128,768]{2,1,0:T(8,128)(2,1)}, u32[]{:S(2)}, u32[]{:S(2)}) collective-permute-start(bf16[8,128,768]{2,1,0:T(8,128)(2,1)} %x_own.1), channel_id=1, source_target_pairs={{0,4},{1,5},{2,6},{3,7},{4,0},{5,1},{6,2},{7,3},{8,12},{9,13},{10,... | collective-permute-start | bytes 4718600 | tf_op jit(solution)/shard_map/ppermute | solution.py:260
  1.2 43.8 %collective-permute-start.2 = (bf16[8,128,768]{2,1,0:T(8,128)(2,1)}, bf16[8,128,768]{2,1,0:T(8,128)(2,1)}, u32[]{:S(2)}, u32[]{:S(2)}) collective-permute-start(bf16[8,128,768]{2,1,0:T(8,128)(2,1)} %cot_own.1), channel_id=1, source_target_pairs={{0,4},{1,5},{2,6},{3,7},{4,0},{5,1},{6,2},{7,3},{8,12},{9,13},{10,... | collective-permute-start | bytes 4718600 | tf_op jit(solution)/shard_map/ppermute | solution.py:260
  4.7 3.9 %collective-permute-start.3 = (bf16[288,128]{1,0:T(8,128)(2,1)}, bf16[288,128]{1,0:T(8,128)(2,1)}, u32[]{:S(2)}, u32[]{:S(2)}) collective-permute-start(bf16[288,128]{1,0:T(8,128)(2,1)} %get-tuple-element.62), channel_id=1, source_target_pairs={{0,4},{1,5},{2,6},{3,7},{4,0},{5,1},{6,2},{7,3},{8,12},{9,13},{10,... | collective-permute-start | bytes 221192 | tf_op jit(solution)/shard_map/ppermute | solution.py:260
  7.4 1.2 collective-permute-start.4
  9.5 7.8 %collective-permute-start.12 = (bf16[608,128]{1,0:T(8,128)(2,1)S(1)}, bf16[608,128]{1,0:T(8,128)(2,1)S(1)}, u32[]{:S(2)}, u32[]{:S(2)}) collective-permute-start(bf16[608,128]{1,0:T(8,128)(2,1)S(1)} %pad_maximum_fusion.refs_0_), channel_id=1, source_target_pairs={{0,16},{1,17},{2,18},{3,19},{4,20},{5,21},{6,22},{7,23},{8,24},{9,... | collective-permute-start | bytes 466952 | tf_op jit(solution)/shard_map/ppermute | solution.py:260
  12.2 1.5 collective-permute-start
  12.2 7.3 %collective-permute-start.8 = (bf16[608,128]{1,0:T(8,128)(2,1)S(1)}, bf16[608,128]{1,0:T(8,128)(2,1)S(1)}, u32[]{:S(2)}, u32[]{:S(2)}) collective-permute-start(bf16[608,128]{1,0:T(8,128)(2,1)S(1)} %pad_maximum_fusion.refs_0_), channel_id=1, source_target_pairs={{0,8},{1,9},{2,10},{3,11},{4,12},{5,13},{6,14},{7,15},{8,0},{9,1},... | collective-permute-start | bytes 466952 | tf_op jit(solution)/shard_map/ppermute | solution.py:260
  13.7 8.8 %collective-permute-start.7 = (bf16[608,128]{1,0:T(8,128)(2,1)S(1)}, bf16[608,128]{1,0:T(8,128)(2,1)S(1)}, u32[]{:S(2)}, u32[]{:S(2)}) collective-permute-start(bf16[608,128]{1,0:T(8,128)(2,1)S(1)} %pad_maximum_fusion.refs_0_), channel_id=1, source_target_pairs={{0,3},{1,2},{2,1},{3,0},{4,7},{5,6},{6,5},{7,4},{8,11},{9,10},{10,... | collective-permute-start | bytes 466952 | tf_op jit(solution)/shard_map/ppermute | solution.py:260
  17.3 13.6 %collective-permute-start.6 = (bf16[608,128]{1,0:T(8,128)(2,1)S(1)}, bf16[608,128]{1,0:T(8,128)(2,1)S(1)}, u32[]{:S(2)}, u32[]{:S(2)}) collective-permute-start(bf16[608,128]{1,0:T(8,128)(2,1)S(1)} %pad_maximum_fusion.refs_0_), channel_id=1, source_target_pairs={{0,2},{1,3},{2,0},{3,1},{4,6},{5,7},{6,4},{7,5},{8,10},{9,11},{10,... | collective-permute-start | bytes 466952 | tf_op jit(solution)/shard_map/ppermute | solution.py:260
  19.6 11.8 %collective-permute-start.5 = (bf16[608,128]{1,0:T(8,128)(2,1)S(1)}, bf16[608,128]{1,0:T(8,128)(2,1)S(1)}, u32[]{:S(2)}, u32[]{:S(2)}) collective-permute-start(bf16[608,128]{1,0:T(8,128)(2,1)S(1)} %pad_maximum_fusion.refs_0_), channel_id=1, source_target_pairs={{0,1},{1,0},{2,3},{3,2},{4,5},{5,4},{6,7},{7,6},{8,9},{9,8},{10,11... | collective-permute-start | bytes 466952 | tf_op jit(solution)/shard_map/ppermute | solution.py:260
  22.4 10.1 %collective-permute-start.16 = (bf16[608,128]{1,0:T(8,128)(2,1)S(1)}, bf16[608,128]{1,0:T(8,128)(2,1)S(1)}, u32[]{:S(2)}, u32[]{:S(2)}) collective-permute-start(bf16[608,128]{1,0:T(8,128)(2,1)S(1)} %collective-permute-done.12.refs_8_), channel_id=1, source_target_pairs={{0,8},{1,9},{2,10},{3,11},{4,12},{5,13},{6,14},{7,15},{8,0},{9,1},... | collective-permute-start | bytes 466952 | tf_op jit(solution)/shard_map/ppermute | solution.py:260
  30.8 7.0 %collective-permute-start.15 = (bf16[608,128]{1,0:T(8,128)(2,1)S(1)}, bf16[608,128]{1,0:T(8,128)(2,1)S(1)}, u32[]{:S(2)}, u32[]{:S(2)}) collective-permute-start(bf16[608,128]{1,0:T(8,128)(2,1)S(1)} %collective-permute-done.7.refs_3_), channel_id=1, source_target_pairs={{0,16},{1,17},{2,18},{3,19},{4,20},{5,21},{6,22},{7,23},{8,24},{9,... | collective-permute-start | bytes 466952 | tf_op jit(solution)/shard_map/ppermute | solution.py:260
  31.4 7.5 %collective-permute-start.11 = (bf16[608,128]{1,0:T(8,128)(2,1)S(1)}, bf16[608,128]{1,0:T(8,128)(2,1)S(1)}, u32[]{:S(2)}, u32[]{:S(2)}) collective-permute-start(bf16[608,128]{1,0:T(8,128)(2,1)S(1)} %collective-permute-done.7.refs_3_), channel_id=1, source_target_pairs={{0,8},{1,9},{2,10},{3,11},{4,12},{5,13},{6,14},{7,15},{8,0},{9,1},... | collective-permute-start | bytes 466952 | tf_op jit(solution)/shard_map/ppermute | solution.py:260
  32.5 7.3 %collective-permute-start.14 = (bf16[608,128]{1,0:T(8,128)(2,1)S(1)}, bf16[608,128]{1,0:T(8,128)(2,1)S(1)}, u32[]{:S(2)}, u32[]{:S(2)}) collective-permute-start(bf16[608,128]{1,0:T(8,128)(2,1)S(1)} %collective-permute-done.6.refs_2_), channel_id=1, source_target_pairs={{0,16},{1,17},{2,18},{3,19},{4,20},{5,21},{6,22},{7,23},{8,24},{9,... | collective-permute-start | bytes 466952 | tf_op jit(solution)/shard_map/ppermute | solution.py:260
  37.8 6.1 %collective-permute-start.9 = (bf16[608,128]{1,0:T(8,128)(2,1)S(1)}, bf16[608,128]{1,0:T(8,128)(2,1)S(1)}, u32[]{:S(2)}, u32[]{:S(2)}) collective-permute-start(bf16[608,128]{1,0:T(8,128)(2,1)S(1)} %collective-permute-done.5.refs_1_), channel_id=1, source_target_pairs={{0,8},{1,9},{2,10},{3,11},{4,12},{5,13},{6,14},{7,15},{8,0},{9,1},... | collective-permute-start | bytes 466952 | tf_op jit(solution)/shard_map/ppermute | solution.py:260
  38.9 13.0 %collective-permute-start.10 = (bf16[608,128]{1,0:T(8,128)(2,1)S(1)}, bf16[608,128]{1,0:T(8,128)(2,1)S(1)}, u32[]{:S(2)}, u32[]{:S(2)}) collective-permute-start(bf16[608,128]{1,0:T(8,128)(2,1)S(1)} %collective-permute-done.6.refs_2_), channel_id=1, source_target_pairs={{0,8},{1,9},{2,10},{3,11},{4,12},{5,13},{6,14},{7,15},{8,0},{9,1},... | collective-permute-start | bytes 466952 | tf_op jit(solution)/shard_map/ppermute | solution.py:260
  39.8 12.1 %collective-permute-start.13 = (bf16[608,128]{1,0:T(8,128)(2,1)S(1)}, bf16[608,128]{1,0:T(8,128)(2,1)S(1)}, u32[]{:S(2)}, u32[]{:S(2)}) collective-permute-start(bf16[608,128]{1,0:T(8,128)(2,1)S(1)} %collective-permute-done.5.refs_1_), channel_id=1, source_target_pairs={{0,16},{1,17},{2,18},{3,19},{4,20},{5,21},{6,22},{7,23},{8,24},{9,... | collective-permute-start | bytes 466952 | tf_op jit(solution)/shard_map/ppermute | solution.py:260
  43.9 8.0 %collective-permute-start.19 = (bf16[608,128]{1,0:T(8,128)(2,1)S(1)}, bf16[608,128]{1,0:T(8,128)(2,1)S(1)}, u32[]{:S(2)}, u32[]{:S(2)}) collective-permute-start(bf16[608,128]{1,0:T(8,128)(2,1)S(1)} %collective-permute-done.11.refs_7_), channel_id=1, source_target_pairs={{0,16},{1,17},{2,18},{3,19},{4,20},{5,21},{6,22},{7,23},{8,24},{9,... | collective-permute-start | bytes 466952 | tf_op jit(solution)/shard_map/ppermute | solution.py:260
  43.9 8.0 %collective-permute-start.18 = (bf16[608,128]{1,0:T(8,128)(2,1)S(1)}, bf16[608,128]{1,0:T(8,128)(2,1)S(1)}, u32[]{:S(2)}, u32[]{:S(2)}) collective-permute-start(bf16[608,128]{1,0:T(8,128)(2,1)S(1)} %collective-permute-done.14.refs_10_), channel_id=1, source_target_pairs={{0,8},{1,9},{2,10},{3,11},{4,12},{5,13},{6,14},{7,15},{8,0},{9,1},... | collective-permute-start | bytes 466952 | tf_op jit(solution)/shard_map/ppermute | solution.py:260
  45.0 6.9 %collective-permute-start.17 = (bf16[608,128]{1,0:T(8,128)(2,1)S(1)}, bf16[608,128]{1,0:T(8,128)(2,1)S(1)}, u32[]{:S(2)}, u32[]{:S(2)}) collective-permute-start(bf16[608,128]{1,0:T(8,128)(2,1)S(1)} %collective-permute-done.9.refs_5_), channel_id=1, source_target_pairs={{0,16},{1,17},{2,18},{3,19},{4,20},{5,21},{6,22},{7,23},{8,24},{9,... | collective-permute-start | bytes 466952 | tf_op jit(solution)/shard_map/ppermute | solution.py:260
  63.8 62.9 %copy-start.12 = (f32[8,768]{1,0:T(8,128)}, f32[8,768]{1,0:T(8,128)S(1)}, u32[]{:S(2)}) copy-start(f32[8,768]{1,0:T(8,128)S(1)} %get-tuple-element.65.vecs) | copy-start | bytes 73732
  63.8 62.9 %copy-start.37 = (f32[1,1536]{1,0:T(1,128)}, f32[1,1536]{1,0:T(1,128)S(1)}, u32[]{:S(2)}) copy-start(f32[1,1536]{1,0:T(1,128)S(1)} %get-tuple-element.66.inner_bias) | copy-start | bytes 18436
  63.8 63.6 %copy-start.3 = (bf16[2048,768]{1,0:T(8,128)(2,1)}, bf16[2048,768]{1,0:T(8,128)(2,1)S(1)}, u32[]{:S(2)}) copy-start(bf16[2048,768]{1,0:T(8,128)(2,1)S(1)} %get-tuple-element.63.part_own) | copy-start | bytes 9437188
  63.8 62.9 %collective-permute-start.20 = (bf16[2048,768]{1,0:T(8,128)(2,1)S(1)}, bf16[2048,768]{1,0:T(8,128)(2,1)S(1)}, u32[]{:S(2)}, u32[]{:S(2)}) collective-permute-start(bf16[2048,768]{1,0:T(8,128)(2,1)S(1)} %get-tuple-element.63.part_own), channel_id=1, source_target_pairs={{0,4},{1,5},{2,6},{3,7},{4,0},{5,1},{6,2},{7,3},{8,12},{9,13},{10,... | collective-permute-start | bytes 9437192 | tf_op jit(solution)/shard_map/ppermute | solution.py:260
  63.8 5.9 %collective-permute-start.21 = (bf16[576,128]{1,0:T(8,128)(2,1)S(1)}, bf16[576,128]{1,0:T(8,128)(2,1)S(1)}, u32[]{:S(2)}, u32[]{:S(2)}) collective-permute-start(bf16[576,128]{1,0:T(8,128)(2,1)S(1)} %get-tuple-element.68), channel_id=1, source_target_pairs={{0,4},{1,5},{2,6},{3,7},{4,0},{5,1},{6,2},{7,3},{8,12},{9,13},{10,... | collective-permute-start | bytes 442376 | tf_op jit(solution)/shard_map/ppermute | solution.py:260
  69.7 9.1 %collective-permute-start.29 = (bf16[1152,128]{1,0:T(8,128)(2,1)S(1)}, bf16[1152,128]{1,0:T(8,128)(2,1)S(1)}, u32[]{:S(2)}, u32[]{:S(2)}) collective-permute-start(bf16[1152,128]{1,0:T(8,128)(2,1)S(1)} %constant_dynamic-update-slice_fusion.refs_0_), channel_id=1, source_target_pairs={{0,16},{1,17},{2,18},{3,19},{4,20},{5,21},{6,22},{7,23},{8,24},{9,... | collective-permute-start | bytes 884744 | tf_op jit(solution)/shard_map/ppermute | solution.py:260
  69.8 9.1 %collective-permute-start.25 = (bf16[1152,128]{1,0:T(8,128)(2,1)S(1)}, bf16[1152,128]{1,0:T(8,128)(2,1)S(1)}, u32[]{:S(2)}, u32[]{:S(2)}) collective-permute-start(bf16[1152,128]{1,0:T(8,128)(2,1)S(1)} %constant_dynamic-update-slice_fusion.refs_0_), channel_id=1, source_target_pairs={{0,8},{1,9},{2,10},{3,11},{4,12},{5,13},{6,14},{7,15},{8,0},{9,1},... | collective-permute-start | bytes 884744 | tf_op jit(solution)/shard_map/ppermute | solution.py:260
  70.8 11.7 %collective-permute-start.24 = (bf16[1152,128]{1,0:T(8,128)(2,1)S(1)}, bf16[1152,128]{1,0:T(8,128)(2,1)S(1)}, u32[]{:S(2)}, u32[]{:S(2)}) collective-permute-start(bf16[1152,128]{1,0:T(8,128)(2,1)S(1)} %constant_dynamic-update-slice_fusion.refs_0_), channel_id=1, source_target_pairs={{0,3},{1,2},{2,1},{3,0},{4,7},{5,6},{6,5},{7,4},{8,11},{9,10},{10,... | collective-permute-start | bytes 884744 | tf_op jit(solution)/shard_map/ppermute | solution.py:260
  73.3 24.0 %collective-permute-start.23 = (bf16[1152,128]{1,0:T(8,128)(2,1)S(1)}, bf16[1152,128]{1,0:T(8,128)(2,1)S(1)}, u32[]{:S(2)}, u32[]{:S(2)}) collective-permute-start(bf16[1152,128]{1,0:T(8,128)(2,1)S(1)} %constant_dynamic-update-slice_fusion.refs_0_), channel_id=1, source_target_pairs={{0,2},{1,3},{2,0},{3,1},{4,6},{5,7},{6,4},{7,5},{8,10},{9,11},{10,... | collective-permute-start | bytes 884744 | tf_op jit(solution)/shard_map/ppermute | solution.py:260
  78.8 19.7 %collective-permute-start.22 = (bf16[1152,128]{1,0:T(8,128)(2,1)S(1)}, bf16[1152,128]{1,0:T(8,128)(2,1)S(1)}, u32[]{:S(2)}, u32[]{:S(2)}) collective-permute-start(bf16[1152,128]{1,0:T(8,128)(2,1)S(1)} %constant_dynamic-update-slice_fusion.refs_0_), channel_id=1, source_target_pairs={{0,1},{1,0},{2,3},{3,2},{4,5},{5,4},{6,7},{7,6},{8,9},{9,8},{10,11... | collective-permute-start | bytes 884744 | tf_op jit(solution)/shard_map/ppermute | solution.py:260
  78.9 21.3 %collective-permute-start.33 = (bf16[1152,128]{1,0:T(8,128)(2,1)S(1)}, bf16[1152,128]{1,0:T(8,128)(2,1)S(1)}, u32[]{:S(2)}, u32[]{:S(2)}) collective-permute-start(bf16[1152,128]{1,0:T(8,128)(2,1)S(1)} %collective-permute-done.29.refs_8_), channel_id=1, source_target_pairs={{0,8},{1,9},{2,10},{3,11},{4,12},{5,13},{6,14},{7,15},{8,0},{9,1},... | collective-permute-start | bytes 884744 | tf_op jit(solution)/shard_map/ppermute | solution.py:260
  82.5 18.6 %collective-permute-start.32 = (bf16[1152,128]{1,0:T(8,128)(2,1)S(1)}, bf16[1152,128]{1,0:T(8,128)(2,1)S(1)}, u32[]{:S(2)}, u32[]{:S(2)}) collective-permute-start(bf16[1152,128]{1,0:T(8,128)(2,1)S(1)} %collective-permute-done.24.refs_3_), channel_id=1, source_target_pairs={{0,16},{1,17},{2,18},{3,19},{4,20},{5,21},{6,22},{7,23},{8,24},{9,... | collective-permute-start | bytes 884744 | tf_op jit(solution)/shard_map/ppermute | solution.py:260
  97.4 9.9 %collective-permute-start.28 = (bf16[1152,128]{1,0:T(8,128)(2,1)S(1)}, bf16[1152,128]{1,0:T(8,128)(2,1)S(1)}, u32[]{:S(2)}, u32[]{:S(2)}) collective-permute-start(bf16[1152,128]{1,0:T(8,128)(2,1)S(1)} %collective-permute-done.24.refs_3_), channel_id=1, source_target_pairs={{0,8},{1,9},{2,10},{3,11},{4,12},{5,13},{6,14},{7,15},{8,0},{9,1},... | collective-permute-start | bytes 884744 | tf_op jit(solution)/shard_map/ppermute | solution.py:260
  98.6 10.4 %collective-permute-start.31 = (bf16[1152,128]{1,0:T(8,128)(2,1)S(1)}, bf16[1152,128]{1,0:T(8,128)(2,1)S(1)}, u32[]{:S(2)}, u32[]{:S(2)}) collective-permute-start(bf16[1152,128]{1,0:T(8,128)(2,1)S(1)} %collective-permute-done.23.refs_2_), channel_id=1, source_target_pairs={{0,16},{1,17},{2,18},{3,19},{4,20},{5,21},{6,22},{7,23},{8,24},{9,... | collective-permute-start | bytes 884744 | tf_op jit(solution)/shard_map/ppermute | solution.py:260
  100.3 13.4 %collective-permute-start.27 = (bf16[1152,128]{1,0:T(8,128)(2,1)S(1)}, bf16[1152,128]{1,0:T(8,128)(2,1)S(1)}, u32[]{:S(2)}, u32[]{:S(2)}) collective-permute-start(bf16[1152,128]{1,0:T(8,128)(2,1)S(1)} %collective-permute-done.23.refs_2_), channel_id=1, source_target_pairs={{0,8},{1,9},{2,10},{3,11},{4,12},{5,13},{6,14},{7,15},{8,0},{9,1},... | collective-permute-start | bytes 884744 | tf_op jit(solution)/shard_map/ppermute | solution.py:260
  101.1 18.9 %collective-permute-start.26 = (bf16[1152,128]{1,0:T(8,128)(2,1)S(1)}, bf16[1152,128]{1,0:T(8,128)(2,1)S(1)}, u32[]{:S(2)}, u32[]{:S(2)}) collective-permute-start(bf16[1152,128]{1,0:T(8,128)(2,1)S(1)} %collective-permute-done.22.refs_1_), channel_id=1, source_target_pairs={{0,8},{1,9},{2,10},{3,11},{4,12},{5,13},{6,14},{7,15},{8,0},{9,1},... | collective-permute-start | bytes 884744 | tf_op jit(solution)/shard_map/ppermute | solution.py:260
  107.3 14.3 %collective-permute-start.30 = (bf16[1152,128]{1,0:T(8,128)(2,1)S(1)}, bf16[1152,128]{1,0:T(8,128)(2,1)S(1)}, u32[]{:S(2)}, u32[]{:S(2)}) collective-permute-start(bf16[1152,128]{1,0:T(8,128)(2,1)S(1)} %collective-permute-done.22.refs_1_), channel_id=1, source_target_pairs={{0,16},{1,17},{2,18},{3,19},{4,20},{5,21},{6,22},{7,23},{8,24},{9,... | collective-permute-start | bytes 884744 | tf_op jit(solution)/shard_map/ppermute | solution.py:260
  109.0 12.6 %collective-permute-start.36 = (bf16[1152,128]{1,0:T(8,128)(2,1)S(1)}, bf16[1152,128]{1,0:T(8,128)(2,1)S(1)}, u32[]{:S(2)}, u32[]{:S(2)}) collective-permute-start(bf16[1152,128]{1,0:T(8,128)(2,1)S(1)} %collective-permute-done.28.refs_7_), channel_id=1, source_target_pairs={{0,16},{1,17},{2,18},{3,19},{4,20},{5,21},{6,22},{7,23},{8,24},{9,... | collective-permute-start | bytes 884744 | tf_op jit(solution)/shard_map/ppermute | solution.py:260
  113.7 10.6 %collective-permute-start.35 = (bf16[1152,128]{1,0:T(8,128)(2,1)S(1)}, bf16[1152,128]{1,0:T(8,128)(2,1)S(1)}, u32[]{:S(2)}, u32[]{:S(2)}) collective-permute-start(bf16[1152,128]{1,0:T(8,128)(2,1)S(1)} %collective-permute-done.31.refs_10_), channel_id=1, source_target_pairs={{0,8},{1,9},{2,10},{3,11},{4,12},{5,13},{6,14},{7,15},{8,0},{9,1},... | collective-permute-start | bytes 884744 | tf_op jit(solution)/shard_map/ppermute | solution.py:260
  120.0 6.7 %collective-permute-start.34 = (bf16[1152,128]{1,0:T(8,128)(2,1)S(1)}, bf16[1152,128]{1,0:T(8,128)(2,1)S(1)}, u32[]{:S(2)}, u32[]{:S(2)}) collective-permute-start(bf16[1152,128]{1,0:T(8,128)(2,1)S(1)} %collective-permute-done.26.refs_5_), channel_id=1, source_target_pairs={{0,16},{1,17},{2,18},{3,19},{4,20},{5,21},{6,22},{7,23},{8,24},{9,... | collective-permute-start | bytes 884744 | tf_op jit(solution)/shard_map/ppermute | solution.py:260
  149.4 12.3 %collective-permute-start.52 = (bf16[2,1152,128]{2,1,0:T(8,128)(2,1)}, bf16[2,1152,128]{2,1,0:T(8,128)(2,1)S(1)}, u32[]{:S(2)}, u32[]{:S(2)}) collective-permute-start(bf16[2,1152,128]{2,1,0:T(8,128)(2,1)} %get-tuple-element.96), channel_id=1, source_target_pairs={{0,8},{1,9},{2,10},{3,11},{4,12},{5,13},{6,14},{7,15},{8,0},{9,1},... | collective-permute-start | bytes 1769480 | tf_op jit(solution)/shard_map/ppermute | solution.py:260
  150.7 45.4 %collective-permute-start.38 = (bf16[2048,768]{1,0:T(8,128)(2,1)}, bf16[2048,768]{1,0:T(8,128)(2,1)}, u32[]{:S(2)}, u32[]{:S(2)}) collective-permute-start(bf16[2048,768]{1,0:T(8,128)(2,1)} %get-tuple-element.71.back_own), channel_id=1, source_target_pairs={{0,4},{1,5},{2,6},{3,7},{4,0},{5,1},{6,2},{7,3},{8,12},{9,13},{10,... | collective-permute-start | bytes 9437192 | tf_op jit(solution)/shard_map/ppermute | solution.py:260
  150.7 24.1 %collective-permute-start.55 = (bf16[2,1152,128]{2,1,0:T(8,128)(2,1)}, bf16[2,1152,128]{2,1,0:T(8,128)(2,1)S(1)}, u32[]{:S(2)}, u32[]{:S(2)}) collective-permute-start(bf16[2,1152,128]{2,1,0:T(8,128)(2,1)} %get-tuple-element.99), channel_id=1, source_target_pairs={{0,16},{1,17},{2,18},{3,19},{4,20},{5,21},{6,22},{7,23},{8,24},{9,... | collective-permute-start | bytes 1769480 | tf_op jit(solution)/shard_map/ppermute | solution.py:260
  156.4 18.6 %collective-permute-start.51 = (bf16[2,1152,128]{2,1,0:T(8,128)(2,1)}, bf16[2,1152,128]{2,1,0:T(8,128)(2,1)}, u32[]{:S(2)}, u32[]{:S(2)}) collective-permute-start(bf16[2,1152,128]{2,1,0:T(8,128)(2,1)} %get-tuple-element.94), channel_id=1, source_target_pairs={{0,8},{1,9},{2,10},{3,11},{4,12},{5,13},{6,14},{7,15},{8,0},{9,1},... | collective-permute-start | bytes 1769480 | tf_op jit(solution)/shard_map/ppermute | solution.py:260
  163.0 25.4 %collective-permute-start.53 = (bf16[2,1152,128]{2,1,0:T(8,128)(2,1)S(1)}, bf16[2,1152,128]{2,1,0:T(8,128)(2,1)}, u32[]{:S(2)}, u32[]{:S(2)}) collective-permute-start(bf16[2,1152,128]{2,1,0:T(8,128)(2,1)S(1)} %add_convert_fusion.2), channel_id=1, source_target_pairs={{0,16},{1,17},{2,18},{3,19},{4,20},{5,21},{6,22},{7,23},{8,24},{9,... | collective-permute-start | bytes 1769480 | tf_op jit(solution)/shard_map/ppermute | solution.py:260
  174.6 21.2 %collective-permute-start.57 = (bf16[2,1152,128]{2,1,0:T(8,128)(2,1)}, bf16[2,1152,128]{2,1,0:T(8,128)(2,1)S(1)}, u32[]{:S(2)}, u32[]{:S(2)}) collective-permute-start(bf16[2,1152,128]{2,1,0:T(8,128)(2,1)} %get-tuple-element.100), channel_id=1, source_target_pairs={{0,16},{1,17},{2,18},{3,19},{4,20},{5,21},{6,22},{7,23},{8,24},{9,... | collective-permute-start | bytes 1769480 | tf_op jit(solution)/shard_map/ppermute | solution.py:260
  174.9 20.9 %collective-permute-start.56 = (bf16[2,1152,128]{2,1,0:T(8,128)(2,1)S(1)}, bf16[2,1152,128]{2,1,0:T(8,128)(2,1)S(1)}, u32[]{:S(2)}, u32[]{:S(2)}) collective-permute-start(bf16[2,1152,128]{2,1,0:T(8,128)(2,1)S(1)} %add_convert_fusion.1), channel_id=1, source_target_pairs={{0,8},{1,9},{2,10},{3,11},{4,12},{5,13},{6,14},{7,15},{8,0},{9,1},... | collective-permute-start | bytes 1769480 | tf_op jit(solution)/shard_map/ppermute | solution.py:260
  190.3 30.0 %collective-permute-start.54 = (bf16[1152,128]{1,0:T(8,128)(2,1)S(1)}, bf16[1152,128]{1,0:T(8,128)(2,1)S(1)}, u32[]{:S(2)}, u32[]{:S(2)}) collective-permute-start(bf16[1152,128]{1,0:T(8,128)(2,1)S(1)} %fusion.6), channel_id=1, source_target_pairs={{0,1},{1,0},{2,3},{3,2},{4,5},{5,4},{6,7},{7,6},{8,9},{9,8},{10,11... | collective-permute-start | bytes 884744 | tf_op jit(solution)/shard_map/ppermute | solution.py:260
  213.0 7.1 %collective-permute-start.41 = (bf16[2,608,128]{2,1,0:T(8,128)(2,1)}, bf16[2,608,128]{2,1,0:T(8,128)(2,1)S(1)}, u32[]{:S(2)}, u32[]{:S(2)}) collective-permute-start(bf16[2,608,128]{2,1,0:T(8,128)(2,1)} %get-tuple-element.85), channel_id=1, source_target_pairs={{0,8},{1,9},{2,10},{3,11},{4,12},{5,13},{6,14},{7,15},{8,0},{9,1},... | collective-permute-start | bytes 933896 | tf_op jit(solution)/shard_map/ppermute | solution.py:260
  215.0 14.5 %collective-permute-start.58 = (bf16[1152,128]{1,0:T(8,128)(2,1)S(1)}, bf16[1152,128]{1,0:T(8,128)(2,1)S(1)}, u32[]{:S(2)}, u32[]{:S(2)}) collective-permute-start(bf16[1152,128]{1,0:T(8,128)(2,1)S(1)} %get-tuple-element.109), channel_id=1, source_target_pairs={{0,2},{1,3},{2,0},{3,1},{4,6},{5,7},{6,4},{7,5},{8,10},{9,11},{10,... | collective-permute-start | bytes 884744 | tf_op jit(solution)/shard_map/ppermute | solution.py:260
  215.1 19.5 %collective-permute-start.59 = (bf16[1152,128]{1,0:T(8,128)(2,1)S(1)}, bf16[1152,128]{1,0:T(8,128)(2,1)S(1)}, u32[]{:S(2)}, u32[]{:S(2)}) collective-permute-start(bf16[1152,128]{1,0:T(8,128)(2,1)S(1)} %get-tuple-element.110), channel_id=1, source_target_pairs={{0,3},{1,2},{2,1},{3,0},{4,7},{5,6},{6,5},{7,4},{8,11},{9,10},{10,... | collective-permute-start | bytes 884744 | tf_op jit(solution)/shard_map/ppermute | solution.py:260
  219.1 54.1 %collective-permute-start.37 = (bf16[2048,768]{1,0:T(8,128)(2,1)S(1)}, bf16[2048,768]{1,0:T(8,128)(2,1)S(1)}, u32[]{:S(2)}, u32[]{:S(2)}) collective-permute-start(bf16[2048,768]{1,0:T(8,128)(2,1)S(1)} %mlp_out.1.out_own), channel_id=1, source_target_pairs={{0,4},{1,5},{2,6},{3,7},{4,0},{5,1},{6,2},{7,3},{8,12},{9,13},{10,... | collective-permute-start | bytes 9437192 | tf_op jit(solution)/shard_map/ppermute | solution.py:260
  220.1 53.1 %collective-permute-start.39 = (bf16[2048,768]{1,0:T(8,128)(2,1)S(1)}, bf16[2048,768]{1,0:T(8,128)(2,1)S(1)}, u32[]{:S(2)}, u32[]{:S(2)}) collective-permute-start(bf16[2048,768]{1,0:T(8,128)(2,1)S(1)} %get-tuple-element.79.back_own), channel_id=1, source_target_pairs={{0,4},{1,5},{2,6},{3,7},{4,0},{5,1},{6,2},{7,3},{8,12},{9,13},{10,... | collective-permute-start | bytes 9437192 | tf_op jit(solution)/shard_map/ppermute | solution.py:260
  220.2 24.7 %collective-permute-start.40 = (bf16[2,608,128]{2,1,0:T(8,128)(2,1)S(1)}, bf16[2,608,128]{2,1,0:T(8,128)(2,1)S(1)}, u32[]{:S(2)}, u32[]{:S(2)}) collective-permute-start(bf16[2,608,128]{2,1,0:T(8,128)(2,1)S(1)} %get-tuple-element.83), channel_id=1, source_target_pairs={{0,8},{1,9},{2,10},{3,11},{4,12},{5,13},{6,14},{7,15},{8,0},{9,1},... | collective-permute-start | bytes 933896 | tf_op jit(solution)/shard_map/ppermute | solution.py:260
  229.5 13.3 %collective-permute-start.44 = (bf16[2,608,128]{2,1,0:T(8,128)(2,1)S(1)}, bf16[2,608,128]{2,1,0:T(8,128)(2,1)S(1)}, u32[]{:S(2)}, u32[]{:S(2)}) collective-permute-start(bf16[2,608,128]{2,1,0:T(8,128)(2,1)S(1)} %get-tuple-element.88), channel_id=1, source_target_pairs={{0,16},{1,17},{2,18},{3,19},{4,20},{5,21},{6,22},{7,23},{8,24},{9,... | collective-permute-start | bytes 933896 | tf_op jit(solution)/shard_map/ppermute | solution.py:260
  234.6 14.2 %collective-permute-start.42 = (bf16[2,608,128]{2,1,0:T(8,128)(2,1)S(1)}, bf16[2,608,128]{2,1,0:T(8,128)(2,1)S(1)}, u32[]{:S(2)}, u32[]{:S(2)}) collective-permute-start(bf16[2,608,128]{2,1,0:T(8,128)(2,1)S(1)} %add_convert_fusion.5), channel_id=1, source_target_pairs={{0,16},{1,17},{2,18},{3,19},{4,20},{5,21},{6,22},{7,23},{8,24},{9,... | collective-permute-start | bytes 933896 | tf_op jit(solution)/shard_map/ppermute | solution.py:260
  242.8 9.2 %collective-permute-start.46 = (bf16[2,608,128]{2,1,0:T(8,128)(2,1)S(1)}, bf16[2,608,128]{2,1,0:T(8,128)(2,1)S(1)}, u32[]{:S(2)}, u32[]{:S(2)}) collective-permute-start(bf16[2,608,128]{2,1,0:T(8,128)(2,1)S(1)} %get-tuple-element.89), channel_id=1, source_target_pairs={{0,16},{1,17},{2,18},{3,19},{4,20},{5,21},{6,22},{7,23},{8,24},{9,... | collective-permute-start | bytes 933896 | tf_op jit(solution)/shard_map/ppermute | solution.py:260
  245.0 7.1 %collective-permute-start.45 = (bf16[2,608,128]{2,1,0:T(8,128)(2,1)S(1)}, bf16[2,608,128]{2,1,0:T(8,128)(2,1)S(1)}, u32[]{:S(2)}, u32[]{:S(2)}) collective-permute-start(bf16[2,608,128]{2,1,0:T(8,128)(2,1)S(1)} %add_convert_fusion.4), channel_id=1, source_target_pairs={{0,8},{1,9},{2,10},{3,11},{4,12},{5,13},{6,14},{7,15},{8,0},{9,1},... | collective-permute-start | bytes 933896 | tf_op jit(solution)/shard_map/ppermute | solution.py:260
  248.9 6.6 %collective-permute-start.43 = (bf16[608,128]{1,0:T(8,128)(2,1)S(1)}, bf16[608,128]{1,0:T(8,128)(2,1)S(1)}, u32[]{:S(2)}, u32[]{:S(2)}) collective-permute-start(bf16[608,128]{1,0:T(8,128)(2,1)S(1)} %fusion.7), channel_id=1, source_target_pairs={{0,1},{1,0},{2,3},{3,2},{4,5},{5,4},{6,7},{7,6},{8,9},{9,8},{10,11... | collective-permute-start | bytes 466952 | tf_op jit(solution)/shard_map/ppermute | solution.py:260
  252.3 12.6 %collective-permute-start.47 = (bf16[608,128]{1,0:T(8,128)(2,1)S(1)}, bf16[608,128]{1,0:T(8,128)(2,1)S(1)}, u32[]{:S(2)}, u32[]{:S(2)}) collective-permute-start(bf16[608,128]{1,0:T(8,128)(2,1)S(1)} %get-tuple-element.115), channel_id=1, source_target_pairs={{0,2},{1,3},{2,0},{3,1},{4,6},{5,7},{6,4},{7,5},{8,10},{9,11},{10,... | collective-permute-start | bytes 466952 | tf_op jit(solution)/shard_map/ppermute | solution.py:260
  252.8 12.0 %collective-permute-start.48 = (bf16[608,128]{1,0:T(8,128)(2,1)S(1)}, bf16[608,128]{1,0:T(8,128)(2,1)S(1)}, u32[]{:S(2)}, u32[]{:S(2)}) collective-permute-start(bf16[608,128]{1,0:T(8,128)(2,1)S(1)} %get-tuple-element.116), channel_id=1, source_target_pairs={{0,3},{1,2},{2,1},{3,0},{4,7},{5,6},{6,5},{7,4},{8,11},{9,10},{10,... | collective-permute-start | bytes 466952 | tf_op jit(solution)/shard_map/ppermute | solution.py:260
  255.5 12.0 %collective-permute-start.60 = (f32[576,128]{1,0:T(8,128)S(1)}, f32[576,128]{1,0:T(8,128)S(1)}, u32[]{:S(2)}, u32[]{:S(2)}) collective-permute-start(f32[576,128]{1,0:T(8,128)S(1)} %get-tuple-element.107), channel_id=1, source_target_pairs={{0,4},{1,5},{2,6},{3,7},{4,0},{5,1},{6,2},{7,3},{8,12},{9,13},{10,... | collective-permute-start | bytes 884744 | tf_op jit(solution)/shard_map/ppermute | solution.py:260
  264.9 4.7 %collective-permute-start.49 = (f32[288,128]{1,0:T(8,128)S(1)}, f32[288,128]{1,0:T(8,128)S(1)}, u32[]{:S(2)}, u32[]{:S(2)}) collective-permute-start(f32[288,128]{1,0:T(8,128)S(1)} %get-tuple-element.113), channel_id=1, source_target_pairs={{0,4},{1,5},{2,6},{3,7},{4,0},{5,1},{6,2},{7,3},{8,12},{9,13},{10,... | collective-permute-start | bytes 442376 | tf_op jit(solution)/shard_map/ppermute | solution.py:260
  266.9 2.7 collective-permute-start.50
  (61 other events, 1022.5 us)

commit v3 on v2

--- a/solution.py
+++ b/solution.py
@@ -1,3 +1,4 @@
+import functools
 import math
 
 import jax
@@ -252,8 +253,6 @@
 TO_Y = pairs_of(lambda y, x, c, z: (1 - y, x, c, z))
 TO_CORE = pairs_of(lambda y, x, c, z: (y, x, 1 - c, z))
 TO_Z = [pairs_of(lambda y, x, c, z, k=k: (y, x, c, z ^ k)) for k in range(4)]
-SWAP_ATTN = pairs_of(lambda y, x, c, z: (y, x, c if y and x else 1 - c, z))
-SWAP_MLP = pairs_of(lambda y, x, c, z: (y, x, c if y else 1 - c, z))
 
 
 def send(value, pairs):
@@ -276,7 +275,21 @@
     return (j // 6) * 12 + 6 * core + j % 6
 
 
-def cut_masters(idx, attn, mlp, keep_a, send_a, keep_m, send_m, half_a, half_m):
+def shifted(idx, vector, out):
+    lane = lax.broadcasted_iota(jnp.int32, (3, ROW), 1)
+    out[...] = jnp.zeros(out.shape, f32)
+    for k in range(4):
+
+        @pl.when(idx[4] == k)
+        def _():
+            turned = pltpu.roll(vector[...], 32 * k, 1) if k else vector[...]
+            at = 2 * k
+            out[at : at + 3, :] = jnp.where(lane >= 32 * k, turned, 0.0)
+            if k:
+                out[at + 1 : at + 4, :] += jnp.where(lane < 32 * k, turned, 0.0)
+
+
+def cut_masters(idx, attn, mlp, small, keep_a, send_a, keep_m, send_m, place, half_a, half_m):
     wide, core = idx[0], idx[3]
 
     @pl.when(wide < 6)
@@ -307,10 +320,13 @@
 
     first_a = jnp.where(wide < 6, core, 0)
     first_m = jnp.where(wide < 4, core, 0)
-    keep_a[...] = half_a[first_a]
-    send_a[...] = half_a[1 - first_a]
+    keep_a[0:288, :] = half_a[first_a]
+    send_a[0:288, :] = half_a[1 - first_a]
     keep_m[...] = half_m[first_m]
     send_m[...] = half_m[1 - first_m]
+    shifted(idx, small, place)
+    keep_a[288:304, :] = place[...].astype(bf16)
+    send_a[288:304, :] = place[...].astype(bf16)
 
 
 def pack_rows(idx, vis_own, vis_other, x_own, x_other, cot_own, cot_other, x_out, cot_out, meta, fill):
@@ -371,6 +387,10 @@
     return yy * 2 + xx, jnp.bitwise_xor(z, k)
 
 
+def pair_of(n):
+    return n // 4 * 2 + n % 2
+
+
 def core_of(idx, part):
     return 1 - idx[3] if part else idx[3]
 
@@ -408,18 +428,29 @@
     return expo * (1.0 / jnp.sum(expo, -1, keepdims=True))
 
 
+def probabilities_by_key(both, keys, mask):
+    scores = dot(keys, both, ((1,), (1,))) * (1.0 / math.sqrt(HD))
+    scores = jnp.where(mask, scores, -1e30)
+    expo = jnp.exp(scores - jnp.max(scores, 0, keepdims=True))
+    return expo * (1.0 / jnp.sum(expo, 0, keepdims=True))
+
+
+def one_above_other(wide):
+    return jnp.concatenate([wide[:, :BIN], wide[:, BIN:]], axis=0)
+
+
 def side_by_side(stacked):
     return jnp.concatenate([stacked[:BIN], stacked[BIN:]], axis=1)
 
 
-def attn_forward(meta, idx, x_ref, *refs):
-    pieces = refs[:16]
-    qkv_ref, context_ref, part_ref, w_qkv, w_out, vecs, shift, inner_bias, small = refs[16:]
-
-    @pl.when(pl.program_id(0) == 0)
-    def _():
+def attn_forward(phase, meta, idx, x_ref, *refs):
+    pairs = refs[:8]
+    qkv_ref, context_ref, part_ref, w_qkv, w_out, vecs, shift, inner_bias, small = refs[8:]
+
+    if phase == 0:
         small[...] = jnp.zeros(small.shape, f32)
-        for n, piece in enumerate(pieces):
+        for n in range(16):
+            piece = pairs[pair_of(n)].at[n % 4 // 2]
             chip, z = owner_of(idx, n // 4, n % 4)
 
             @pl.when(chip < 3)
@@ -452,8 +483,7 @@
         high = jnp.where(own, lanes_of(small, 54, 6), lanes_of(small, 60, 6))
         inner_bias[...] = jnp.concatenate([low, high], axis=1)
 
-    @pl.when(pl.program_id(0) < meta[0])
-    def _():
+    if phase == 1:
         normed, _ = standard(x_ref[...].astype(f32))
         first_in = (normed * vecs[0:1, :] + vecs[1:2, :]).astype(bf16)
         qkv_ref[...] = (dot(first_in, w_qkv[...]) + shift[...]).astype(bf16)
@@ -492,15 +522,13 @@
     return x_ref[...].astype(f32) + parts + vecs[2:3, :]
 
 
-def mlp_both(meta, idx, x_ref, part_own, part_other, cot_ref, vecs, inner_bias, *refs):
+def mlp_both(phase, meta, idx, x_ref, part_own, part_other, cot_ref, vecs, inner_bias, *refs):
     pieces = refs[:16]
     (active_ref, back_ref, w_two, sums, inner_sum) = refs[16:21]
     outs = refs[21:29]
     w_one, acc_one, acc_two = refs[29:]
-    step = pl.program_id(0)
-
-    @pl.when(step == 0)
-    def _():
+
+    if phase == 0:
         acc_one[...] = jnp.zeros(acc_one.shape, f32)
         acc_two[...] = jnp.zeros(acc_two.shape, f32)
         sums[...] = jnp.zeros(sums.shape, f32)
@@ -523,8 +551,7 @@
                 for j in range(6):
                     w_two[to, j * ROW : (j + 1) * ROW] = piece[j * 192 : (j + 1) * 192, :]
 
-    @pl.when(pl.program_id(0) < meta[0])
-    def _():
+    if phase == 1:
         normed, _ = standard(middle_of(x_ref, part_own, part_other, vecs))
         second_in = (normed * vecs[3:4, :] + vecs[4:5, :]).astype(bf16)
         grad = cot_ref[...]
@@ -546,11 +573,10 @@
         sums[1:2, :] += jnp.sum(back, 0, keepdims=True)
         sums[2:3, :] += jnp.sum(grad.astype(f32), 0, keepdims=True)
 
-    @pl.when(step == pl.num_programs(0) - 1)
-    def _():
+    if phase == 2:
         for n in range(16):
             chip, z = owner_of(idx, n // 4, n % 4)
-            out, k = outs[n // 2], n % 2
+            out, k = outs[pair_of(n)], n % 4 // 2
 
             @pl.when(chip < 2)
             def _():
@@ -568,27 +594,23 @@
                     out[k, j * 192 : (j + 1) * 192, :] = acc_two[rows, j * ROW : (j + 1) * ROW].astype(bf16)
 
 
-def mlp_out(meta, active_ref, w_two, part_ref):
-    @pl.when(pl.program_id(0) < meta[0])
-    def _():
+def hand_on(phase, meta, idx, source, target):
+    if phase == 1:
+        target[...] = source[...]
+
+
+def mlp_out(phase, meta, idx, active_ref, w_two, part_ref):
+    if phase == 1:
         part_ref[...] = dot(active_ref[...], w_two[...]).astype(bf16)
 
 
-def attn_backward(meta, idx, x_ref, part_own, part_other, cot_ref, back_own, back_other, qkv_ref, context_ref,
-                  w_qkv, w_out, vecs, sums_in, inner_sum, *refs):
-    grad_ref, back_ref = refs[:2]
-    outs = refs[2:10]
-    acc_qkv, acc_out, sums, small, grads = refs[10:]
-    step = pl.program_id(0)
-
-    @pl.when(step == 0)
-    def _():
-        acc_qkv[...] = jnp.zeros(acc_qkv.shape, f32)
+def middle_backward(phase, meta, idx, x_ref, part_own, part_other, cot_ref, back_own, back_other, context_ref, w_out, vecs,
+                    grad_ref, grad_context_ref, acc_out, sums):
+    if phase == 0:
         acc_out[...] = jnp.zeros(acc_out.shape, f32)
         sums[...] = jnp.zeros(sums.shape, f32)
 
-    @pl.when(pl.program_id(0) < meta[0])
-    def _():
+    if phase == 1:
         normed, factor = standard(middle_of(x_ref, part_own, part_other, vecs))
         scaled = (back_own[...].astype(f32) + back_other[...].astype(f32)) * vecs[3:4, :]
         through = scaled - jnp.mean(scaled, -1, keepdims=True)
@@ -596,29 +618,45 @@
         grad_middle = cot_ref[...].astype(f32) + factor * through
         grad_ref[...] = grad_middle
         grad_proj = grad_middle.astype(bf16)
-        context = context_ref[...]
-        acc_out[...] += dot(context, grad_proj, ((0,), (0,)))
-        sums[2:3, :] += jnp.sum(grad_proj.astype(f32), 0, keepdims=True)
-        grad_context = dot(grad_proj, w_out[...], ((1,), (1,))).astype(bf16)
+        acc_out[...] += dot(context_ref[...], grad_proj, ((0,), (0,)))
+        sums[0:1, :] += jnp.sum(grad_proj.astype(f32), 0, keepdims=True)
+        grad_context_ref[...] = dot(grad_proj, w_out[...], ((1,), (1,))).astype(bf16)
+
+
+def heads_backward(phase, meta, idx, qkv_ref, grad_context_ref, grads):
+    if phase == 1:
         scale = 1.0 / math.sqrt(HD)
         for b in range(BLOCK // BIN):
-            mask = same_sample(meta, step * (BLOCK // BIN) + b)
-            mask = jnp.concatenate([mask, mask], axis=0)
+            mask = same_sample(meta, pl.program_id(0) * (BLOCK // BIN) + b)
+            mask = jnp.concatenate([mask, mask], axis=1)
             rows = slice(b * BIN, (b + 1) * BIN)
             for h in range(3):
                 cols = [slice((3 * t + h) * ROW, (3 * t + h + 1) * ROW) for t in range(3)]
                 query, keys, values = (qkv_ref[rows, cols[t]] for t in range(3))
-                probs = probabilities(query, keys, mask)
-                grad_out = halves(grad_context[rows, h * ROW : (h + 1) * ROW])
-                grad_values = dot(probs.astype(bf16), grad_out, ((0,), (0,)))
-                grad_probs = dot(grad_out, values, ((1,), (1,)))
-                total = jnp.sum(grad_probs * probs, -1, keepdims=True)
+                both = halves(query)
+                probs = probabilities_by_key(both, keys, mask)
+                grad_out = halves(grad_context_ref[rows, h * ROW : (h + 1) * ROW])
+                grad_values = dot(probs.astype(bf16), grad_out)
+                grad_probs = dot(values, grad_out, ((1,), (1,)))
+                total = jnp.sum(grad_probs * probs, 0, keepdims=True)
                 grad_scores = (probs * (grad_probs - total)).astype(bf16)
-                grad_query = dot(side_by_side(grad_scores), halves(keys)) * scale
-                grad_keys = dot(grad_scores, halves(query), ((0,), (0,))) * scale
+                grad_keys = dot(grad_scores, both) * scale
+                grad_query = dot(one_above_other(grad_scores), halves(keys), ((0,), (0,))) * scale
                 grads[rows, cols[0]] = grad_query.astype(bf16)
                 grads[rows, cols[1]] = grad_keys.astype(bf16)
                 grads[rows, cols[2]] = grad_values.astype(bf16)
+
+
+def first_backward(phase, meta, idx, x_ref, grads, w_qkv, acc_out, vecs, sums_in, inner_sum, sums_out, *refs):
+    back_ref = refs[0]
+    outs = refs[1:9]
+    acc_qkv, sums, small = refs[9:]
+
+    if phase == 0:
+        acc_qkv[...] = jnp.zeros(acc_qkv.shape, f32)
+        sums[...] = jnp.zeros(sums.shape, f32)
+
+    if phase == 1:
         normed, _ = standard(x_ref[...].astype(f32))
         first_in = (normed * vecs[0:1, :] + vecs[1:2, :]).astype(bf16)
         grad_qkv = grads[...]
@@ -630,11 +668,9 @@
         sums[3:4, 0 : D // 2] += jnp.sum(grad_qkv[:, 0 : D // 2].astype(f32), 0, keepdims=True)
         sums[3:4, D // 2 : D] += jnp.sum(grad_qkv[:, D : D + D // 2].astype(f32), 0, keepdims=True)
 
-    @pl.when(step == pl.num_programs(0) - 1)
-    def _():
+    if phase == 2:
         small[...] = jnp.zeros(small.shape, f32)
-        first = idx[3] == 0
-        once = jnp.where(first, 1.0, 0.0)
+        once = jnp.where(idx[3] == 0, 1.0, 0.0)
 
         def put(at, rows):
             for j in range(rows.shape[1] // ROW):
@@ -643,7 +679,7 @@
 
         put(0, sums[0:1, :])
         put(6, sums[1:2, :])
-        put(24, sums[2:3, :] * once)
+        put(24, sums_out[0:1, :] * once)
         put(30, sums_in[0:1, :])
         put(36, sums_in[1:2, :])
         put(66, sums_in[2:3, :] * once)
@@ -658,7 +694,7 @@
 
         for n in range(16):
             chip, z = owner_of(idx, n // 4, n % 4)
-            out, k = outs[n // 2], n % 2
+            out, k = outs[pair_of(n)], n % 4 // 2
 
             @pl.when(chip < 3)
             def _():
@@ -680,12 +716,10 @@
                 out[k, 576 + part * 16 : 592 + part * 16, :] = small[group].astype(bf16)
 
 
-def finish_rows(meta, idx, x_ref, part_own, part_other, out_own, out_other, grad_ref, back_own, back_other, vecs,
+def finish_rows(phase, meta, idx, x_ref, part_own, part_other, out_own, out_other, grad_ref, back_own, back_other, vecs,
                 output, grad_samples, packed_out, packed_grad):
-    step = pl.program_id(0)
-    @pl.when(pl.program_id(0) < meta[0])
-    def _():
-        at = pl.ds(pl.multiple_of(step * BLOCK, BLOCK), BLOCK)
+    if phase == 1:
+        at = pl.ds(pl.multiple_of(pl.program_id(0) * BLOCK, BLOCK), BLOCK)
         parts = out_own[...].astype(f32) + out_other[...].astype(f32)
         result = middle_of(x_ref, part_own, part_other, vecs) + parts + vecs[5:6, :]
         packed_out[at, :] = result.astype(bf16)
@@ -695,8 +729,7 @@
         through = through - normed * jnp.mean(scaled * normed, -1, keepdims=True)
         packed_grad[at, :] = (grad_ref[...] + factor * through).astype(bf16)
 
-    @pl.when(step == pl.num_programs(0) - 1)
-    def _():
+    if phase == 2:
         output[...] = jnp.zeros(output.shape, bf16)
         grad_samples[...] = jnp.zeros(grad_samples.shape, bf16)
         row = lax.broadcasted_iota(jnp.int32, (16, D), 0)
@@ -719,11 +752,18 @@
         out[...] = new
 
 
-def step_mlp(idx, master, first, second, keep, other, new, new_first, new_second, half, grad):
+def step_mlp(idx, master, first, second, keep, mine, other, new, new_first, new_second, half, grad):
     wide, core = idx[0], idx[3]
-    mine = jnp.where(wide < 4, core, 0)
-    half[mine] = keep[...]
-    half[1 - mine] = other[...]
+    at = jnp.where(wide < 4, core, 0)
+    half[at] = keep[...]
+
+    @pl.when(wide < 4)
+    def _():
+        half[1 - at] = other[...]
+
+    @pl.when(wide >= 4)
+    def _():
+        half[1 - at] = mine[...]
 
     @pl.when(wide < 4)
     def _():
@@ -739,12 +779,19 @@
     update_refs(master, first, second, grad[...], (new, new_first, new_second), 0.1, rate_matrix)
 
 
-def step_attn(idx, master, first, second, keep, other, master_s, first_s, second_s, keep_s, other_s,
-              new, new_first, new_second, new_s, new_first_s, new_second_s, half, grad):
+def step_attn(idx, master, first, second, keep, mine, other, master_s, first_s, second_s, keep_s, other_s,
+              new, new_first, new_second, new_s, new_first_s, new_second_s, half, grad, place, small_grad):
     wide, core = idx[0], idx[3]
-    mine = jnp.where(wide < 6, core, 0)
-    half[mine] = keep[...]
-    half[1 - mine] = other[...]
+    at = jnp.where(wide < 6, core, 0)
+    half[at] = keep[...]
+
+    @pl.when(wide < 6)
+    def _():
+        half[1 - at] = other[...]
+
+    @pl.when(wide >= 6)
+    def _():
+        half[1 - at] = mine[...]
 
     @pl.when(wide < 6)
     def _():
@@ -758,95 +805,255 @@
             grad[pl.ds(j, 96, stride=6), :] = half[j // 3, (j % 3) * 96 : (j % 3 + 1) * 96, :]
 
     update_refs(master, first, second, grad[...], (new, new_first, new_second), 0.1, rate_matrix)
-    update_refs(master_s, first_s, second_s, keep_s[...] + other_s[...], (new_s, new_first_s, new_second_s), 0.0, rate_small)
-
-
-def gather_chips(piece):
-    by = {(0, 0): piece}
-    by[1, 0] = send(piece, TO_X)
-    by[2, 0] = send(piece, TO_Y)
-    by[0, 1] = send(piece, TO_Z[1])
-    by[3, 0] = send(by[2, 0], TO_X)
-    by[0, 2] = send(piece, TO_Z[2])
-    by[0, 3] = send(piece, TO_Z[3])
-    for k in (1, 2, 3):
-        by[1, k] = send(by[0, k], TO_X)
-        by[2, k] = send(by[0, k], TO_Y)
-        by[3, k] = send(by[1, k], TO_Y) if k % 2 else send(by[2, k], TO_X)
-    return [by[column, k] for column in range(4) for k in range(4)]
+    place[...] = keep_s[...] + other_s[...]
+    lane = lax.broadcasted_iota(jnp.int32, (3, ROW), 1)
+    for k in range(4):
+
+        @pl.when(idx[4] == k)
+        def _():
+            at = 2 * k
+            both = jnp.where(lane >= 32 * k, place[at : at + 3, :], place[at + 1 : at + 4, :])
+            small_grad[...] = pltpu.roll(both, ROW - 32 * k, 1) if k else both
+
+    update_refs(master_s, first_s, second_s, small_grad[...], (new_s, new_first_s, new_second_s), 0.0, rate_small)
 
 
 def plus(*terms):
     return sum(t.astype(f32) for t in terms)
 
 
-def scatter_chips(own_low, own_high, x_low, x_high, y_low, y_high, both_low, both_high):
-    from_x = send(both_low, TO_X)
-    from_y = send(both_high, TO_Y)
-    x_low_in = send(x_low, TO_X)
-    y_high_in = send(y_high, TO_Y)
-    y_low_in = send(plus(y_low, from_x).astype(bf16), TO_Y)
-    x_high_in = send(plus(x_high, from_y).astype(bf16), TO_X)
-    low = plus(own_low, x_low_in, y_low_in)
-    high = plus(own_high, x_high_in, y_high_in)
-    others = [send(t.astype(bf16), TO_Z[k]) for k, t in ((1, low[1]), (2, high[0]), (3, high[1]))]
-    return plus(low[0], *others)
+def nothing(idx, out):
+    out[...] = jnp.zeros(out.shape, f32)
+
+
+def lay_attn(idx, keep, mine, other, piece):
+    piece[0:288, :] = keep[0:288, :]
+    piece[576:592, :] = keep[288:304, :]
+    piece[592:608, :] = other[288:304, :]
+
+    @pl.when(idx[0] < 6)
+    def _():
+        piece[288:576, :] = other[0:288, :]
+
+    @pl.when(idx[0] >= 6)
+    def _():
+        piece[288:576, :] = mine[0:288, :]
+
+
+def lay_mlp(idx, keep, mine, other, piece):
+    piece[0:576, :] = keep[...]
+
+    @pl.when(idx[0] < 4)
+    def _():
+        piece[576:1152, :] = other[...]
+
+    @pl.when(idx[0] >= 4)
+    def _():
+        piece[576:1152, :] = mine[...]
+
+
+def lay_out(*refs):
+    at = 0
+    for ref in refs[:-1]:
+        refs[-1][at : at + ref.shape[0], :] = ref[...]
+        at += ref.shape[0]
+
+
+def pair_up(first, second, pair):
+    pair[0] = first[...]
+    pair[1] = second[...]
+
+
+def add_low(*refs):
+    refs[-1][...] = plus(*(r[...] for r in refs[:-1])).astype(bf16)
+
+
+def add_near_far(*refs):
+    terms, (near, far) = refs[:-2], refs[-2:]
+    near[...] = plus(*(r[0] for r in terms))
+    far[...] = plus(*(r[1] for r in terms)).astype(bf16)
+
+
+def add_last(half, near, other, *outs):
+    total = near[...] + other[...].astype(f32)
+    outs[0][...] = total[:half]
+    outs[1][...] = total[half : 2 * half]
+    for n, out in enumerate(outs[2:]):
+        out[...] = total[2 * half + 16 * n : 2 * half + 16 * n + 16]
+
+
+SENDS = {
+    "cv": ("visible", TO_CORE),
+    "cs": ("samples", TO_CORE),
+    "cc": ("cotangent", TO_CORE),
+    "sa": ("send_a", TO_CORE),
+    "sm": ("send_m", TO_CORE),
+    "z2a": ("pa", TO_Z[2]),
+    "zOa": ("Ea", TO_Z[1]),
+    "xEa": ("Ea", TO_X),
+    "yEa": ("Ea", TO_Y),
+    "xOa": ("zOa", TO_X),
+    "yOa": ("zOa", TO_Y),
+    "dEa": ("yEa", TO_X),
+    "dOa": ("xOa", TO_Y),
+    "z1m": ("pm", TO_Z[1]),
+    "z2m": ("pm2", TO_Z[2]),
+    "z3m": ("z2m", TO_Z[1]),
+    "x0m": ("pm", TO_X),
+    "y0m": ("pm", TO_Y),
+    "x1m": ("z1m", TO_X),
+    "y1m": ("z1m", TO_Y),
+    "x2m": ("z2m", TO_X),
+    "y2m": ("z2m", TO_Y),
+    "x3m": ("z3m", TO_X),
+    "y3m": ("z3m", TO_Y),
+    "d0m": ("y0m", TO_X),
+    "d1m": ("d0m", TO_Z[1]),
+    "d2m": ("x2m", TO_Y),
+    "d3m": ("d2m", TO_Z[1]),
+    "pt": ("part", TO_CORE),
+    "bk": ("back", TO_CORE),
+    "ot": ("out_part", TO_CORE),
+    "fb": ("first_back_2", TO_CORE),
+}
+for group in "am":
+    SENDS |= {
+        "rE" + group: ("dE" + group + "_grad", TO_X),
+        "rO" + group: ("dO" + group + "_grad", TO_Y),
+        "pE" + group: ("xE" + group + "_grad", TO_X),
+        "pO" + group: ("yO" + group + "_grad", TO_Y),
+        "qE" + group: ("aE" + group, TO_Y),
+        "qO" + group: ("aO" + group, TO_X),
+        "wO" + group: ("so" + group, TO_Z[1]),
+        "w2" + group: ("far" + group, TO_Z[2]),
+        "g" + group: ("other" + group, TO_CORE),
+    }
+SENDS["gs"] = ("other_small", TO_CORE)
+PAIR_NAMES = ("E{}_grad", "O{}_grad", "xE{}_grad", "xO{}_grad", "yE{}_grad", "yO{}_grad", "dE{}_grad", "dO{}_grad")
+
+AFTER = {
+    "pa": ("cs", "cc", "cv"),
+    "pm": ("pa",),
+    "Ea": ("meta",),
+    "pm2": ("Ea",),
+    "fwd": ("x1m", "y1m", "x0m", "y0m"),
+    "there": ("x3m", "y3m", "d1m", "d2m", "d3m", "x2m", "d0m", "vecs"),
+    "mlp": ("there",),
+    "bw1": ("out_part",),
+    "aEm": ("grad_context",),
+    "aOm": ("grad_context",),
+    "bw2": ("aEm", "aOm"),
+    "bw3": ("ot",),
+    "som": ("first_back",),
+    "hand": ("som",),
+    "aEa": ("farm",),
+    "fin": ("soa",),
+    "sza": ("output",),
+    "sua": ("done_m",),
+}
+
+ORDER = (
+    "+cv", "+cs", "+cc", "=cut", "+sa", "+sm", "=pack", "=pa", "+z2a", "=pm", "+z1m", "+x0m", "+y0m",
+    "=Ea", "=pm2", "+z2m", "+zOa", "+xEa", "+yEa", "+x1m", "+y1m", "+dEa", "+yOa", "+z3m", "+xOa", "+y2m", "+x2m",
+    "+d0m", "+dOa", "+y3m", "+x3m", "+d2m", "=fwd", "+pt", "+d1m", "+d3m", "=there",
+    "=mlp", "+rEm", "+rOm", "+bk", "=mout", "+ot", "=bw1", "=aEm", "=aOm", "+qOm", "+qEm", "+pEm", "+pOm", "=bw2",
+    "=bw3", "+rEa", "+rOa", "=som", "=hand", "+fb", "+wOm", "=szm", "+w2m", "=aEa", "=aOa", "+qOa", "+qEa", "+pEa", "+pOa",
+    "=soa", "+wOa", "=fin", "=sum", "+gm", "=om", "=sza", "+w2a", "=sua", "+ga", "+gs", "=oa",
+)
 
 
 SMEM = pl.BlockSpec(memory_space=pltpu.SMEM)
-
-
-def whole(shape):
-    return pl.BlockSpec(shape, lambda i, *_: (0,) * len(shape))
-
-
-def once_in(shape):
-    return pl.BlockSpec(shape, lambda i, *_: (0,) * len(shape), pipeline_mode=pl.Buffered(1))
-
-
-def rows_spec(width):
-    return pl.BlockSpec((BLOCK, width), lambda i, meta, *_: (jnp.minimum(i, meta[0] - 1), 0))
+VMEM = pl.BlockSpec(memory_space=pltpu.VMEM)
+ANY = pl.BlockSpec(memory_space=pl.ANY)
 
 
 def array(shape, dtype=bf16):
     return jax.ShapeDtypeStruct(shape, dtype)
 
 
+def large(shape, dtype=bf16):
+    return pltpu.HBM(shape, dtype)
+
+
 def params(mib):
     return pltpu.CompilerParams(vmem_limit_bytes=mib << 20)
 
 
-def cost(flops, nbytes):
-    return pl.CostEstimate(flops=flops, bytes_accessed=nbytes, transcendentals=0)
-
-
-def over_blocks(body, steps, scalars, in_specs, out_specs, out_shape, scratch, mib, flops, nbytes, name):
-    return pl.pallas_call(
-        body,
-        grid_spec=pltpu.PrefetchScalarGridSpec(
-            num_scalar_prefetch=scalars, grid=(steps,), in_specs=in_specs, out_specs=out_specs, scratch_shapes=scratch
-        ),
-        out_shape=out_shape,
-        compiler_params=params(mib),
-        cost_estimate=cost(flops, nbytes),
-        name=name,
-    )
-
-
-def at_once(body, in_specs, out_specs, out_shape, scratch, mib, flops, nbytes, name):
-    return pl.pallas_call(
-        body,
-        in_specs=in_specs,
-        out_specs=out_specs,
-        out_shape=out_shape,
-        scratch_shapes=scratch,
-        compiler_params=params(mib),
-        cost_estimate=cost(flops, nbytes),
-        name=name,
-    )
-
-
-VMEM = pl.BlockSpec(memory_space=pltpu.VMEM)
+SCALE = 10**9
+COSTS = {
+    "attn_forward": 11, "mlp_both": 23, "mlp_out": 20, "middle_backward": 8, "heads_backward": 25, "first_backward": 25,
+    "finish_rows": 8, "pack_rows": 6, "all_there": 60,
+}
+
+
+def cost(name):
+    return pl.CostEstimate(flops=COSTS.get(name, 1) * SCALE, bytes_accessed=1, transcendentals=0)
+
+
+def in_hbm(value):
+    return pltpu.with_memory_space_constraint(value, pltpu.HBM)
+
+
+def full(value):
+    return pl.BlockSpec(value.shape, lambda i: (0,) * len(value.shape))
+
+
+def over_blocks(body, rows_in, fixed_in, rows_out, fixed_out, scratch, mib, name, after=()):
+    many = rows_in + [w for w, _, _ in rows_out]
+    n_in, n_out = len(rows_in), len(rows_out)
+
+    def kernel(meta, idx, *refs):
+        refs = refs[: n_in + fixed_in] + refs[n_in + fixed_in + len(after) :]
+        rows, fixed, lines, rest = (
+            refs[:n_in], refs[n_in : n_in + fixed_in], refs[n_in + fixed_in :][:n_out], refs[n_in + fixed_in + n_out :]
+        )
+        body(0, meta, idx, *rows, *fixed, *lines, *rest)
+
+        def one(*blocks):
+            body(1, meta, idx, *blocks[:n_in], *fixed, *blocks[n_in:], *rest)
+
+        specs = [pl.BlockSpec((BLOCK, w), lambda i: (i, 0)) for w in many]
+        pltpu.emit_pipeline(one, grid=(meta[0],), in_specs=specs[:n_in], out_specs=specs[n_in:])(*rows, *lines)
+        body(2, meta, idx, *rows, *fixed, *lines, *rest)
+
+    def called(meta, idx, *args):
+        return pl.pallas_call(
+            kernel,
+            grid=(1,),
+            in_specs=[SMEM, SMEM] + [ANY] * n_in + [full(a) for a in args[n_in:]] + [ANY] * len(after),
+            out_specs=[ANY] * n_out + [full(a) for a in fixed_out],
+            out_shape=[large((n, w), t) for w, t, n in rows_out] + fixed_out,
+            scratch_shapes=scratch,
+            compiler_params=params(mib),
+            cost_estimate=cost(name),
+            name=name,
+        )(meta, idx, *args, *after)
+
+    return called
+
+
+def at_once(body, scalars, outs, scratch, mib, name, after=(), copied=False):
+    def kernel(*refs):
+        n = len(refs) - len(scratch) - len(outs) - len(after)
+        body(*refs[:n], *refs[n + len(after) :])
+
+    def called(*args):
+        grid = {"grid": (1,)} if copied else {}
+        blocks = [full(a) if copied else VMEM for a in args[scalars:]]
+        arrays = [in_hbm(a) for a in args[scalars:]] if copied else args[scalars:]
+        return pl.pallas_call(
+            kernel,
+            in_specs=[SMEM] * scalars + blocks + [ANY] * len(after),
+            out_specs=[SMEM if a.dtype == jnp.int32 else full(a) if copied else VMEM for a in outs],
+            out_shape=outs,
+            scratch_shapes=scratch,
+            compiler_params=params(mib),
+            cost_estimate=cost(name),
+            name=name,
+            **grid,
+        )(*args[:scalars], *arrays, *after)
+
+    return called
 
 
 def on_core(
@@ -871,86 +1078,168 @@
     def lanes(flat):
         return flat.reshape(-1, ROW)
 
-    def spread(vector):
-        return lanes(lax.dynamic_update_slice(jnp.zeros((16 * ROW,), f32), vector, (z * 288,)))
-
-    small_low = spread(master_small).astype(bf16)
+    def three_rows(vector):
+        return lanes(jnp.pad(vector, (0, 3 * ROW - vector.shape[0])))
+
     half_a, half_m = (288, ROW), (576, ROW)
-    keep_a, send_a, keep_m, send_m = at_once(
-        cut_masters, [SMEM, VMEM, VMEM], [VMEM] * 4,
-        [array(half_a), array(half_a), array(half_m), array(half_m)],
-        [pltpu.VMEM((2, *half_a), bf16), pltpu.VMEM((2, *half_m), bf16)], 16, 10**9, 2 * 10**6, "cut_masters",
-    )(idx, lanes(master_attn), lanes(master_mlp))
-    piece_a = jnp.concatenate([keep_a, send(send_a, SWAP_ATTN), small_low, send(small_low, TO_CORE)])
-    pieces_a = gather_chips(piece_a)
-    piece_m = jnp.concatenate([keep_m, send(send_m, SWAP_MLP)])
-    pieces_m = gather_chips(piece_m)
-
-    x, cot, meta = at_once(
-        pack_rows, [SMEM, SMEM, SMEM] + [VMEM] * 4, [VMEM, VMEM, SMEM],
-        [array((rows, D)), array((rows, D)), array((64,), jnp.int32)],
-        [pltpu.SMEM((16,), jnp.int32)], 32, 10**9, 12 * 10**6, "pack_rows",
-    )(idx, visible, send(visible, TO_CORE), samples, send(samples, TO_CORE), cotangent, send(cotangent, TO_CORE))
-    steps = rows // BLOCK
-
-    row_d, row_half, row_qkv, row_inner = rows_spec(D), rows_spec(D // 2), rows_spec(3 * D // 2), rows_spec(FF // 2)
-    qkv, context, part, w_qkv, w_out, vecs, shift, inner_bias = over_blocks(
-        attn_forward, steps, 2, [row_d] + [once_in((608, ROW))] * 16,
-        [row_qkv, row_half, row_d, whole((D, 3 * D // 2)), whole((D // 2, D)), whole((8, D)), whole((1, 3 * D // 2)), whole((1, FF // 2))],
-        [array((rows, 3 * D // 2)), array((rows, D // 2)), array((rows, D)), array((D, 3 * D // 2)), array((D // 2, D)),
-         array((8, D), f32), array((1, 3 * D // 2), f32), array((1, FF // 2), f32)],
-        [pltpu.VMEM((8, 16, ROW), f32)], 32, 5 * 10**9, 10**7, "attn_forward",
-    )(meta, idx, x, *pieces_a)
-    part_other = send(part, TO_CORE)
-
-    pair_m = (2, 1152, ROW)
-    mlp = over_blocks(
-        mlp_both, steps, 2, [row_d] * 4 + [once_in((8, D)), once_in((1, FF // 2))] + [once_in((1152, ROW))] * 16,
-        [row_inner, row_d, whole((FF // 2, D)), whole((8, D)), whole((1, FF // 2))] + [whole(pair_m)] * 8,
-        [array((rows, FF // 2)), array((rows, D)), array((FF // 2, D)), array((8, D), f32), array((1, FF // 2), f32)] + [array(pair_m)] * 8,
-        [pltpu.VMEM((D, FF // 2), bf16), pltpu.VMEM((D, FF // 2), f32), pltpu.VMEM((FF // 2, D), f32)],
-        56, 10**10, 2 * 10**7, "mlp_both",
-    )(meta, idx, x, part, part_other, cot, vecs, inner_bias, *pieces_m)
-    active, back, w_two, sums, inner_sum = mlp[:5]
-    back_other = send(back, TO_CORE)
-    summed_m = scatter_chips(*mlp[5:])
-
-    out_part = over_blocks(
-        mlp_out, steps, 1, [row_inner, once_in((FF // 2, D))], row_d, array((rows, D)), [], 16, 10**9, 10**7, "mlp_out",
-    )(meta, active, w_two)
-    out_other = send(out_part, TO_CORE)
-
-    pair_a = (2, 608, ROW)
-    attn = over_blocks(
-        attn_backward, steps, 2,
-        [row_d] * 6 + [row_qkv, row_half, once_in((D, 3 * D // 2)), once_in((D // 2, D)), once_in((8, D)), once_in((8, D)), once_in((1, FF // 2))],
-        [row_d, row_d] + [whole(pair_a)] * 8,
-        [array((rows, D), f32), array((rows, D))] + [array(pair_a)] * 8,
-        [pltpu.VMEM((D, 3 * D // 2), f32), pltpu.VMEM((D // 2, D), f32), pltpu.VMEM((8, D), f32), pltpu.VMEM((8, 16, ROW), f32),
-         pltpu.VMEM((BLOCK, 3 * D // 2), bf16)],
-        40, 8 * 10**9, 10**7, "attn_backward",
-    )(meta, idx, x, part, part_other, cot, back, back_other, qkv, context, w_qkv, w_out, vecs, sums, inner_sum)
-    grad_middle, first_back = attn[:2]
-    first_other = send(first_back, TO_CORE)
-    summed_a = scatter_chips(*attn[2:])
-
-    output, grad_samples = over_blocks(
-        finish_rows, steps, 2, [row_d] * 8 + [once_in((8, D))],
-        [whole((count, length, D))] * 2, [array((count, length, D))] * 2,
-        [pltpu.VMEM((rows, D), bf16)] * 2, 32, 10**9, 10**7, "finish_rows",
-    )(meta, idx, x, part, part_other, out_part, out_other, grad_middle, first_back, first_other, vecs)
-
     shape_m, shape_a, shape_s = (1152, ROW), (576, ROW), (16, ROW)
-    new_mlp = at_once(
-        step_mlp, [SMEM] + [VMEM] * 5, [VMEM] * 3, [array(shape_m, f32)] * 3,
-        [pltpu.VMEM((2, *half_m), f32), pltpu.VMEM(shape_m, f32)], 16, 10**9, 4 * 10**6, "step_mlp",
-    )(idx, lanes(master_mlp), lanes(first_mlp), lanes(second_mlp), summed_m[:576], send(summed_m[576:], SWAP_MLP))
-    new_attn = at_once(
-        step_attn, [SMEM] + [VMEM] * 10, [VMEM] * 6, [array(shape_a, f32)] * 3 + [array(shape_s, f32)] * 3,
-        [pltpu.VMEM((2, *half_a), f32), pltpu.VMEM(shape_a, f32)], 16, 10**9, 2 * 10**6, "step_attn",
-    )(idx, lanes(master_attn), lanes(first_attn), lanes(second_attn), summed_a[:288], send(summed_a[288:576], SWAP_ATTN),
-      spread(master_small), spread(first_small), spread(second_small), summed_a[576:592], send(summed_a[592:], TO_CORE))
-    new_small = [lax.dynamic_slice(v.reshape(-1), (z * 288,), (288,)) for v in new_attn[3:]]
+    pair_a, pair_m = (2, 608, ROW), (2, 1152, ROW)
+
+    def after(name):
+        return tuple(v[n] for n in AFTER.get(name, ()))
+
+    v = {"visible": visible, "samples": samples, "cotangent": cotangent}
+
+    def hbm(*names):
+        return tuple(v[n] if n in SENDS else in_hbm(v[n]) for n in names)
+
+    def cut():
+        swap_a = (304, ROW)
+        v["keep_a"], v["send_a"], v["keep_m"], v["send_m"] = at_once(
+            cut_masters, 1, [array(swap_a), array(swap_a), array(half_m), array(half_m)],
+            [pltpu.VMEM(shape_s, f32), pltpu.VMEM((2, *half_a), bf16), pltpu.VMEM((2, *half_m), bf16)], 8, "cut_masters", after("cut"), True,
+        )(idx, lanes(master_attn), lanes(master_mlp), three_rows(master_small))
+
+    def piece_a():
+        v["pa"] = at_once(lay_attn, 1, [array((608, ROW))], [], 8, "piece_attn", after("pa"))(
+            idx, v["keep_a"], v["send_a"], v["sa"]
+        )[0]
+
+    def even_a():
+        v["Ea"] = at_once(
+            pair_up, 0, [array(pair_a)], [], 8, "pair_up", after("Ea")
+        )(v["pa"], v["z2a"])[0]
+
+    def piece_m():
+        v["pm"] = at_once(lay_mlp, 1, [array(shape_m)], [], 8, "piece_mlp", after("pm"))(
+            idx, v["keep_m"], v["send_m"], v["sm"]
+        )[0]
+
+    def again_m():
+        v["pm2"] = at_once(lay_out, 0, [array(shape_m)], [], 8, "piece_again", after("pm2"))(v["pm"])[0]
+
+    def pack():
+        v["x"], v["cot"], v["meta"] = at_once(
+            pack_rows, 3, [large((rows, D)), large((rows, D)), array((64,), jnp.int32)],
+            [pltpu.SMEM((16,), jnp.int32)], 32, "pack_rows", after("pack"),
+        )(idx, visible, v["cv"], in_hbm(samples), v["cs"], in_hbm(cotangent), v["cc"])
+
+    def forward():
+        outs = [large((D, 3 * D // 2)), large((D // 2, D)), array((8, D), f32), array((1, 3 * D // 2), f32), array((1, FF // 2), f32)]
+        (v["qkv"], v["context"], v["part"], v["w_qkv"], v["w_out"], v["vecs"], shift, v["inner_bias"]) = over_blocks(
+            attn_forward, [D], 8, [(3 * D // 2, bf16, rows), (D // 2, bf16, rows), (D, bf16, rows)], outs,
+            [pltpu.VMEM((8, 16, ROW), f32)], 24, "attn_forward", after("fwd"),
+        )(v["meta"], idx, *hbm("x"), v["Ea"], *(v[n] for n in ("zOa", "xEa", "xOa", "yEa", "yOa", "dEa", "dOa")))
+
+    def there():
+        v["there"] = at_once(nothing, 1, [array((8, ROW), f32)], [], 4, "all_there", after("there"))(idx)[0]
+
+    def middle():
+        return hbm("x", "part", "pt")
+
+    def mlp():
+        pieces = [v["pm"] if c + k == "z0" else v[c + k + "m"] for c in "zxyd" for k in "0123"]
+        done = over_blocks(
+            mlp_both, [D] * 4, 18, [(FF // 2, bf16, rows), (D, bf16, rows)],
+            [large((FF // 2, D)), array((8, D), f32), array((1, FF // 2), f32)] + [array(pair_m)] * 8,
+            [pltpu.VMEM((D, FF // 2), bf16), pltpu.VMEM((D, FF // 2), f32), pltpu.VMEM((FF // 2, D), f32)],
+            48, "mlp_both", after("mlp"),
+        )(v["meta"], idx, *middle(), *hbm("cot"), v["vecs"], v["inner_bias"], *pieces)
+        v["active"], v["back"], v["w_two"], v["sums"], v["inner_sum"] = done[:5]
+        v.update(zip((n.format("m") for n in PAIR_NAMES), done[5:]))
+
+    def out_rows():
+        v["out_part"] = over_blocks(mlp_out, [FF // 2], 1, [(D, bf16, rows)], [], [], 16, "mlp_out", after("mout"))(
+            v["meta"], idx, *hbm("active", "w_two")
+        )[0]
+
+    def backward_1():
+        v["grad_middle"], v["grad_context"], v["acc_out"], v["sums_out"] = over_blocks(
+            middle_backward, [D] * 6 + [D // 2], 2, [(D, f32, rows), (D // 2, bf16, rows)],
+            [large((D // 2, D), f32), array((8, D), f32)], [], 16, "middle_backward", after("bw1"),
+        )(v["meta"], idx, *middle(), *hbm("cot", "back", "bk", "context", "w_out"), v["vecs"])
+
+    def backward_2():
+        v["grad_qkv"] = over_blocks(
+            heads_backward, [3 * D // 2, D // 2], 0, [(3 * D // 2, bf16, rows)], [], [], 16, "heads_backward", after("bw2"),
+        )(v["meta"], idx, *hbm("qkv", "grad_context"))[0]
+
+    def backward_3():
+        done = over_blocks(
+            first_backward, [D, 3 * D // 2], 6, [(D, bf16, rows)], [array(pair_a)] * 8,
+            [pltpu.VMEM((D, 3 * D // 2), f32), pltpu.VMEM((8, D), f32), pltpu.VMEM((8, 16, ROW), f32)],
+            20, "first_backward", after("bw3"),
+        )(v["meta"], idx, *hbm("x", "grad_qkv"), *hbm("w_qkv", "acc_out"), *(v[n] for n in ("vecs", "sums", "inner_sum", "sums_out")))
+        v["first_back"] = done[0]
+        v.update(zip((n.format("a") for n in PAIR_NAMES), done[1:]))
+
+    def again_back():
+        v["first_back_2"] = over_blocks(hand_on, [D], 0, [(D, bf16, rows)], [], [], 8, "hand_on", after("hand"))(
+            v["meta"], idx, *hbm("first_back")
+        )[0]
+
+    def finish():
+        v["output"], v["grad_samples"] = over_blocks(
+            finish_rows, [D] * 8, 1, [], [large((count, length, D))] * 2, [pltpu.VMEM((rows, D), bf16)] * 2, 24, "finish_rows", after("fin"),
+        )(v["meta"], idx, *middle(), *hbm("out_part", "ot", "grad_middle", "first_back", "fb"), v["vecs"])
+
+    def adds(g):
+        pair, half = (pair_a, 288) if g == "a" else (pair_m, 576)
+
+        def add(body, terms, outs, name):
+            return at_once(
+                body, 0, outs, [], 24, name + g, after(name + g)
+            )(*(v[t] for t in terms))
+
+        def even_in():
+            v["aE" + g] = add(add_low, [f"yE{g}_grad", "rE" + g], [array(pair)], "aE")[0]
+
+        def odd_in():
+            v["aO" + g] = add(add_low, [f"xO{g}_grad", "rO" + g], [array(pair)], "aO")[0]
+
+        def odd_sum():
+            v["so" + g] = add(add_low, [f"O{g}_grad", "pO" + g, "qO" + g], [array(pair)], "so")[0]
+
+        def even_sum():
+            v["near" + g], v["far" + g] = add(
+                add_near_far, [f"E{g}_grad", "pE" + g, "qE" + g, "wO" + g], [array(pair[1:], f32), array(pair[1:])], "sz"
+            )
+
+        def last_sum():
+            outs = [array((half, ROW), f32)] * 2 + ([array(shape_s, f32)] * 2 if g == "a" else [])
+            done = add(functools.partial(add_last, half), ["near" + g, "w2" + g], outs, "su")
+            v["own" + g], v["other" + g] = done[:2]
+            if g == "a":
+                v["own_small"], v["other_small"] = done[2:]
+
+        return {"aE" + g: even_in, "aO" + g: odd_in, "so" + g: odd_sum, "sz" + g: even_sum, "su" + g: last_sum}
+
+    def optimize_m():
+        v["new_mlp"] = at_once(
+            step_mlp, 1, [array(shape_m, f32)] * 3,
+            [pltpu.VMEM((2, *half_m), f32), pltpu.VMEM(shape_m, f32)], 16, "step_mlp", after("om"),
+        )(idx, lanes(master_mlp), lanes(first_mlp), lanes(second_mlp), v["ownm"], v["otherm"], v["gm"])
+        v["done_m"] = v["new_mlp"][0]
+
+    def optimize_a():
+        v["new_attn"] = at_once(
+            step_attn, 1, [array(shape_a, f32)] * 3 + [array((3, ROW), f32)] * 3,
+            [pltpu.VMEM((2, *half_a), f32), pltpu.VMEM(shape_a, f32), pltpu.VMEM(shape_s, f32), pltpu.VMEM((3, ROW), f32)], 16, "step_attn", after("oa"),
+        )(idx, lanes(master_attn), lanes(first_attn), lanes(second_attn), v["owna"], v["othera"], v["ga"],
+          three_rows(master_small), three_rows(first_small), three_rows(second_small), v["own_small"], v["gs"])
+
+    works = {"cut": cut, "pa": piece_a, "Ea": even_a, "pm": piece_m, "pm2": again_m, "pack": pack, "there": there, "fwd": forward, "mlp": mlp, "mout": out_rows,
+             "bw1": backward_1, "bw2": backward_2, "bw3": backward_3, "hand": again_back, "fin": finish, "om": optimize_m, "oa": optimize_a, **adds("m"), **adds("a")}
+    for step in ORDER:
+        kind, name = step[0], step[1:]
+        if kind == "+":
+            source, pairs = SENDS[name]
+            v[name] = send(v[source], pairs)
+        elif kind == "=":
+            works[name]()
+
+    new_mlp, new_attn, output, grad_samples = v["new_mlp"], v["new_attn"], v["output"], v["grad_samples"]
+    new_small = [a.reshape(-1)[:288] for a in new_attn[3:]]
     return (output, grad_samples, *(v.reshape(-1) for v in new_attn[:3]), *(v.reshape(-1) for v in new_mlp), *new_small)
 
 

time: 284 us -> 220 us (0.77); the launches traced: 280 us -> 219 us
  waiting for transfers between devices: 113 us -> 63.8 us
  starting transfers between devices: 84 us -> 66.1 us
  Pallas kernels: 61.1 us -> 76.3 us
  other arithmetic: 4.89 us -> 0 us
  local copies, waits for them, and re-layouts: 15.5 us -> 11.5 us
    ppermute x61 -> x51, waiting for transfers between devices: 113 us -> 63.8 us  [send(): return lax.ppermute(value, AXES, pairs)]
    ppermute x61 -> x51, starting transfers between devices: 84 us -> 66.1 us  [send(): return lax.ppermute(value, AXES, pairs)]
    pallas_call x9 -> x27, Pallas kernels: 61.1 us -> 76.3 us  [the longest x8 62.6 us: called(): pl.pallas_call(kernel, grid=(1,), in_specs=[SMEM, SMEM] + [ANY] * n_in +...]
    unnamed x129 -> x44, local copies, waits for them, and re-layouts: 12.6 us -> 10.1 us
  transfers between devices with their start and end apart: 61 -> 51, of which waited for: 24 -> 15; matrix products, arithmetic and copies ran while one was open for 3% -> 1% of each run, Pallas kernels for 10% -> 25%
where the time goes in v3:
time: 220 us; the launch traced here: 219 us
  Pallas kernels  76.3 us (35%)
  starting transfers between devices  66.1 us (30%)
  waiting for transfers between devices  63.8 us (29%)
  local copies, waits for them, and re-layouts  11.5 us (5%)
    ppermute x51, starting transfers between devices, send(): return lax.ppermute(value, AXES, pairs)  66.1 us
    ppermute x51, waiting for transfers between devices, send(): return lax.ppermute(value, AXES, pairs)  63.8 us
    pallas_call x8, Pallas kernels, called(): pl.pallas_call(kernel, grid=(1,), in_specs=[SMEM, SMEM] + [ANY] * n_in +...  62.6 us
    pallas_call x19, Pallas kernels, called(): pl.pallas_call(kernel, in_specs=[SMEM] * scalars + blocks + [ANY] * len(a...  13.6 us
    unnamed x44, local copies, waits for them, and re-layouts  10.1 us
  transfers between devices with their start and end apart: 51, of which 15 were waited for; matrix products, arithmetic and copies ran while one was open for 1% of the time, Pallas kernels for 25%

profile of v3, /device:TPU:0, one launch (start us, length us, event | category | flops | bytes accessed | tf_op | source)
XLA Modules:
  0.0 218.7 jit_solution(9375920613075471052)
XLA Ops:
  1.3 1.3 pad_bitcast_fusion.2.refs_3_.refs_7_
  2.6 1.3 cut_masters.1
  4.9 1.8 collective-permute-done.refs_2_.refs_6_
  7.4 4.0 %collective-permute-start.4 = (bf16[608,128]{1,0:T(8,128)(2,1)S(1)}, bf16[608,128]{1,0:T(8,128)(2,1)S(1)}, u32[]{:S(2)}, u32[]{:S(2)}) collective-permute-start(bf16[608,128]{1,0:T(8,128)(2,1)S(1)} %piece_attn.1.refs_0_.refs_4_), channel_id=1, source_target_pairs={{0,2},{1,3},{2,0},{3,1},{4,6},{5,7},{6,4},{7,5},{8,10},{9,11},{10,... | collective-permute-start | bytes 466952 | tf_op jit(solution)/shard_map/ppermute | solution.py:259
  12.0 1.6 collective-permute-start.13
  13.6 1.5 collective-permute-start.16
  15.1 1.5 collective-permute-start.17
  16.6 5.4 %pack_rows.1 = (bf16[2048,768]{1,0:T(8,128)(2,1)}, bf16[2048,768]{1,0:T(8,128)(2,1)}, s32[64]{0:T(128)S(1)}) custom-call(s32[5]{0:T(128)S(1)} %stack.23.refs_0_.idx, s32[8]{0:T(128)S(1)} %copy-done.11, s32[8]{0:T(128)S(1)} %collective-permute-done.refs_2_.refs_6_, bf16[8,128,768]{2,1,0:T(8,128)(2,1)} %refs_3_.1, ...), custom_call_target="tpu_custom_call" | custom-call | flops 6000000000 | bytes 1 | tf_op jit(solution)/shard_map/pack_rows/pallas_call | solution.py:1044
  22.6 0.6 collective-permute-start.8
  23.3 1.7 collective-permute-start.19
  25.0 1.5 collective-permute-start.6
  26.5 8.9 %collective-permute-done.5.refs_2_ = bf16[2,608,128]{2,1,0:T(8,128)(2,1)S(1)} collective-permute-done((bf16[2,608,128]{2,1,0:T(8,128)(2,1)S(1)}, bf16[2,608,128]{2,1,0:T(8,128)(2,1)S(1)}, u32[]{:S(2)}, u32[]{:S(2)}) %collective-permute-start.5) | collective-permute-done | bytes 311328 | tf_op jit(solution)/shard_map/ppermute | solution.py:259
  35.3 0.7 collective-permute-start.7
  36.0 1.4 collective-permute-start.14
  37.4 0.8 collective-permute-done.19.refs_8_
  38.1 1.6 collective-permute-start.15
  39.7 1.5 collective-permute-start.25
  41.7 10.2 %collective-permute-done.14.refs_9_.refs_11_ = bf16[1152,128]{1,0:T(8,128)(2,1)S(1)} collective-permute-done((bf16[1152,128]{1,0:T(8,128)(2,1)S(1)}, bf16[1152,128]{1,0:T(8,128)(2,1)S(1)}, u32[]{:S(2)}, u32[]{:S(2)}) %collective-permute-start.14) | collective-permute-done | bytes 294944 | tf_op jit(solution)/shard_map/ppermute | solution.py:259
  51.9 0.7 collective-permute-start.10
  52.6 1.5 collective-permute-start.9
  54.7 3.6 %collective-permute-done.25.refs_7_.refs_18_ = bf16[1152,128]{1,0:T(8,128)(2,1)S(1)} collective-permute-done((bf16[1152,128]{1,0:T(8,128)(2,1)S(1)}, bf16[1152,128]{1,0:T(8,128)(2,1)S(1)}, u32[]{:S(2)}, u32[]{:S(2)}) %collective-permute-start.25) | collective-permute-done | bytes 294944 | tf_op jit(solution)/shard_map/ppermute | solution.py:259
  58.3 6.3 %collective-permute-done.21.refs_6_.refs_12_ = bf16[1152,128]{1,0:T(8,128)(2,1)S(1)} collective-permute-done((bf16[1152,128]{1,0:T(8,128)(2,1)S(1)}, bf16[1152,128]{1,0:T(8,128)(2,1)S(1)}, u32[]{:S(2)}, u32[]{:S(2)}) %collective-permute-start.21) | collective-permute-done | bytes 294944 | tf_op jit(solution)/shard_map/ppermute | solution.py:259
  64.6 0.7 collective-permute-start.27
  65.3 1.3 collective-permute-start.23
  66.6 1.9 collective-permute-done.10.refs_7_
  68.5 0.7 collective-permute-start.22
  69.2 5.3 %collective-permute-done.27.refs_4_.refs_20_ = bf16[1152,128]{1,0:T(8,128)(2,1)S(1)} collective-permute-done((bf16[1152,128]{1,0:T(8,128)(2,1)S(1)}, bf16[1152,128]{1,0:T(8,128)(2,1)S(1)}, u32[]{:S(2)}, u32[]{:S(2)}) %collective-permute-start.27) | collective-permute-done | bytes 294944 | tf_op jit(solution)/shard_map/ppermute | solution.py:259
  74.5 0.7 collective-permute-start.24
  75.2 8.9 %attn_forward.1 = (bf16[2048,1152]{1,0:T(8,128)(2,1)}, bf16[2048,384]{1,0:T(8,128)(2,1)}, bf16[2048,768]{1,0:T(8,128)(2,1)}, bf16[768,1152]{1,0:T(8,128)(2,1)}, ...) custom-call(s32[64]{0:T(128)S(1)} %get-tuple-element.72.refs_2_.meta, ...), custom_call_target="tpu_custom_call" | custom-call | flops 11000000512 | bytes 1 | tf_op jit(solution)/shard_map/attn_forward/pallas_call | solution.py:1020
  84.7 5.3 %collective-permute-done.18.refs_2_ = bf16[2048,768]{1,0:T(8,128)(2,1)S(1)} collective-permute-done((bf16[2048,768]{1,0:T(8,128)(2,1)}, bf16[2048,768]{1,0:T(8,128)(2,1)S(1)}, u32[]{:S(2)}, u32[]{:S(2)}) %collective-permute-start.18) | collective-permute-done | bytes 3145760 | tf_op jit(solution)/shard_map/ppermute | solution.py:259
  90.0 1.6 copy-done.2
  91.6 18.0 %mlp_both.1 = (bf16[2048,1536]{1,0:T(8,128)(2,1)}, bf16[2048,768]{1,0:T(8,128)(2,1)}, bf16[1536,768]{1,0:T(8,128)(2,1)}, f32[8,768]{1,0:T(8,128)S(1)}, f32[1,153...) custom-call(s32[64]{0:T(128)S(1)} %get-tuple-element.72.refs_2_.meta, ...), custom_call_target="tpu_custom_call" | custom-call | flops 23000000512 | bytes 1 | tf_op jit(solution)/shard_map/mlp_both/pallas_call | solution.py:1020
  109.8 1.3 collective-permute-start.32
  111.1 0.7 collective-permute-start.31
  111.8 5.3 %mlp_out.1.refs_9_.refs_3_ = bf16[2048,768]{1,0:T(8,128)(2,1)} custom-call(s32[64]{0:T(128)S(1)} %get-tuple-element.72.refs_2_.meta, s32[5]{0:T(128)S(1)} %stack.23.refs_0_.idx, bf16[2048,1536]{1,0:T(8,128)(2,1)} %get-tuple-element.82.refs_0_, bf16[1536,768]{1,0:T(8,128)(2,1)} %get-tuple-element.83.refs_1_), custom_call_target="tpu_custom_call" | custom-call | flops 20000000000 | bytes 1 | tf_op jit(solution)/shard_map/mlp_out/pallas_call | solution.py:1020
  117.1 1.5 collective-permute-start.33
  118.6 1.9 copy-done.4
  120.5 6.9 %middle_backward.1 = (f32[2048,768]{1,0:T(8,128)}, bf16[2048,384]{1,0:T(8,128)(2,1)}, f32[384,768]{1,0:T(8,128)}, f32[8,768]{1,0:T(8,128)S(1)}) custom-call(s32[64]{0:T(128)S(1)} %get-tuple-element.72.refs_2_.meta, s32[5]{0:T(128)S(1)} %stack.23.refs_0_.idx, bf16[2048,768]{1,0:T(8,128)(2,1)} %get-tuple-element.73.refs_0_, ...), custom_call_target="tpu_custom_call" | custom-call | flops 8000000000 | bytes 1 | tf_op jit(solution)/shard_map/middle_backward/pallas_call | solution.py:1020
  127.4 1.4 copy-done.14
  129.0 0.6 collective-permute-start.34
  129.6 0.7 copy-done.15
  130.4 6.9 %heads_backward.1.refs_1_ = bf16[2048,1152]{1,0:T(8,128)(2,1)} custom-call(s32[64]{0:T(128)S(1)} %get-tuple-element.72.refs_2_.meta, s32[5]{0:T(128)S(1)} %stack.23.refs_0_.idx, bf16[2048,1152]{1,0:T(8,128)(2,1)} %get-tuple-element.88.refs_0_, bf16[2048,384]{1,0:T(8,128)(2,1)} %get-tuple-element.89.refs_2_.refs_1_, bf16[2,1152,128]{2,1,0:T(8,128)(2,1)S(1)} %aEm.1.refs_2_, ...), custom_call_target="tpu_custom_call" | custom-call | flops 24999999488 | bytes 1 | tf_op jit(solution)/shard_map/heads_backward/pallas_call | solution.py:1020
  137.3 7.7 %first_backward.1 = (bf16[2048,768]{1,0:T(8,128)(2,1)}, bf16[2,608,128]{2,1,0:T(8,128)(2,1)S(1)}, bf16[2,608,128]{2,1,0:T(8,128)(2,1)S(1)}, bf16[2,608,128]{2,1,...) custom-call(s32[64]{0:T(128)S(1)} %get-tuple-element.72.refs_2_.meta, ...), custom_call_target="tpu_custom_call" | custom-call | flops 24999999488 | bytes 1 | tf_op jit(solution)/shard_map/first_backward/pallas_call | solution.py:1020
  145.0 1.9 copy-done
  147.1 2.5 %hand_on.1 = bf16[2048,768]{1,0:T(8,128)(2,1)} custom-call(s32[64]{0:T(128)S(1)} %get-tuple-element.72.refs_2_.meta, s32[5]{0:T(128)S(1)} %stack.23.refs_0_.idx, bf16[2048,768]{1,0:T(8,128)(2,1)} %get-tuple-element.99.refs_3_.refs_0_.refs_6_, bf16[2,1152,128]{2,1,0:T(8,128)(2,1)S(1)} %som.1.refs_1_), custom_call_target="tpu_custom_call" | custom-call | flops 1000000000 | bytes 1 | tf_op jit(solution)/shard_map/hand_on/pallas_call | solution.py:1020
  149.8 0.6 collective-permute-start.41
  150.5 1.2 collective-permute-start.42
  151.7 13.6 %collective-permute-start.43 = (bf16[2,1152,128]{2,1,0:T(8,128)(2,1)S(1)}, bf16[2,1152,128]{2,1,0:T(8,128)(2,1)S(1)}, u32[]{:S(2)}, u32[]{:S(2)}) collective-permute-start(bf16[2,1152,128]{2,1,0:T(8,128)(2,1)S(1)} %som.1.refs_1_), channel_id=1, source_target_pairs={{0,1},{1,0},{2,3},{3,2},{4,5},{5,4},{6,7},{7,6},{8,9},{9,8},{10,11... | collective-permute-start | bytes 1769480 | tf_op jit(solution)/shard_map/ppermute | solution.py:259
  165.3 9.0 %collective-permute-done.37.refs_1_ = bf16[2,608,128]{2,1,0:T(8,128)(2,1)S(1)} collective-permute-done((bf16[2,608,128]{2,1,0:T(8,128)(2,1)S(1)}, bf16[2,608,128]{2,1,0:T(8,128)(2,1)S(1)}, u32[]{:S(2)}, u32[]{:S(2)}) %collective-permute-start.37) | collective-permute-done | bytes 311328 | tf_op jit(solution)/shard_map/ppermute | solution.py:259
  174.8 1.7 collective-permute-start.38
  176.8 2.0 collective-permute-done.43.refs_3_
  179.1 0.9 collective-permute-start.47
  180.0 2.5 %collective-permute-done.36.refs_1_ = bf16[2,608,128]{2,1,0:T(8,128)(2,1)S(1)} collective-permute-done((bf16[2,608,128]{2,1,0:T(8,128)(2,1)S(1)}, bf16[2,608,128]{2,1,0:T(8,128)(2,1)S(1)}, u32[]{:S(2)}, u32[]{:S(2)}) %collective-permute-start.36) | collective-permute-done | bytes 311328 | tf_op jit(solution)/shard_map/ppermute | solution.py:259
  182.5 1.4 collective-permute-start.39
  183.9 1.2 collective-permute-done.38.refs_2_
  185.2 12.9 %collective-permute-start.45 = (bf16[2,608,128]{2,1,0:T(8,128)(2,1)S(1)}, bf16[2,608,128]{2,1,0:T(8,128)(2,1)S(1)}, u32[]{:S(2)}, u32[]{:S(2)}) collective-permute-start(bf16[2,608,128]{2,1,0:T(8,128)(2,1)S(1)} %soa.1.refs_9_), channel_id=1, source_target_pairs={{0,1},{1,0},{2,3},{3,2},{4,5},{5,4},{6,7},{7,6},{8,9},{9,8},{10,11... | collective-permute-start | bytes 933896 | tf_op jit(solution)/shard_map/ppermute | solution.py:259
  198.7 6.5 %finish_rows.1 = (bf16[8,128,768]{2,1,0:T(8,128)(2,1)}, bf16[8,128,768]{2,1,0:T(8,128)(2,1)}) custom-call(s32[64]{0:T(128)S(1)} %get-tuple-element.72.refs_2_.meta, s32[5]{0:T(128)S(1)} %stack.23.refs_0_.idx, bf16[2048,768]{1,0:T(8,128)(2,1)} %get-tuple-element.73.refs_0_, bf16[2048,768]{1,0:T(8,128)(2,1)} %get-tuple-element.78.refs_1_, ...), custom_call_target="tpu_custom_call" | custom-call | flops 8000000000 | bytes 1 | tf_op jit(solution)/shard_map/finish_rows/pallas_call | solution.py:1020
  205.2 1.5 copy-done.12
  206.9 0.9 collective-permute-start.46
  208.0 2.1 step_mlp.1
  210.1 4.2 %collective-permute-done.46.refs_1_ = bf16[608,128]{1,0:T(8,128)(2,1)S(1)} collective-permute-done((bf16[608,128]{1,0:T(8,128)(2,1)S(1)}, bf16[608,128]{1,0:T(8,128)(2,1)S(1)}, u32[]{:S(2)}, u32[]{:S(2)}) %collective-permute-start.46) | collective-permute-done | bytes 155680 | tf_op jit(solution)/shard_map/ppermute | solution.py:259
  214.3 1.1 copy-done.13
  216.0 0.9 collective-permute-done.50.refs_11_
  216.9 1.8 step_attn.1
  (112 shorter events, 8.5 us)
Async XLA Ops:
  0.6 3.9 %copy-start.11 = (s32[8]{0:T(128)S(1)}, s32[8]{0:T(128)}, u32[]{:S(2)}) copy-start(s32[8]{0:T(128)} %refs_1_.1) | copy-start | bytes 100
  0.7 6.1 %collective-permute-start.1 = (bf16[8,128,768]{2,1,0:T(8,128)(2,1)}, bf16[8,128,768]{2,1,0:T(8,128)(2,1)S(1)}, u32[]{:S(2)}, u32[]{:S(2)}) collective-permute-start(bf16[8,128,768]{2,1,0:T(8,128)(2,1)} %refs_3_.1), channel_id=1, source_target_pairs={{0,4},{1,5},{2,6},{3,7},{4,0},{5,1},{6,2},{7,3},{8,12},{9,13},{10,... | collective-permute-start | bytes 4718600 | tf_op jit(solution)/shard_map/ppermute | solution.py:259
  1.2 5.6 %collective-permute-start.2 = (bf16[8,128,768]{2,1,0:T(8,128)(2,1)}, bf16[8,128,768]{2,1,0:T(8,128)(2,1)S(1)}, u32[]{:S(2)}, u32[]{:S(2)}) collective-permute-start(bf16[8,128,768]{2,1,0:T(8,128)(2,1)} %refs_5_.1), channel_id=1, source_target_pairs={{0,4},{1,5},{2,6},{3,7},{4,0},{5,1},{6,2},{7,3},{8,12},{9,13},{10,... | collective-permute-start | bytes 4718600 | tf_op jit(solution)/shard_map/ppermute | solution.py:259
  3.9 2.8 %collective-permute-start.3 = (bf16[304,128]{1,0:T(8,128)(2,1)S(1)}, bf16[304,128]{1,0:T(8,128)(2,1)S(1)}, u32[]{:S(2)}, u32[]{:S(2)}) collective-permute-start(bf16[304,128]{1,0:T(8,128)(2,1)S(1)} %get-tuple-element.75.refs_2_), channel_id=1, source_target_pairs={{0,4},{1,5},{2,6},{3,7},{4,0},{5,1},{6,2},{7,3},{8,12},{9,13},{10,... | collective-permute-start | bytes 233480 | tf_op jit(solution)/shard_map/ppermute | solution.py:259
  4.4 7.0 %collective-permute-start.12 = (bf16[576,128]{1,0:T(8,128)(2,1)S(1)}, bf16[576,128]{1,0:T(8,128)(2,1)S(1)}, u32[]{:S(2)}, u32[]{:S(2)}) collective-permute-start(bf16[576,128]{1,0:T(8,128)(2,1)S(1)} %get-tuple-element.77.refs_2_), channel_id=1, source_target_pairs={{0,4},{1,5},{2,6},{3,7},{4,0},{5,1},{6,2},{7,3},{8,12},{9,13},{10,... | collective-permute-start | bytes 442376 | tf_op jit(solution)/shard_map/ppermute | solution.py:259
  4.5 2.3 %collective-permute-start = (s32[8]{0:T(128)S(1)}, s32[8]{0:T(128)S(1)}, u32[]{:S(2)}, u32[]{:S(2)}) collective-permute-start(s32[8]{0:T(128)S(1)} %copy-done.11), channel_id=1, source_target_pairs={{0,4},{1,5},{2,6},{3,7},{4,0},{5,1},{6,2},{7,3},{8,12},{9,13},{10,... | collective-permute-start | bytes 104 | tf_op jit(solution)/shard_map/ppermute | solution.py:259
  7.4 14.7 %collective-permute-start.4 = (bf16[608,128]{1,0:T(8,128)(2,1)S(1)}, bf16[608,128]{1,0:T(8,128)(2,1)S(1)}, u32[]{:S(2)}, u32[]{:S(2)}) collective-permute-start(bf16[608,128]{1,0:T(8,128)(2,1)S(1)} %piece_attn.1.refs_0_.refs_4_), channel_id=1, source_target_pairs={{0,2},{1,3},{2,0},{3,1},{4,6},{5,7},{6,4},{7,5},{8,10},{9,11},{10,... | collective-permute-start | bytes 466952 | tf_op jit(solution)/shard_map/ppermute | solution.py:259
  12.0 11.3 %collective-permute-start.13 = (bf16[1152,128]{1,0:T(8,128)(2,1)S(1)}, bf16[1152,128]{1,0:T(8,128)(2,1)S(1)}, u32[]{:S(2)}, u32[]{:S(2)}) collective-permute-start(bf16[1152,128]{1,0:T(8,128)(2,1)S(1)} %piece_mlp.1.refs_0_.refs_6_), channel_id=1, source_target_pairs={{0,1},{1,0},{2,3},{3,2},{4,5},{5,4},{6,7},{7,6},{8,9},{9,8},{10,11... | collective-permute-start | bytes 884744 | tf_op jit(solution)/shard_map/ppermute | solution.py:259
  13.6 11.4 %collective-permute-start.16 = (bf16[1152,128]{1,0:T(8,128)(2,1)S(1)}, bf16[1152,128]{1,0:T(8,128)(2,1)S(1)}, u32[]{:S(2)}, u32[]{:S(2)}) collective-permute-start(bf16[1152,128]{1,0:T(8,128)(2,1)S(1)} %piece_mlp.1.refs_0_.refs_6_), channel_id=1, source_target_pairs={{0,8},{1,9},{2,10},{3,11},{4,12},{5,13},{6,14},{7,15},{8,0},{9,1},... | collective-permute-start | bytes 884744 | tf_op jit(solution)/shard_map/ppermute | solution.py:259
  15.1 20.9 %collective-permute-start.17 = (bf16[1152,128]{1,0:T(8,128)(2,1)S(1)}, bf16[1152,128]{1,0:T(8,128)(2,1)S(1)}, u32[]{:S(2)}, u32[]{:S(2)}) collective-permute-start(bf16[1152,128]{1,0:T(8,128)(2,1)S(1)} %piece_mlp.1.refs_0_.refs_6_), channel_id=1, source_target_pairs={{0,16},{1,17},{2,18},{3,19},{4,20},{5,21},{6,22},{7,23},{8,24},{9,... | collective-permute-start | bytes 884744 | tf_op jit(solution)/shard_map/ppermute | solution.py:259
  22.1 13.2 %collective-permute-start.5 = (bf16[2,608,128]{2,1,0:T(8,128)(2,1)S(1)}, bf16[2,608,128]{2,1,0:T(8,128)(2,1)S(1)}, u32[]{:S(2)}, u32[]{:S(2)}) collective-permute-start(bf16[2,608,128]{2,1,0:T(8,128)(2,1)S(1)} %pair_up.1.refs_1_), channel_id=1, source_target_pairs={{0,1},{1,0},{2,3},{3,2},{4,5},{5,4},{6,7},{7,6},{8,9},{9,8},{10,11... | collective-permute-start | bytes 933896 | tf_op jit(solution)/shard_map/ppermute | solution.py:259
  22.6 17.1 %collective-permute-start.8 = (bf16[2,608,128]{2,1,0:T(8,128)(2,1)S(1)}, bf16[2,608,128]{2,1,0:T(8,128)(2,1)S(1)}, u32[]{:S(2)}, u32[]{:S(2)}) collective-permute-start(bf16[2,608,128]{2,1,0:T(8,128)(2,1)S(1)} %pair_up.1.refs_1_), channel_id=1, source_target_pairs={{0,16},{1,17},{2,18},{3,19},{4,20},{5,21},{6,22},{7,23},{8,24},{9,... | collective-permute-start | bytes 933896 | tf_op jit(solution)/shard_map/ppermute | solution.py:259
  23.3 14.9 %collective-permute-start.19 = (bf16[1152,128]{1,0:T(8,128)(2,1)S(1)}, bf16[1152,128]{1,0:T(8,128)(2,1)S(1)}, u32[]{:S(2)}, u32[]{:S(2)}) collective-permute-start(bf16[1152,128]{1,0:T(8,128)(2,1)S(1)} %piece_again.1), channel_id=1, source_target_pairs={{0,2},{1,3},{2,0},{3,1},{4,6},{5,7},{6,4},{7,5},{8,10},{9,11},{10,... | collective-permute-start | bytes 884744 | tf_op jit(solution)/shard_map/ppermute | solution.py:259
  25.0 16.2 %collective-permute-start.6 = (bf16[2,608,128]{2,1,0:T(8,128)(2,1)S(1)}, bf16[2,608,128]{2,1,0:T(8,128)(2,1)S(1)}, u32[]{:S(2)}, u32[]{:S(2)}) collective-permute-start(bf16[2,608,128]{2,1,0:T(8,128)(2,1)S(1)} %pair_up.1.refs_1_), channel_id=1, source_target_pairs={{0,8},{1,9},{2,10},{3,11},{4,12},{5,13},{6,14},{7,15},{8,0},{9,1},... | collective-permute-start | bytes 933896 | tf_op jit(solution)/shard_map/ppermute | solution.py:259
  35.3 18.8 %collective-permute-start.7 = (bf16[2,608,128]{2,1,0:T(8,128)(2,1)S(1)}, bf16[2,608,128]{2,1,0:T(8,128)(2,1)S(1)}, u32[]{:S(2)}, u32[]{:S(2)}) collective-permute-start(bf16[2,608,128]{2,1,0:T(8,128)(2,1)S(1)} %collective-permute-done.5.refs_2_), channel_id=1, source_target_pairs={{0,8},{1,9},{2,10},{3,11},{4,12},{5,13},{6,14},{7,15},{8,0},{9,1},... | collective-permute-start | bytes 933896 | tf_op jit(solution)/shard_map/ppermute | solution.py:259
  36.0 15.9 %collective-permute-start.14 = (bf16[1152,128]{1,0:T(8,128)(2,1)S(1)}, bf16[1152,128]{1,0:T(8,128)(2,1)S(1)}, u32[]{:S(2)}, u32[]{:S(2)}) collective-permute-start(bf16[1152,128]{1,0:T(8,128)(2,1)S(1)} %collective-permute-done.13.refs_7_), channel_id=1, source_target_pairs={{0,8},{1,9},{2,10},{3,11},{4,12},{5,13},{6,14},{7,15},{8,0},{9,1},... | collective-permute-start | bytes 884744 | tf_op jit(solution)/shard_map/ppermute | solution.py:259
  38.1 14.5 %collective-permute-start.15 = (bf16[1152,128]{1,0:T(8,128)(2,1)S(1)}, bf16[1152,128]{1,0:T(8,128)(2,1)S(1)}, u32[]{:S(2)}, u32[]{:S(2)}) collective-permute-start(bf16[1152,128]{1,0:T(8,128)(2,1)S(1)} %collective-permute-done.13.refs_7_), channel_id=1, source_target_pairs={{0,16},{1,17},{2,18},{3,19},{4,20},{5,21},{6,22},{7,23},{8,24},{9,... | collective-permute-start | bytes 884744 | tf_op jit(solution)/shard_map/ppermute | solution.py:259
  39.7 18.5 %collective-permute-start.25 = (bf16[1152,128]{1,0:T(8,128)(2,1)S(1)}, bf16[1152,128]{1,0:T(8,128)(2,1)S(1)}, u32[]{:S(2)}, u32[]{:S(2)}) collective-permute-start(bf16[1152,128]{1,0:T(8,128)(2,1)S(1)} %collective-permute-done.17.refs_12_.refs_14_), channel_id=1, source_target_pairs={{0,8},{1,9},{2,10},{3,11},{4,12},{5,13},{6,14},{7,15},{8,0},{9,1},... | collective-permute-start | bytes 884744 | tf_op jit(solution)/shard_map/ppermute | solution.py:259
  41.2 23.4 %collective-permute-start.21 = (bf16[1152,128]{1,0:T(8,128)(2,1)S(1)}, bf16[1152,128]{1,0:T(8,128)(2,1)S(1)}, u32[]{:S(2)}, u32[]{:S(2)}) collective-permute-start(bf16[1152,128]{1,0:T(8,128)(2,1)S(1)} %collective-permute-done.19.refs_8_), channel_id=1, source_target_pairs={{0,8},{1,9},{2,10},{3,11},{4,12},{5,13},{6,14},{7,15},{8,0},{9,1},... | collective-permute-start | bytes 884744 | tf_op jit(solution)/shard_map/ppermute | solution.py:259
  51.9 16.5 %collective-permute-start.10 = (bf16[2,608,128]{2,1,0:T(8,128)(2,1)S(1)}, bf16[2,608,128]{2,1,0:T(8,128)(2,1)S(1)}, u32[]{:S(2)}, u32[]{:S(2)}) collective-permute-start(bf16[2,608,128]{2,1,0:T(8,128)(2,1)S(1)} %collective-permute-done.8.refs_5_), channel_id=1, source_target_pairs={{0,8},{1,9},{2,10},{3,11},{4,12},{5,13},{6,14},{7,15},{8,0},{9,1},... | collective-permute-start | bytes 933896 | tf_op jit(solution)/shard_map/ppermute | solution.py:259
  52.6 15.9 %collective-permute-start.9 = (bf16[2,608,128]{2,1,0:T(8,128)(2,1)S(1)}, bf16[2,608,128]{2,1,0:T(8,128)(2,1)S(1)}, u32[]{:S(2)}, u32[]{:S(2)}) collective-permute-start(bf16[2,608,128]{2,1,0:T(8,128)(2,1)S(1)} %collective-permute-done.5.refs_2_), channel_id=1, source_target_pairs={{0,16},{1,17},{2,18},{3,19},{4,20},{5,21},{6,22},{7,23},{8,24},{9,... | collective-permute-start | bytes 933896 | tf_op jit(solution)/shard_map/ppermute | solution.py:259
  54.2 21.1 %collective-permute-start.11 = (bf16[2,608,128]{2,1,0:T(8,128)(2,1)S(1)}, bf16[2,608,128]{2,1,0:T(8,128)(2,1)S(1)}, u32[]{:S(2)}, u32[]{:S(2)}) collective-permute-start(bf16[2,608,128]{2,1,0:T(8,128)(2,1)S(1)} %collective-permute-done.7.refs_4_), channel_id=1, source_target_pairs={{0,16},{1,17},{2,18},{3,19},{4,20},{5,21},{6,22},{7,23},{8,24},{9,... | collective-permute-start | bytes 933896 | tf_op jit(solution)/shard_map/ppermute | solution.py:259
  58.3 7.0 %collective-permute-start.20 = (bf16[1152,128]{1,0:T(8,128)(2,1)S(1)}, bf16[1152,128]{1,0:T(8,128)(2,1)S(1)}, u32[]{:S(2)}, u32[]{:S(2)}) collective-permute-start(bf16[1152,128]{1,0:T(8,128)(2,1)S(1)} %collective-permute-done.19.refs_8_), channel_id=1, source_target_pairs={{0,1},{1,0},{2,3},{3,2},{4,5},{5,4},{6,7},{7,6},{8,9},{9,8},{10,11... | collective-permute-start | bytes 884744 | tf_op jit(solution)/shard_map/ppermute | solution.py:259
  64.6 9.9 %collective-permute-start.27 = (bf16[1152,128]{1,0:T(8,128)(2,1)S(1)}, bf16[1152,128]{1,0:T(8,128)(2,1)S(1)}, u32[]{:S(2)}, u32[]{:S(2)}) collective-permute-start(bf16[1152,128]{1,0:T(8,128)(2,1)S(1)} %collective-permute-done.21.refs_6_.refs_12_), channel_id=1, source_target_pairs={{0,16},{1,17},{2,18},{3,19},{4,20},{5,21},{6,22},{7,23},{8,24},{9,... | collective-permute-start | bytes 884744 | tf_op jit(solution)/shard_map/ppermute | solution.py:259
  65.3 19.4 %collective-permute-start.23 = (bf16[1152,128]{1,0:T(8,128)(2,1)S(1)}, bf16[1152,128]{1,0:T(8,128)(2,1)S(1)}, u32[]{:S(2)}, u32[]{:S(2)}) collective-permute-start(bf16[1152,128]{1,0:T(8,128)(2,1)S(1)} %collective-permute-done.19.refs_8_), channel_id=1, source_target_pairs={{0,16},{1,17},{2,18},{3,19},{4,20},{5,21},{6,22},{7,23},{8,24},{9,... | collective-permute-start | bytes 884744 | tf_op jit(solution)/shard_map/ppermute | solution.py:259
  68.5 15.6 %collective-permute-start.26 = (bf16[1152,128]{1,0:T(8,128)(2,1)S(1)}, bf16[1152,128]{1,0:T(8,128)(2,1)S(1)}, u32[]{:S(2)}, u32[]{:S(2)}) collective-permute-start(bf16[1152,128]{1,0:T(8,128)(2,1)S(1)} %collective-permute-done.25.refs_7_.refs_18_), channel_id=1, source_target_pairs={{0,1},{1,0},{2,3},{3,2},{4,5},{5,4},{6,7},{7,6},{8,9},{9,8},{10,11... | collective-permute-start | bytes 884744 | tf_op jit(solution)/shard_map/ppermute | solution.py:259
  68.5 15.6 %collective-permute-start.22 = (bf16[1152,128]{1,0:T(8,128)(2,1)S(1)}, bf16[1152,128]{1,0:T(8,128)(2,1)S(1)}, u32[]{:S(2)}, u32[]{:S(2)}) collective-permute-start(bf16[1152,128]{1,0:T(8,128)(2,1)S(1)} %collective-permute-done.20.refs_9_), channel_id=1, source_target_pairs={{0,8},{1,9},{2,10},{3,11},{4,12},{5,13},{6,14},{7,15},{8,0},{9,1},... | collective-permute-start | bytes 884744 | tf_op jit(solution)/shard_map/ppermute | solution.py:259
  74.5 9.6 %collective-permute-start.24 = (bf16[1152,128]{1,0:T(8,128)(2,1)S(1)}, bf16[1152,128]{1,0:T(8,128)(2,1)S(1)}, u32[]{:S(2)}, u32[]{:S(2)}) collective-permute-start(bf16[1152,128]{1,0:T(8,128)(2,1)S(1)} %collective-permute-done.20.refs_9_), channel_id=1, source_target_pairs={{0,16},{1,17},{2,18},{3,19},{4,20},{5,21},{6,22},{7,23},{8,24},{9,... | collective-permute-start | bytes 884744 | tf_op jit(solution)/shard_map/ppermute | solution.py:259
  75.2 8.9 %collective-permute-start.28 = (bf16[1152,128]{1,0:T(8,128)(2,1)S(1)}, bf16[1152,128]{1,0:T(8,128)(2,1)S(1)}, u32[]{:S(2)}, u32[]{:S(2)}) collective-permute-start(bf16[1152,128]{1,0:T(8,128)(2,1)S(1)} %collective-permute-done.27.refs_4_.refs_20_), channel_id=1, source_target_pairs={{0,1},{1,0},{2,3},{3,2},{4,5},{5,4},{6,7},{7,6},{8,9},{9,8},{10,11... | collective-permute-start | bytes 884744 | tf_op jit(solution)/shard_map/ppermute | solution.py:259
  84.1 5.9 %collective-permute-start.18 = (bf16[2048,768]{1,0:T(8,128)(2,1)}, bf16[2048,768]{1,0:T(8,128)(2,1)S(1)}, u32[]{:S(2)}, u32[]{:S(2)}) collective-permute-start(bf16[2048,768]{1,0:T(8,128)(2,1)} %get-tuple-element.78.refs_1_), channel_id=1, source_target_pairs={{0,4},{1,5},{2,6},{3,7},{4,0},{5,1},{6,2},{7,3},{8,12},{9,13},{10,... | collective-permute-start | bytes 9437192 | tf_op jit(solution)/shard_map/ppermute | solution.py:259
  109.6 9.0 %collective-permute-start.30 = (bf16[2048,768]{1,0:T(8,128)(2,1)}, bf16[2048,768]{1,0:T(8,128)(2,1)S(1)}, u32[]{:S(2)}, u32[]{:S(2)}) collective-permute-start(bf16[2048,768]{1,0:T(8,128)(2,1)} %get-tuple-element.84.refs_4_), channel_id=1, source_target_pairs={{0,4},{1,5},{2,6},{3,7},{4,0},{5,1},{6,2},{7,3},{8,12},{9,13},{10,... | collective-permute-start | bytes 9437192 | tf_op jit(solution)/shard_map/ppermute | solution.py:259
  109.8 17.7 %collective-permute-start.32 = (bf16[2,1152,128]{2,1,0:T(8,128)(2,1)}, bf16[2,1152,128]{2,1,0:T(8,128)(2,1)S(1)}, u32[]{:S(2)}, u32[]{:S(2)}) collective-permute-start(bf16[2,1152,128]{2,1,0:T(8,128)(2,1)} %get-tuple-element.93), channel_id=1, source_target_pairs={{0,16},{1,17},{2,18},{3,19},{4,20},{5,21},{6,22},{7,23},{8,24},{9,... | collective-permute-start | bytes 1769480 | tf_op jit(solution)/shard_map/ppermute | solution.py:259
  111.1 18.5 %collective-permute-start.31 = (bf16[2,1152,128]{2,1,0:T(8,128)(2,1)}, bf16[2,1152,128]{2,1,0:T(8,128)(2,1)S(1)}, u32[]{:S(2)}, u32[]{:S(2)}) collective-permute-start(bf16[2,1152,128]{2,1,0:T(8,128)(2,1)} %get-tuple-element.91), channel_id=1, source_target_pairs={{0,8},{1,9},{2,10},{3,11},{4,12},{5,13},{6,14},{7,15},{8,0},{9,1},... | collective-permute-start | bytes 1769480 | tf_op jit(solution)/shard_map/ppermute | solution.py:259
  111.8 5.3 %copy-start.21 = (bf16[2,1152,128]{2,1,0:T(8,128)(2,1)S(1)}, bf16[2,1152,128]{2,1,0:T(8,128)(2,1)}, u32[]{:S(2)}) copy-start(bf16[2,1152,128]{2,1,0:T(8,128)(2,1)} %get-tuple-element.101) | copy-start | bytes 1769476
  111.8 6.8 %copy-start.3 = (bf16[2048,768]{1,0:T(8,128)(2,1)S(1)}, bf16[2048,768]{1,0:T(8,128)(2,1)}, u32[]{:S(2)}) copy-start(bf16[2048,768]{1,0:T(8,128)(2,1)} %copy-done.2) | copy-start | bytes 9437188
  117.1 20.2 %collective-permute-start.29 = (bf16[2048,768]{1,0:T(8,128)(2,1)}, bf16[2048,768]{1,0:T(8,128)(2,1)S(1)}, u32[]{:S(2)}, u32[]{:S(2)}) collective-permute-start(bf16[2048,768]{1,0:T(8,128)(2,1)} %mlp_out.1.refs_9_.refs_3_), channel_id=1, source_target_pairs={{0,4},{1,5},{2,6},{3,7},{4,0},{5,1},{6,2},{7,3},{8,12},{9,13},{10,... | collective-permute-start | bytes 9437192 | tf_op jit(solution)/shard_map/ppermute | solution.py:259
  117.1 27.9 %collective-permute-start.33 = (bf16[2,1152,128]{2,1,0:T(8,128)(2,1)S(1)}, bf16[2,1152,128]{2,1,0:T(8,128)(2,1)S(1)}, u32[]{:S(2)}, u32[]{:S(2)}) collective-permute-start(bf16[2,1152,128]{2,1,0:T(8,128)(2,1)S(1)} %copy-done.21), channel_id=1, source_target_pairs={{0,16},{1,17},{2,18},{3,19},{4,20},{5,21},{6,22},{7,23},{8,24},{9,... | collective-permute-start | bytes 1769480 | tf_op jit(solution)/shard_map/ppermute | solution.py:259
  120.5 6.9 %copy-start.17 = (bf16[2,1152,128]{2,1,0:T(8,128)(2,1)S(1)}, bf16[2,1152,128]{2,1,0:T(8,128)(2,1)}, u32[]{:S(2)}) copy-start(bf16[2,1152,128]{2,1,0:T(8,128)(2,1)} %get-tuple-element.92.refs_0_) | copy-start | bytes 1769476
  120.5 9.1 %copy-start.16 = (bf16[2,1152,128]{2,1,0:T(8,128)(2,1)S(1)}, bf16[2,1152,128]{2,1,0:T(8,128)(2,1)}, u32[]{:S(2)}) copy-start(bf16[2,1152,128]{2,1,0:T(8,128)(2,1)} %get-tuple-element.90.refs_0_) | copy-start | bytes 1769476
  129.0 16.0 %collective-permute-start.34 = (bf16[2,1152,128]{2,1,0:T(8,128)(2,1)S(1)}, bf16[2,1152,128]{2,1,0:T(8,128)(2,1)S(1)}, u32[]{:S(2)}, u32[]{:S(2)}) collective-permute-start(bf16[2,1152,128]{2,1,0:T(8,128)(2,1)S(1)} %aOm.1.refs_3_), channel_id=1, source_target_pairs={{0,8},{1,9},{2,10},{3,11},{4,12},{5,13},{6,14},{7,15},{8,0},{9,1},... | collective-permute-start | bytes 1769480 | tf_op jit(solution)/shard_map/ppermute | solution.py:259
  147.1 2.7 %copy-start.20 = (bf16[2,1152,128]{2,1,0:T(8,128)(2,1)S(1)}, bf16[2,1152,128]{2,1,0:T(8,128)(2,1)}, u32[]{:S(2)}) copy-start(bf16[2,1152,128]{2,1,0:T(8,128)(2,1)} %get-tuple-element.113) | copy-start | bytes 1769476
  149.6 49.1 %collective-permute-start.35 = (bf16[2048,768]{1,0:T(8,128)(2,1)}, bf16[2048,768]{1,0:T(8,128)(2,1)S(1)}, u32[]{:S(2)}, u32[]{:S(2)}) collective-permute-start(bf16[2048,768]{1,0:T(8,128)(2,1)} %hand_on.1), channel_id=1, source_target_pairs={{0,4},{1,5},{2,6},{3,7},{4,0},{5,1},{6,2},{7,3},{8,12},{9,13},{10,... | collective-permute-start | bytes 9437192 | tf_op jit(solution)/shard_map/ppermute | solution.py:259
  149.8 24.9 %collective-permute-start.41 = (bf16[2,1152,128]{2,1,0:T(8,128)(2,1)S(1)}, bf16[2,1152,128]{2,1,0:T(8,128)(2,1)S(1)}, u32[]{:S(2)}, u32[]{:S(2)}) collective-permute-start(bf16[2,1152,128]{2,1,0:T(8,128)(2,1)S(1)} %copy-done.20), channel_id=1, source_target_pairs={{0,8},{1,9},{2,10},{3,11},{4,12},{5,13},{6,14},{7,15},{8,0},{9,1},... | collective-permute-start | bytes 1769480 | tf_op jit(solution)/shard_map/ppermute | solution.py:259
  150.5 26.0 %collective-permute-start.42 = (bf16[2,1152,128]{2,1,0:T(8,128)(2,1)S(1)}, bf16[2,1152,128]{2,1,0:T(8,128)(2,1)S(1)}, u32[]{:S(2)}, u32[]{:S(2)}) collective-permute-start(bf16[2,1152,128]{2,1,0:T(8,128)(2,1)S(1)} %aEm.1.refs_2_), channel_id=1, source_target_pairs={{0,16},{1,17},{2,18},{3,19},{4,20},{5,21},{6,22},{7,23},{8,24},{9,... | collective-permute-start | bytes 1769480 | tf_op jit(solution)/shard_map/ppermute | solution.py:259
  151.7 27.1 %collective-permute-start.43 = (bf16[2,1152,128]{2,1,0:T(8,128)(2,1)S(1)}, bf16[2,1152,128]{2,1,0:T(8,128)(2,1)S(1)}, u32[]{:S(2)}, u32[]{:S(2)}) collective-permute-start(bf16[2,1152,128]{2,1,0:T(8,128)(2,1)S(1)} %som.1.refs_1_), channel_id=1, source_target_pairs={{0,1},{1,0},{2,3},{3,2},{4,5},{5,4},{6,7},{7,6},{8,9},{9,8},{10,11... | collective-permute-start | bytes 1769480 | tf_op jit(solution)/shard_map/ppermute | solution.py:259
  165.3 9.1 %collective-permute-start.37 = (bf16[2,608,128]{2,1,0:T(8,128)(2,1)S(1)}, bf16[2,608,128]{2,1,0:T(8,128)(2,1)S(1)}, u32[]{:S(2)}, u32[]{:S(2)}) collective-permute-start(bf16[2,608,128]{2,1,0:T(8,128)(2,1)S(1)} %get-tuple-element.105), channel_id=1, source_target_pairs={{0,16},{1,17},{2,18},{3,19},{4,20},{5,21},{6,22},{7,23},{8,24},{9,... | collective-permute-start | bytes 933896 | tf_op jit(solution)/shard_map/ppermute | solution.py:259
  174.3 8.2 %collective-permute-start.36 = (bf16[2,608,128]{2,1,0:T(8,128)(2,1)S(1)}, bf16[2,608,128]{2,1,0:T(8,128)(2,1)S(1)}, u32[]{:S(2)}, u32[]{:S(2)}) collective-permute-start(bf16[2,608,128]{2,1,0:T(8,128)(2,1)S(1)} %get-tuple-element.103), channel_id=1, source_target_pairs={{0,16},{1,17},{2,18},{3,19},{4,20},{5,21},{6,22},{7,23},{8,24},{9,... | collective-permute-start | bytes 933896 | tf_op jit(solution)/shard_map/ppermute | solution.py:259
  174.8 10.4 %collective-permute-start.38 = (bf16[2,608,128]{2,1,0:T(8,128)(2,1)S(1)}, bf16[2,608,128]{2,1,0:T(8,128)(2,1)S(1)}, u32[]{:S(2)}, u32[]{:S(2)}) collective-permute-start(bf16[2,608,128]{2,1,0:T(8,128)(2,1)S(1)} %aOa.1), channel_id=1, source_target_pairs={{0,8},{1,9},{2,10},{3,11},{4,12},{5,13},{6,14},{7,15},{8,0},{9,1},... | collective-permute-start | bytes 933896 | tf_op jit(solution)/shard_map/ppermute | solution.py:259
  176.5 21.7 %collective-permute-start.40 = (bf16[2,608,128]{2,1,0:T(8,128)(2,1)S(1)}, bf16[2,608,128]{2,1,0:T(8,128)(2,1)S(1)}, u32[]{:S(2)}, u32[]{:S(2)}) collective-permute-start(bf16[2,608,128]{2,1,0:T(8,128)(2,1)S(1)} %get-tuple-element.111), channel_id=1, source_target_pairs={{0,8},{1,9},{2,10},{3,11},{4,12},{5,13},{6,14},{7,15},{8,0},{9,1},... | collective-permute-start | bytes 933896 | tf_op jit(solution)/shard_map/ppermute | solution.py:259
  179.1 19.5 %collective-permute-start.47 = (bf16[1152,128]{1,0:T(8,128)(2,1)S(1)}, bf16[1152,128]{1,0:T(8,128)(2,1)S(1)}, u32[]{:S(2)}, u32[]{:S(2)}) collective-permute-start(bf16[1152,128]{1,0:T(8,128)(2,1)S(1)} %get-tuple-element.114.refs_2_), channel_id=1, source_target_pairs={{0,2},{1,3},{2,0},{3,1},{4,6},{5,7},{6,4},{7,5},{8,10},{9,11},{10,... | collective-permute-start | bytes 884744 | tf_op jit(solution)/shard_map/ppermute | solution.py:259
  182.5 22.7 %collective-permute-start.39 = (bf16[2,608,128]{2,1,0:T(8,128)(2,1)S(1)}, bf16[2,608,128]{2,1,0:T(8,128)(2,1)S(1)}, u32[]{:S(2)}, u32[]{:S(2)}) collective-permute-start(bf16[2,608,128]{2,1,0:T(8,128)(2,1)S(1)} %get-tuple-element.109), channel_id=1, source_target_pairs={{0,8},{1,9},{2,10},{3,11},{4,12},{5,13},{6,14},{7,15},{8,0},{9,1},... | collective-permute-start | bytes 933896 | tf_op jit(solution)/shard_map/ppermute | solution.py:259
  185.2 20.0 %collective-permute-start.45 = (bf16[2,608,128]{2,1,0:T(8,128)(2,1)S(1)}, bf16[2,608,128]{2,1,0:T(8,128)(2,1)S(1)}, u32[]{:S(2)}, u32[]{:S(2)}) collective-permute-start(bf16[2,608,128]{2,1,0:T(8,128)(2,1)S(1)} %soa.1.refs_9_), channel_id=1, source_target_pairs={{0,1},{1,0},{2,3},{3,2},{4,5},{5,4},{6,7},{7,6},{8,9},{9,8},{10,11... | collective-permute-start | bytes 933896 | tf_op jit(solution)/shard_map/ppermute | solution.py:259
  198.2 7.0 %collective-permute-start.44 = (bf16[2,608,128]{2,1,0:T(8,128)(2,1)S(1)}, bf16[2,608,128]{2,1,0:T(8,128)(2,1)S(1)}, u32[]{:S(2)}, u32[]{:S(2)}) collective-permute-start(bf16[2,608,128]{2,1,0:T(8,128)(2,1)S(1)} %aEa.1), channel_id=1, source_target_pairs={{0,16},{1,17},{2,18},{3,19},{4,20},{5,21},{6,22},{7,23},{8,24},{9,... | collective-permute-start | bytes 933896 | tf_op jit(solution)/shard_map/ppermute | solution.py:259
  198.6 9.2 %collective-permute-start.48 = (f32[576,128]{1,0:T(8,128)S(1)}, f32[576,128]{1,0:T(8,128)S(1)}, u32[]{:S(2)}, u32[]{:S(2)}) collective-permute-start(f32[576,128]{1,0:T(8,128)S(1)} %get-tuple-element.119.refs_5_), channel_id=1, source_target_pairs={{0,4},{1,5},{2,6},{3,7},{4,0},{5,1},{6,2},{7,3},{8,12},{9,13},{10,... | collective-permute-start | bytes 884744 | tf_op jit(solution)/shard_map/ppermute | solution.py:259
  205.2 2.7 %copy-start.7 = (f32[147456]{0:T(1024)S(1)}, f32[147456]{0:T(1024)}, u32[]{:S(2)}) copy-start(f32[147456]{0:T(1024)} %param.20) | copy-start | bytes 1769476
  206.9 7.4 %collective-permute-start.46 = (bf16[608,128]{1,0:T(8,128)(2,1)S(1)}, bf16[608,128]{1,0:T(8,128)(2,1)S(1)}, u32[]{:S(2)}, u32[]{:S(2)}) collective-permute-start(bf16[608,128]{1,0:T(8,128)(2,1)S(1)} %get-tuple-element.116), channel_id=1, source_target_pairs={{0,2},{1,3},{2,0},{3,1},{4,6},{5,7},{6,4},{7,5},{8,10},{9,11},{10,... | collective-permute-start | bytes 466952 | tf_op jit(solution)/shard_map/ppermute | solution.py:259
  207.9 8.1 %copy-start.18 = (f32[288]{0:T(512)S(1)}, f32[288]{0:T(512)}, u32[]{:S(2)}) copy-start(f32[288]{0:T(512)} %param.23) | copy-start | bytes 3460
  207.9 8.1 %copy-start.19 = (f32[288]{0:T(512)S(1)}, f32[288]{0:T(512)}, u32[]{:S(2)}) copy-start(f32[288]{0:T(512)} %param.22) | copy-start | bytes 3460
  207.9 9.0 %copy-start.1 = (f32[3,128]{1,0:T(4,128)S(1)}, f32[3,128]{1,0:T(4,128)}, u32[]{:S(2)}) copy-start(f32[3,128]{1,0:T(4,128)} %pad_bitcast_fusion.2.refs_3_.refs_7_) | copy-start | bytes 4612
  207.9 9.0 %copy-start.8 = (f32[73728]{0:T(1024)S(1)}, f32[73728]{0:T(1024)}, u32[]{:S(2)}) copy-start(f32[73728]{0:T(1024)} %param.15) | copy-start | bytes 884740
  207.9 8.9 %copy-start.9 = (f32[73728]{0:T(1024)S(1)}, f32[73728]{0:T(1024)}, u32[]{:S(2)}) copy-start(f32[73728]{0:T(1024)} %param.16) | copy-start | bytes 884740
  207.9 8.9 %copy-start.10 = (f32[73728]{0:T(1024)S(1)}, f32[73728]{0:T(1024)}, u32[]{:S(2)}) copy-start(f32[73728]{0:T(1024)} %param.17) | copy-start | bytes 884740
  215.4 1.5 collective-permute-start.49
  215.5 1.4 collective-permute-start.50
  (9 other events, 16.2 us)

commit v4 on v3

--- a/solution.py
+++ b/solution.py
@@ -901,13 +901,13 @@
     "z3m": ("z2m", TO_Z[1]),
     "x0m": ("pm", TO_X),
     "y0m": ("pm", TO_Y),
-    "x1m": ("z1m", TO_X),
-    "y1m": ("z1m", TO_Y),
+    "x1m": ("h1m", TO_X),
+    "y1m": ("h1m", TO_Y),
     "x2m": ("z2m", TO_X),
     "y2m": ("z2m", TO_Y),
     "x3m": ("z3m", TO_X),
     "y3m": ("z3m", TO_Y),
-    "d0m": ("y0m", TO_X),
+    "d0m": ("h0m", TO_X),
     "d1m": ("d0m", TO_Z[1]),
     "d2m": ("x2m", TO_Y),
     "d3m": ("d2m", TO_Z[1]),
@@ -931,12 +931,15 @@
 SENDS["gs"] = ("other_small", TO_CORE)
 PAIR_NAMES = ("E{}_grad", "O{}_grad", "xE{}_grad", "xO{}_grad", "yE{}_grad", "yO{}_grad", "dE{}_grad", "dO{}_grad")
 
+IN_HBM = ("first_back", "out_part", "grad_context", "output")
 AFTER = {
     "pa": ("cs", "cc", "cv"),
     "pm": ("pa",),
     "Ea": ("meta",),
     "pm2": ("Ea",),
-    "fwd": ("x1m", "y1m", "x0m", "y0m"),
+    "h1m": ("xOa",),
+    "h0m": ("xOa",),
+    "fwd": ("x0m", "y0m", "z2m"),
     "there": ("x3m", "y3m", "d1m", "d2m", "d3m", "x2m", "d0m", "vecs"),
     "mlp": ("there",),
     "bw1": ("out_part",),
@@ -944,7 +947,7 @@
     "aOm": ("grad_context",),
     "bw2": ("aEm", "aOm"),
     "bw3": ("ot",),
-    "som": ("first_back",),
+    "som": ("first_back", "qEm", "pEm"),
     "hand": ("som",),
     "aEa": ("farm",),
     "fin": ("soa",),
@@ -954,7 +957,7 @@
 
 ORDER = (
     "+cv", "+cs", "+cc", "=cut", "+sa", "+sm", "=pack", "=pa", "+z2a", "=pm", "+z1m", "+x0m", "+y0m",
-    "=Ea", "=pm2", "+z2m", "+zOa", "+xEa", "+yEa", "+x1m", "+y1m", "+dEa", "+yOa", "+z3m", "+xOa", "+y2m", "+x2m",
+    "=Ea", "=pm2", "+z2m", "+zOa", "+xEa", "+yEa", "+dEa", "+yOa", "+z3m", "+xOa", "=h1m", "=h0m", "+x1m", "+y1m", "+y2m", "+x2m",
     "+d0m", "+dOa", "+y3m", "+x3m", "+d2m", "=fwd", "+pt", "+d1m", "+d3m", "=there",
     "=mlp", "+rEm", "+rOm", "+bk", "=mout", "+ot", "=bw1", "=aEm", "=aOm", "+qOm", "+qEm", "+pEm", "+pOm", "=bw2",
     "=bw3", "+rEa", "+rOa", "=som", "=hand", "+fb", "+wOm", "=szm", "+w2m", "=aEa", "=aOa", "+qOa", "+qEa", "+pEa", "+pOa",
@@ -1086,7 +1089,7 @@
     pair_a, pair_m = (2, 608, ROW), (2, 1152, ROW)
 
     def after(name):
-        return tuple(v[n] for n in AFTER.get(name, ()))
+        return tuple(in_hbm(v[n]) if n in IN_HBM else v[n] for n in AFTER.get(name, ()))
 
     v = {"visible": visible, "samples": samples, "cotangent": cotangent}
 
@@ -1130,6 +1133,12 @@
             attn_forward, [D], 8, [(3 * D // 2, bf16, rows), (D // 2, bf16, rows), (D, bf16, rows)], outs,
             [pltpu.VMEM((8, 16, ROW), f32)], 24, "attn_forward", after("fwd"),
         )(v["meta"], idx, *hbm("x"), v["Ea"], *(v[n] for n in ("zOa", "xEa", "xOa", "yEa", "yOa", "dEa", "dOa")))
+
+    def hold_1():
+        v["h1m"] = at_once(lay_out, 0, [array(shape_m)], [], 8, "hold_first", after("h1m"))(v["z1m"])[0]
+
+    def hold_0():
+        v["h0m"] = at_once(lay_out, 0, [array(shape_m)], [], 8, "hold_own", after("h0m"))(v["y0m"])[0]
 
     def there():
         v["there"] = at_once(nothing, 1, [array((8, ROW), f32)], [], 4, "all_there", after("there"))(idx)[0]
@@ -1228,15 +1237,23 @@
         )(idx, lanes(master_attn), lanes(first_attn), lanes(second_attn), v["owna"], v["othera"], v["ga"],
           three_rows(master_small), three_rows(first_small), three_rows(second_small), v["own_small"], v["gs"])
 
-    works = {"cut": cut, "pa": piece_a, "Ea": even_a, "pm": piece_m, "pm2": again_m, "pack": pack, "there": there, "fwd": forward, "mlp": mlp, "mout": out_rows,
+    works = {"cut": cut, "pa": piece_a, "Ea": even_a, "pm": piece_m, "pm2": again_m, "pack": pack, "there": there, "h1m": hold_1, "h0m": hold_0, "fwd": forward, "mlp": mlp, "mout": out_rows,
              "bw1": backward_1, "bw2": backward_2, "bw3": backward_3, "hand": again_back, "fin": finish, "om": optimize_m, "oa": optimize_a, **adds("m"), **adds("a")}
-    for step in ORDER:
-        kind, name = step[0], step[1:]
-        if kind == "+":
-            source, pairs = SENDS[name]
-            v[name] = send(v[source], pairs)
-        elif kind == "=":
-            works[name]()
+    todo = list(ORDER)
+    while todo:
+        left = []
+        for step in todo:
+            kind, name = step[0], step[1:]
+            try:
+                if kind == "+":
+                    source, pairs = SENDS[name]
+                    v[name] = send(v[source], pairs)
+                else:
+                    works[name]()
+            except KeyError:
+                left.append(step)
+        assert len(left) < len(todo), left
+        todo = left
 
     new_mlp, new_attn, output, grad_samples = v["new_mlp"], v["new_attn"], v["output"], v["grad_samples"]
     new_small = [a.reshape(-1)[:288] for a in new_attn[3:]]

time: 220 us -> 210 us (0.955); the launches traced: 219 us -> 211 us
  local copies, waits for them, and re-layouts: 11.5 us -> 4.17 us
  starting transfers between devices: 66.1 us -> 59.1 us
  waiting for transfers between devices: 63.8 us -> 70.4 us
    unnamed x44 -> x34, local copies, waits for them, and re-layouts: 10.1 us -> 2.82 us
    ppermute x51, starting transfers between devices: 66.1 us -> 59.1 us  [send(): return lax.ppermute(value, AXES, pairs)]
    ppermute x51, waiting for transfers between devices: 63.8 us -> 70.4 us  [send(): return lax.ppermute(value, AXES, pairs)]
    pallas_call x19 -> x21, Pallas kernels: 13.6 us -> 13.7 us  [called(): pl.pallas_call(kernel, in_specs=[SMEM] * scalars + blocks + [ANY] * len(a...]
  transfers between devices with their start and end apart: 51 -> 51, of which waited for: 15 -> 19; matrix products, arithmetic and copies ran while one was open for 1% -> 1% of each run, Pallas kernels for 25% -> 26%
where the time goes in v4:
time: 210 us; the launch traced here: 211 us
  Pallas kernels  76.5 us (36%)
  waiting for transfers between devices  70.4 us (34%)
  starting transfers between devices  59.1 us (28%)
  local copies, waits for them, and re-layouts  4.17 us (2%)
    ppermute x51, waiting for transfers between devices, send(): return lax.ppermute(value, AXES, pairs)  70.4 us
    pallas_call x8, Pallas kernels, called(): pl.pallas_call(kernel, grid=(1,), in_specs=[SMEM, SMEM] + [ANY] * n_in +...  62.8 us
    ppermute x51, starting transfers between devices, send(): return lax.ppermute(value, AXES, pairs)  59.1 us
    pallas_call x21, Pallas kernels, called(): pl.pallas_call(kernel, in_specs=[SMEM] * scalars + blocks + [ANY] * len(a...  13.7 us
  transfers between devices with their start and end apart: 51, of which 19 were waited for; matrix products, arithmetic and copies ran while one was open for 1% of the time, Pallas kernels for 26%

profile of v4, /device:TPU:0, one launch (start us, length us, event | category | flops | bytes accessed | tf_op | source)
XLA Modules:
  0.0 211.1 jit_solution(11689380512384016973)
XLA Ops:
  1.3 1.3 pad_bitcast_fusion.2.refs_3_.refs_7_
  2.6 1.3 cut_masters.1
  4.9 1.6 collective-permute-done.refs_2_.refs_6_
  7.2 4.0 %collective-permute-start.4 = (bf16[608,128]{1,0:T(8,128)(2,1)S(1)}, bf16[608,128]{1,0:T(8,128)(2,1)S(1)}, u32[]{:S(2)}, u32[]{:S(2)}) collective-permute-start(bf16[608,128]{1,0:T(8,128)(2,1)S(1)} %piece_attn.1.refs_0_.refs_4_), channel_id=1, source_target_pairs={{0,2},{1,3},{2,0},{3,1},{4,6},{5,7},{6,4},{7,5},{8,10},{9,11},{10,... | collective-permute-start | bytes 466952 | tf_op jit(solution)/shard_map/ppermute | solution.py:259
  11.3 5.4 %pack_rows.1 = (bf16[2048,768]{1,0:T(8,128)(2,1)}, bf16[2048,768]{1,0:T(8,128)(2,1)}, s32[64]{0:T(128)S(1)}) custom-call(s32[5]{0:T(128)S(1)} %stack.23.refs_0_.idx, s32[8]{0:T(128)S(1)} %copy-done.9, s32[8]{0:T(128)S(1)} %collective-permute-done.refs_2_.refs_6_, bf16[8,128,768]{2,1,0:T(8,128)(2,1)} %refs_3_.1, ...), custom_call_target="tpu_custom_call" | custom-call | flops 6000000000 | bytes 1 | tf_op jit(solution)/shard_map/pack_rows/pallas_call | solution.py:1047
  16.7 2.2 %collective-permute-done.4.refs_1_ = bf16[608,128]{1,0:T(8,128)(2,1)S(1)} collective-permute-done((bf16[608,128]{1,0:T(8,128)(2,1)S(1)}, bf16[608,128]{1,0:T(8,128)(2,1)S(1)}, u32[]{:S(2)}, u32[]{:S(2)}) %collective-permute-start.4) | collective-permute-done | bytes 155680 | tf_op jit(solution)/shard_map/ppermute | solution.py:259
  18.9 0.8 collective-permute-start.5
  20.3 1.6 collective-permute-start.13
  21.9 1.5 collective-permute-start.14
  23.4 3.4 %collective-permute-start.15 = (bf16[1152,128]{1,0:T(8,128)(2,1)S(1)}, bf16[1152,128]{1,0:T(8,128)(2,1)S(1)}, u32[]{:S(2)}, u32[]{:S(2)}) collective-permute-start(bf16[1152,128]{1,0:T(8,128)(2,1)S(1)} %piece_again.1), channel_id=1, source_target_pairs={{0,2},{1,3},{2,0},{3,1},{4,6},{5,7},{6,4},{7,5},{8,10},{9,11},{10,... | collective-permute-start | bytes 884744 | tf_op jit(solution)/shard_map/ppermute | solution.py:259
  26.9 2.2 %collective-permute-done.13.refs_9_.refs_10_ = bf16[1152,128]{1,0:T(8,128)(2,1)S(1)} collective-permute-done((bf16[1152,128]{1,0:T(8,128)(2,1)S(1)}, bf16[1152,128]{1,0:T(8,128)(2,1)S(1)}, u32[]{:S(2)}, u32[]{:S(2)}) %collective-permute-start.13) | collective-permute-done | bytes 294944 | tf_op jit(solution)/shard_map/ppermute | solution.py:259
  29.0 1.5 collective-permute-start.8
  30.6 1.5 collective-permute-start.6
  32.1 2.8 %collective-permute-start.7 = (bf16[2,608,128]{2,1,0:T(8,128)(2,1)S(1)}, bf16[2,608,128]{2,1,0:T(8,128)(2,1)S(1)}, u32[]{:S(2)}, u32[]{:S(2)}) collective-permute-start(bf16[2,608,128]{2,1,0:T(8,128)(2,1)S(1)} %collective-permute-done.5.refs_2_), channel_id=1, source_target_pairs={{0,8},{1,9},{2,10},{3,11},{4,12},{5,13},{6,14},{7,15},{8,0},{9,1},... | collective-permute-start | bytes 933896 | tf_op jit(solution)/shard_map/ppermute | solution.py:259
  34.9 4.8 %collective-permute-done.15.refs_11_.refs_8_ = bf16[1152,128]{1,0:T(8,128)(2,1)S(1)} collective-permute-done((bf16[1152,128]{1,0:T(8,128)(2,1)S(1)}, bf16[1152,128]{1,0:T(8,128)(2,1)S(1)}, u32[]{:S(2)}, u32[]{:S(2)}) %collective-permute-start.15) | collective-permute-done | bytes 294944 | tf_op jit(solution)/shard_map/ppermute | solution.py:259
  40.5 1.2 collective-permute-start.18
  41.7 1.5 collective-permute-start.9
  43.2 1.5 collective-permute-start.10
  44.7 2.8 %collective-permute-done.7.refs_4_.refs_1_ = bf16[2,608,128]{2,1,0:T(8,128)(2,1)S(1)} collective-permute-done((bf16[2,608,128]{2,1,0:T(8,128)(2,1)S(1)}, bf16[2,608,128]{2,1,0:T(8,128)(2,1)S(1)}, u32[]{:S(2)}, u32[]{:S(2)}) %collective-permute-start.7) | collective-permute-done | bytes 311328 | tf_op jit(solution)/shard_map/ppermute | solution.py:259
  47.5 1.2 collective-permute-start.11
  48.8 5.1 %collective-permute-done.20.refs_6_.refs_12_ = bf16[1152,128]{1,0:T(8,128)(2,1)S(1)} collective-permute-done((bf16[1152,128]{1,0:T(8,128)(2,1)S(1)}, bf16[1152,128]{1,0:T(8,128)(2,1)S(1)}, u32[]{:S(2)}, u32[]{:S(2)}) %collective-permute-start.20) | collective-permute-done | bytes 294944 | tf_op jit(solution)/shard_map/ppermute | solution.py:259
  53.8 1.2 collective-permute-start.27
  55.1 0.8 collective-permute-start.25
  55.9 4.6 %collective-permute-done.10.refs_7_ = bf16[2,608,128]{2,1,0:T(8,128)(2,1)S(1)} collective-permute-done((bf16[2,608,128]{2,1,0:T(8,128)(2,1)S(1)}, bf16[2,608,128]{2,1,0:T(8,128)(2,1)S(1)}, u32[]{:S(2)}, u32[]{:S(2)}) %collective-permute-start.10) | collective-permute-done | bytes 311328 | tf_op jit(solution)/shard_map/ppermute | solution.py:259
  60.5 1.2 collective-permute-start.23
  61.7 0.8 collective-permute-start.21
  62.5 2.5 %collective-permute-done.27.refs_4_.refs_20_ = bf16[1152,128]{1,0:T(8,128)(2,1)S(1)} collective-permute-done((bf16[1152,128]{1,0:T(8,128)(2,1)S(1)}, bf16[1152,128]{1,0:T(8,128)(2,1)S(1)}, u32[]{:S(2)}, u32[]{:S(2)}) %collective-permute-start.27) | collective-permute-done | bytes 294944 | tf_op jit(solution)/shard_map/ppermute | solution.py:259
  65.0 1.5 collective-permute-start.24
  66.8 0.6 collective-permute-start.28
  67.4 1.4 collective-permute-start.26
  68.9 8.9 %attn_forward.1 = (bf16[2048,1152]{1,0:T(8,128)(2,1)}, bf16[2048,384]{1,0:T(8,128)(2,1)}, bf16[2048,768]{1,0:T(8,128)(2,1)}, bf16[768,1152]{1,0:T(8,128)(2,1)}, ...) custom-call(s32[64]{0:T(128)S(1)} %get-tuple-element.72.refs_2_.meta, ...), custom_call_target="tpu_custom_call" | custom-call | flops 11000000512 | bytes 1 | tf_op jit(solution)/shard_map/attn_forward/pallas_call | solution.py:1023
  77.7 1.5 collective-permute-start.19
  80.3 4.1 %collective-permute-done.19.refs_11_ = bf16[1152,128]{1,0:T(8,128)(2,1)S(1)} collective-permute-done((bf16[1152,128]{1,0:T(8,128)(2,1)S(1)}, bf16[1152,128]{1,0:T(8,128)(2,1)S(1)}, u32[]{:S(2)}, u32[]{:S(2)}) %collective-permute-start.19) | collective-permute-done | bytes 294944 | tf_op jit(solution)/shard_map/ppermute | solution.py:259
  84.5 1.5 collective-permute-done.22.refs_15_
  86.0 1.7 copy-done.1
  87.6 18.0 %mlp_both.1 = (bf16[2048,1536]{1,0:T(8,128)(2,1)}, bf16[2048,768]{1,0:T(8,128)(2,1)}, bf16[1536,768]{1,0:T(8,128)(2,1)}, f32[8,768]{1,0:T(8,128)S(1)}, f32[1,153...) custom-call(s32[64]{0:T(128)S(1)} %get-tuple-element.72.refs_2_.meta, ...), custom_call_target="tpu_custom_call" | custom-call | flops 23000000512 | bytes 1 | tf_op jit(solution)/shard_map/mlp_both/pallas_call | solution.py:1023
  105.6 1.3 collective-permute-start.32
  107.5 5.5 %mlp_out.1.refs_9_.refs_3_ = bf16[2048,768]{1,0:T(8,128)(2,1)} custom-call(s32[64]{0:T(128)S(1)} %get-tuple-element.72.refs_2_.meta, s32[5]{0:T(128)S(1)} %stack.23.refs_0_.idx, bf16[2048,1536]{1,0:T(8,128)(2,1)} %get-tuple-element.82.refs_0_, bf16[1536,768]{1,0:T(8,128)(2,1)} %get-tuple-element.83.refs_1_), custom_call_target="tpu_custom_call" | custom-call | flops 20000000000 | bytes 1 | tf_op jit(solution)/shard_map/mlp_out/pallas_call | solution.py:1023
  113.0 1.2 collective-permute-start.33
  114.2 1.0 collective-permute-start.36
  115.2 6.9 %middle_backward.1 = (f32[2048,768]{1,0:T(8,128)}, bf16[2048,384]{1,0:T(8,128)(2,1)}, f32[384,768]{1,0:T(8,128)}, f32[8,768]{1,0:T(8,128)S(1)}) custom-call(s32[64]{0:T(128)S(1)} %get-tuple-element.72.refs_2_.meta, s32[5]{0:T(128)S(1)} %stack.23.refs_0_.idx, bf16[2048,768]{1,0:T(8,128)(2,1)} %get-tuple-element.73.refs_0_, ...), custom_call_target="tpu_custom_call" | custom-call | flops 8000000000 | bytes 1 | tf_op jit(solution)/shard_map/middle_backward/pallas_call | solution.py:1023
  122.3 1.1 collective-permute-start.34
  123.5 1.2 collective-permute-start.35
  124.7 6.9 %heads_backward.1.refs_1_ = bf16[2048,1152]{1,0:T(8,128)(2,1)} custom-call(s32[64]{0:T(128)S(1)} %get-tuple-element.72.refs_2_.meta, s32[5]{0:T(128)S(1)} %stack.23.refs_0_.idx, bf16[2048,1152]{1,0:T(8,128)(2,1)} %get-tuple-element.88.refs_0_, bf16[2048,384]{1,0:T(8,128)(2,1)} %get-tuple-element.89.refs_2_.refs_1_, bf16[2,1152,128]{2,1,0:T(8,128)(2,1)S(1)} %aEm.1.refs_2_, ...), custom_call_target="tpu_custom_call" | custom-call | flops 24999999488 | bytes 1 | tf_op jit(solution)/shard_map/heads_backward/pallas_call | solution.py:1023
  131.6 7.6 %first_backward.1 = (bf16[2048,768]{1,0:T(8,128)(2,1)}, bf16[2,608,128]{2,1,0:T(8,128)(2,1)S(1)}, bf16[2,608,128]{2,1,0:T(8,128)(2,1)S(1)}, bf16[2,608,128]{2,1,...) custom-call(s32[64]{0:T(128)S(1)} %get-tuple-element.72.refs_2_.meta, ...), custom_call_target="tpu_custom_call" | custom-call | flops 24999999488 | bytes 1 | tf_op jit(solution)/shard_map/first_backward/pallas_call | solution.py:1023
  139.3 8.4 %collective-permute-done.34.refs_2_ = bf16[2,1152,128]{2,1,0:T(8,128)(2,1)S(1)} collective-permute-done((bf16[2,1152,128]{2,1,0:T(8,128)(2,1)S(1)}, bf16[2,1152,128]{2,1,0:T(8,128)(2,1)S(1)}, u32[]{:S(2)}, u32[]{:S(2)}) %collective-permute-start.34) | collective-permute-done | bytes 589856 | tf_op jit(solution)/shard_map/ppermute | solution.py:259
  148.0 2.5 %hand_on.1 = bf16[2048,768]{1,0:T(8,128)(2,1)} custom-call(s32[64]{0:T(128)S(1)} %get-tuple-element.72.refs_2_.meta, s32[5]{0:T(128)S(1)} %stack.23.refs_0_.idx, bf16[2048,768]{1,0:T(8,128)(2,1)} %get-tuple-element.99.refs_3_.refs_0_.refs_6_, bf16[2,1152,128]{2,1,0:T(8,128)(2,1)S(1)} %som.1.refs_1_), custom_call_target="tpu_custom_call" | custom-call | flops 1000000000 | bytes 1 | tf_op jit(solution)/shard_map/hand_on/pallas_call | solution.py:1023
  151.0 0.9 collective-permute-start.39
  151.9 1.2 collective-permute-start.38
  153.0 8.2 %collective-permute-done.39.refs_1_ = bf16[2,608,128]{2,1,0:T(8,128)(2,1)S(1)} collective-permute-done((bf16[2,608,128]{2,1,0:T(8,128)(2,1)S(1)}, bf16[2,608,128]{2,1,0:T(8,128)(2,1)S(1)}, u32[]{:S(2)}, u32[]{:S(2)}) %collective-permute-start.39) | collective-permute-done | bytes 311328 | tf_op jit(solution)/shard_map/ppermute | solution.py:259
  161.3 0.7 collective-permute-start.40
  162.0 1.4 collective-permute-start.42
  163.4 2.8 %collective-permute-done.43.refs_3_ = bf16[2,1152,128]{2,1,0:T(8,128)(2,1)S(1)} collective-permute-done((bf16[2,1152,128]{2,1,0:T(8,128)(2,1)S(1)}, bf16[2,1152,128]{2,1,0:T(8,128)(2,1)S(1)}, u32[]{:S(2)}, u32[]{:S(2)}) %collective-permute-start.43) | collective-permute-done | bytes 589856 | tf_op jit(solution)/shard_map/ppermute | solution.py:259
  166.5 9.5 %collective-permute-start.47 = (bf16[1152,128]{1,0:T(8,128)(2,1)S(1)}, bf16[1152,128]{1,0:T(8,128)(2,1)S(1)}, u32[]{:S(2)}, u32[]{:S(2)}) collective-permute-start(bf16[1152,128]{1,0:T(8,128)(2,1)S(1)} %get-tuple-element.114.refs_2_), channel_id=1, source_target_pairs={{0,2},{1,3},{2,0},{3,1},{4,6},{5,7},{6,4},{7,5},{8,10},{9,11},{10,... | collective-permute-start | bytes 884744 | tf_op jit(solution)/shard_map/ppermute | solution.py:259
  176.2 1.8 collective-permute-start.45
  178.1 0.6 collective-permute-start.44
  178.7 10.6 %collective-permute-done.47.refs_1_ = bf16[1152,128]{1,0:T(8,128)(2,1)S(1)} collective-permute-done((bf16[1152,128]{1,0:T(8,128)(2,1)S(1)}, bf16[1152,128]{1,0:T(8,128)(2,1)S(1)}, u32[]{:S(2)}, u32[]{:S(2)}) %collective-permute-start.47) | collective-permute-done | bytes 294944 | tf_op jit(solution)/shard_map/ppermute | solution.py:259
  189.4 6.5 %finish_rows.1 = (bf16[8,128,768]{2,1,0:T(8,128)(2,1)}, bf16[8,128,768]{2,1,0:T(8,128)(2,1)}) custom-call(s32[64]{0:T(128)S(1)} %get-tuple-element.72.refs_2_.meta, s32[5]{0:T(128)S(1)} %stack.23.refs_0_.idx, bf16[2048,768]{1,0:T(8,128)(2,1)} %get-tuple-element.73.refs_0_, bf16[2048,768]{1,0:T(8,128)(2,1)} %get-tuple-element.78.refs_1_, ...), custom_call_target="tpu_custom_call" | custom-call | flops 8000000000 | bytes 1 | tf_op jit(solution)/shard_map/finish_rows/pallas_call | solution.py:1023
  196.1 1.2 collective-permute-start.46
  197.4 2.1 step_mlp.1
  199.5 7.3 %collective-permute-done.46.refs_1_ = bf16[608,128]{1,0:T(8,128)(2,1)S(1)} collective-permute-done((bf16[608,128]{1,0:T(8,128)(2,1)S(1)}, bf16[608,128]{1,0:T(8,128)(2,1)S(1)}, u32[]{:S(2)}, u32[]{:S(2)}) %collective-permute-start.46) | collective-permute-done | bytes 155680 | tf_op jit(solution)/shard_map/ppermute | solution.py:259
  206.8 1.1 copy-done.10
  208.5 0.9 collective-permute-done.50.refs_11_
  209.4 1.8 step_attn.1
  (104 shorter events, 8.5 us)
Async XLA Ops:
  0.6 3.8 %copy-start.9 = (s32[8]{0:T(128)S(1)}, s32[8]{0:T(128)}, u32[]{:S(2)}) copy-start(s32[8]{0:T(128)} %refs_1_.1) | copy-start | bytes 100
  0.7 5.9 %collective-permute-start.1 = (bf16[8,128,768]{2,1,0:T(8,128)(2,1)}, bf16[8,128,768]{2,1,0:T(8,128)(2,1)S(1)}, u32[]{:S(2)}, u32[]{:S(2)}) collective-permute-start(bf16[8,128,768]{2,1,0:T(8,128)(2,1)} %refs_3_.1), channel_id=1, source_target_pairs={{0,4},{1,5},{2,6},{3,7},{4,0},{5,1},{6,2},{7,3},{8,12},{9,13},{10,... | collective-permute-start | bytes 4718600 | tf_op jit(solution)/shard_map/ppermute | solution.py:259
  1.2 5.5 %collective-permute-start.2 = (bf16[8,128,768]{2,1,0:T(8,128)(2,1)}, bf16[8,128,768]{2,1,0:T(8,128)(2,1)S(1)}, u32[]{:S(2)}, u32[]{:S(2)}) collective-permute-start(bf16[8,128,768]{2,1,0:T(8,128)(2,1)} %refs_5_.1), channel_id=1, source_target_pairs={{0,4},{1,5},{2,6},{3,7},{4,0},{5,1},{6,2},{7,3},{8,12},{9,13},{10,... | collective-permute-start | bytes 4718600 | tf_op jit(solution)/shard_map/ppermute | solution.py:259
  3.9 2.6 %collective-permute-start.3 = (bf16[304,128]{1,0:T(8,128)(2,1)S(1)}, bf16[304,128]{1,0:T(8,128)(2,1)S(1)}, u32[]{:S(2)}, u32[]{:S(2)}) collective-permute-start(bf16[304,128]{1,0:T(8,128)(2,1)S(1)} %get-tuple-element.75.refs_2_), channel_id=1, source_target_pairs={{0,4},{1,5},{2,6},{3,7},{4,0},{5,1},{6,2},{7,3},{8,12},{9,13},{10,... | collective-permute-start | bytes 233480 | tf_op jit(solution)/shard_map/ppermute | solution.py:259
  4.4 2.1 %collective-permute-start = (s32[8]{0:T(128)S(1)}, s32[8]{0:T(128)S(1)}, u32[]{:S(2)}, u32[]{:S(2)}) collective-permute-start(s32[8]{0:T(128)S(1)} %copy-done.9), channel_id=1, source_target_pairs={{0,4},{1,5},{2,6},{3,7},{4,0},{5,1},{6,2},{7,3},{8,12},{9,13},{10,... | collective-permute-start | bytes 104 | tf_op jit(solution)/shard_map/ppermute | solution.py:259
  4.5 15.2 %collective-permute-start.12 = (bf16[576,128]{1,0:T(8,128)(2,1)S(1)}, bf16[576,128]{1,0:T(8,128)(2,1)S(1)}, u32[]{:S(2)}, u32[]{:S(2)}) collective-permute-start(bf16[576,128]{1,0:T(8,128)(2,1)S(1)} %get-tuple-element.77.refs_2_), channel_id=1, source_target_pairs={{0,4},{1,5},{2,6},{3,7},{4,0},{5,1},{6,2},{7,3},{8,12},{9,13},{10,... | collective-permute-start | bytes 442376 | tf_op jit(solution)/shard_map/ppermute | solution.py:259
  7.2 11.7 %collective-permute-start.4 = (bf16[608,128]{1,0:T(8,128)(2,1)S(1)}, bf16[608,128]{1,0:T(8,128)(2,1)S(1)}, u32[]{:S(2)}, u32[]{:S(2)}) collective-permute-start(bf16[608,128]{1,0:T(8,128)(2,1)S(1)} %piece_attn.1.refs_0_.refs_4_), channel_id=1, source_target_pairs={{0,2},{1,3},{2,0},{3,1},{4,6},{5,7},{6,4},{7,5},{8,10},{9,11},{10,... | collective-permute-start | bytes 466952 | tf_op jit(solution)/shard_map/ppermute | solution.py:259
  18.9 13.1 %collective-permute-start.5 = (bf16[2,608,128]{2,1,0:T(8,128)(2,1)S(1)}, bf16[2,608,128]{2,1,0:T(8,128)(2,1)S(1)}, u32[]{:S(2)}, u32[]{:S(2)}) collective-permute-start(bf16[2,608,128]{2,1,0:T(8,128)(2,1)S(1)} %pair_up.1.refs_1_), channel_id=1, source_target_pairs={{0,1},{1,0},{2,3},{3,2},{4,5},{5,4},{6,7},{7,6},{8,9},{9,8},{10,11... | collective-permute-start | bytes 933896 | tf_op jit(solution)/shard_map/ppermute | solution.py:259
  20.3 8.7 %collective-permute-start.13 = (bf16[1152,128]{1,0:T(8,128)(2,1)S(1)}, bf16[1152,128]{1,0:T(8,128)(2,1)S(1)}, u32[]{:S(2)}, u32[]{:S(2)}) collective-permute-start(bf16[1152,128]{1,0:T(8,128)(2,1)S(1)} %piece_mlp.1.refs_0_.refs_6_), channel_id=1, source_target_pairs={{0,8},{1,9},{2,10},{3,11},{4,12},{5,13},{6,14},{7,15},{8,0},{9,1},... | collective-permute-start | bytes 884744 | tf_op jit(solution)/shard_map/ppermute | solution.py:259
  21.9 8.7 %collective-permute-start.14 = (bf16[1152,128]{1,0:T(8,128)(2,1)S(1)}, bf16[1152,128]{1,0:T(8,128)(2,1)S(1)}, u32[]{:S(2)}, u32[]{:S(2)}) collective-permute-start(bf16[1152,128]{1,0:T(8,128)(2,1)S(1)} %piece_mlp.1.refs_0_.refs_6_), channel_id=1, source_target_pairs={{0,16},{1,17},{2,18},{3,19},{4,20},{5,21},{6,22},{7,23},{8,24},{9,... | collective-permute-start | bytes 884744 | tf_op jit(solution)/shard_map/ppermute | solution.py:259
  23.4 16.3 %collective-permute-start.15 = (bf16[1152,128]{1,0:T(8,128)(2,1)S(1)}, bf16[1152,128]{1,0:T(8,128)(2,1)S(1)}, u32[]{:S(2)}, u32[]{:S(2)}) collective-permute-start(bf16[1152,128]{1,0:T(8,128)(2,1)S(1)} %piece_again.1), channel_id=1, source_target_pairs={{0,2},{1,3},{2,0},{3,1},{4,6},{5,7},{6,4},{7,5},{8,10},{9,11},{10,... | collective-permute-start | bytes 884744 | tf_op jit(solution)/shard_map/ppermute | solution.py:259
  26.8 13.7 %collective-permute-start.17 = (bf16[1152,128]{1,0:T(8,128)(2,1)S(1)}, bf16[1152,128]{1,0:T(8,128)(2,1)S(1)}, u32[]{:S(2)}, u32[]{:S(2)}) collective-permute-start(bf16[1152,128]{1,0:T(8,128)(2,1)S(1)} %piece_mlp.1.refs_0_.refs_6_), channel_id=1, source_target_pairs={{0,1},{1,0},{2,3},{3,2},{4,5},{5,4},{6,7},{7,6},{8,9},{9,8},{10,11... | collective-permute-start | bytes 884744 | tf_op jit(solution)/shard_map/ppermute | solution.py:259
  29.0 12.7 %collective-permute-start.8 = (bf16[2,608,128]{2,1,0:T(8,128)(2,1)S(1)}, bf16[2,608,128]{2,1,0:T(8,128)(2,1)S(1)}, u32[]{:S(2)}, u32[]{:S(2)}) collective-permute-start(bf16[2,608,128]{2,1,0:T(8,128)(2,1)S(1)} %pair_up.1.refs_1_), channel_id=1, source_target_pairs={{0,16},{1,17},{2,18},{3,19},{4,20},{5,21},{6,22},{7,23},{8,24},{9,... | collective-permute-start | bytes 933896 | tf_op jit(solution)/shard_map/ppermute | solution.py:259
  30.6 12.7 %collective-permute-start.6 = (bf16[2,608,128]{2,1,0:T(8,128)(2,1)S(1)}, bf16[2,608,128]{2,1,0:T(8,128)(2,1)S(1)}, u32[]{:S(2)}, u32[]{:S(2)}) collective-permute-start(bf16[2,608,128]{2,1,0:T(8,128)(2,1)S(1)} %pair_up.1.refs_1_), channel_id=1, source_target_pairs={{0,8},{1,9},{2,10},{3,11},{4,12},{5,13},{6,14},{7,15},{8,0},{9,1},... | collective-permute-start | bytes 933896 | tf_op jit(solution)/shard_map/ppermute | solution.py:259
  32.1 15.5 %collective-permute-start.7 = (bf16[2,608,128]{2,1,0:T(8,128)(2,1)S(1)}, bf16[2,608,128]{2,1,0:T(8,128)(2,1)S(1)}, u32[]{:S(2)}, u32[]{:S(2)}) collective-permute-start(bf16[2,608,128]{2,1,0:T(8,128)(2,1)S(1)} %collective-permute-done.5.refs_2_), channel_id=1, source_target_pairs={{0,8},{1,9},{2,10},{3,11},{4,12},{5,13},{6,14},{7,15},{8,0},{9,1},... | collective-permute-start | bytes 933896 | tf_op jit(solution)/shard_map/ppermute | solution.py:259
  39.7 14.2 %collective-permute-start.20 = (bf16[1152,128]{1,0:T(8,128)(2,1)S(1)}, bf16[1152,128]{1,0:T(8,128)(2,1)S(1)}, u32[]{:S(2)}, u32[]{:S(2)}) collective-permute-start(bf16[1152,128]{1,0:T(8,128)(2,1)S(1)} %collective-permute-done.15.refs_11_.refs_8_), channel_id=1, source_target_pairs={{0,8},{1,9},{2,10},{3,11},{4,12},{5,13},{6,14},{7,15},{8,0},{9,1},... | collective-permute-start | bytes 884744 | tf_op jit(solution)/shard_map/ppermute | solution.py:259
  40.5 14.5 %collective-permute-start.18 = (bf16[1152,128]{1,0:T(8,128)(2,1)S(1)}, bf16[1152,128]{1,0:T(8,128)(2,1)S(1)}, u32[]{:S(2)}, u32[]{:S(2)}) collective-permute-start(bf16[1152,128]{1,0:T(8,128)(2,1)S(1)} %collective-permute-done.15.refs_11_.refs_8_), channel_id=1, source_target_pairs={{0,1},{1,0},{2,3},{3,2},{4,5},{5,4},{6,7},{7,6},{8,9},{9,8},{10,11... | collective-permute-start | bytes 884744 | tf_op jit(solution)/shard_map/ppermute | solution.py:259
  41.7 20.0 %collective-permute-start.9 = (bf16[2,608,128]{2,1,0:T(8,128)(2,1)S(1)}, bf16[2,608,128]{2,1,0:T(8,128)(2,1)S(1)}, u32[]{:S(2)}, u32[]{:S(2)}) collective-permute-start(bf16[2,608,128]{2,1,0:T(8,128)(2,1)S(1)} %collective-permute-done.5.refs_2_), channel_id=1, source_target_pairs={{0,16},{1,17},{2,18},{3,19},{4,20},{5,21},{6,22},{7,23},{8,24},{9,... | collective-permute-start | bytes 933896 | tf_op jit(solution)/shard_map/ppermute | solution.py:259
  43.2 17.3 %collective-permute-start.10 = (bf16[2,608,128]{2,1,0:T(8,128)(2,1)S(1)}, bf16[2,608,128]{2,1,0:T(8,128)(2,1)S(1)}, u32[]{:S(2)}, u32[]{:S(2)}) collective-permute-start(bf16[2,608,128]{2,1,0:T(8,128)(2,1)S(1)} %collective-permute-done.8.refs_5_), channel_id=1, source_target_pairs={{0,8},{1,9},{2,10},{3,11},{4,12},{5,13},{6,14},{7,15},{8,0},{9,1},... | collective-permute-start | bytes 933896 | tf_op jit(solution)/shard_map/ppermute | solution.py:259
  47.5 19.9 %collective-permute-start.11 = (bf16[2,608,128]{2,1,0:T(8,128)(2,1)S(1)}, bf16[2,608,128]{2,1,0:T(8,128)(2,1)S(1)}, u32[]{:S(2)}, u32[]{:S(2)}) collective-permute-start(bf16[2,608,128]{2,1,0:T(8,128)(2,1)S(1)} %collective-permute-done.7.refs_4_.refs_1_), channel_id=1, source_target_pairs={{0,16},{1,17},{2,18},{3,19},{4,20},{5,21},{6,22},{7,23},{8,24},{9,... | collective-permute-start | bytes 933896 | tf_op jit(solution)/shard_map/ppermute | solution.py:259
  53.8 11.2 %collective-permute-start.27 = (bf16[1152,128]{1,0:T(8,128)(2,1)S(1)}, bf16[1152,128]{1,0:T(8,128)(2,1)S(1)}, u32[]{:S(2)}, u32[]{:S(2)}) collective-permute-start(bf16[1152,128]{1,0:T(8,128)(2,1)S(1)} %collective-permute-done.20.refs_6_.refs_12_), channel_id=1, source_target_pairs={{0,16},{1,17},{2,18},{3,19},{4,20},{5,21},{6,22},{7,23},{8,24},{9,... | collective-permute-start | bytes 884744 | tf_op jit(solution)/shard_map/ppermute | solution.py:259
  55.1 11.8 %collective-permute-start.25 = (bf16[1152,128]{1,0:T(8,128)(2,1)S(1)}, bf16[1152,128]{1,0:T(8,128)(2,1)S(1)}, u32[]{:S(2)}, u32[]{:S(2)}) collective-permute-start(bf16[1152,128]{1,0:T(8,128)(2,1)S(1)} %hold_own.1), channel_id=1, source_target_pairs={{0,8},{1,9},{2,10},{3,11},{4,12},{5,13},{6,14},{7,15},{8,0},{9,1},... | collective-permute-start | bytes 884744 | tf_op jit(solution)/shard_map/ppermute | solution.py:259
  60.5 19.8 %collective-permute-start.23 = (bf16[1152,128]{1,0:T(8,128)(2,1)S(1)}, bf16[1152,128]{1,0:T(8,128)(2,1)S(1)}, u32[]{:S(2)}, u32[]{:S(2)}) collective-permute-start(bf16[1152,128]{1,0:T(8,128)(2,1)S(1)} %collective-permute-done.15.refs_11_.refs_8_), channel_id=1, source_target_pairs={{0,16},{1,17},{2,18},{3,19},{4,20},{5,21},{6,22},{7,23},{8,24},{9,... | collective-permute-start | bytes 884744 | tf_op jit(solution)/shard_map/ppermute | solution.py:259
  61.7 16.0 %collective-permute-start.21 = (bf16[1152,128]{1,0:T(8,128)(2,1)S(1)}, bf16[1152,128]{1,0:T(8,128)(2,1)S(1)}, u32[]{:S(2)}, u32[]{:S(2)}) collective-permute-start(bf16[1152,128]{1,0:T(8,128)(2,1)S(1)} %collective-permute-done.18.refs_9_), channel_id=1, source_target_pairs={{0,8},{1,9},{2,10},{3,11},{4,12},{5,13},{6,14},{7,15},{8,0},{9,1},... | collective-permute-start | bytes 884744 | tf_op jit(solution)/shard_map/ppermute | solution.py:259
  65.0 14.2 %collective-permute-start.24 = (bf16[1152,128]{1,0:T(8,128)(2,1)S(1)}, bf16[1152,128]{1,0:T(8,128)(2,1)S(1)}, u32[]{:S(2)}, u32[]{:S(2)}) collective-permute-start(bf16[1152,128]{1,0:T(8,128)(2,1)S(1)} %collective-permute-done.18.refs_9_), channel_id=1, source_target_pairs={{0,16},{1,17},{2,18},{3,19},{4,20},{5,21},{6,22},{7,23},{8,24},{9,... | collective-permute-start | bytes 884744 | tf_op jit(solution)/shard_map/ppermute | solution.py:259
  66.8 12.9 %collective-permute-start.28 = (bf16[1152,128]{1,0:T(8,128)(2,1)S(1)}, bf16[1152,128]{1,0:T(8,128)(2,1)S(1)}, u32[]{:S(2)}, u32[]{:S(2)}) collective-permute-start(bf16[1152,128]{1,0:T(8,128)(2,1)S(1)} %collective-permute-done.27.refs_4_.refs_20_), channel_id=1, source_target_pairs={{0,1},{1,0},{2,3},{3,2},{4,5},{5,4},{6,7},{7,6},{8,9},{9,8},{10,11... | collective-permute-start | bytes 884744 | tf_op jit(solution)/shard_map/ppermute | solution.py:259
  67.4 12.3 %collective-permute-start.26 = (bf16[1152,128]{1,0:T(8,128)(2,1)S(1)}, bf16[1152,128]{1,0:T(8,128)(2,1)S(1)}, u32[]{:S(2)}, u32[]{:S(2)}) collective-permute-start(bf16[1152,128]{1,0:T(8,128)(2,1)S(1)} %collective-permute-done.25.refs_7_.refs_18_), channel_id=1, source_target_pairs={{0,1},{1,0},{2,3},{3,2},{4,5},{5,4},{6,7},{7,6},{8,9},{9,8},{10,11... | collective-permute-start | bytes 884744 | tf_op jit(solution)/shard_map/ppermute | solution.py:259
  77.7 6.7 %collective-permute-start.19 = (bf16[1152,128]{1,0:T(8,128)(2,1)S(1)}, bf16[1152,128]{1,0:T(8,128)(2,1)S(1)}, u32[]{:S(2)}, u32[]{:S(2)}) collective-permute-start(bf16[1152,128]{1,0:T(8,128)(2,1)S(1)} %hold_first.1), channel_id=1, source_target_pairs={{0,8},{1,9},{2,10},{3,11},{4,12},{5,13},{6,14},{7,15},{8,0},{9,1},... | collective-permute-start | bytes 884744 | tf_op jit(solution)/shard_map/ppermute | solution.py:259
  79.2 6.7 %collective-permute-start.22 = (bf16[1152,128]{1,0:T(8,128)(2,1)S(1)}, bf16[1152,128]{1,0:T(8,128)(2,1)S(1)}, u32[]{:S(2)}, u32[]{:S(2)}) collective-permute-start(bf16[1152,128]{1,0:T(8,128)(2,1)S(1)} %hold_first.1), channel_id=1, source_target_pairs={{0,16},{1,17},{2,18},{3,19},{4,20},{5,21},{6,22},{7,23},{8,24},{9,... | collective-permute-start | bytes 884744 | tf_op jit(solution)/shard_map/ppermute | solution.py:259
  79.7 6.2 %collective-permute-start.16 = (bf16[2048,768]{1,0:T(8,128)(2,1)}, bf16[2048,768]{1,0:T(8,128)(2,1)S(1)}, u32[]{:S(2)}, u32[]{:S(2)}) collective-permute-start(bf16[2048,768]{1,0:T(8,128)(2,1)} %get-tuple-element.78.refs_1_), channel_id=1, source_target_pairs={{0,4},{1,5},{2,6},{3,7},{4,0},{5,1},{6,2},{7,3},{8,12},{9,13},{10,... | collective-permute-start | bytes 9437192 | tf_op jit(solution)/shard_map/ppermute | solution.py:259
  86.0 1.7 copy-start.1
  105.6 8.6 %collective-permute-start.30 = (bf16[2048,768]{1,0:T(8,128)(2,1)}, bf16[2048,768]{1,0:T(8,128)(2,1)S(1)}, u32[]{:S(2)}, u32[]{:S(2)}) collective-permute-start(bf16[2048,768]{1,0:T(8,128)(2,1)} %get-tuple-element.84.refs_4_), channel_id=1, source_target_pairs={{0,4},{1,5},{2,6},{3,7},{4,0},{5,1},{6,2},{7,3},{8,12},{9,13},{10,... | collective-permute-start | bytes 9437192 | tf_op jit(solution)/shard_map/ppermute | solution.py:259
  105.6 16.5 %collective-permute-start.32 = (bf16[2,1152,128]{2,1,0:T(8,128)(2,1)}, bf16[2,1152,128]{2,1,0:T(8,128)(2,1)S(1)}, u32[]{:S(2)}, u32[]{:S(2)}) collective-permute-start(bf16[2,1152,128]{2,1,0:T(8,128)(2,1)} %get-tuple-element.93), channel_id=1, source_target_pairs={{0,16},{1,17},{2,18},{3,19},{4,20},{5,21},{6,22},{7,23},{8,24},{9,... | collective-permute-start | bytes 1769480 | tf_op jit(solution)/shard_map/ppermute | solution.py:259
  107.0 16.4 %collective-permute-start.31 = (bf16[2,1152,128]{2,1,0:T(8,128)(2,1)}, bf16[2,1152,128]{2,1,0:T(8,128)(2,1)S(1)}, u32[]{:S(2)}, u32[]{:S(2)}) collective-permute-start(bf16[2,1152,128]{2,1,0:T(8,128)(2,1)} %get-tuple-element.91), channel_id=1, source_target_pairs={{0,8},{1,9},{2,10},{3,11},{4,12},{5,13},{6,14},{7,15},{8,0},{9,1},... | collective-permute-start | bytes 1769480 | tf_op jit(solution)/shard_map/ppermute | solution.py:259
  107.5 5.5 %copy-start.16 = (bf16[2,1152,128]{2,1,0:T(8,128)(2,1)S(1)}, bf16[2,1152,128]{2,1,0:T(8,128)(2,1)}, u32[]{:S(2)}) copy-start(bf16[2,1152,128]{2,1,0:T(8,128)(2,1)} %get-tuple-element.101) | copy-start | bytes 1769476
  107.5 6.7 %copy-start.15 = (bf16[2,1152,128]{2,1,0:T(8,128)(2,1)S(1)}, bf16[2,1152,128]{2,1,0:T(8,128)(2,1)}, u32[]{:S(2)}) copy-start(bf16[2,1152,128]{2,1,0:T(8,128)(2,1)} %get-tuple-element.102) | copy-start | bytes 1769476
  107.5 7.7 %copy-start.2 = (bf16[2048,768]{1,0:T(8,128)(2,1)S(1)}, bf16[2048,768]{1,0:T(8,128)(2,1)}, u32[]{:S(2)}) copy-start(bf16[2048,768]{1,0:T(8,128)(2,1)} %copy-done.1) | copy-start | bytes 9437188
  113.0 18.7 %collective-permute-start.29 = (bf16[2048,768]{1,0:T(8,128)(2,1)}, bf16[2048,768]{1,0:T(8,128)(2,1)S(1)}, u32[]{:S(2)}, u32[]{:S(2)}) collective-permute-start(bf16[2048,768]{1,0:T(8,128)(2,1)} %mlp_out.1.refs_9_.refs_3_), channel_id=1, source_target_pairs={{0,4},{1,5},{2,6},{3,7},{4,0},{5,1},{6,2},{7,3},{8,12},{9,13},{10,... | collective-permute-start | bytes 9437192 | tf_op jit(solution)/shard_map/ppermute | solution.py:259
  113.0 26.3 %collective-permute-start.33 = (bf16[2,1152,128]{2,1,0:T(8,128)(2,1)S(1)}, bf16[2,1152,128]{2,1,0:T(8,128)(2,1)S(1)}, u32[]{:S(2)}, u32[]{:S(2)}) collective-permute-start(bf16[2,1152,128]{2,1,0:T(8,128)(2,1)S(1)} %copy-done.16), channel_id=1, source_target_pairs={{0,16},{1,17},{2,18},{3,19},{4,20},{5,21},{6,22},{7,23},{8,24},{9,... | collective-permute-start | bytes 1769480 | tf_op jit(solution)/shard_map/ppermute | solution.py:259
  114.2 25.1 %collective-permute-start.36 = (bf16[2,1152,128]{2,1,0:T(8,128)(2,1)S(1)}, bf16[2,1152,128]{2,1,0:T(8,128)(2,1)S(1)}, u32[]{:S(2)}, u32[]{:S(2)}) collective-permute-start(bf16[2,1152,128]{2,1,0:T(8,128)(2,1)S(1)} %copy-done.15), channel_id=1, source_target_pairs={{0,8},{1,9},{2,10},{3,11},{4,12},{5,13},{6,14},{7,15},{8,0},{9,1},... | collective-permute-start | bytes 1769480 | tf_op jit(solution)/shard_map/ppermute | solution.py:259
  115.2 6.9 %copy-start.12 = (bf16[2,1152,128]{2,1,0:T(8,128)(2,1)S(1)}, bf16[2,1152,128]{2,1,0:T(8,128)(2,1)}, u32[]{:S(2)}) copy-start(bf16[2,1152,128]{2,1,0:T(8,128)(2,1)} %get-tuple-element.92.refs_0_) | copy-start | bytes 1769476
  122.3 25.5 %collective-permute-start.34 = (bf16[2,1152,128]{2,1,0:T(8,128)(2,1)S(1)}, bf16[2,1152,128]{2,1,0:T(8,128)(2,1)S(1)}, u32[]{:S(2)}, u32[]{:S(2)}) collective-permute-start(bf16[2,1152,128]{2,1,0:T(8,128)(2,1)S(1)} %aOm.1.refs_3_), channel_id=1, source_target_pairs={{0,8},{1,9},{2,10},{3,11},{4,12},{5,13},{6,14},{7,15},{8,0},{9,1},... | collective-permute-start | bytes 1769480 | tf_op jit(solution)/shard_map/ppermute | solution.py:259
  123.5 24.2 %collective-permute-start.35 = (bf16[2,1152,128]{2,1,0:T(8,128)(2,1)S(1)}, bf16[2,1152,128]{2,1,0:T(8,128)(2,1)S(1)}, u32[]{:S(2)}, u32[]{:S(2)}) collective-permute-start(bf16[2,1152,128]{2,1,0:T(8,128)(2,1)S(1)} %aEm.1.refs_2_), channel_id=1, source_target_pairs={{0,16},{1,17},{2,18},{3,19},{4,20},{5,21},{6,22},{7,23},{8,24},{9,... | collective-permute-start | bytes 1769480 | tf_op jit(solution)/shard_map/ppermute | solution.py:259
  150.4 39.0 %collective-permute-start.37 = (bf16[2048,768]{1,0:T(8,128)(2,1)}, bf16[2048,768]{1,0:T(8,128)(2,1)S(1)}, u32[]{:S(2)}, u32[]{:S(2)}) collective-permute-start(bf16[2048,768]{1,0:T(8,128)(2,1)} %hand_on.1), channel_id=1, source_target_pairs={{0,4},{1,5},{2,6},{3,7},{4,0},{5,1},{6,2},{7,3},{8,12},{9,13},{10,... | collective-permute-start | bytes 9437192 | tf_op jit(solution)/shard_map/ppermute | solution.py:259
  150.4 15.7 %collective-permute-start.43 = (bf16[2,1152,128]{2,1,0:T(8,128)(2,1)S(1)}, bf16[2,1152,128]{2,1,0:T(8,128)(2,1)S(1)}, u32[]{:S(2)}, u32[]{:S(2)}) collective-permute-start(bf16[2,1152,128]{2,1,0:T(8,128)(2,1)S(1)} %som.1.refs_1_), channel_id=1, source_target_pairs={{0,1},{1,0},{2,3},{3,2},{4,5},{5,4},{6,7},{7,6},{8,9},{9,8},{10,11... | collective-permute-start | bytes 1769480 | tf_op jit(solution)/shard_map/ppermute | solution.py:259
  151.0 10.2 %collective-permute-start.39 = (bf16[2,608,128]{2,1,0:T(8,128)(2,1)S(1)}, bf16[2,608,128]{2,1,0:T(8,128)(2,1)S(1)}, u32[]{:S(2)}, u32[]{:S(2)}) collective-permute-start(bf16[2,608,128]{2,1,0:T(8,128)(2,1)S(1)} %get-tuple-element.106), channel_id=1, source_target_pairs={{0,16},{1,17},{2,18},{3,19},{4,20},{5,21},{6,22},{7,23},{8,24},{9,... | collective-permute-start | bytes 933896 | tf_op jit(solution)/shard_map/ppermute | solution.py:259
  151.9 24.1 %collective-permute-start.38 = (bf16[2,608,128]{2,1,0:T(8,128)(2,1)S(1)}, bf16[2,608,128]{2,1,0:T(8,128)(2,1)S(1)}, u32[]{:S(2)}, u32[]{:S(2)}) collective-permute-start(bf16[2,608,128]{2,1,0:T(8,128)(2,1)S(1)} %get-tuple-element.104), channel_id=1, source_target_pairs={{0,16},{1,17},{2,18},{3,19},{4,20},{5,21},{6,22},{7,23},{8,24},{9,... | collective-permute-start | bytes 933896 | tf_op jit(solution)/shard_map/ppermute | solution.py:259
  161.3 14.8 %collective-permute-start.40 = (bf16[2,608,128]{2,1,0:T(8,128)(2,1)S(1)}, bf16[2,608,128]{2,1,0:T(8,128)(2,1)S(1)}, u32[]{:S(2)}, u32[]{:S(2)}) collective-permute-start(bf16[2,608,128]{2,1,0:T(8,128)(2,1)S(1)} %aOa.1), channel_id=1, source_target_pairs={{0,8},{1,9},{2,10},{3,11},{4,12},{5,13},{6,14},{7,15},{8,0},{9,1},... | collective-permute-start | bytes 933896 | tf_op jit(solution)/shard_map/ppermute | solution.py:259
  162.0 16.0 %collective-permute-start.42 = (bf16[2,608,128]{2,1,0:T(8,128)(2,1)S(1)}, bf16[2,608,128]{2,1,0:T(8,128)(2,1)S(1)}, u32[]{:S(2)}, u32[]{:S(2)}) collective-permute-start(bf16[2,608,128]{2,1,0:T(8,128)(2,1)S(1)} %get-tuple-element.112), channel_id=1, source_target_pairs={{0,8},{1,9},{2,10},{3,11},{4,12},{5,13},{6,14},{7,15},{8,0},{9,1},... | collective-permute-start | bytes 933896 | tf_op jit(solution)/shard_map/ppermute | solution.py:259
  166.5 22.8 %collective-permute-start.47 = (bf16[1152,128]{1,0:T(8,128)(2,1)S(1)}, bf16[1152,128]{1,0:T(8,128)(2,1)S(1)}, u32[]{:S(2)}, u32[]{:S(2)}) collective-permute-start(bf16[1152,128]{1,0:T(8,128)(2,1)S(1)} %get-tuple-element.114.refs_2_), channel_id=1, source_target_pairs={{0,2},{1,3},{2,0},{3,1},{4,6},{5,7},{6,4},{7,5},{8,10},{9,11},{10,... | collective-permute-start | bytes 884744 | tf_op jit(solution)/shard_map/ppermute | solution.py:259
  176.0 19.9 %collective-permute-start.41 = (bf16[2,608,128]{2,1,0:T(8,128)(2,1)S(1)}, bf16[2,608,128]{2,1,0:T(8,128)(2,1)S(1)}, u32[]{:S(2)}, u32[]{:S(2)}) collective-permute-start(bf16[2,608,128]{2,1,0:T(8,128)(2,1)S(1)} %get-tuple-element.110), channel_id=1, source_target_pairs={{0,8},{1,9},{2,10},{3,11},{4,12},{5,13},{6,14},{7,15},{8,0},{9,1},... | collective-permute-start | bytes 933896 | tf_op jit(solution)/shard_map/ppermute | solution.py:259
  176.2 19.7 %collective-permute-start.45 = (bf16[2,608,128]{2,1,0:T(8,128)(2,1)S(1)}, bf16[2,608,128]{2,1,0:T(8,128)(2,1)S(1)}, u32[]{:S(2)}, u32[]{:S(2)}) collective-permute-start(bf16[2,608,128]{2,1,0:T(8,128)(2,1)S(1)} %soa.1.refs_9_), channel_id=1, source_target_pairs={{0,1},{1,0},{2,3},{3,2},{4,5},{5,4},{6,7},{7,6},{8,9},{9,8},{10,11... | collective-permute-start | bytes 933896 | tf_op jit(solution)/shard_map/ppermute | solution.py:259
  178.1 17.8 %collective-permute-start.44 = (bf16[2,608,128]{2,1,0:T(8,128)(2,1)S(1)}, bf16[2,608,128]{2,1,0:T(8,128)(2,1)S(1)}, u32[]{:S(2)}, u32[]{:S(2)}) collective-permute-start(bf16[2,608,128]{2,1,0:T(8,128)(2,1)S(1)} %aEa.1), channel_id=1, source_target_pairs={{0,16},{1,17},{2,18},{3,19},{4,20},{5,21},{6,22},{7,23},{8,24},{9,... | collective-permute-start | bytes 933896 | tf_op jit(solution)/shard_map/ppermute | solution.py:259
  189.3 7.9 %collective-permute-start.48 = (f32[576,128]{1,0:T(8,128)S(1)}, f32[576,128]{1,0:T(8,128)S(1)}, u32[]{:S(2)}, u32[]{:S(2)}) collective-permute-start(f32[576,128]{1,0:T(8,128)S(1)} %get-tuple-element.119.refs_5_), channel_id=1, source_target_pairs={{0,4},{1,5},{2,6},{3,7},{4,0},{5,1},{6,2},{7,3},{8,12},{9,13},{10,... | collective-permute-start | bytes 884744 | tf_op jit(solution)/shard_map/ppermute | solution.py:259
  195.9 1.4 copy-start.5
  196.1 10.7 %collective-permute-start.46 = (bf16[608,128]{1,0:T(8,128)(2,1)S(1)}, bf16[608,128]{1,0:T(8,128)(2,1)S(1)}, u32[]{:S(2)}, u32[]{:S(2)}) collective-permute-start(bf16[608,128]{1,0:T(8,128)(2,1)S(1)} %get-tuple-element.116), channel_id=1, source_target_pairs={{0,2},{1,3},{2,0},{3,1},{4,6},{5,7},{6,4},{7,5},{8,10},{9,11},{10,... | collective-permute-start | bytes 466952 | tf_op jit(solution)/shard_map/ppermute | solution.py:259
  197.3 11.1 %copy-start.13 = (f32[288]{0:T(512)S(1)}, f32[288]{0:T(512)}, u32[]{:S(2)}) copy-start(f32[288]{0:T(512)} %param.23) | copy-start | bytes 3460
  197.3 11.1 %copy-start.14 = (f32[288]{0:T(512)S(1)}, f32[288]{0:T(512)}, u32[]{:S(2)}) copy-start(f32[288]{0:T(512)} %param.22) | copy-start | bytes 3460
  197.3 12.0 %copy-start = (f32[3,128]{1,0:T(4,128)S(1)}, f32[3,128]{1,0:T(4,128)}, u32[]{:S(2)}) copy-start(f32[3,128]{1,0:T(4,128)} %pad_bitcast_fusion.2.refs_3_.refs_7_) | copy-start | bytes 4612
  197.3 12.0 %copy-start.6 = (f32[73728]{0:T(1024)S(1)}, f32[73728]{0:T(1024)}, u32[]{:S(2)}) copy-start(f32[73728]{0:T(1024)} %param.15) | copy-start | bytes 884740
  197.3 12.0 %copy-start.7 = (f32[73728]{0:T(1024)S(1)}, f32[73728]{0:T(1024)}, u32[]{:S(2)}) copy-start(f32[73728]{0:T(1024)} %param.16) | copy-start | bytes 884740
  197.4 12.0 %copy-start.8 = (f32[73728]{0:T(1024)S(1)}, f32[73728]{0:T(1024)}, u32[]{:S(2)}) copy-start(f32[73728]{0:T(1024)} %param.17) | copy-start | bytes 884740
  207.9 1.5 collective-permute-start.49
  208.0 1.3 collective-permute-start.50
  (4 other events, 5.1 us)

commit v5 on v3

--- a/solution.py
+++ b/solution.py
@@ -501,20 +501,21 @@
         part_ref[...] = dot(context_ref[...], w_out[...]).astype(bf16)
 
 
-ERF_TOP = (0.00022905065861350646, 0.0034082910107109506, 0.050955695062380861, 0.18520832239976145, 1.128379143519084)
-ERF_BOTTOM = (-1.1791602954361697e-7, 0.000023547966471313185, 0.0010179625278914885, 0.014070470171167667,
-              0.11098505178285362, 0.49746925110067538, 1.0)
-
-
-def error_function(v):
-    v = jnp.clip(v, -3.832506856900711, 3.832506856900711)
-    square = v * v
-    top, bottom = jnp.full_like(v, ERF_TOP[0]), jnp.full_like(v, ERF_BOTTOM[0])
-    for a in ERF_TOP[1:]:
-        top = top * square + a
-    for b in ERF_BOTTOM[1:]:
-        bottom = bottom * square + b
-    return v * top / bottom
+TAIL = (0.5 * 0.254829592, 0.5 * -0.284496736, 0.5 * 1.421413741, 0.5 * -1.453152027, 0.5 * 1.061405429)
+
+
+def normal_curves(u):
+    t = 1.0 / (1.0 + (0.3275911 * inv_root_two) * jnp.abs(u))
+    expo = jnp.exp(-0.5 * u * u)
+    series = TAIL[4]
+    for a in TAIL[3::-1]:
+        series = series * t + a
+    tail = series * t * expo
+    return jnp.where(u < 0.0, tail, 1.0 - tail), expo * inv_root_tau
+
+
+def block_of(rows):
+    return rows.at[pl.ds(pl.multiple_of(pl.program_id(0) * BLOCK, BLOCK), BLOCK), :]
 
 
 def middle_of(x_ref, part_own, part_other, vecs):
@@ -522,18 +523,28 @@
     return x_ref[...].astype(f32) + parts + vecs[2:3, :]
 
 
-def mlp_both(phase, meta, idx, x_ref, part_own, part_other, cot_ref, vecs, inner_bias, *refs):
+def mlp_both(phase, meta, idx, x_ref, part_own, cot_ref, vecs, inner_bias, other_rows, *refs):
     pieces = refs[:16]
-    (active_ref, back_ref, w_two, sums, inner_sum) = refs[16:21]
+    active_ref, back_ref, w_two_out, sums, inner_sum = refs[16:21]
     outs = refs[21:29]
-    w_one, acc_one, acc_two = refs[29:]
+    w_one, w_two, acc_one, acc_two, stage, arrived, written = refs[29:]
+
+    def to_stage(n):
+        return pltpu.make_async_copy(pieces[n], stage.at[n], arrived.at[n])
+
+    def to_output():
+        return pltpu.make_async_copy(w_two, w_two_out, written)
 
     if phase == 0:
+        for n in range(16):
+            to_stage(n).start()
         acc_one[...] = jnp.zeros(acc_one.shape, f32)
         acc_two[...] = jnp.zeros(acc_two.shape, f32)
         sums[...] = jnp.zeros(sums.shape, f32)
         inner_sum[...] = jnp.zeros(inner_sum.shape, f32)
-        for n, piece in enumerate(pieces):
+        for n in range(16):
+            to_stage(n).wait()
+            piece = stage.at[n]
             chip, z = owner_of(idx, n // 4, n % 4)
 
             @pl.when(chip < 2)
@@ -551,29 +562,34 @@
                 for j in range(6):
                     w_two[to, j * ROW : (j + 1) * ROW] = piece[j * 192 : (j + 1) * 192, :]
 
+        to_output().start()
+
     if phase == 1:
-        normed, _ = standard(middle_of(x_ref, part_own, part_other, vecs))
+        normed, _ = standard(middle_of(x_ref, part_own, block_of(other_rows), vecs))
         second_in = (normed * vecs[3:4, :] + vecs[4:5, :]).astype(bf16)
         grad = cot_ref[...]
         back = jnp.zeros((BLOCK, D), f32)
+        inner_grads = []
         for n in range(2):
             cols = slice(n * D, (n + 1) * D)
             inner = dot(second_in, w_one[:, cols]) + inner_bias[:, cols]
-            bell = 0.5 * (1.0 + error_function(inner * inv_root_two))
+            bell, bump = normal_curves(inner)
             active = (inner * bell).astype(bf16)
             active_ref[:, cols] = active
-            slope = bell + inner * jnp.exp(-0.5 * inner * inner) * inv_root_tau
+            slope = bell + inner * bump
             grad_inner = (dot(grad, w_two[cols, :], ((1,), (1,))) * slope).astype(bf16)
+            inner_grads.append(grad_inner)
             acc_two[cols, :] += dot(active, grad, ((0,), (0,)))
-            acc_one[:, cols] += dot(second_in, grad_inner, ((0,), (0,)))
             inner_sum[:, cols] += jnp.sum(grad_inner.astype(f32), 0, keepdims=True)
             back = back + dot(grad_inner, w_one[:, cols], ((1,), (1,)))
+        acc_one[...] += dot(second_in, jnp.concatenate(inner_grads, axis=1), ((0,), (0,)))
         back_ref[...] = back.astype(bf16)
         sums[0:1, :] += jnp.sum(back * normed, 0, keepdims=True)
         sums[1:2, :] += jnp.sum(back, 0, keepdims=True)
         sums[2:3, :] += jnp.sum(grad.astype(f32), 0, keepdims=True)
 
     if phase == 2:
+        to_output().wait()
         for n in range(16):
             chip, z = owner_of(idx, n // 4, n % 4)
             out, k = outs[pair_of(n)], n % 4 // 2
@@ -594,17 +610,12 @@
                     out[k, j * 192 : (j + 1) * 192, :] = acc_two[rows, j * ROW : (j + 1) * ROW].astype(bf16)
 
 
-def hand_on(phase, meta, idx, source, target):
-    if phase == 1:
-        target[...] = source[...]
-
-
 def mlp_out(phase, meta, idx, active_ref, w_two, part_ref):
     if phase == 1:
         part_ref[...] = dot(active_ref[...], w_two[...]).astype(bf16)
 
 
-def middle_backward(phase, meta, idx, x_ref, part_own, part_other, cot_ref, back_own, back_other, context_ref, w_out, vecs,
+def middle_backward(phase, meta, idx, x_ref, part_own, part_other, cot_ref, back_own, context_ref, w_out, vecs, other_rows,
                     grad_ref, grad_context_ref, acc_out, sums):
     if phase == 0:
         acc_out[...] = jnp.zeros(acc_out.shape, f32)
@@ -612,7 +623,7 @@
 
     if phase == 1:
         normed, factor = standard(middle_of(x_ref, part_own, part_other, vecs))
-        scaled = (back_own[...].astype(f32) + back_other[...].astype(f32)) * vecs[3:4, :]
+        scaled = (back_own[...].astype(f32) + block_of(other_rows)[...].astype(f32)) * vecs[3:4, :]
         through = scaled - jnp.mean(scaled, -1, keepdims=True)
         through = through - normed * jnp.mean(scaled * normed, -1, keepdims=True)
         grad_middle = cot_ref[...].astype(f32) + factor * through
@@ -901,13 +912,13 @@
     "z3m": ("z2m", TO_Z[1]),
     "x0m": ("pm", TO_X),
     "y0m": ("pm", TO_Y),
-    "x1m": ("z1m", TO_X),
-    "y1m": ("z1m", TO_Y),
+    "x1m": ("h1m", TO_X),
+    "y1m": ("h1m", TO_Y),
     "x2m": ("z2m", TO_X),
     "y2m": ("z2m", TO_Y),
     "x3m": ("z3m", TO_X),
     "y3m": ("z3m", TO_Y),
-    "d0m": ("y0m", TO_X),
+    "d0m": ("h0m", TO_X),
     "d1m": ("d0m", TO_Z[1]),
     "d2m": ("x2m", TO_Y),
     "d3m": ("d2m", TO_Z[1]),
@@ -931,12 +942,19 @@
 SENDS["gs"] = ("other_small", TO_CORE)
 PAIR_NAMES = ("E{}_grad", "O{}_grad", "xE{}_grad", "xO{}_grad", "yE{}_grad", "yO{}_grad", "dE{}_grad", "dO{}_grad")
 
+IN_HBM = ("first_back", "out_part", "grad_context", "output", "done_m")
 AFTER = {
+    "sum": ("fara",),
+    "szm": ("aEa",),
+    "soa": ("aEa",),
+    "aOa": ("rEa",),
     "pa": ("cs", "cc", "cv"),
     "pm": ("pa",),
     "Ea": ("meta",),
     "pm2": ("Ea",),
-    "fwd": ("x1m", "y1m", "x0m", "y0m"),
+    "h1m": ("xOa",),
+    "h0m": ("xOa",),
+    "fwd": ("x0m", "y0m", "z2m"),
     "there": ("x3m", "y3m", "d1m", "d2m", "d3m", "x2m", "d0m", "vecs"),
     "mlp": ("there",),
     "bw1": ("out_part",),
@@ -944,21 +962,18 @@
     "aOm": ("grad_context",),
     "bw2": ("aEm", "aOm"),
     "bw3": ("ot",),
-    "som": ("first_back",),
-    "hand": ("som",),
-    "aEa": ("farm",),
+    "som": ("qEm", "pEm"),
     "fin": ("soa",),
     "sza": ("output",),
     "sua": ("done_m",),
 }
 
 ORDER = (
-    "+cv", "+cs", "+cc", "=cut", "+sa", "+sm", "=pack", "=pa", "+z2a", "=pm", "+z1m", "+x0m", "+y0m",
-    "=Ea", "=pm2", "+z2m", "+zOa", "+xEa", "+yEa", "+x1m", "+y1m", "+dEa", "+yOa", "+z3m", "+xOa", "+y2m", "+x2m",
-    "+d0m", "+dOa", "+y3m", "+x3m", "+d2m", "=fwd", "+pt", "+d1m", "+d3m", "=there",
-    "=mlp", "+rEm", "+rOm", "+bk", "=mout", "+ot", "=bw1", "=aEm", "=aOm", "+qOm", "+qEm", "+pEm", "+pOm", "=bw2",
-    "=bw3", "+rEa", "+rOa", "=som", "=hand", "+fb", "+wOm", "=szm", "+w2m", "=aEa", "=aOa", "+qOa", "+qEa", "+pEa", "+pOa",
-    "=soa", "+wOa", "=fin", "=sum", "+gm", "=om", "=sza", "+w2a", "=sua", "+ga", "+gs", "=oa",
+    "+cv", "+cs", "+cc", "=cut", "+sa", "+sm", "=pack", "=pa", "+z2a", "=pm", "+z1m", "+x0m", "+y0m", "=Ea", "=pm2", "+z2m",
+    "+zOa", "+xEa", "+yEa", "+dEa", "+yOa", "+z3m", "+xOa", "=h1m", "=h0m", "+x1m", "+y1m", "+y2m", "+x2m", "+d0m", "+dOa", "+y3m",
+    "+x3m", "+d2m", "=fwd", "+pt", "+d1m", "+d3m", "=there", "=mlp", "+rEm", "+rOm", "+bk", "=mout", "+ot", "=bw1", "=aEm", "=aOm",
+    "+qOm", "+qEm", "+pEm", "+pOm", "=bw2", "=bw3", "+rEa", "+rOa", "=som", "+fb", "+wOm", "=aEa", "=aOa", "+qOa", "+qEa", "+pEa",
+    "+pOa", "=soa", "+wOa", "=fin", "=sza", "+w2a", "=szm", "+w2m", "=sum", "+gm", "=om", "=sua", "+ga", "+gs", "=oa",
 )
 
 
@@ -998,7 +1013,7 @@
     return pl.BlockSpec(value.shape, lambda i: (0,) * len(value.shape))
 
 
-def over_blocks(body, rows_in, fixed_in, rows_out, fixed_out, scratch, mib, name, after=()):
+def over_blocks(body, rows_in, fixed_in, rows_out, fixed_out, scratch, mib, name, after=(), far=None):
     many = rows_in + [w for w, _, _ in rows_out]
     n_in, n_out = len(rows_in), len(rows_out)
 
@@ -1016,17 +1031,22 @@
         pltpu.emit_pipeline(one, grid=(meta[0],), in_specs=specs[:n_in], out_specs=specs[n_in:])(*rows, *lines)
         body(2, meta, idx, *rows, *fixed, *lines, *rest)
 
+    def fixed_specs(arrays, first):
+        if far is None:
+            return [full(a) for a in arrays]
+        return [ANY if first + n in far else VMEM for n in range(len(arrays))]
+
     def called(meta, idx, *args):
         return pl.pallas_call(
             kernel,
-            grid=(1,),
-            in_specs=[SMEM, SMEM] + [ANY] * n_in + [full(a) for a in args[n_in:]] + [ANY] * len(after),
-            out_specs=[ANY] * n_out + [full(a) for a in fixed_out],
+            in_specs=[SMEM, SMEM] + [ANY] * n_in + fixed_specs(args[n_in:], 0) + [ANY] * len(after),
+            out_specs=[ANY] * n_out + fixed_specs(fixed_out, fixed_in),
             out_shape=[large((n, w), t) for w, t, n in rows_out] + fixed_out,
             scratch_shapes=scratch,
             compiler_params=params(mib),
             cost_estimate=cost(name),
             name=name,
+            **({"grid": (1,)} if far is None else {}),
         )(meta, idx, *args, *after)
 
     return called
@@ -1086,7 +1106,7 @@
     pair_a, pair_m = (2, 608, ROW), (2, 1152, ROW)
 
     def after(name):
-        return tuple(v[n] for n in AFTER.get(name, ()))
+        return tuple(in_hbm(v[n]) if n in IN_HBM else v[n] for n in AFTER.get(name, ()))
 
     v = {"visible": visible, "samples": samples, "cotangent": cotangent}
 
@@ -1131,6 +1151,12 @@
             [pltpu.VMEM((8, 16, ROW), f32)], 24, "attn_forward", after("fwd"),
         )(v["meta"], idx, *hbm("x"), v["Ea"], *(v[n] for n in ("zOa", "xEa", "xOa", "yEa", "yOa", "dEa", "dOa")))
 
+    def hold_1():
+        v["h1m"] = at_once(lay_out, 0, [array(shape_m)], [], 8, "hold_first", after("h1m"))(v["z1m"])[0]
+
+    def hold_0():
+        v["h0m"] = at_once(lay_out, 0, [array(shape_m)], [], 8, "hold_own", after("h0m"))(v["y0m"])[0]
+
     def there():
         v["there"] = at_once(nothing, 1, [array((8, ROW), f32)], [], 4, "all_there", after("there"))(idx)[0]
 
@@ -1140,11 +1166,12 @@
     def mlp():
         pieces = [v["pm"] if c + k == "z0" else v[c + k + "m"] for c in "zxyd" for k in "0123"]
         done = over_blocks(
-            mlp_both, [D] * 4, 18, [(FF // 2, bf16, rows), (D, bf16, rows)],
+            mlp_both, [D] * 3, 19, [(FF // 2, bf16, rows), (D, bf16, rows)],
             [large((FF // 2, D)), array((8, D), f32), array((1, FF // 2), f32)] + [array(pair_m)] * 8,
-            [pltpu.VMEM((D, FF // 2), bf16), pltpu.VMEM((D, FF // 2), f32), pltpu.VMEM((FF // 2, D), f32)],
-            48, "mlp_both", after("mlp"),
-        )(v["meta"], idx, *middle(), *hbm("cot"), v["vecs"], v["inner_bias"], *pieces)
+            [pltpu.VMEM((D, FF // 2), bf16), pltpu.VMEM((FF // 2, D), bf16), pltpu.VMEM((D, FF // 2), f32), pltpu.VMEM((FF // 2, D), f32),
+             pltpu.VMEM((16, *shape_m), bf16), pltpu.SemaphoreType.DMA((16,)), pltpu.SemaphoreType.DMA],
+            40, "mlp_both", after("mlp"), {*range(3, 19), 19},
+        )(v["meta"], idx, *hbm("x", "part", "cot"), v["vecs"], v["inner_bias"], v["pt"], *pieces)
         v["active"], v["back"], v["w_two"], v["sums"], v["inner_sum"] = done[:5]
         v.update(zip((n.format("m") for n in PAIR_NAMES), done[5:]))
 
@@ -1155,9 +1182,9 @@
 
     def backward_1():
         v["grad_middle"], v["grad_context"], v["acc_out"], v["sums_out"] = over_blocks(
-            middle_backward, [D] * 6 + [D // 2], 2, [(D, f32, rows), (D // 2, bf16, rows)],
+            middle_backward, [D] * 5 + [D // 2], 3, [(D, f32, rows), (D // 2, bf16, rows)],
             [large((D // 2, D), f32), array((8, D), f32)], [], 16, "middle_backward", after("bw1"),
-        )(v["meta"], idx, *middle(), *hbm("cot", "back", "bk", "context", "w_out"), v["vecs"])
+        )(v["meta"], idx, *middle(), *hbm("cot", "back", "context", "w_out"), v["vecs"], v["bk"])
 
     def backward_2():
         v["grad_qkv"] = over_blocks(
@@ -1173,15 +1200,10 @@
         v["first_back"] = done[0]
         v.update(zip((n.format("a") for n in PAIR_NAMES), done[1:]))
 
-    def again_back():
-        v["first_back_2"] = over_blocks(hand_on, [D], 0, [(D, bf16, rows)], [], [], 8, "hand_on", after("hand"))(
-            v["meta"], idx, *hbm("first_back")
-        )[0]
-
     def finish():
         v["output"], v["grad_samples"] = over_blocks(
             finish_rows, [D] * 8, 1, [], [large((count, length, D))] * 2, [pltpu.VMEM((rows, D), bf16)] * 2, 24, "finish_rows", after("fin"),
-        )(v["meta"], idx, *middle(), *hbm("out_part", "ot", "grad_middle", "first_back", "fb"), v["vecs"])
+        )(v["meta"], idx, *middle(), *hbm("out_part", "ot", "grad_middle", "first_back_2", "fb"), v["vecs"])
 
     def adds(g):
         pair, half = (pair_a, 288) if g == "a" else (pair_m, 576)
@@ -1198,7 +1220,21 @@
             v["aO" + g] = add(add_low, [f"xO{g}_grad", "rO" + g], [array(pair)], "aO")[0]
 
         def odd_sum():
-            v["so" + g] = add(add_low, [f"O{g}_grad", "pO" + g, "qO" + g], [array(pair)], "so")[0]
+            terms = [f"O{g}_grad", "pO" + g, "qO" + g]
+            if g == "a":
+                v["so" + g] = add(add_low, terms, [array(pair)], "so")[0]
+                return
+            waited = after("som")
+            v["som"], v["first_back_2"] = pl.pallas_call(
+                lambda a, b, c, *refs: add_low(a, b, c, refs[-2]),
+                in_specs=[VMEM] * 3 + [ANY] * (1 + len(waited)),
+                out_specs=[VMEM, ANY],
+                out_shape=[array(pair), large((rows, D))],
+                input_output_aliases={3: 1},
+                compiler_params=params(24),
+                cost_estimate=cost("som"),
+                name="som",
+            )(*(v[t] for t in terms), in_hbm(v["first_back"]), *waited)
 
         def even_sum():
             v["near" + g], v["far" + g] = add(
@@ -1216,7 +1252,7 @@
 
     def optimize_m():
         v["new_mlp"] = at_once(
-            step_mlp, 1, [array(shape_m, f32)] * 3,
+            step_mlp, 1, [large(shape_m, f32)] * 3,
             [pltpu.VMEM((2, *half_m), f32), pltpu.VMEM(shape_m, f32)], 16, "step_mlp", after("om"),
         )(idx, lanes(master_mlp), lanes(first_mlp), lanes(second_mlp), v["ownm"], v["otherm"], v["gm"])
         v["done_m"] = v["new_mlp"][0]
@@ -1228,14 +1264,14 @@
         )(idx, lanes(master_attn), lanes(first_attn), lanes(second_attn), v["owna"], v["othera"], v["ga"],
           three_rows(master_small), three_rows(first_small), three_rows(second_small), v["own_small"], v["gs"])
 
-    works = {"cut": cut, "pa": piece_a, "Ea": even_a, "pm": piece_m, "pm2": again_m, "pack": pack, "there": there, "fwd": forward, "mlp": mlp, "mout": out_rows,
-             "bw1": backward_1, "bw2": backward_2, "bw3": backward_3, "hand": again_back, "fin": finish, "om": optimize_m, "oa": optimize_a, **adds("m"), **adds("a")}
+    works = {"cut": cut, "pa": piece_a, "Ea": even_a, "pm": piece_m, "pm2": again_m, "pack": pack, "there": there, "h1m": hold_1, "h0m": hold_0, "fwd": forward, "mlp": mlp, "mout": out_rows,
+             "bw1": backward_1, "bw2": backward_2, "bw3": backward_3, "fin": finish, "om": optimize_m, "oa": optimize_a, **adds("m"), **adds("a")}
     for step in ORDER:
         kind, name = step[0], step[1:]
         if kind == "+":
             source, pairs = SENDS[name]
             v[name] = send(v[source], pairs)
-        elif kind == "=":
+        else:
             works[name]()
 
     new_mlp, new_attn, output, grad_samples = v["new_mlp"], v["new_attn"], v["output"], v["grad_samples"]

time: 220 us -> 197 us (0.90)
  local copies, waits for them, and re-layouts: 11.5 us -> 1.4 us
  starting transfers between devices: 66.1 us -> 59.4 us
  Pallas kernels: 76.3 us -> 71.3 us
  waiting for transfers between devices: 63.8 us -> 61.3 us
    unnamed x44 -> x20, local copies, waits for them, and re-layouts: 10.1 us -> 0.05 us
    ppermute x51, starting transfers between devices: 66.1 us -> 59.4 us  [send(): return lax.ppermute(value, AXES, pairs)]
    pallas_call x8, Pallas kernels: 62.6 us -> 57.9 us  [the longest x7 57.7 us: called(): pl.pallas_call(kernel, in_specs=[SMEM, SMEM] + [ANY] * n_in + fixed_specs...]
    ppermute x51, waiting for transfers between devices: 63.8 us -> 61.3 us  [send(): return lax.ppermute(value, AXES, pairs)]
    pallas_call x19 -> x20, Pallas kernels: 13.6 us -> 13.4 us  [called(): pl.pallas_call(kernel, in_specs=[SMEM] * scalars + blocks + [ANY] * len(a...]
  transfers between devices with their start and end apart: 51 -> 51, of which waited for: 15 -> 24; matrix products, arithmetic and copies ran while one was open for 1% -> 1% of each run, Pallas kernels for 25% -> 27%
where the time goes in v5:
time: 197 us; the launch traced here: 194 us
  Pallas kernels  71.3 us (36%)
  waiting for transfers between devices  61.3 us (31%)
  starting transfers between devices  59.4 us (30%)
    ppermute x51, waiting for transfers between devices, send(): return lax.ppermute(value, AXES, pairs)  61.3 us
    ppermute x51, starting transfers between devices, send(): return lax.ppermute(value, AXES, pairs)  59.4 us
    pallas_call x7, Pallas kernels, called(): pl.pallas_call(kernel, in_specs=[SMEM, SMEM] + [ANY] * n_in + fixed_specs...  57.7 us
    pallas_call x20, Pallas kernels, called(): pl.pallas_call(kernel, in_specs=[SMEM] * scalars + blocks + [ANY] * len(a...  13.4 us
  transfers between devices with their start and end apart: 51, of which 24 were waited for; matrix products, arithmetic and copies ran while one was open for 1% of the time, Pallas kernels for 27%

profile of v5, /device:TPU:0, one launch (start us, length us, event | category | flops | bytes accessed | tf_op | source)
XLA Modules:
  0.0 194.3 jit_solution(16307912457487664440)
XLA Ops:
  1.3 1.3 pad_bitcast_fusion.2.refs_3_.refs_7_
  2.6 1.3 cut_masters.1
  4.9 1.6 collective-permute-done.refs_2_.refs_6_
  7.2 4.0 %collective-permute-start.4 = (bf16[608,128]{1,0:T(8,128)(2,1)S(1)}, bf16[608,128]{1,0:T(8,128)(2,1)S(1)}, u32[]{:S(2)}, u32[]{:S(2)}) collective-permute-start(bf16[608,128]{1,0:T(8,128)(2,1)S(1)} %piece_attn.1.refs_0_.refs_4_), channel_id=1, source_target_pairs={{0,2},{1,3},{2,0},{3,1},{4,6},{5,7},{6,4},{7,5},{8,10},{9,11},{10,... | collective-permute-start | bytes 466952 | tf_op jit(solution)/shard_map/ppermute | solution.py:259
  11.3 5.3 %pack_rows.1 = (bf16[2048,768]{1,0:T(8,128)(2,1)}, bf16[2048,768]{1,0:T(8,128)(2,1)}, s32[64]{0:T(128)S(1)}) custom-call(s32[5]{0:T(128)S(1)} %stack.23.refs_0_.idx, s32[8]{0:T(128)S(1)} %copy-done.7, s32[8]{0:T(128)S(1)} %collective-permute-done.refs_2_.refs_6_, bf16[8,128,768]{2,1,0:T(8,128)(2,1)} %refs_3_.1, ...), custom_call_target="tpu_custom_call" | custom-call | flops 6000000000 | bytes 1 | tf_op jit(solution)/shard_map/pack_rows/pallas_call | solution.py:1064
  16.6 2.3 %collective-permute-done.4.refs_1_ = bf16[608,128]{1,0:T(8,128)(2,1)S(1)} collective-permute-done((bf16[608,128]{1,0:T(8,128)(2,1)S(1)}, bf16[608,128]{1,0:T(8,128)(2,1)S(1)}, u32[]{:S(2)}, u32[]{:S(2)}) %collective-permute-start.4) | collective-permute-done | bytes 155680 | tf_op jit(solution)/shard_map/ppermute | solution.py:259
  18.9 0.8 collective-permute-start.5
  20.3 1.6 collective-permute-start.13
  21.9 1.5 collective-permute-start.14
  23.4 3.4 %collective-permute-start.15 = (bf16[1152,128]{1,0:T(8,128)(2,1)S(1)}, bf16[1152,128]{1,0:T(8,128)(2,1)S(1)}, u32[]{:S(2)}, u32[]{:S(2)}) collective-permute-start(bf16[1152,128]{1,0:T(8,128)(2,1)S(1)} %piece_again.1), channel_id=1, source_target_pairs={{0,2},{1,3},{2,0},{3,1},{4,6},{5,7},{6,4},{7,5},{8,10},{9,11},{10,... | collective-permute-start | bytes 884744 | tf_op jit(solution)/shard_map/ppermute | solution.py:259
  26.9 2.2 %collective-permute-done.13.refs_9_.refs_10_ = bf16[1152,128]{1,0:T(8,128)(2,1)S(1)} collective-permute-done((bf16[1152,128]{1,0:T(8,128)(2,1)S(1)}, bf16[1152,128]{1,0:T(8,128)(2,1)S(1)}, u32[]{:S(2)}, u32[]{:S(2)}) %collective-permute-start.13) | collective-permute-done | bytes 294944 | tf_op jit(solution)/shard_map/ppermute | solution.py:259
  29.0 1.5 collective-permute-start.8
  30.6 1.5 collective-permute-start.6
  32.1 2.8 %collective-permute-start.7 = (bf16[2,608,128]{2,1,0:T(8,128)(2,1)S(1)}, bf16[2,608,128]{2,1,0:T(8,128)(2,1)S(1)}, u32[]{:S(2)}, u32[]{:S(2)}) collective-permute-start(bf16[2,608,128]{2,1,0:T(8,128)(2,1)S(1)} %collective-permute-done.5.refs_2_), channel_id=1, source_target_pairs={{0,8},{1,9},{2,10},{3,11},{4,12},{5,13},{6,14},{7,15},{8,0},{9,1},... | collective-permute-start | bytes 933896 | tf_op jit(solution)/shard_map/ppermute | solution.py:259
  34.9 4.8 %collective-permute-done.15.refs_11_.refs_8_ = bf16[1152,128]{1,0:T(8,128)(2,1)S(1)} collective-permute-done((bf16[1152,128]{1,0:T(8,128)(2,1)S(1)}, bf16[1152,128]{1,0:T(8,128)(2,1)S(1)}, u32[]{:S(2)}, u32[]{:S(2)}) %collective-permute-start.15) | collective-permute-done | bytes 294944 | tf_op jit(solution)/shard_map/ppermute | solution.py:259
  40.5 1.2 collective-permute-start.18
  41.7 1.5 collective-permute-start.9
  43.2 1.5 collective-permute-start.10
  44.7 2.8 %collective-permute-done.7.refs_4_.refs_1_ = bf16[2,608,128]{2,1,0:T(8,128)(2,1)S(1)} collective-permute-done((bf16[2,608,128]{2,1,0:T(8,128)(2,1)S(1)}, bf16[2,608,128]{2,1,0:T(8,128)(2,1)S(1)}, u32[]{:S(2)}, u32[]{:S(2)}) %collective-permute-start.7) | collective-permute-done | bytes 311328 | tf_op jit(solution)/shard_map/ppermute | solution.py:259
  47.5 1.2 collective-permute-start.11
  48.8 5.1 %collective-permute-done.20.refs_6_.refs_12_ = bf16[1152,128]{1,0:T(8,128)(2,1)S(1)} collective-permute-done((bf16[1152,128]{1,0:T(8,128)(2,1)S(1)}, bf16[1152,128]{1,0:T(8,128)(2,1)S(1)}, u32[]{:S(2)}, u32[]{:S(2)}) %collective-permute-start.20) | collective-permute-done | bytes 294944 | tf_op jit(solution)/shard_map/ppermute | solution.py:259
  53.8 1.2 collective-permute-start.27
  55.1 0.8 collective-permute-start.25
  55.9 4.6 %collective-permute-done.10.refs_7_ = bf16[2,608,128]{2,1,0:T(8,128)(2,1)S(1)} collective-permute-done((bf16[2,608,128]{2,1,0:T(8,128)(2,1)S(1)}, bf16[2,608,128]{2,1,0:T(8,128)(2,1)S(1)}, u32[]{:S(2)}, u32[]{:S(2)}) %collective-permute-start.10) | collective-permute-done | bytes 311328 | tf_op jit(solution)/shard_map/ppermute | solution.py:259
  60.5 1.2 collective-permute-start.23
  61.7 0.8 collective-permute-start.21
  62.5 2.5 %collective-permute-done.27.refs_4_.refs_20_ = bf16[1152,128]{1,0:T(8,128)(2,1)S(1)} collective-permute-done((bf16[1152,128]{1,0:T(8,128)(2,1)S(1)}, bf16[1152,128]{1,0:T(8,128)(2,1)S(1)}, u32[]{:S(2)}, u32[]{:S(2)}) %collective-permute-start.27) | collective-permute-done | bytes 294944 | tf_op jit(solution)/shard_map/ppermute | solution.py:259
  65.0 1.5 collective-permute-start.24
  67.4 1.4 collective-permute-start.26
  68.9 8.9 %attn_forward.1 = (bf16[2048,1152]{1,0:T(8,128)(2,1)}, bf16[2048,384]{1,0:T(8,128)(2,1)}, bf16[2048,768]{1,0:T(8,128)(2,1)}, bf16[768,1152]{1,0:T(8,128)(2,1)}, ...) custom-call(s32[64]{0:T(128)S(1)} %get-tuple-element.74.refs_2_.meta, ...), custom_call_target="tpu_custom_call" | custom-call | flops 11000000512 | bytes 1 | tf_op jit(solution)/shard_map/attn_forward/pallas_call | solution.py:1040
  77.8 1.5 collective-permute-start.19
  80.3 4.1 %collective-permute-done.19.refs_11_ = bf16[1152,128]{1,0:T(8,128)(2,1)S(1)} collective-permute-done((bf16[1152,128]{1,0:T(8,128)(2,1)S(1)}, bf16[1152,128]{1,0:T(8,128)(2,1)S(1)}, u32[]{:S(2)}, u32[]{:S(2)}) %collective-permute-start.19) | collective-permute-done | bytes 294944 | tf_op jit(solution)/shard_map/ppermute | solution.py:259
  84.5 1.5 collective-permute-done.22.refs_15_
  86.0 15.9 %mlp_both.1 = (bf16[2048,1536]{1,0:T(8,128)(2,1)}, bf16[2048,768]{1,0:T(8,128)(2,1)}, bf16[1536,768]{1,0:T(8,128)(2,1)}, f32[8,768]{1,0:T(8,128)S(1)}, f32[1,153...) custom-call(s32[64]{0:T(128)S(1)} %get-tuple-element.74.refs_2_.meta, ...), custom_call_target="tpu_custom_call" | custom-call | flops 23000000512 | bytes 1 | tf_op jit(solution)/shard_map/mlp_both/pallas_call | solution.py:1040
  102.0 1.0 collective-permute-start.34
  103.0 0.8 collective-permute-start.32
  103.8 5.2 %mlp_out.1.refs_9_.refs_3_ = bf16[2048,768]{1,0:T(8,128)(2,1)} custom-call(s32[64]{0:T(128)S(1)} %get-tuple-element.74.refs_2_.meta, s32[5]{0:T(128)S(1)} %stack.23.refs_0_.idx, bf16[2048,1536]{1,0:T(8,128)(2,1)} %get-tuple-element.84.refs_0_, bf16[1536,768]{1,0:T(8,128)(2,1)} %get-tuple-element.85.refs_1_), custom_call_target="tpu_custom_call" | custom-call | flops 20000000000 | bytes 1 | tf_op jit(solution)/shard_map/mlp_out/pallas_call | solution.py:1040
  109.0 1.2 collective-permute-start.31
  110.2 1.1 collective-permute-start.36
  111.3 6.8 %middle_backward.1 = (f32[2048,768]{1,0:T(8,128)}, bf16[2048,384]{1,0:T(8,128)(2,1)}, f32[384,768]{1,0:T(8,128)}, f32[8,768]{1,0:T(8,128)S(1)}) custom-call(s32[64]{0:T(128)S(1)} %get-tuple-element.74.refs_2_.meta, s32[5]{0:T(128)S(1)} %stack.23.refs_0_.idx, bf16[2048,768]{1,0:T(8,128)(2,1)} %get-tuple-element.75.refs_0_, ...), custom_call_target="tpu_custom_call" | custom-call | flops 8000000000 | bytes 1 | tf_op jit(solution)/shard_map/middle_backward/pallas_call | solution.py:1040
  118.3 1.3 collective-permute-start.35
  120.5 6.8 %heads_backward.1.refs_1_ = bf16[2048,1152]{1,0:T(8,128)(2,1)} custom-call(s32[64]{0:T(128)S(1)} %get-tuple-element.74.refs_2_.meta, s32[5]{0:T(128)S(1)} %stack.23.refs_0_.idx, bf16[2048,1152]{1,0:T(8,128)(2,1)} %get-tuple-element.95.refs_0_, bf16[2048,384]{1,0:T(8,128)(2,1)} %get-tuple-element.94.refs_2_.refs_1_, bf16[2,1152,128]{2,1,0:T(8,128)(2,1)S(1)} %aEm.1.refs_2_, ...), custom_call_target="tpu_custom_call" | custom-call | flops 24999999488 | bytes 1 | tf_op jit(solution)/shard_map/heads_backward/pallas_call | solution.py:1040
  127.3 7.6 %first_backward.1 = (bf16[2048,768]{1,0:T(8,128)(2,1)}, bf16[2,608,128]{2,1,0:T(8,128)(2,1)S(1)}, bf16[2,608,128]{2,1,0:T(8,128)(2,1)S(1)}, bf16[2,608,128]{2,1,...) custom-call(s32[64]{0:T(128)S(1)} %get-tuple-element.74.refs_2_.meta, ...), custom_call_target="tpu_custom_call" | custom-call | flops 24999999488 | bytes 1 | tf_op jit(solution)/shard_map/first_backward/pallas_call | solution.py:1040
  135.0 8.7 %collective-permute-done.35.refs_1_.refs_2_ = bf16[2,1152,128]{2,1,0:T(8,128)(2,1)S(1)} collective-permute-done((bf16[2,1152,128]{2,1,0:T(8,128)(2,1)S(1)}, bf16[2,1152,128]{2,1,0:T(8,128)(2,1)S(1)}, u32[]{:S(2)}, u32[]{:S(2)}) %collective-permute-start.35) | collective-permute-done | bytes 589856 | tf_op jit(solution)/shard_map/ppermute | solution.py:259
  143.9 1.2 collective-permute-start.40
  145.1 1.2 collective-permute-start.39
  146.3 4.8 %collective-permute-start.46 = (bf16[2,1152,128]{2,1,0:T(8,128)(2,1)S(1)}, bf16[2,1152,128]{2,1,0:T(8,128)(2,1)S(1)}, u32[]{:S(2)}, u32[]{:S(2)}) collective-permute-start(bf16[2,1152,128]{2,1,0:T(8,128)(2,1)S(1)} %get-tuple-element.119), channel_id=1, source_target_pairs={{0,1},{1,0},{2,3},{3,2},{4,5},{5,4},{6,7},{7,6},{8,9},{9,8},{10,11... | collective-permute-start | bytes 1769480 | tf_op jit(solution)/shard_map/ppermute | solution.py:259
  151.1 1.7 collective-permute-start.38
  152.8 0.9 collective-permute-done.40.refs_2_.refs_1_
  153.7 1.6 collective-permute-done.39.refs_1_
  155.4 0.9 collective-permute-start.41
  156.4 1.1 collective-permute-start.42
  157.6 3.7 %collective-permute-done.38.refs_1_ = bf16[2,608,128]{2,1,0:T(8,128)(2,1)S(1)} collective-permute-done((bf16[2,608,128]{2,1,0:T(8,128)(2,1)S(1)}, bf16[2,608,128]{2,1,0:T(8,128)(2,1)S(1)}, u32[]{:S(2)}, u32[]{:S(2)}) %collective-permute-start.38) | collective-permute-done | bytes 311328 | tf_op jit(solution)/shard_map/ppermute | solution.py:259
  161.2 1.2 collective-permute-start.43
  162.4 3.4 %collective-permute-done.41.refs_2_ = bf16[2,608,128]{2,1,0:T(8,128)(2,1)S(1)} collective-permute-done((bf16[2,608,128]{2,1,0:T(8,128)(2,1)S(1)}, bf16[2,608,128]{2,1,0:T(8,128)(2,1)S(1)}, u32[]{:S(2)}, u32[]{:S(2)}) %collective-permute-start.41) | collective-permute-done | bytes 311328 | tf_op jit(solution)/shard_map/ppermute | solution.py:259
  165.9 5.7 %collective-permute-start.44 = (bf16[2,608,128]{2,1,0:T(8,128)(2,1)S(1)}, bf16[2,608,128]{2,1,0:T(8,128)(2,1)S(1)}, u32[]{:S(2)}, u32[]{:S(2)}) collective-permute-start(bf16[2,608,128]{2,1,0:T(8,128)(2,1)S(1)} %soa.1.refs_9_), channel_id=1, source_target_pairs={{0,1},{1,0},{2,3},{3,2},{4,5},{5,4},{6,7},{7,6},{8,9},{9,8},{10,11... | collective-permute-start | bytes 933896 | tf_op jit(solution)/shard_map/ppermute | solution.py:259
  172.0 6.4 %finish_rows.1 = (bf16[8,128,768]{2,1,0:T(8,128)(2,1)}, bf16[8,128,768]{2,1,0:T(8,128)(2,1)}) custom-call(s32[64]{0:T(128)S(1)} %get-tuple-element.74.refs_2_.meta, s32[5]{0:T(128)S(1)} %stack.23.refs_0_.idx, bf16[2048,768]{1,0:T(8,128)(2,1)} %get-tuple-element.75.refs_0_, bf16[2048,768]{1,0:T(8,128)(2,1)} %get-tuple-element.80.refs_1_, ...), custom_call_target="tpu_custom_call" | custom-call | flops 8000000000 | bytes 1 | tf_op jit(solution)/shard_map/finish_rows/pallas_call | solution.py:1040
  178.4 1.1 collective-permute-done.44.refs_3_
  179.7 3.4 %collective-permute-done.47.refs_1_ = bf16[1152,128]{1,0:T(8,128)(2,1)S(1)} collective-permute-done((bf16[1152,128]{1,0:T(8,128)(2,1)S(1)}, bf16[1152,128]{1,0:T(8,128)(2,1)S(1)}, u32[]{:S(2)}, u32[]{:S(2)}) %collective-permute-start.47) | collective-permute-done | bytes 294944 | tf_op jit(solution)/shard_map/ppermute | solution.py:259
  183.5 1.3 collective-permute-done.48.refs_6_
  184.9 2.1 %step_mlp.1 = (f32[1152,128]{1,0:T(8,128)}, f32[1152,128]{1,0:T(8,128)}, f32[1152,128]{1,0:T(8,128)}) custom-call(s32[5]{0:T(128)S(1)} %stack.23.refs_0_.idx, f32[1152,128]{1,0:T(8,128)S(1)} %bitcast.30, f32[1152,128]{1,0:T(8,128)S(1)} %bitcast.31, f32[1152,128]{1,0:T(8,128)S(1)} %bitcast.32, f32[576,128]{1,0:T(8,128)S(1)} %get-tuple-element.122.refs_4_, ...), custom_call_target="tpu_custom_call" | custom-call | flops 1000000000 | bytes 1 | tf_op jit(solution)/shard_map/step_mlp/pallas_call | solution.py:1064
  187.0 4.0 %collective-permute-done.45.refs_1_ = bf16[608,128]{1,0:T(8,128)(2,1)S(1)} collective-permute-done((bf16[608,128]{1,0:T(8,128)(2,1)S(1)}, bf16[608,128]{1,0:T(8,128)(2,1)S(1)}, u32[]{:S(2)}, u32[]{:S(2)}) %collective-permute-start.45) | collective-permute-done | bytes 155680 | tf_op jit(solution)/shard_map/ppermute | solution.py:259
  191.6 0.9 collective-permute-done.50.refs_11_
  192.5 1.8 step_attn.1
  (89 shorter events, 9.2 us)
Async XLA Ops:
  0.6 3.8 %copy-start.7 = (s32[8]{0:T(128)S(1)}, s32[8]{0:T(128)}, u32[]{:S(2)}) copy-start(s32[8]{0:T(128)} %refs_1_.1) | copy-start | bytes 100
  0.7 5.9 %collective-permute-start.1 = (bf16[8,128,768]{2,1,0:T(8,128)(2,1)}, bf16[8,128,768]{2,1,0:T(8,128)(2,1)S(1)}, u32[]{:S(2)}, u32[]{:S(2)}) collective-permute-start(bf16[8,128,768]{2,1,0:T(8,128)(2,1)} %refs_3_.1), channel_id=1, source_target_pairs={{0,4},{1,5},{2,6},{3,7},{4,0},{5,1},{6,2},{7,3},{8,12},{9,13},{10,... | collective-permute-start | bytes 4718600 | tf_op jit(solution)/shard_map/ppermute | solution.py:259
  1.2 5.5 %collective-permute-start.2 = (bf16[8,128,768]{2,1,0:T(8,128)(2,1)}, bf16[8,128,768]{2,1,0:T(8,128)(2,1)S(1)}, u32[]{:S(2)}, u32[]{:S(2)}) collective-permute-start(bf16[8,128,768]{2,1,0:T(8,128)(2,1)} %refs_5_.1), channel_id=1, source_target_pairs={{0,4},{1,5},{2,6},{3,7},{4,0},{5,1},{6,2},{7,3},{8,12},{9,13},{10,... | collective-permute-start | bytes 4718600 | tf_op jit(solution)/shard_map/ppermute | solution.py:259
  3.9 2.6 %collective-permute-start.3 = (bf16[304,128]{1,0:T(8,128)(2,1)S(1)}, bf16[304,128]{1,0:T(8,128)(2,1)S(1)}, u32[]{:S(2)}, u32[]{:S(2)}) collective-permute-start(bf16[304,128]{1,0:T(8,128)(2,1)S(1)} %get-tuple-element.77.refs_2_), channel_id=1, source_target_pairs={{0,4},{1,5},{2,6},{3,7},{4,0},{5,1},{6,2},{7,3},{8,12},{9,13},{10,... | collective-permute-start | bytes 233480 | tf_op jit(solution)/shard_map/ppermute | solution.py:259
  4.4 2.1 %collective-permute-start = (s32[8]{0:T(128)S(1)}, s32[8]{0:T(128)S(1)}, u32[]{:S(2)}, u32[]{:S(2)}) collective-permute-start(s32[8]{0:T(128)S(1)} %copy-done.7), channel_id=1, source_target_pairs={{0,4},{1,5},{2,6},{3,7},{4,0},{5,1},{6,2},{7,3},{8,12},{9,13},{10,... | collective-permute-start | bytes 104 | tf_op jit(solution)/shard_map/ppermute | solution.py:259
  4.5 15.2 %collective-permute-start.12 = (bf16[576,128]{1,0:T(8,128)(2,1)S(1)}, bf16[576,128]{1,0:T(8,128)(2,1)S(1)}, u32[]{:S(2)}, u32[]{:S(2)}) collective-permute-start(bf16[576,128]{1,0:T(8,128)(2,1)S(1)} %get-tuple-element.79.refs_2_), channel_id=1, source_target_pairs={{0,4},{1,5},{2,6},{3,7},{4,0},{5,1},{6,2},{7,3},{8,12},{9,13},{10,... | collective-permute-start | bytes 442376 | tf_op jit(solution)/shard_map/ppermute | solution.py:259
  7.2 11.7 %collective-permute-start.4 = (bf16[608,128]{1,0:T(8,128)(2,1)S(1)}, bf16[608,128]{1,0:T(8,128)(2,1)S(1)}, u32[]{:S(2)}, u32[]{:S(2)}) collective-permute-start(bf16[608,128]{1,0:T(8,128)(2,1)S(1)} %piece_attn.1.refs_0_.refs_4_), channel_id=1, source_target_pairs={{0,2},{1,3},{2,0},{3,1},{4,6},{5,7},{6,4},{7,5},{8,10},{9,11},{10,... | collective-permute-start | bytes 466952 | tf_op jit(solution)/shard_map/ppermute | solution.py:259
  18.9 13.1 %collective-permute-start.5 = (bf16[2,608,128]{2,1,0:T(8,128)(2,1)S(1)}, bf16[2,608,128]{2,1,0:T(8,128)(2,1)S(1)}, u32[]{:S(2)}, u32[]{:S(2)}) collective-permute-start(bf16[2,608,128]{2,1,0:T(8,128)(2,1)S(1)} %pair_up.1.refs_1_), channel_id=1, source_target_pairs={{0,1},{1,0},{2,3},{3,2},{4,5},{5,4},{6,7},{7,6},{8,9},{9,8},{10,11... | collective-permute-start | bytes 933896 | tf_op jit(solution)/shard_map/ppermute | solution.py:259
  20.3 8.7 %collective-permute-start.13 = (bf16[1152,128]{1,0:T(8,128)(2,1)S(1)}, bf16[1152,128]{1,0:T(8,128)(2,1)S(1)}, u32[]{:S(2)}, u32[]{:S(2)}) collective-permute-start(bf16[1152,128]{1,0:T(8,128)(2,1)S(1)} %piece_mlp.1.refs_0_.refs_6_), channel_id=1, source_target_pairs={{0,8},{1,9},{2,10},{3,11},{4,12},{5,13},{6,14},{7,15},{8,0},{9,1},... | collective-permute-start | bytes 884744 | tf_op jit(solution)/shard_map/ppermute | solution.py:259
  21.9 8.7 %collective-permute-start.14 = (bf16[1152,128]{1,0:T(8,128)(2,1)S(1)}, bf16[1152,128]{1,0:T(8,128)(2,1)S(1)}, u32[]{:S(2)}, u32[]{:S(2)}) collective-permute-start(bf16[1152,128]{1,0:T(8,128)(2,1)S(1)} %piece_mlp.1.refs_0_.refs_6_), channel_id=1, source_target_pairs={{0,16},{1,17},{2,18},{3,19},{4,20},{5,21},{6,22},{7,23},{8,24},{9,... | collective-permute-start | bytes 884744 | tf_op jit(solution)/shard_map/ppermute | solution.py:259
  23.4 16.3 %collective-permute-start.15 = (bf16[1152,128]{1,0:T(8,128)(2,1)S(1)}, bf16[1152,128]{1,0:T(8,128)(2,1)S(1)}, u32[]{:S(2)}, u32[]{:S(2)}) collective-permute-start(bf16[1152,128]{1,0:T(8,128)(2,1)S(1)} %piece_again.1), channel_id=1, source_target_pairs={{0,2},{1,3},{2,0},{3,1},{4,6},{5,7},{6,4},{7,5},{8,10},{9,11},{10,... | collective-permute-start | bytes 884744 | tf_op jit(solution)/shard_map/ppermute | solution.py:259
  26.8 13.7 %collective-permute-start.17 = (bf16[1152,128]{1,0:T(8,128)(2,1)S(1)}, bf16[1152,128]{1,0:T(8,128)(2,1)S(1)}, u32[]{:S(2)}, u32[]{:S(2)}) collective-permute-start(bf16[1152,128]{1,0:T(8,128)(2,1)S(1)} %piece_mlp.1.refs_0_.refs_6_), channel_id=1, source_target_pairs={{0,1},{1,0},{2,3},{3,2},{4,5},{5,4},{6,7},{7,6},{8,9},{9,8},{10,11... | collective-permute-start | bytes 884744 | tf_op jit(solution)/shard_map/ppermute | solution.py:259
  29.0 12.7 %collective-permute-start.8 = (bf16[2,608,128]{2,1,0:T(8,128)(2,1)S(1)}, bf16[2,608,128]{2,1,0:T(8,128)(2,1)S(1)}, u32[]{:S(2)}, u32[]{:S(2)}) collective-permute-start(bf16[2,608,128]{2,1,0:T(8,128)(2,1)S(1)} %pair_up.1.refs_1_), channel_id=1, source_target_pairs={{0,16},{1,17},{2,18},{3,19},{4,20},{5,21},{6,22},{7,23},{8,24},{9,... | collective-permute-start | bytes 933896 | tf_op jit(solution)/shard_map/ppermute | solution.py:259
  30.6 12.7 %collective-permute-start.6 = (bf16[2,608,128]{2,1,0:T(8,128)(2,1)S(1)}, bf16[2,608,128]{2,1,0:T(8,128)(2,1)S(1)}, u32[]{:S(2)}, u32[]{:S(2)}) collective-permute-start(bf16[2,608,128]{2,1,0:T(8,128)(2,1)S(1)} %pair_up.1.refs_1_), channel_id=1, source_target_pairs={{0,8},{1,9},{2,10},{3,11},{4,12},{5,13},{6,14},{7,15},{8,0},{9,1},... | collective-permute-start | bytes 933896 | tf_op jit(solution)/shard_map/ppermute | solution.py:259
  32.1 15.5 %collective-permute-start.7 = (bf16[2,608,128]{2,1,0:T(8,128)(2,1)S(1)}, bf16[2,608,128]{2,1,0:T(8,128)(2,1)S(1)}, u32[]{:S(2)}, u32[]{:S(2)}) collective-permute-start(bf16[2,608,128]{2,1,0:T(8,128)(2,1)S(1)} %collective-permute-done.5.refs_2_), channel_id=1, source_target_pairs={{0,8},{1,9},{2,10},{3,11},{4,12},{5,13},{6,14},{7,15},{8,0},{9,1},... | collective-permute-start | bytes 933896 | tf_op jit(solution)/shard_map/ppermute | solution.py:259
  39.7 14.2 %collective-permute-start.20 = (bf16[1152,128]{1,0:T(8,128)(2,1)S(1)}, bf16[1152,128]{1,0:T(8,128)(2,1)S(1)}, u32[]{:S(2)}, u32[]{:S(2)}) collective-permute-start(bf16[1152,128]{1,0:T(8,128)(2,1)S(1)} %collective-permute-done.15.refs_11_.refs_8_), channel_id=1, source_target_pairs={{0,8},{1,9},{2,10},{3,11},{4,12},{5,13},{6,14},{7,15},{8,0},{9,1},... | collective-permute-start | bytes 884744 | tf_op jit(solution)/shard_map/ppermute | solution.py:259
  40.5 14.5 %collective-permute-start.18 = (bf16[1152,128]{1,0:T(8,128)(2,1)S(1)}, bf16[1152,128]{1,0:T(8,128)(2,1)S(1)}, u32[]{:S(2)}, u32[]{:S(2)}) collective-permute-start(bf16[1152,128]{1,0:T(8,128)(2,1)S(1)} %collective-permute-done.15.refs_11_.refs_8_), channel_id=1, source_target_pairs={{0,1},{1,0},{2,3},{3,2},{4,5},{5,4},{6,7},{7,6},{8,9},{9,8},{10,11... | collective-permute-start | bytes 884744 | tf_op jit(solution)/shard_map/ppermute | solution.py:259
  41.7 20.0 %collective-permute-start.9 = (bf16[2,608,128]{2,1,0:T(8,128)(2,1)S(1)}, bf16[2,608,128]{2,1,0:T(8,128)(2,1)S(1)}, u32[]{:S(2)}, u32[]{:S(2)}) collective-permute-start(bf16[2,608,128]{2,1,0:T(8,128)(2,1)S(1)} %collective-permute-done.5.refs_2_), channel_id=1, source_target_pairs={{0,16},{1,17},{2,18},{3,19},{4,20},{5,21},{6,22},{7,23},{8,24},{9,... | collective-permute-start | bytes 933896 | tf_op jit(solution)/shard_map/ppermute | solution.py:259
  43.2 17.3 %collective-permute-start.10 = (bf16[2,608,128]{2,1,0:T(8,128)(2,1)S(1)}, bf16[2,608,128]{2,1,0:T(8,128)(2,1)S(1)}, u32[]{:S(2)}, u32[]{:S(2)}) collective-permute-start(bf16[2,608,128]{2,1,0:T(8,128)(2,1)S(1)} %collective-permute-done.8.refs_5_), channel_id=1, source_target_pairs={{0,8},{1,9},{2,10},{3,11},{4,12},{5,13},{6,14},{7,15},{8,0},{9,1},... | collective-permute-start | bytes 933896 | tf_op jit(solution)/shard_map/ppermute | solution.py:259
  47.5 19.9 %collective-permute-start.11 = (bf16[2,608,128]{2,1,0:T(8,128)(2,1)S(1)}, bf16[2,608,128]{2,1,0:T(8,128)(2,1)S(1)}, u32[]{:S(2)}, u32[]{:S(2)}) collective-permute-start(bf16[2,608,128]{2,1,0:T(8,128)(2,1)S(1)} %collective-permute-done.7.refs_4_.refs_1_), channel_id=1, source_target_pairs={{0,16},{1,17},{2,18},{3,19},{4,20},{5,21},{6,22},{7,23},{8,24},{9,... | collective-permute-start | bytes 933896 | tf_op jit(solution)/shard_map/ppermute | solution.py:259
  53.8 11.2 %collective-permute-start.27 = (bf16[1152,128]{1,0:T(8,128)(2,1)S(1)}, bf16[1152,128]{1,0:T(8,128)(2,1)S(1)}, u32[]{:S(2)}, u32[]{:S(2)}) collective-permute-start(bf16[1152,128]{1,0:T(8,128)(2,1)S(1)} %collective-permute-done.20.refs_6_.refs_12_), channel_id=1, source_target_pairs={{0,16},{1,17},{2,18},{3,19},{4,20},{5,21},{6,22},{7,23},{8,24},{9,... | collective-permute-start | bytes 884744 | tf_op jit(solution)/shard_map/ppermute | solution.py:259
  55.1 11.8 %collective-permute-start.25 = (bf16[1152,128]{1,0:T(8,128)(2,1)S(1)}, bf16[1152,128]{1,0:T(8,128)(2,1)S(1)}, u32[]{:S(2)}, u32[]{:S(2)}) collective-permute-start(bf16[1152,128]{1,0:T(8,128)(2,1)S(1)} %hold_own.1), channel_id=1, source_target_pairs={{0,8},{1,9},{2,10},{3,11},{4,12},{5,13},{6,14},{7,15},{8,0},{9,1},... | collective-permute-start | bytes 884744 | tf_op jit(solution)/shard_map/ppermute | solution.py:259
  60.5 19.8 %collective-permute-start.23 = (bf16[1152,128]{1,0:T(8,128)(2,1)S(1)}, bf16[1152,128]{1,0:T(8,128)(2,1)S(1)}, u32[]{:S(2)}, u32[]{:S(2)}) collective-permute-start(bf16[1152,128]{1,0:T(8,128)(2,1)S(1)} %collective-permute-done.15.refs_11_.refs_8_), channel_id=1, source_target_pairs={{0,16},{1,17},{2,18},{3,19},{4,20},{5,21},{6,22},{7,23},{8,24},{9,... | collective-permute-start | bytes 884744 | tf_op jit(solution)/shard_map/ppermute | solution.py:259
  61.7 16.0 %collective-permute-start.21 = (bf16[1152,128]{1,0:T(8,128)(2,1)S(1)}, bf16[1152,128]{1,0:T(8,128)(2,1)S(1)}, u32[]{:S(2)}, u32[]{:S(2)}) collective-permute-start(bf16[1152,128]{1,0:T(8,128)(2,1)S(1)} %collective-permute-done.18.refs_9_), channel_id=1, source_target_pairs={{0,8},{1,9},{2,10},{3,11},{4,12},{5,13},{6,14},{7,15},{8,0},{9,1},... | collective-permute-start | bytes 884744 | tf_op jit(solution)/shard_map/ppermute | solution.py:259
  65.0 14.2 %collective-permute-start.24 = (bf16[1152,128]{1,0:T(8,128)(2,1)S(1)}, bf16[1152,128]{1,0:T(8,128)(2,1)S(1)}, u32[]{:S(2)}, u32[]{:S(2)}) collective-permute-start(bf16[1152,128]{1,0:T(8,128)(2,1)S(1)} %collective-permute-done.18.refs_9_), channel_id=1, source_target_pairs={{0,16},{1,17},{2,18},{3,19},{4,20},{5,21},{6,22},{7,23},{8,24},{9,... | collective-permute-start | bytes 884744 | tf_op jit(solution)/shard_map/ppermute | solution.py:259
  66.8 12.9 %collective-permute-start.28 = (bf16[1152,128]{1,0:T(8,128)(2,1)S(1)}, bf16[1152,128]{1,0:T(8,128)(2,1)S(1)}, u32[]{:S(2)}, u32[]{:S(2)}) collective-permute-start(bf16[1152,128]{1,0:T(8,128)(2,1)S(1)} %collective-permute-done.27.refs_4_.refs_20_), channel_id=1, source_target_pairs={{0,1},{1,0},{2,3},{3,2},{4,5},{5,4},{6,7},{7,6},{8,9},{9,8},{10,11... | collective-permute-start | bytes 884744 | tf_op jit(solution)/shard_map/ppermute | solution.py:259
  67.4 12.3 %collective-permute-start.26 = (bf16[1152,128]{1,0:T(8,128)(2,1)S(1)}, bf16[1152,128]{1,0:T(8,128)(2,1)S(1)}, u32[]{:S(2)}, u32[]{:S(2)}) collective-permute-start(bf16[1152,128]{1,0:T(8,128)(2,1)S(1)} %collective-permute-done.25.refs_7_.refs_18_), channel_id=1, source_target_pairs={{0,1},{1,0},{2,3},{3,2},{4,5},{5,4},{6,7},{7,6},{8,9},{9,8},{10,11... | collective-permute-start | bytes 884744 | tf_op jit(solution)/shard_map/ppermute | solution.py:259
  77.8 6.7 %collective-permute-start.19 = (bf16[1152,128]{1,0:T(8,128)(2,1)S(1)}, bf16[1152,128]{1,0:T(8,128)(2,1)S(1)}, u32[]{:S(2)}, u32[]{:S(2)}) collective-permute-start(bf16[1152,128]{1,0:T(8,128)(2,1)S(1)} %hold_first.1), channel_id=1, source_target_pairs={{0,8},{1,9},{2,10},{3,11},{4,12},{5,13},{6,14},{7,15},{8,0},{9,1},... | collective-permute-start | bytes 884744 | tf_op jit(solution)/shard_map/ppermute | solution.py:259
  79.2 6.7 %collective-permute-start.22 = (bf16[1152,128]{1,0:T(8,128)(2,1)S(1)}, bf16[1152,128]{1,0:T(8,128)(2,1)S(1)}, u32[]{:S(2)}, u32[]{:S(2)}) collective-permute-start(bf16[1152,128]{1,0:T(8,128)(2,1)S(1)} %hold_first.1), channel_id=1, source_target_pairs={{0,16},{1,17},{2,18},{3,19},{4,20},{5,21},{6,22},{7,23},{8,24},{9,... | collective-permute-start | bytes 884744 | tf_op jit(solution)/shard_map/ppermute | solution.py:259
  79.8 6.2 %collective-permute-start.16 = (bf16[2048,768]{1,0:T(8,128)(2,1)}, bf16[2048,768]{1,0:T(8,128)(2,1)S(1)}, u32[]{:S(2)}, u32[]{:S(2)}) collective-permute-start(bf16[2048,768]{1,0:T(8,128)(2,1)} %get-tuple-element.80.refs_1_), channel_id=1, source_target_pairs={{0,4},{1,5},{2,6},{3,7},{4,0},{5,1},{6,2},{7,3},{8,12},{9,13},{10,... | collective-permute-start | bytes 9437192 | tf_op jit(solution)/shard_map/ppermute | solution.py:259
  101.9 8.3 %collective-permute-start.30 = (bf16[2048,768]{1,0:T(8,128)(2,1)}, bf16[2048,768]{1,0:T(8,128)(2,1)S(1)}, u32[]{:S(2)}, u32[]{:S(2)}) collective-permute-start(bf16[2048,768]{1,0:T(8,128)(2,1)} %get-tuple-element.86.refs_4_), channel_id=1, source_target_pairs={{0,4},{1,5},{2,6},{3,7},{4,0},{5,1},{6,2},{7,3},{8,12},{9,13},{10,... | collective-permute-start | bytes 9437192 | tf_op jit(solution)/shard_map/ppermute | solution.py:259
  102.0 16.2 %collective-permute-start.34 = (bf16[2,1152,128]{2,1,0:T(8,128)(2,1)S(1)}, bf16[2,1152,128]{2,1,0:T(8,128)(2,1)S(1)}, u32[]{:S(2)}, u32[]{:S(2)}) collective-permute-start(bf16[2,1152,128]{2,1,0:T(8,128)(2,1)S(1)} %get-tuple-element.97), channel_id=1, source_target_pairs={{0,8},{1,9},{2,10},{3,11},{4,12},{5,13},{6,14},{7,15},{8,0},{9,1},... | collective-permute-start | bytes 1769480 | tf_op jit(solution)/shard_map/ppermute | solution.py:259
  103.0 16.6 %collective-permute-start.32 = (bf16[2,1152,128]{2,1,0:T(8,128)(2,1)S(1)}, bf16[2,1152,128]{2,1,0:T(8,128)(2,1)S(1)}, u32[]{:S(2)}, u32[]{:S(2)}) collective-permute-start(bf16[2,1152,128]{2,1,0:T(8,128)(2,1)S(1)} %get-tuple-element.93), channel_id=1, source_target_pairs={{0,16},{1,17},{2,18},{3,19},{4,20},{5,21},{6,22},{7,23},{8,24},{9,... | collective-permute-start | bytes 1769480 | tf_op jit(solution)/shard_map/ppermute | solution.py:259
  109.0 18.3 %collective-permute-start.29 = (bf16[2048,768]{1,0:T(8,128)(2,1)}, bf16[2048,768]{1,0:T(8,128)(2,1)S(1)}, u32[]{:S(2)}, u32[]{:S(2)}) collective-permute-start(bf16[2048,768]{1,0:T(8,128)(2,1)} %mlp_out.1.refs_9_.refs_3_), channel_id=1, source_target_pairs={{0,4},{1,5},{2,6},{3,7},{4,0},{5,1},{6,2},{7,3},{8,12},{9,13},{10,... | collective-permute-start | bytes 9437192 | tf_op jit(solution)/shard_map/ppermute | solution.py:259
  109.0 26.0 %collective-permute-start.31 = (bf16[2,1152,128]{2,1,0:T(8,128)(2,1)S(1)}, bf16[2,1152,128]{2,1,0:T(8,128)(2,1)S(1)}, u32[]{:S(2)}, u32[]{:S(2)}) collective-permute-start(bf16[2,1152,128]{2,1,0:T(8,128)(2,1)S(1)} %get-tuple-element.91), channel_id=1, source_target_pairs={{0,16},{1,17},{2,18},{3,19},{4,20},{5,21},{6,22},{7,23},{8,24},{9,... | collective-permute-start | bytes 1769480 | tf_op jit(solution)/shard_map/ppermute | solution.py:259
  110.2 24.7 %collective-permute-start.36 = (bf16[2,1152,128]{2,1,0:T(8,128)(2,1)S(1)}, bf16[2,1152,128]{2,1,0:T(8,128)(2,1)S(1)}, u32[]{:S(2)}, u32[]{:S(2)}) collective-permute-start(bf16[2,1152,128]{2,1,0:T(8,128)(2,1)S(1)} %get-tuple-element.104), channel_id=1, source_target_pairs={{0,8},{1,9},{2,10},{3,11},{4,12},{5,13},{6,14},{7,15},{8,0},{9,1},... | collective-permute-start | bytes 1769480 | tf_op jit(solution)/shard_map/ppermute | solution.py:259
  118.3 25.3 %collective-permute-start.35 = (bf16[2,1152,128]{2,1,0:T(8,128)(2,1)S(1)}, bf16[2,1152,128]{2,1,0:T(8,128)(2,1)S(1)}, u32[]{:S(2)}, u32[]{:S(2)}) collective-permute-start(bf16[2,1152,128]{2,1,0:T(8,128)(2,1)S(1)} %aEm.1.refs_2_), channel_id=1, source_target_pairs={{0,16},{1,17},{2,18},{3,19},{4,20},{5,21},{6,22},{7,23},{8,24},{9,... | collective-permute-start | bytes 1769480 | tf_op jit(solution)/shard_map/ppermute | solution.py:259
  119.8 23.8 %collective-permute-start.33 = (bf16[2,1152,128]{2,1,0:T(8,128)(2,1)S(1)}, bf16[2,1152,128]{2,1,0:T(8,128)(2,1)S(1)}, u32[]{:S(2)}, u32[]{:S(2)}) collective-permute-start(bf16[2,1152,128]{2,1,0:T(8,128)(2,1)S(1)} %aOm.1.refs_3_), channel_id=1, source_target_pairs={{0,8},{1,9},{2,10},{3,11},{4,12},{5,13},{6,14},{7,15},{8,0},{9,1},... | collective-permute-start | bytes 1769480 | tf_op jit(solution)/shard_map/ppermute | solution.py:259
  143.8 28.2 %collective-permute-start.37 = (bf16[2048,768]{1,0:T(8,128)(2,1)}, bf16[2048,768]{1,0:T(8,128)(2,1)S(1)}, u32[]{:S(2)}, u32[]{:S(2)}) collective-permute-start(bf16[2048,768]{1,0:T(8,128)(2,1)} %get-tuple-element.105.refs_6_), channel_id=1, source_target_pairs={{0,4},{1,5},{2,6},{3,7},{4,0},{5,1},{6,2},{7,3},{8,12},{9,13},{10,... | collective-permute-start | bytes 9437192 | tf_op jit(solution)/shard_map/ppermute | solution.py:259
  143.9 9.8 %collective-permute-start.40 = (bf16[2,608,128]{2,1,0:T(8,128)(2,1)S(1)}, bf16[2,608,128]{2,1,0:T(8,128)(2,1)S(1)}, u32[]{:S(2)}, u32[]{:S(2)}) collective-permute-start(bf16[2,608,128]{2,1,0:T(8,128)(2,1)S(1)} %get-tuple-element.110), channel_id=1, source_target_pairs={{0,8},{1,9},{2,10},{3,11},{4,12},{5,13},{6,14},{7,15},{8,0},{9,1},... | collective-permute-start | bytes 933896 | tf_op jit(solution)/shard_map/ppermute | solution.py:259
  145.1 10.2 %collective-permute-start.39 = (bf16[2,608,128]{2,1,0:T(8,128)(2,1)S(1)}, bf16[2,608,128]{2,1,0:T(8,128)(2,1)S(1)}, u32[]{:S(2)}, u32[]{:S(2)}) collective-permute-start(bf16[2,608,128]{2,1,0:T(8,128)(2,1)S(1)} %get-tuple-element.109), channel_id=1, source_target_pairs={{0,16},{1,17},{2,18},{3,19},{4,20},{5,21},{6,22},{7,23},{8,24},{9,... | collective-permute-start | bytes 933896 | tf_op jit(solution)/shard_map/ppermute | solution.py:259
  146.3 25.3 %collective-permute-start.46 = (bf16[2,1152,128]{2,1,0:T(8,128)(2,1)S(1)}, bf16[2,1152,128]{2,1,0:T(8,128)(2,1)S(1)}, u32[]{:S(2)}, u32[]{:S(2)}) collective-permute-start(bf16[2,1152,128]{2,1,0:T(8,128)(2,1)S(1)} %get-tuple-element.119), channel_id=1, source_target_pairs={{0,1},{1,0},{2,3},{3,2},{4,5},{5,4},{6,7},{7,6},{8,9},{9,8},{10,11... | collective-permute-start | bytes 1769480 | tf_op jit(solution)/shard_map/ppermute | solution.py:259
  151.1 10.1 %collective-permute-start.38 = (bf16[2,608,128]{2,1,0:T(8,128)(2,1)S(1)}, bf16[2,608,128]{2,1,0:T(8,128)(2,1)S(1)}, u32[]{:S(2)}, u32[]{:S(2)}) collective-permute-start(bf16[2,608,128]{2,1,0:T(8,128)(2,1)S(1)} %get-tuple-element.107), channel_id=1, source_target_pairs={{0,16},{1,17},{2,18},{3,19},{4,20},{5,21},{6,22},{7,23},{8,24},{9,... | collective-permute-start | bytes 933896 | tf_op jit(solution)/shard_map/ppermute | solution.py:259
  155.4 10.4 %collective-permute-start.41 = (bf16[2,608,128]{2,1,0:T(8,128)(2,1)S(1)}, bf16[2,608,128]{2,1,0:T(8,128)(2,1)S(1)}, u32[]{:S(2)}, u32[]{:S(2)}) collective-permute-start(bf16[2,608,128]{2,1,0:T(8,128)(2,1)S(1)} %aOa.1), channel_id=1, source_target_pairs={{0,8},{1,9},{2,10},{3,11},{4,12},{5,13},{6,14},{7,15},{8,0},{9,1},... | collective-permute-start | bytes 933896 | tf_op jit(solution)/shard_map/ppermute | solution.py:259
  156.4 22.1 %collective-permute-start.42 = (bf16[2,608,128]{2,1,0:T(8,128)(2,1)S(1)}, bf16[2,608,128]{2,1,0:T(8,128)(2,1)S(1)}, u32[]{:S(2)}, u32[]{:S(2)}) collective-permute-start(bf16[2,608,128]{2,1,0:T(8,128)(2,1)S(1)} %get-tuple-element.115), channel_id=1, source_target_pairs={{0,8},{1,9},{2,10},{3,11},{4,12},{5,13},{6,14},{7,15},{8,0},{9,1},... | collective-permute-start | bytes 933896 | tf_op jit(solution)/shard_map/ppermute | solution.py:259
  161.2 17.2 %collective-permute-start.43 = (bf16[2,608,128]{2,1,0:T(8,128)(2,1)S(1)}, bf16[2,608,128]{2,1,0:T(8,128)(2,1)S(1)}, u32[]{:S(2)}, u32[]{:S(2)}) collective-permute-start(bf16[2,608,128]{2,1,0:T(8,128)(2,1)S(1)} %aEa.1.refs_3_.refs_4_), channel_id=1, source_target_pairs={{0,16},{1,17},{2,18},{3,19},{4,20},{5,21},{6,22},{7,23},{8,24},{9,... | collective-permute-start | bytes 933896 | tf_op jit(solution)/shard_map/ppermute | solution.py:259
  165.9 13.6 %collective-permute-start.44 = (bf16[2,608,128]{2,1,0:T(8,128)(2,1)S(1)}, bf16[2,608,128]{2,1,0:T(8,128)(2,1)S(1)}, u32[]{:S(2)}, u32[]{:S(2)}) collective-permute-start(bf16[2,608,128]{2,1,0:T(8,128)(2,1)S(1)} %soa.1.refs_9_), channel_id=1, source_target_pairs={{0,1},{1,0},{2,3},{3,2},{4,5},{5,4},{6,7},{7,6},{8,9},{9,8},{10,11... | collective-permute-start | bytes 933896 | tf_op jit(solution)/shard_map/ppermute | solution.py:259
  171.9 11.1 %collective-permute-start.47 = (bf16[1152,128]{1,0:T(8,128)(2,1)S(1)}, bf16[1152,128]{1,0:T(8,128)(2,1)S(1)}, u32[]{:S(2)}, u32[]{:S(2)}) collective-permute-start(bf16[1152,128]{1,0:T(8,128)(2,1)S(1)} %get-tuple-element.121), channel_id=1, source_target_pairs={{0,2},{1,3},{2,0},{3,1},{4,6},{5,7},{6,4},{7,5},{8,10},{9,11},{10,... | collective-permute-start | bytes 884744 | tf_op jit(solution)/shard_map/ppermute | solution.py:259
  179.5 5.3 %copy-start.1 = (f32[147456]{0:T(1024)S(1)}, f32[147456]{0:T(1024)}, u32[]{:S(2)}) copy-start(f32[147456]{0:T(1024)} %param.18) | copy-start | bytes 1769476
  179.5 5.3 %copy-start.2 = (f32[147456]{0:T(1024)S(1)}, f32[147456]{0:T(1024)}, u32[]{:S(2)}) copy-start(f32[147456]{0:T(1024)} %param.19) | copy-start | bytes 1769476
  179.5 5.3 %copy-start.3 = (f32[147456]{0:T(1024)S(1)}, f32[147456]{0:T(1024)}, u32[]{:S(2)}) copy-start(f32[147456]{0:T(1024)} %param.20) | copy-start | bytes 1769476
  183.1 1.6 collective-permute-start.48
  183.2 7.8 %collective-permute-start.45 = (bf16[608,128]{1,0:T(8,128)(2,1)S(1)}, bf16[608,128]{1,0:T(8,128)(2,1)S(1)}, u32[]{:S(2)}, u32[]{:S(2)}) collective-permute-start(bf16[608,128]{1,0:T(8,128)(2,1)S(1)} %get-tuple-element.117.refs_2_), channel_id=1, source_target_pairs={{0,2},{1,3},{2,0},{3,1},{4,6},{5,7},{6,4},{7,5},{8,10},{9,11},{10,... | collective-permute-start | bytes 466952 | tf_op jit(solution)/shard_map/ppermute | solution.py:259
  184.8 6.8 %copy-start.8 = (f32[288]{0:T(512)S(1)}, f32[288]{0:T(512)}, u32[]{:S(2)}) copy-start(f32[288]{0:T(512)} %param.23) | copy-start | bytes 3460
  184.8 6.8 %copy-start.9 = (f32[288]{0:T(512)S(1)}, f32[288]{0:T(512)}, u32[]{:S(2)}) copy-start(f32[288]{0:T(512)} %param.22) | copy-start | bytes 3460
  184.8 7.7 %copy-start = (f32[3,128]{1,0:T(4,128)S(1)}, f32[3,128]{1,0:T(4,128)}, u32[]{:S(2)}) copy-start(f32[3,128]{1,0:T(4,128)} %pad_bitcast_fusion.2.refs_3_.refs_7_) | copy-start | bytes 4612
  184.8 7.7 %copy-start.4 = (f32[73728]{0:T(1024)S(1)}, f32[73728]{0:T(1024)}, u32[]{:S(2)}) copy-start(f32[73728]{0:T(1024)} %param.15) | copy-start | bytes 884740
  184.8 7.7 %copy-start.5 = (f32[73728]{0:T(1024)S(1)}, f32[73728]{0:T(1024)}, u32[]{:S(2)}) copy-start(f32[73728]{0:T(1024)} %param.16) | copy-start | bytes 884740
  184.9 7.7 %copy-start.6 = (f32[73728]{0:T(1024)S(1)}, f32[73728]{0:T(1024)}, u32[]{:S(2)}) copy-start(f32[73728]{0:T(1024)} %param.17) | copy-start | bytes 884740
  191.0 1.5 collective-permute-start.49
  191.2 1.3 collective-permute-start.50

commit v6 on v5

--- a/solution.py
+++ b/solution.py
@@ -641,21 +641,22 @@
             mask = same_sample(meta, pl.program_id(0) * (BLOCK // BIN) + b)
             mask = jnp.concatenate([mask, mask], axis=1)
             rows = slice(b * BIN, (b + 1) * BIN)
+            cols = [[slice((3 * t + h) * ROW, (3 * t + h + 1) * ROW) for t in range(3)] for h in range(3)]
+            both = [halves(qkv_ref[rows, cols[h][0]]) for h in range(3)]
+            outs = [halves(grad_context_ref[rows, h * ROW : (h + 1) * ROW]) for h in range(3)]
+            probs = [probabilities_by_key(both[h], qkv_ref[rows, cols[h][1]], mask) for h in range(3)]
+            grad_probs = [dot(qkv_ref[rows, cols[h][2]], outs[h], ((1,), (1,))) for h in range(3)]
             for h in range(3):
-                cols = [slice((3 * t + h) * ROW, (3 * t + h + 1) * ROW) for t in range(3)]
-                query, keys, values = (qkv_ref[rows, cols[t]] for t in range(3))
-                both = halves(query)
-                probs = probabilities_by_key(both, keys, mask)
-                grad_out = halves(grad_context_ref[rows, h * ROW : (h + 1) * ROW])
-                grad_values = dot(probs.astype(bf16), grad_out)
-                grad_probs = dot(values, grad_out, ((1,), (1,)))
-                total = jnp.sum(grad_probs * probs, 0, keepdims=True)
-                grad_scores = (probs * (grad_probs - total)).astype(bf16)
-                grad_keys = dot(grad_scores, both) * scale
-                grad_query = dot(one_above_other(grad_scores), halves(keys), ((0,), (0,))) * scale
-                grads[rows, cols[0]] = grad_query.astype(bf16)
-                grads[rows, cols[1]] = grad_keys.astype(bf16)
-                grads[rows, cols[2]] = grad_values.astype(bf16)
+                grads[rows, cols[h][2]] = dot(probs[h].astype(bf16), outs[h]).astype(bf16)
+            scores = []
+            for h in range(3):
+                total = jnp.sum(grad_probs[h] * probs[h], 0, keepdims=True)
+                scores.append((probs[h] * (grad_probs[h] - total)).astype(bf16))
+            for h in range(3):
+                grads[rows, cols[h][1]] = (dot(scores[h], both[h]) * scale).astype(bf16)
+            for h in range(3):
+                keys = halves(qkv_ref[rows, cols[h][1]])
+                grads[rows, cols[h][0]] = (dot(one_above_other(scores[h]), keys, ((0,), (0,))) * scale).astype(bf16)
 
 
 def first_backward(phase, meta, idx, x_ref, grads, w_qkv, acc_out, vecs, sums_in, inner_sum, sums_out, *refs):

time: 197 us -> 196 us (level)
  waiting for transfers between devices: 61.3 us -> 63.6 us
    ppermute x51, waiting for transfers between devices: 61.3 us -> 63.6 us  [send(): return lax.ppermute(value, AXES, pairs)]
  transfers between devices with their start and end apart: 51 -> 51, of which waited for: 24 -> 24; matrix products, arithmetic and copies ran while one was open for 1% -> 1% of each run, Pallas kernels for 27% -> 26%
where the time goes in v6:
time: 196 us; the launch traced here: 195 us
  Pallas kernels  69.5 us (35%)
  waiting for transfers between devices  63.6 us (32%)
  starting transfers between devices  59.1 us (30%)
    ppermute x51, waiting for transfers between devices, send(): return lax.ppermute(value, AXES, pairs)  63.6 us
    ppermute x51, starting transfers between devices, send(): return lax.ppermute(value, AXES, pairs)  59.1 us
    pallas_call x7, Pallas kernels, called(): pl.pallas_call(kernel, in_specs=[SMEM, SMEM] + [ANY] * n_in + fixed_specs...  55.9 us
    pallas_call x20, Pallas kernels, called(): pl.pallas_call(kernel, in_specs=[SMEM] * scalars + blocks + [ANY] * len(a...  13.4 us
  transfers between devices with their start and end apart: 51, of which 24 were waited for; matrix products, arithmetic and copies ran while one was open for 1% of the time, Pallas kernels for 26%

profile of v6, /device:TPU:0, one launch (start us, length us, event | category | flops | bytes accessed | tf_op | source)
XLA Modules:
  0.0 194.5 jit_solution(6240022560462877320)
XLA Ops:
  1.3 1.3 pad_bitcast_fusion.2.refs_3_.refs_7_
  2.6 1.3 cut_masters.1
  4.9 1.6 collective-permute-done.refs_2_.refs_6_
  7.2 4.0 %collective-permute-start.4 = (bf16[608,128]{1,0:T(8,128)(2,1)S(1)}, bf16[608,128]{1,0:T(8,128)(2,1)S(1)}, u32[]{:S(2)}, u32[]{:S(2)}) collective-permute-start(bf16[608,128]{1,0:T(8,128)(2,1)S(1)} %piece_attn.1.refs_0_.refs_4_), channel_id=1, source_target_pairs={{0,2},{1,3},{2,0},{3,1},{4,6},{5,7},{6,4},{7,5},{8,10},{9,11},{10,... | collective-permute-start | bytes 466952 | tf_op jit(solution)/shard_map/ppermute | solution.py:259
  11.3 5.3 %pack_rows.1 = (bf16[2048,768]{1,0:T(8,128)(2,1)}, bf16[2048,768]{1,0:T(8,128)(2,1)}, s32[64]{0:T(128)S(1)}) custom-call(s32[5]{0:T(128)S(1)} %stack.23.refs_0_.idx, s32[8]{0:T(128)S(1)} %copy-done.7, s32[8]{0:T(128)S(1)} %collective-permute-done.refs_2_.refs_6_, bf16[8,128,768]{2,1,0:T(8,128)(2,1)} %refs_3_.1, ...), custom_call_target="tpu_custom_call" | custom-call | flops 6000000000 | bytes 1 | tf_op jit(solution)/shard_map/pack_rows/pallas_call | solution.py:1065
  16.6 2.3 %collective-permute-done.4.refs_1_ = bf16[608,128]{1,0:T(8,128)(2,1)S(1)} collective-permute-done((bf16[608,128]{1,0:T(8,128)(2,1)S(1)}, bf16[608,128]{1,0:T(8,128)(2,1)S(1)}, u32[]{:S(2)}, u32[]{:S(2)}) %collective-permute-start.4) | collective-permute-done | bytes 155680 | tf_op jit(solution)/shard_map/ppermute | solution.py:259
  18.9 0.8 collective-permute-start.5
  20.3 1.6 collective-permute-start.13
  21.9 1.5 collective-permute-start.14
  23.4 3.4 %collective-permute-start.15 = (bf16[1152,128]{1,0:T(8,128)(2,1)S(1)}, bf16[1152,128]{1,0:T(8,128)(2,1)S(1)}, u32[]{:S(2)}, u32[]{:S(2)}) collective-permute-start(bf16[1152,128]{1,0:T(8,128)(2,1)S(1)} %piece_again.1), channel_id=1, source_target_pairs={{0,2},{1,3},{2,0},{3,1},{4,6},{5,7},{6,4},{7,5},{8,10},{9,11},{10,... | collective-permute-start | bytes 884744 | tf_op jit(solution)/shard_map/ppermute | solution.py:259
  26.9 2.2 %collective-permute-done.13.refs_9_.refs_10_ = bf16[1152,128]{1,0:T(8,128)(2,1)S(1)} collective-permute-done((bf16[1152,128]{1,0:T(8,128)(2,1)S(1)}, bf16[1152,128]{1,0:T(8,128)(2,1)S(1)}, u32[]{:S(2)}, u32[]{:S(2)}) %collective-permute-start.13) | collective-permute-done | bytes 294944 | tf_op jit(solution)/shard_map/ppermute | solution.py:259
  29.0 1.5 collective-permute-start.8
  30.6 1.5 collective-permute-start.6
  32.1 2.8 %collective-permute-start.7 = (bf16[2,608,128]{2,1,0:T(8,128)(2,1)S(1)}, bf16[2,608,128]{2,1,0:T(8,128)(2,1)S(1)}, u32[]{:S(2)}, u32[]{:S(2)}) collective-permute-start(bf16[2,608,128]{2,1,0:T(8,128)(2,1)S(1)} %collective-permute-done.5.refs_2_), channel_id=1, source_target_pairs={{0,8},{1,9},{2,10},{3,11},{4,12},{5,13},{6,14},{7,15},{8,0},{9,1},... | collective-permute-start | bytes 933896 | tf_op jit(solution)/shard_map/ppermute | solution.py:259
  34.9 4.8 %collective-permute-done.15.refs_11_.refs_8_ = bf16[1152,128]{1,0:T(8,128)(2,1)S(1)} collective-permute-done((bf16[1152,128]{1,0:T(8,128)(2,1)S(1)}, bf16[1152,128]{1,0:T(8,128)(2,1)S(1)}, u32[]{:S(2)}, u32[]{:S(2)}) %collective-permute-start.15) | collective-permute-done | bytes 294944 | tf_op jit(solution)/shard_map/ppermute | solution.py:259
  40.5 1.2 collective-permute-start.18
  41.7 1.5 collective-permute-start.9
  43.2 1.5 collective-permute-start.10
  44.7 2.8 %collective-permute-done.7.refs_4_.refs_1_ = bf16[2,608,128]{2,1,0:T(8,128)(2,1)S(1)} collective-permute-done((bf16[2,608,128]{2,1,0:T(8,128)(2,1)S(1)}, bf16[2,608,128]{2,1,0:T(8,128)(2,1)S(1)}, u32[]{:S(2)}, u32[]{:S(2)}) %collective-permute-start.7) | collective-permute-done | bytes 311328 | tf_op jit(solution)/shard_map/ppermute | solution.py:259
  47.5 1.2 collective-permute-start.11
  48.8 5.1 %collective-permute-done.20.refs_6_.refs_12_ = bf16[1152,128]{1,0:T(8,128)(2,1)S(1)} collective-permute-done((bf16[1152,128]{1,0:T(8,128)(2,1)S(1)}, bf16[1152,128]{1,0:T(8,128)(2,1)S(1)}, u32[]{:S(2)}, u32[]{:S(2)}) %collective-permute-start.20) | collective-permute-done | bytes 294944 | tf_op jit(solution)/shard_map/ppermute | solution.py:259
  53.8 1.2 collective-permute-start.27
  55.1 0.8 collective-permute-start.25
  55.9 4.6 %collective-permute-done.10.refs_7_ = bf16[2,608,128]{2,1,0:T(8,128)(2,1)S(1)} collective-permute-done((bf16[2,608,128]{2,1,0:T(8,128)(2,1)S(1)}, bf16[2,608,128]{2,1,0:T(8,128)(2,1)S(1)}, u32[]{:S(2)}, u32[]{:S(2)}) %collective-permute-start.10) | collective-permute-done | bytes 311328 | tf_op jit(solution)/shard_map/ppermute | solution.py:259
  60.5 1.2 collective-permute-start.23
  61.7 0.8 collective-permute-start.21
  62.5 2.5 %collective-permute-done.27.refs_4_.refs_20_ = bf16[1152,128]{1,0:T(8,128)(2,1)S(1)} collective-permute-done((bf16[1152,128]{1,0:T(8,128)(2,1)S(1)}, bf16[1152,128]{1,0:T(8,128)(2,1)S(1)}, u32[]{:S(2)}, u32[]{:S(2)}) %collective-permute-start.27) | collective-permute-done | bytes 294944 | tf_op jit(solution)/shard_map/ppermute | solution.py:259
  65.0 1.5 collective-permute-start.24
  67.4 1.4 collective-permute-start.26
  68.9 8.9 %attn_forward.1 = (bf16[2048,1152]{1,0:T(8,128)(2,1)}, bf16[2048,384]{1,0:T(8,128)(2,1)}, bf16[2048,768]{1,0:T(8,128)(2,1)}, bf16[768,1152]{1,0:T(8,128)(2,1)}, ...) custom-call(s32[64]{0:T(128)S(1)} %get-tuple-element.74.refs_2_.meta, ...), custom_call_target="tpu_custom_call" | custom-call | flops 11000000512 | bytes 1 | tf_op jit(solution)/shard_map/attn_forward/pallas_call | solution.py:1041
  77.8 1.5 collective-permute-start.19
  80.3 4.1 %collective-permute-done.19.refs_11_ = bf16[1152,128]{1,0:T(8,128)(2,1)S(1)} collective-permute-done((bf16[1152,128]{1,0:T(8,128)(2,1)S(1)}, bf16[1152,128]{1,0:T(8,128)(2,1)S(1)}, u32[]{:S(2)}, u32[]{:S(2)}) %collective-permute-start.19) | collective-permute-done | bytes 294944 | tf_op jit(solution)/shard_map/ppermute | solution.py:259
  84.5 1.5 collective-permute-done.22.refs_15_
  86.0 15.9 %mlp_both.1 = (bf16[2048,1536]{1,0:T(8,128)(2,1)}, bf16[2048,768]{1,0:T(8,128)(2,1)}, bf16[1536,768]{1,0:T(8,128)(2,1)}, f32[8,768]{1,0:T(8,128)S(1)}, f32[1,153...) custom-call(s32[64]{0:T(128)S(1)} %get-tuple-element.74.refs_2_.meta, ...), custom_call_target="tpu_custom_call" | custom-call | flops 23000000512 | bytes 1 | tf_op jit(solution)/shard_map/mlp_both/pallas_call | solution.py:1041
  102.0 1.0 collective-permute-start.34
  103.0 0.8 collective-permute-start.32
  103.8 5.2 %mlp_out.1.refs_9_.refs_3_ = bf16[2048,768]{1,0:T(8,128)(2,1)} custom-call(s32[64]{0:T(128)S(1)} %get-tuple-element.74.refs_2_.meta, s32[5]{0:T(128)S(1)} %stack.23.refs_0_.idx, bf16[2048,1536]{1,0:T(8,128)(2,1)} %get-tuple-element.84.refs_0_, bf16[1536,768]{1,0:T(8,128)(2,1)} %get-tuple-element.85.refs_1_), custom_call_target="tpu_custom_call" | custom-call | flops 20000000000 | bytes 1 | tf_op jit(solution)/shard_map/mlp_out/pallas_call | solution.py:1041
  109.0 1.2 collective-permute-start.31
  110.2 1.1 collective-permute-start.36
  111.3 6.8 %middle_backward.1 = (f32[2048,768]{1,0:T(8,128)}, bf16[2048,384]{1,0:T(8,128)(2,1)}, f32[384,768]{1,0:T(8,128)}, f32[8,768]{1,0:T(8,128)S(1)}) custom-call(s32[64]{0:T(128)S(1)} %get-tuple-element.74.refs_2_.meta, s32[5]{0:T(128)S(1)} %stack.23.refs_0_.idx, bf16[2048,768]{1,0:T(8,128)(2,1)} %get-tuple-element.75.refs_0_, ...), custom_call_target="tpu_custom_call" | custom-call | flops 8000000000 | bytes 1 | tf_op jit(solution)/shard_map/middle_backward/pallas_call | solution.py:1041
  118.3 1.3 collective-permute-start.35
  119.8 0.7 collective-permute-start.33
  120.5 5.1 %heads_backward.1.refs_1_ = bf16[2048,1152]{1,0:T(8,128)(2,1)} custom-call(s32[64]{0:T(128)S(1)} %get-tuple-element.74.refs_2_.meta, s32[5]{0:T(128)S(1)} %stack.23.refs_0_.idx, bf16[2048,1152]{1,0:T(8,128)(2,1)} %get-tuple-element.95.refs_0_, bf16[2048,384]{1,0:T(8,128)(2,1)} %get-tuple-element.94.refs_2_.refs_1_, bf16[2,1152,128]{2,1,0:T(8,128)(2,1)S(1)} %aEm.1.refs_2_, ...), custom_call_target="tpu_custom_call" | custom-call | flops 24999999488 | bytes 1 | tf_op jit(solution)/shard_map/heads_backward/pallas_call | solution.py:1041
  125.5 7.6 %first_backward.1 = (bf16[2048,768]{1,0:T(8,128)(2,1)}, bf16[2,608,128]{2,1,0:T(8,128)(2,1)S(1)}, bf16[2,608,128]{2,1,0:T(8,128)(2,1)S(1)}, bf16[2,608,128]{2,1,...) custom-call(s32[64]{0:T(128)S(1)} %get-tuple-element.74.refs_2_.meta, ...), custom_call_target="tpu_custom_call" | custom-call | flops 24999999488 | bytes 1 | tf_op jit(solution)/shard_map/first_backward/pallas_call | solution.py:1041
  133.2 10.5 %collective-permute-done.35.refs_1_.refs_2_ = bf16[2,1152,128]{2,1,0:T(8,128)(2,1)S(1)} collective-permute-done((bf16[2,1152,128]{2,1,0:T(8,128)(2,1)S(1)}, bf16[2,1152,128]{2,1,0:T(8,128)(2,1)S(1)}, u32[]{:S(2)}, u32[]{:S(2)}) %collective-permute-start.35) | collective-permute-done | bytes 589856 | tf_op jit(solution)/shard_map/ppermute | solution.py:259
  143.9 1.2 collective-permute-start.40
  145.1 1.2 collective-permute-start.39
  146.3 5.7 %collective-permute-start.46 = (bf16[2,1152,128]{2,1,0:T(8,128)(2,1)S(1)}, bf16[2,1152,128]{2,1,0:T(8,128)(2,1)S(1)}, u32[]{:S(2)}, u32[]{:S(2)}) collective-permute-start(bf16[2,1152,128]{2,1,0:T(8,128)(2,1)S(1)} %get-tuple-element.119), channel_id=1, source_target_pairs={{0,1},{1,0},{2,3},{3,2},{4,5},{5,4},{6,7},{7,6},{8,9},{9,8},{10,11... | collective-permute-start | bytes 1769480 | tf_op jit(solution)/shard_map/ppermute | solution.py:259
  152.3 1.4 collective-permute-done.40.refs_2_.refs_1_
  153.7 1.1 collective-permute-done.39.refs_1_
  154.9 1.4 collective-permute-start.41
  156.4 0.7 collective-permute-start.42
  157.1 4.1 %collective-permute-done.38.refs_1_ = bf16[2,608,128]{2,1,0:T(8,128)(2,1)S(1)} collective-permute-done((bf16[2,608,128]{2,1,0:T(8,128)(2,1)S(1)}, bf16[2,608,128]{2,1,0:T(8,128)(2,1)S(1)}, u32[]{:S(2)}, u32[]{:S(2)}) %collective-permute-start.38) | collective-permute-done | bytes 311328 | tf_op jit(solution)/shard_map/ppermute | solution.py:259
  161.2 1.2 collective-permute-start.43
  162.4 2.9 %collective-permute-done.41.refs_2_ = bf16[2,608,128]{2,1,0:T(8,128)(2,1)S(1)} collective-permute-done((bf16[2,608,128]{2,1,0:T(8,128)(2,1)S(1)}, bf16[2,608,128]{2,1,0:T(8,128)(2,1)S(1)}, u32[]{:S(2)}, u32[]{:S(2)}) %collective-permute-start.41) | collective-permute-done | bytes 311328 | tf_op jit(solution)/shard_map/ppermute | solution.py:259
  165.4 5.7 %collective-permute-start.44 = (bf16[2,608,128]{2,1,0:T(8,128)(2,1)S(1)}, bf16[2,608,128]{2,1,0:T(8,128)(2,1)S(1)}, u32[]{:S(2)}, u32[]{:S(2)}) collective-permute-start(bf16[2,608,128]{2,1,0:T(8,128)(2,1)S(1)} %soa.1.refs_9_), channel_id=1, source_target_pairs={{0,1},{1,0},{2,3},{3,2},{4,5},{5,4},{6,7},{7,6},{8,9},{9,8},{10,11... | collective-permute-start | bytes 933896 | tf_op jit(solution)/shard_map/ppermute | solution.py:259
  171.5 6.4 %finish_rows.1 = (bf16[8,128,768]{2,1,0:T(8,128)(2,1)}, bf16[8,128,768]{2,1,0:T(8,128)(2,1)}) custom-call(s32[64]{0:T(128)S(1)} %get-tuple-element.74.refs_2_.meta, s32[5]{0:T(128)S(1)} %stack.23.refs_0_.idx, bf16[2048,768]{1,0:T(8,128)(2,1)} %get-tuple-element.75.refs_0_, bf16[2048,768]{1,0:T(8,128)(2,1)} %get-tuple-element.80.refs_1_, ...), custom_call_target="tpu_custom_call" | custom-call | flops 8000000000 | bytes 1 | tf_op jit(solution)/shard_map/finish_rows/pallas_call | solution.py:1041
  177.9 1.3 collective-permute-done.44.refs_3_
  179.4 4.0 %collective-permute-done.47.refs_1_ = bf16[1152,128]{1,0:T(8,128)(2,1)S(1)} collective-permute-done((bf16[1152,128]{1,0:T(8,128)(2,1)S(1)}, bf16[1152,128]{1,0:T(8,128)(2,1)S(1)}, u32[]{:S(2)}, u32[]{:S(2)}) %collective-permute-start.47) | collective-permute-done | bytes 294944 | tf_op jit(solution)/shard_map/ppermute | solution.py:259
  184.1 1.0 collective-permute-done.48.refs_6_
  185.2 2.1 %step_mlp.1 = (f32[1152,128]{1,0:T(8,128)}, f32[1152,128]{1,0:T(8,128)}, f32[1152,128]{1,0:T(8,128)}) custom-call(s32[5]{0:T(128)S(1)} %stack.23.refs_0_.idx, f32[1152,128]{1,0:T(8,128)S(1)} %bitcast.30, f32[1152,128]{1,0:T(8,128)S(1)} %bitcast.31, f32[1152,128]{1,0:T(8,128)S(1)} %bitcast.32, f32[576,128]{1,0:T(8,128)S(1)} %get-tuple-element.122.refs_4_, ...), custom_call_target="tpu_custom_call" | custom-call | flops 1000000000 | bytes 1 | tf_op jit(solution)/shard_map/step_mlp/pallas_call | solution.py:1065
  187.3 4.0 %collective-permute-done.45.refs_1_ = bf16[608,128]{1,0:T(8,128)(2,1)S(1)} collective-permute-done((bf16[608,128]{1,0:T(8,128)(2,1)S(1)}, bf16[608,128]{1,0:T(8,128)(2,1)S(1)}, u32[]{:S(2)}, u32[]{:S(2)}) %collective-permute-start.45) | collective-permute-done | bytes 155680 | tf_op jit(solution)/shard_map/ppermute | solution.py:259
  191.9 0.9 collective-permute-done.50.refs_11_
  192.8 1.8 step_attn.1
  (89 shorter events, 9.0 us)
Async XLA Ops:
  0.6 3.8 %copy-start.7 = (s32[8]{0:T(128)S(1)}, s32[8]{0:T(128)}, u32[]{:S(2)}) copy-start(s32[8]{0:T(128)} %refs_1_.1) | copy-start | bytes 100
  0.7 5.9 %collective-permute-start.1 = (bf16[8,128,768]{2,1,0:T(8,128)(2,1)}, bf16[8,128,768]{2,1,0:T(8,128)(2,1)S(1)}, u32[]{:S(2)}, u32[]{:S(2)}) collective-permute-start(bf16[8,128,768]{2,1,0:T(8,128)(2,1)} %refs_3_.1), channel_id=1, source_target_pairs={{0,4},{1,5},{2,6},{3,7},{4,0},{5,1},{6,2},{7,3},{8,12},{9,13},{10,... | collective-permute-start | bytes 4718600 | tf_op jit(solution)/shard_map/ppermute | solution.py:259
  1.2 5.5 %collective-permute-start.2 = (bf16[8,128,768]{2,1,0:T(8,128)(2,1)}, bf16[8,128,768]{2,1,0:T(8,128)(2,1)S(1)}, u32[]{:S(2)}, u32[]{:S(2)}) collective-permute-start(bf16[8,128,768]{2,1,0:T(8,128)(2,1)} %refs_5_.1), channel_id=1, source_target_pairs={{0,4},{1,5},{2,6},{3,7},{4,0},{5,1},{6,2},{7,3},{8,12},{9,13},{10,... | collective-permute-start | bytes 4718600 | tf_op jit(solution)/shard_map/ppermute | solution.py:259
  3.9 2.6 %collective-permute-start.3 = (bf16[304,128]{1,0:T(8,128)(2,1)S(1)}, bf16[304,128]{1,0:T(8,128)(2,1)S(1)}, u32[]{:S(2)}, u32[]{:S(2)}) collective-permute-start(bf16[304,128]{1,0:T(8,128)(2,1)S(1)} %get-tuple-element.77.refs_2_), channel_id=1, source_target_pairs={{0,4},{1,5},{2,6},{3,7},{4,0},{5,1},{6,2},{7,3},{8,12},{9,13},{10,... | collective-permute-start | bytes 233480 | tf_op jit(solution)/shard_map/ppermute | solution.py:259
  4.4 2.1 %collective-permute-start = (s32[8]{0:T(128)S(1)}, s32[8]{0:T(128)S(1)}, u32[]{:S(2)}, u32[]{:S(2)}) collective-permute-start(s32[8]{0:T(128)S(1)} %copy-done.7), channel_id=1, source_target_pairs={{0,4},{1,5},{2,6},{3,7},{4,0},{5,1},{6,2},{7,3},{8,12},{9,13},{10,... | collective-permute-start | bytes 104 | tf_op jit(solution)/shard_map/ppermute | solution.py:259
  4.5 15.2 %collective-permute-start.12 = (bf16[576,128]{1,0:T(8,128)(2,1)S(1)}, bf16[576,128]{1,0:T(8,128)(2,1)S(1)}, u32[]{:S(2)}, u32[]{:S(2)}) collective-permute-start(bf16[576,128]{1,0:T(8,128)(2,1)S(1)} %get-tuple-element.79.refs_2_), channel_id=1, source_target_pairs={{0,4},{1,5},{2,6},{3,7},{4,0},{5,1},{6,2},{7,3},{8,12},{9,13},{10,... | collective-permute-start | bytes 442376 | tf_op jit(solution)/shard_map/ppermute | solution.py:259
  7.2 11.7 %collective-permute-start.4 = (bf16[608,128]{1,0:T(8,128)(2,1)S(1)}, bf16[608,128]{1,0:T(8,128)(2,1)S(1)}, u32[]{:S(2)}, u32[]{:S(2)}) collective-permute-start(bf16[608,128]{1,0:T(8,128)(2,1)S(1)} %piece_attn.1.refs_0_.refs_4_), channel_id=1, source_target_pairs={{0,2},{1,3},{2,0},{3,1},{4,6},{5,7},{6,4},{7,5},{8,10},{9,11},{10,... | collective-permute-start | bytes 466952 | tf_op jit(solution)/shard_map/ppermute | solution.py:259
  18.9 13.1 %collective-permute-start.5 = (bf16[2,608,128]{2,1,0:T(8,128)(2,1)S(1)}, bf16[2,608,128]{2,1,0:T(8,128)(2,1)S(1)}, u32[]{:S(2)}, u32[]{:S(2)}) collective-permute-start(bf16[2,608,128]{2,1,0:T(8,128)(2,1)S(1)} %pair_up.1.refs_1_), channel_id=1, source_target_pairs={{0,1},{1,0},{2,3},{3,2},{4,5},{5,4},{6,7},{7,6},{8,9},{9,8},{10,11... | collective-permute-start | bytes 933896 | tf_op jit(solution)/shard_map/ppermute | solution.py:259
  20.3 8.7 %collective-permute-start.13 = (bf16[1152,128]{1,0:T(8,128)(2,1)S(1)}, bf16[1152,128]{1,0:T(8,128)(2,1)S(1)}, u32[]{:S(2)}, u32[]{:S(2)}) collective-permute-start(bf16[1152,128]{1,0:T(8,128)(2,1)S(1)} %piece_mlp.1.refs_0_.refs_6_), channel_id=1, source_target_pairs={{0,8},{1,9},{2,10},{3,11},{4,12},{5,13},{6,14},{7,15},{8,0},{9,1},... | collective-permute-start | bytes 884744 | tf_op jit(solution)/shard_map/ppermute | solution.py:259
  21.9 8.7 %collective-permute-start.14 = (bf16[1152,128]{1,0:T(8,128)(2,1)S(1)}, bf16[1152,128]{1,0:T(8,128)(2,1)S(1)}, u32[]{:S(2)}, u32[]{:S(2)}) collective-permute-start(bf16[1152,128]{1,0:T(8,128)(2,1)S(1)} %piece_mlp.1.refs_0_.refs_6_), channel_id=1, source_target_pairs={{0,16},{1,17},{2,18},{3,19},{4,20},{5,21},{6,22},{7,23},{8,24},{9,... | collective-permute-start | bytes 884744 | tf_op jit(solution)/shard_map/ppermute | solution.py:259
  23.4 16.3 %collective-permute-start.15 = (bf16[1152,128]{1,0:T(8,128)(2,1)S(1)}, bf16[1152,128]{1,0:T(8,128)(2,1)S(1)}, u32[]{:S(2)}, u32[]{:S(2)}) collective-permute-start(bf16[1152,128]{1,0:T(8,128)(2,1)S(1)} %piece_again.1), channel_id=1, source_target_pairs={{0,2},{1,3},{2,0},{3,1},{4,6},{5,7},{6,4},{7,5},{8,10},{9,11},{10,... | collective-permute-start | bytes 884744 | tf_op jit(solution)/shard_map/ppermute | solution.py:259
  26.8 13.7 %collective-permute-start.17 = (bf16[1152,128]{1,0:T(8,128)(2,1)S(1)}, bf16[1152,128]{1,0:T(8,128)(2,1)S(1)}, u32[]{:S(2)}, u32[]{:S(2)}) collective-permute-start(bf16[1152,128]{1,0:T(8,128)(2,1)S(1)} %piece_mlp.1.refs_0_.refs_6_), channel_id=1, source_target_pairs={{0,1},{1,0},{2,3},{3,2},{4,5},{5,4},{6,7},{7,6},{8,9},{9,8},{10,11... | collective-permute-start | bytes 884744 | tf_op jit(solution)/shard_map/ppermute | solution.py:259
  29.0 12.7 %collective-permute-start.8 = (bf16[2,608,128]{2,1,0:T(8,128)(2,1)S(1)}, bf16[2,608,128]{2,1,0:T(8,128)(2,1)S(1)}, u32[]{:S(2)}, u32[]{:S(2)}) collective-permute-start(bf16[2,608,128]{2,1,0:T(8,128)(2,1)S(1)} %pair_up.1.refs_1_), channel_id=1, source_target_pairs={{0,16},{1,17},{2,18},{3,19},{4,20},{5,21},{6,22},{7,23},{8,24},{9,... | collective-permute-start | bytes 933896 | tf_op jit(solution)/shard_map/ppermute | solution.py:259
  30.6 12.7 %collective-permute-start.6 = (bf16[2,608,128]{2,1,0:T(8,128)(2,1)S(1)}, bf16[2,608,128]{2,1,0:T(8,128)(2,1)S(1)}, u32[]{:S(2)}, u32[]{:S(2)}) collective-permute-start(bf16[2,608,128]{2,1,0:T(8,128)(2,1)S(1)} %pair_up.1.refs_1_), channel_id=1, source_target_pairs={{0,8},{1,9},{2,10},{3,11},{4,12},{5,13},{6,14},{7,15},{8,0},{9,1},... | collective-permute-start | bytes 933896 | tf_op jit(solution)/shard_map/ppermute | solution.py:259
  32.1 15.5 %collective-permute-start.7 = (bf16[2,608,128]{2,1,0:T(8,128)(2,1)S(1)}, bf16[2,608,128]{2,1,0:T(8,128)(2,1)S(1)}, u32[]{:S(2)}, u32[]{:S(2)}) collective-permute-start(bf16[2,608,128]{2,1,0:T(8,128)(2,1)S(1)} %collective-permute-done.5.refs_2_), channel_id=1, source_target_pairs={{0,8},{1,9},{2,10},{3,11},{4,12},{5,13},{6,14},{7,15},{8,0},{9,1},... | collective-permute-start | bytes 933896 | tf_op jit(solution)/shard_map/ppermute | solution.py:259
  39.7 14.2 %collective-permute-start.20 = (bf16[1152,128]{1,0:T(8,128)(2,1)S(1)}, bf16[1152,128]{1,0:T(8,128)(2,1)S(1)}, u32[]{:S(2)}, u32[]{:S(2)}) collective-permute-start(bf16[1152,128]{1,0:T(8,128)(2,1)S(1)} %collective-permute-done.15.refs_11_.refs_8_), channel_id=1, source_target_pairs={{0,8},{1,9},{2,10},{3,11},{4,12},{5,13},{6,14},{7,15},{8,0},{9,1},... | collective-permute-start | bytes 884744 | tf_op jit(solution)/shard_map/ppermute | solution.py:259
  40.5 14.5 %collective-permute-start.18 = (bf16[1152,128]{1,0:T(8,128)(2,1)S(1)}, bf16[1152,128]{1,0:T(8,128)(2,1)S(1)}, u32[]{:S(2)}, u32[]{:S(2)}) collective-permute-start(bf16[1152,128]{1,0:T(8,128)(2,1)S(1)} %collective-permute-done.15.refs_11_.refs_8_), channel_id=1, source_target_pairs={{0,1},{1,0},{2,3},{3,2},{4,5},{5,4},{6,7},{7,6},{8,9},{9,8},{10,11... | collective-permute-start | bytes 884744 | tf_op jit(solution)/shard_map/ppermute | solution.py:259
  41.7 20.0 %collective-permute-start.9 = (bf16[2,608,128]{2,1,0:T(8,128)(2,1)S(1)}, bf16[2,608,128]{2,1,0:T(8,128)(2,1)S(1)}, u32[]{:S(2)}, u32[]{:S(2)}) collective-permute-start(bf16[2,608,128]{2,1,0:T(8,128)(2,1)S(1)} %collective-permute-done.5.refs_2_), channel_id=1, source_target_pairs={{0,16},{1,17},{2,18},{3,19},{4,20},{5,21},{6,22},{7,23},{8,24},{9,... | collective-permute-start | bytes 933896 | tf_op jit(solution)/shard_map/ppermute | solution.py:259
  43.2 17.3 %collective-permute-start.10 = (bf16[2,608,128]{2,1,0:T(8,128)(2,1)S(1)}, bf16[2,608,128]{2,1,0:T(8,128)(2,1)S(1)}, u32[]{:S(2)}, u32[]{:S(2)}) collective-permute-start(bf16[2,608,128]{2,1,0:T(8,128)(2,1)S(1)} %collective-permute-done.8.refs_5_), channel_id=1, source_target_pairs={{0,8},{1,9},{2,10},{3,11},{4,12},{5,13},{6,14},{7,15},{8,0},{9,1},... | collective-permute-start | bytes 933896 | tf_op jit(solution)/shard_map/ppermute | solution.py:259
  47.5 19.9 %collective-permute-start.11 = (bf16[2,608,128]{2,1,0:T(8,128)(2,1)S(1)}, bf16[2,608,128]{2,1,0:T(8,128)(2,1)S(1)}, u32[]{:S(2)}, u32[]{:S(2)}) collective-permute-start(bf16[2,608,128]{2,1,0:T(8,128)(2,1)S(1)} %collective-permute-done.7.refs_4_.refs_1_), channel_id=1, source_target_pairs={{0,16},{1,17},{2,18},{3,19},{4,20},{5,21},{6,22},{7,23},{8,24},{9,... | collective-permute-start | bytes 933896 | tf_op jit(solution)/shard_map/ppermute | solution.py:259
  53.8 11.2 %collective-permute-start.27 = (bf16[1152,128]{1,0:T(8,128)(2,1)S(1)}, bf16[1152,128]{1,0:T(8,128)(2,1)S(1)}, u32[]{:S(2)}, u32[]{:S(2)}) collective-permute-start(bf16[1152,128]{1,0:T(8,128)(2,1)S(1)} %collective-permute-done.20.refs_6_.refs_12_), channel_id=1, source_target_pairs={{0,16},{1,17},{2,18},{3,19},{4,20},{5,21},{6,22},{7,23},{8,24},{9,... | collective-permute-start | bytes 884744 | tf_op jit(solution)/shard_map/ppermute | solution.py:259
  55.1 11.8 %collective-permute-start.25 = (bf16[1152,128]{1,0:T(8,128)(2,1)S(1)}, bf16[1152,128]{1,0:T(8,128)(2,1)S(1)}, u32[]{:S(2)}, u32[]{:S(2)}) collective-permute-start(bf16[1152,128]{1,0:T(8,128)(2,1)S(1)} %hold_own.1), channel_id=1, source_target_pairs={{0,8},{1,9},{2,10},{3,11},{4,12},{5,13},{6,14},{7,15},{8,0},{9,1},... | collective-permute-start | bytes 884744 | tf_op jit(solution)/shard_map/ppermute | solution.py:259
  60.5 19.8 %collective-permute-start.23 = (bf16[1152,128]{1,0:T(8,128)(2,1)S(1)}, bf16[1152,128]{1,0:T(8,128)(2,1)S(1)}, u32[]{:S(2)}, u32[]{:S(2)}) collective-permute-start(bf16[1152,128]{1,0:T(8,128)(2,1)S(1)} %collective-permute-done.15.refs_11_.refs_8_), channel_id=1, source_target_pairs={{0,16},{1,17},{2,18},{3,19},{4,20},{5,21},{6,22},{7,23},{8,24},{9,... | collective-permute-start | bytes 884744 | tf_op jit(solution)/shard_map/ppermute | solution.py:259
  61.7 16.0 %collective-permute-start.21 = (bf16[1152,128]{1,0:T(8,128)(2,1)S(1)}, bf16[1152,128]{1,0:T(8,128)(2,1)S(1)}, u32[]{:S(2)}, u32[]{:S(2)}) collective-permute-start(bf16[1152,128]{1,0:T(8,128)(2,1)S(1)} %collective-permute-done.18.refs_9_), channel_id=1, source_target_pairs={{0,8},{1,9},{2,10},{3,11},{4,12},{5,13},{6,14},{7,15},{8,0},{9,1},... | collective-permute-start | bytes 884744 | tf_op jit(solution)/shard_map/ppermute | solution.py:259
  65.0 14.2 %collective-permute-start.24 = (bf16[1152,128]{1,0:T(8,128)(2,1)S(1)}, bf16[1152,128]{1,0:T(8,128)(2,1)S(1)}, u32[]{:S(2)}, u32[]{:S(2)}) collective-permute-start(bf16[1152,128]{1,0:T(8,128)(2,1)S(1)} %collective-permute-done.18.refs_9_), channel_id=1, source_target_pairs={{0,16},{1,17},{2,18},{3,19},{4,20},{5,21},{6,22},{7,23},{8,24},{9,... | collective-permute-start | bytes 884744 | tf_op jit(solution)/shard_map/ppermute | solution.py:259
  66.8 12.9 %collective-permute-start.28 = (bf16[1152,128]{1,0:T(8,128)(2,1)S(1)}, bf16[1152,128]{1,0:T(8,128)(2,1)S(1)}, u32[]{:S(2)}, u32[]{:S(2)}) collective-permute-start(bf16[1152,128]{1,0:T(8,128)(2,1)S(1)} %collective-permute-done.27.refs_4_.refs_20_), channel_id=1, source_target_pairs={{0,1},{1,0},{2,3},{3,2},{4,5},{5,4},{6,7},{7,6},{8,9},{9,8},{10,11... | collective-permute-start | bytes 884744 | tf_op jit(solution)/shard_map/ppermute | solution.py:259
  67.4 12.3 %collective-permute-start.26 = (bf16[1152,128]{1,0:T(8,128)(2,1)S(1)}, bf16[1152,128]{1,0:T(8,128)(2,1)S(1)}, u32[]{:S(2)}, u32[]{:S(2)}) collective-permute-start(bf16[1152,128]{1,0:T(8,128)(2,1)S(1)} %collective-permute-done.25.refs_7_.refs_18_), channel_id=1, source_target_pairs={{0,1},{1,0},{2,3},{3,2},{4,5},{5,4},{6,7},{7,6},{8,9},{9,8},{10,11... | collective-permute-start | bytes 884744 | tf_op jit(solution)/shard_map/ppermute | solution.py:259
  77.8 6.7 %collective-permute-start.19 = (bf16[1152,128]{1,0:T(8,128)(2,1)S(1)}, bf16[1152,128]{1,0:T(8,128)(2,1)S(1)}, u32[]{:S(2)}, u32[]{:S(2)}) collective-permute-start(bf16[1152,128]{1,0:T(8,128)(2,1)S(1)} %hold_first.1), channel_id=1, source_target_pairs={{0,8},{1,9},{2,10},{3,11},{4,12},{5,13},{6,14},{7,15},{8,0},{9,1},... | collective-permute-start | bytes 884744 | tf_op jit(solution)/shard_map/ppermute | solution.py:259
  79.2 6.7 %collective-permute-start.22 = (bf16[1152,128]{1,0:T(8,128)(2,1)S(1)}, bf16[1152,128]{1,0:T(8,128)(2,1)S(1)}, u32[]{:S(2)}, u32[]{:S(2)}) collective-permute-start(bf16[1152,128]{1,0:T(8,128)(2,1)S(1)} %hold_first.1), channel_id=1, source_target_pairs={{0,16},{1,17},{2,18},{3,19},{4,20},{5,21},{6,22},{7,23},{8,24},{9,... | collective-permute-start | bytes 884744 | tf_op jit(solution)/shard_map/ppermute | solution.py:259
  79.8 6.2 %collective-permute-start.16 = (bf16[2048,768]{1,0:T(8,128)(2,1)}, bf16[2048,768]{1,0:T(8,128)(2,1)S(1)}, u32[]{:S(2)}, u32[]{:S(2)}) collective-permute-start(bf16[2048,768]{1,0:T(8,128)(2,1)} %get-tuple-element.80.refs_1_), channel_id=1, source_target_pairs={{0,4},{1,5},{2,6},{3,7},{4,0},{5,1},{6,2},{7,3},{8,12},{9,13},{10,... | collective-permute-start | bytes 9437192 | tf_op jit(solution)/shard_map/ppermute | solution.py:259
  101.9 8.3 %collective-permute-start.30 = (bf16[2048,768]{1,0:T(8,128)(2,1)}, bf16[2048,768]{1,0:T(8,128)(2,1)S(1)}, u32[]{:S(2)}, u32[]{:S(2)}) collective-permute-start(bf16[2048,768]{1,0:T(8,128)(2,1)} %get-tuple-element.86.refs_4_), channel_id=1, source_target_pairs={{0,4},{1,5},{2,6},{3,7},{4,0},{5,1},{6,2},{7,3},{8,12},{9,13},{10,... | collective-permute-start | bytes 9437192 | tf_op jit(solution)/shard_map/ppermute | solution.py:259
  102.0 16.2 %collective-permute-start.34 = (bf16[2,1152,128]{2,1,0:T(8,128)(2,1)S(1)}, bf16[2,1152,128]{2,1,0:T(8,128)(2,1)S(1)}, u32[]{:S(2)}, u32[]{:S(2)}) collective-permute-start(bf16[2,1152,128]{2,1,0:T(8,128)(2,1)S(1)} %get-tuple-element.97), channel_id=1, source_target_pairs={{0,8},{1,9},{2,10},{3,11},{4,12},{5,13},{6,14},{7,15},{8,0},{9,1},... | collective-permute-start | bytes 1769480 | tf_op jit(solution)/shard_map/ppermute | solution.py:259
  103.0 16.6 %collective-permute-start.32 = (bf16[2,1152,128]{2,1,0:T(8,128)(2,1)S(1)}, bf16[2,1152,128]{2,1,0:T(8,128)(2,1)S(1)}, u32[]{:S(2)}, u32[]{:S(2)}) collective-permute-start(bf16[2,1152,128]{2,1,0:T(8,128)(2,1)S(1)} %get-tuple-element.93), channel_id=1, source_target_pairs={{0,16},{1,17},{2,18},{3,19},{4,20},{5,21},{6,22},{7,23},{8,24},{9,... | collective-permute-start | bytes 1769480 | tf_op jit(solution)/shard_map/ppermute | solution.py:259
  109.0 16.5 %collective-permute-start.29 = (bf16[2048,768]{1,0:T(8,128)(2,1)}, bf16[2048,768]{1,0:T(8,128)(2,1)S(1)}, u32[]{:S(2)}, u32[]{:S(2)}) collective-permute-start(bf16[2048,768]{1,0:T(8,128)(2,1)} %mlp_out.1.refs_9_.refs_3_), channel_id=1, source_target_pairs={{0,4},{1,5},{2,6},{3,7},{4,0},{5,1},{6,2},{7,3},{8,12},{9,13},{10,... | collective-permute-start | bytes 9437192 | tf_op jit(solution)/shard_map/ppermute | solution.py:259
  109.0 24.2 %collective-permute-start.31 = (bf16[2,1152,128]{2,1,0:T(8,128)(2,1)S(1)}, bf16[2,1152,128]{2,1,0:T(8,128)(2,1)S(1)}, u32[]{:S(2)}, u32[]{:S(2)}) collective-permute-start(bf16[2,1152,128]{2,1,0:T(8,128)(2,1)S(1)} %get-tuple-element.91), channel_id=1, source_target_pairs={{0,16},{1,17},{2,18},{3,19},{4,20},{5,21},{6,22},{7,23},{8,24},{9,... | collective-permute-start | bytes 1769480 | tf_op jit(solution)/shard_map/ppermute | solution.py:259
  110.2 22.9 %collective-permute-start.36 = (bf16[2,1152,128]{2,1,0:T(8,128)(2,1)S(1)}, bf16[2,1152,128]{2,1,0:T(8,128)(2,1)S(1)}, u32[]{:S(2)}, u32[]{:S(2)}) collective-permute-start(bf16[2,1152,128]{2,1,0:T(8,128)(2,1)S(1)} %get-tuple-element.104), channel_id=1, source_target_pairs={{0,8},{1,9},{2,10},{3,11},{4,12},{5,13},{6,14},{7,15},{8,0},{9,1},... | collective-permute-start | bytes 1769480 | tf_op jit(solution)/shard_map/ppermute | solution.py:259
  118.3 25.3 %collective-permute-start.35 = (bf16[2,1152,128]{2,1,0:T(8,128)(2,1)S(1)}, bf16[2,1152,128]{2,1,0:T(8,128)(2,1)S(1)}, u32[]{:S(2)}, u32[]{:S(2)}) collective-permute-start(bf16[2,1152,128]{2,1,0:T(8,128)(2,1)S(1)} %aEm.1.refs_2_), channel_id=1, source_target_pairs={{0,16},{1,17},{2,18},{3,19},{4,20},{5,21},{6,22},{7,23},{8,24},{9,... | collective-permute-start | bytes 1769480 | tf_op jit(solution)/shard_map/ppermute | solution.py:259
  119.8 23.8 %collective-permute-start.33 = (bf16[2,1152,128]{2,1,0:T(8,128)(2,1)S(1)}, bf16[2,1152,128]{2,1,0:T(8,128)(2,1)S(1)}, u32[]{:S(2)}, u32[]{:S(2)}) collective-permute-start(bf16[2,1152,128]{2,1,0:T(8,128)(2,1)S(1)} %aOm.1.refs_3_), channel_id=1, source_target_pairs={{0,8},{1,9},{2,10},{3,11},{4,12},{5,13},{6,14},{7,15},{8,0},{9,1},... | collective-permute-start | bytes 1769480 | tf_op jit(solution)/shard_map/ppermute | solution.py:259
  143.8 27.6 %collective-permute-start.37 = (bf16[2048,768]{1,0:T(8,128)(2,1)}, bf16[2048,768]{1,0:T(8,128)(2,1)S(1)}, u32[]{:S(2)}, u32[]{:S(2)}) collective-permute-start(bf16[2048,768]{1,0:T(8,128)(2,1)} %get-tuple-element.105.refs_6_), channel_id=1, source_target_pairs={{0,4},{1,5},{2,6},{3,7},{4,0},{5,1},{6,2},{7,3},{8,12},{9,13},{10,... | collective-permute-start | bytes 9437192 | tf_op jit(solution)/shard_map/ppermute | solution.py:259
  143.9 9.8 %collective-permute-start.40 = (bf16[2,608,128]{2,1,0:T(8,128)(2,1)S(1)}, bf16[2,608,128]{2,1,0:T(8,128)(2,1)S(1)}, u32[]{:S(2)}, u32[]{:S(2)}) collective-permute-start(bf16[2,608,128]{2,1,0:T(8,128)(2,1)S(1)} %get-tuple-element.110), channel_id=1, source_target_pairs={{0,8},{1,9},{2,10},{3,11},{4,12},{5,13},{6,14},{7,15},{8,0},{9,1},... | collective-permute-start | bytes 933896 | tf_op jit(solution)/shard_map/ppermute | solution.py:259
  145.1 9.7 %collective-permute-start.39 = (bf16[2,608,128]{2,1,0:T(8,128)(2,1)S(1)}, bf16[2,608,128]{2,1,0:T(8,128)(2,1)S(1)}, u32[]{:S(2)}, u32[]{:S(2)}) collective-permute-start(bf16[2,608,128]{2,1,0:T(8,128)(2,1)S(1)} %get-tuple-element.109), channel_id=1, source_target_pairs={{0,16},{1,17},{2,18},{3,19},{4,20},{5,21},{6,22},{7,23},{8,24},{9,... | collective-permute-start | bytes 933896 | tf_op jit(solution)/shard_map/ppermute | solution.py:259
  146.3 24.8 %collective-permute-start.46 = (bf16[2,1152,128]{2,1,0:T(8,128)(2,1)S(1)}, bf16[2,1152,128]{2,1,0:T(8,128)(2,1)S(1)}, u32[]{:S(2)}, u32[]{:S(2)}) collective-permute-start(bf16[2,1152,128]{2,1,0:T(8,128)(2,1)S(1)} %get-tuple-element.119), channel_id=1, source_target_pairs={{0,1},{1,0},{2,3},{3,2},{4,5},{5,4},{6,7},{7,6},{8,9},{9,8},{10,11... | collective-permute-start | bytes 1769480 | tf_op jit(solution)/shard_map/ppermute | solution.py:259
  152.0 9.2 %collective-permute-start.38 = (bf16[2,608,128]{2,1,0:T(8,128)(2,1)S(1)}, bf16[2,608,128]{2,1,0:T(8,128)(2,1)S(1)}, u32[]{:S(2)}, u32[]{:S(2)}) collective-permute-start(bf16[2,608,128]{2,1,0:T(8,128)(2,1)S(1)} %get-tuple-element.107), channel_id=1, source_target_pairs={{0,16},{1,17},{2,18},{3,19},{4,20},{5,21},{6,22},{7,23},{8,24},{9,... | collective-permute-start | bytes 933896 | tf_op jit(solution)/shard_map/ppermute | solution.py:259
  154.9 10.4 %collective-permute-start.41 = (bf16[2,608,128]{2,1,0:T(8,128)(2,1)S(1)}, bf16[2,608,128]{2,1,0:T(8,128)(2,1)S(1)}, u32[]{:S(2)}, u32[]{:S(2)}) collective-permute-start(bf16[2,608,128]{2,1,0:T(8,128)(2,1)S(1)} %aOa.1), channel_id=1, source_target_pairs={{0,8},{1,9},{2,10},{3,11},{4,12},{5,13},{6,14},{7,15},{8,0},{9,1},... | collective-permute-start | bytes 933896 | tf_op jit(solution)/shard_map/ppermute | solution.py:259
  156.4 21.6 %collective-permute-start.42 = (bf16[2,608,128]{2,1,0:T(8,128)(2,1)S(1)}, bf16[2,608,128]{2,1,0:T(8,128)(2,1)S(1)}, u32[]{:S(2)}, u32[]{:S(2)}) collective-permute-start(bf16[2,608,128]{2,1,0:T(8,128)(2,1)S(1)} %get-tuple-element.115), channel_id=1, source_target_pairs={{0,8},{1,9},{2,10},{3,11},{4,12},{5,13},{6,14},{7,15},{8,0},{9,1},... | collective-permute-start | bytes 933896 | tf_op jit(solution)/shard_map/ppermute | solution.py:259
  161.2 16.7 %collective-permute-start.43 = (bf16[2,608,128]{2,1,0:T(8,128)(2,1)S(1)}, bf16[2,608,128]{2,1,0:T(8,128)(2,1)S(1)}, u32[]{:S(2)}, u32[]{:S(2)}) collective-permute-start(bf16[2,608,128]{2,1,0:T(8,128)(2,1)S(1)} %aEa.1.refs_3_.refs_4_), channel_id=1, source_target_pairs={{0,16},{1,17},{2,18},{3,19},{4,20},{5,21},{6,22},{7,23},{8,24},{9,... | collective-permute-start | bytes 933896 | tf_op jit(solution)/shard_map/ppermute | solution.py:259
  165.4 13.8 %collective-permute-start.44 = (bf16[2,608,128]{2,1,0:T(8,128)(2,1)S(1)}, bf16[2,608,128]{2,1,0:T(8,128)(2,1)S(1)}, u32[]{:S(2)}, u32[]{:S(2)}) collective-permute-start(bf16[2,608,128]{2,1,0:T(8,128)(2,1)S(1)} %soa.1.refs_9_), channel_id=1, source_target_pairs={{0,1},{1,0},{2,3},{3,2},{4,5},{5,4},{6,7},{7,6},{8,9},{9,8},{10,11... | collective-permute-start | bytes 933896 | tf_op jit(solution)/shard_map/ppermute | solution.py:259
  171.4 12.0 %collective-permute-start.47 = (bf16[1152,128]{1,0:T(8,128)(2,1)S(1)}, bf16[1152,128]{1,0:T(8,128)(2,1)S(1)}, u32[]{:S(2)}, u32[]{:S(2)}) collective-permute-start(bf16[1152,128]{1,0:T(8,128)(2,1)S(1)} %get-tuple-element.121), channel_id=1, source_target_pairs={{0,2},{1,3},{2,0},{3,1},{4,6},{5,7},{6,4},{7,5},{8,10},{9,11},{10,... | collective-permute-start | bytes 884744 | tf_op jit(solution)/shard_map/ppermute | solution.py:259
  179.2 5.8 %copy-start.1 = (f32[147456]{0:T(1024)S(1)}, f32[147456]{0:T(1024)}, u32[]{:S(2)}) copy-start(f32[147456]{0:T(1024)} %param.18) | copy-start | bytes 1769476
  179.3 5.8 %copy-start.2 = (f32[147456]{0:T(1024)S(1)}, f32[147456]{0:T(1024)}, u32[]{:S(2)}) copy-start(f32[147456]{0:T(1024)} %param.19) | copy-start | bytes 1769476
  179.3 5.8 %copy-start.3 = (f32[147456]{0:T(1024)S(1)}, f32[147456]{0:T(1024)}, u32[]{:S(2)}) copy-start(f32[147456]{0:T(1024)} %param.20) | copy-start | bytes 1769476
  183.4 1.6 collective-permute-start.48
  183.5 7.7 %collective-permute-start.45 = (bf16[608,128]{1,0:T(8,128)(2,1)S(1)}, bf16[608,128]{1,0:T(8,128)(2,1)S(1)}, u32[]{:S(2)}, u32[]{:S(2)}) collective-permute-start(bf16[608,128]{1,0:T(8,128)(2,1)S(1)} %get-tuple-element.117.refs_2_), channel_id=1, source_target_pairs={{0,2},{1,3},{2,0},{3,1},{4,6},{5,7},{6,4},{7,5},{8,10},{9,11},{10,... | collective-permute-start | bytes 466952 | tf_op jit(solution)/shard_map/ppermute | solution.py:259
  185.1 6.8 %copy-start.8 = (f32[288]{0:T(512)S(1)}, f32[288]{0:T(512)}, u32[]{:S(2)}) copy-start(f32[288]{0:T(512)} %param.23) | copy-start | bytes 3460
  185.1 6.8 %copy-start.9 = (f32[288]{0:T(512)S(1)}, f32[288]{0:T(512)}, u32[]{:S(2)}) copy-start(f32[288]{0:T(512)} %param.22) | copy-start | bytes 3460
  185.1 7.6 %copy-start = (f32[3,128]{1,0:T(4,128)S(1)}, f32[3,128]{1,0:T(4,128)}, u32[]{:S(2)}) copy-start(f32[3,128]{1,0:T(4,128)} %pad_bitcast_fusion.2.refs_3_.refs_7_) | copy-start | bytes 4612
  185.1 7.6 %copy-start.4 = (f32[73728]{0:T(1024)S(1)}, f32[73728]{0:T(1024)}, u32[]{:S(2)}) copy-start(f32[73728]{0:T(1024)} %param.15) | copy-start | bytes 884740
  185.1 7.6 %copy-start.5 = (f32[73728]{0:T(1024)S(1)}, f32[73728]{0:T(1024)}, u32[]{:S(2)}) copy-start(f32[73728]{0:T(1024)} %param.16) | copy-start | bytes 884740
  185.2 7.6 %copy-start.6 = (f32[73728]{0:T(1024)S(1)}, f32[73728]{0:T(1024)}, u32[]{:S(2)}) copy-start(f32[73728]{0:T(1024)} %param.17) | copy-start | bytes 884740
  191.3 1.5 collective-permute-start.49
  191.4 1.4 collective-permute-start.50
